TPU v7x, 32 devices: a whole 2x2x4 slice. The times are simulated.
32 devices in a mesh: vocab: 8 (over z, y), tok: 4 (over x, core).
Axes of the slice: x: 2, y: 2, z: 4, core: 2. Of those that a mesh axis runs over, the one named last changes fastest.
Arguments:
- hidden: bfloat16 [512, 8192], P('tok', 'vocab'), may hold values from -16 to 16
- head: bfloat16 [4096, 8192], P(('vocab', 'tok')), may hold values from -1 to 1
- factor_rows: bfloat16 [512, 64], P('vocab'), may hold values from -2 to 2
- factor_basis: bfloat16 [64, 8192], replicated, may hold values from -0.0625 to 0.0625
- targets: int32 [512], P('tok'), may hold values from 0 to 4607
- loss_mask: int32 [512], P('tok'), may hold values 0 or 1
Outputs:
- hidden_grad: bfloat16 [512, 8192], P('tok', 'vocab')
- rows_grad: float32 [512, 64], P('vocab')
- basis_grad: float32 [64, 8192], P(None, 'vocab')
All inputs are finite; a program needn't handle non-finite values. No bound on the sum of `loss_mask` on one device may be relied on, other than what follows from the above.
Results may differ from a plain program's by a relative error of at most 0.0095.
Values may be sent and summed in bfloat16 or wider, within the bound.
No kernel may reach another device: no remote copies, remote signals or barrier semaphores. Data moves between devices by JAX's collectives and lax.ppermute only.
A program may use at most 64 MiB of HBM per device.

v0:
```python
import jax
import jax.numpy as jnp
from jax import lax
from jax.sharding import PartitionSpec as P

loss_scale = 64.0


def on_device(hidden, head, factor_rows, factor_basis, targets, loss_mask):
    n_vocab = lax.axis_size("vocab")
    n_tok = lax.axis_size("tok")
    vocab_index = lax.axis_index("vocab")
    rows_here = head.shape[0] * n_tok
    new_here = factor_rows.shape[0]
    width_here = hidden.shape[1]
    contract_last = (((1,), (1,)), ((), ()))
    contract_first = (((0,), (0,)), ((), ()))
    contract_cross = (((0,), (1,)), ((), ()))
    gathered = lax.all_gather(hidden, "vocab", axis=1, tiled=True)
    head_full = lax.all_gather(head, "tok", axis=0, tiled=True)
    frozen = lax.dot_general(gathered, head_full, contract_last, preferred_element_type=jnp.float32)
    hidden_basis = lax.dot_general(
        gathered, factor_basis, contract_last, preferred_element_type=jnp.float32
    ).astype(jnp.bfloat16)
    fresh_logits = lax.dot_general(
        hidden_basis, factor_rows, contract_last, preferred_element_type=jnp.float32
    )
    local_max = jnp.maximum(jnp.max(frozen, axis=1), jnp.max(fresh_logits, axis=1))
    row_top = lax.pmax(local_max, "vocab")
    local_sum = jnp.sum(jnp.exp(frozen - row_top[:, None]), axis=1) + jnp.sum(
        jnp.exp(fresh_logits - row_top[:, None]), axis=1
    )
    sum_exp = lax.psum(local_sum, "vocab")
    frozen_prob = jnp.exp(frozen - row_top[:, None]) / sum_exp[:, None]
    fresh_prob = jnp.exp(fresh_logits - row_top[:, None]) / sum_exp[:, None]
    frozen_offset = targets - vocab_index * rows_here
    fresh_offset = targets - rows_here * n_vocab - vocab_index * new_here
    frozen_hit = (
        lax.broadcasted_iota(jnp.int32, frozen.shape, 1) == frozen_offset[:, None]
    ).astype(jnp.float32)
    fresh_hit = (
        lax.broadcasted_iota(jnp.int32, fresh_logits.shape, 1) == fresh_offset[:, None]
    ).astype(jnp.float32)
    weight_row = loss_scale * loss_mask.astype(jnp.float32)[:, None]
    frozen_grad = (weight_row * (frozen_prob - frozen_hit)).astype(jnp.bfloat16)
    fresh_grad = (weight_row * (fresh_prob - fresh_hit)).astype(jnp.bfloat16)
    mix_term = jnp.dot(fresh_grad, factor_rows, preferred_element_type=jnp.float32)
    mix_total = lax.psum(mix_term, "vocab").astype(jnp.bfloat16)
    grad_part = lax.psum_scatter(
        lax.dot_general(head_full, frozen_grad, contract_cross, preferred_element_type=jnp.float32),
        "vocab",
        scatter_dimension=0,
        tiled=True,
    )
    basis_cols = lax.dynamic_slice_in_dim(factor_basis, vocab_index * width_here, width_here, 1)
    hidden_grad = (
        grad_part.T + jnp.dot(mix_total, basis_cols, preferred_element_type=jnp.float32)
    ).astype(jnp.bfloat16)
    rows_term = lax.dot_general(
        fresh_grad, hidden_basis, contract_first, preferred_element_type=jnp.float32
    )
    basis_term = lax.dot_general(
        mix_total, hidden, contract_first, preferred_element_type=jnp.float32
    )
    rows_grad, basis_grad = (
        lax.psum(rows_term.astype(jnp.bfloat16), "tok").astype(jnp.float32),
        lax.psum(basis_term.astype(jnp.bfloat16), "tok").astype(jnp.float32),
    )
    return (hidden_grad, rows_grad, basis_grad)


def solution(mesh):
    in_specs = (
        P("tok", "vocab"),
        P(("vocab", "tok"), None),
        P("vocab", None),
        P(),
        P("tok"),
        P("tok"),
    )
    out_specs = (P("tok", "vocab"), P("vocab", None), P(None, "vocab"))
    return jax.shard_map(
        on_device, mesh=mesh, in_specs=in_specs, out_specs=out_specs, check_vma=False
    )
```

profile of v0, /device:TPU:0, one launch (start us, length us, event | category | flops | bytes accessed | tf_op | source)
XLA Modules:
  0.0 331.2 jit_solution(12281896518718889513)
XLA Ops:
  7.2 0.0 copy-start
  7.2 0.0 copy-start.2
  7.2 0.0 all-gather.3.cloned.1.call-start
  7.2 0.7 all-gather.3.cloned.1.call-update
  7.9 0.0 all-gather.5.cloned.1.call-start
  8.0 0.7 all-gather.5.cloned.1.call-update
  8.7 0.0 all-reduce.2.cloned.1.call-start
  8.7 0.7 convert_multiply_fusion
  9.4 0.7 add_subtract_fusion
  10.0 52.2 %all-gather.3.cloned.1.call-done = bf16[128,8192]{1,0:T(8,128)(2,1)} async-done(((bf16[128,1024]{1,0:T(8,128)(2,1)}), bf16[128,8192]{1,0:T(8,128)(2,1)}) %all-gather.3.cloned.1.call-update) | async-done | bytes 2097168 | tf_op jit(solution)/shard_map/all_gather | solution.py:19
  62.2 0.0 copy-done
  62.2 2.4 convolution_convert_fusion.2
  64.7 0.1 fusion.12
  64.8 55.8 %all-gather.5.cloned.1.call-done = bf16[512,8192]{1,0:T(8,128)(2,1)} async-done(((bf16[128,8192]{1,0:T(8,128)(2,1)}), bf16[512,8192]{1,0:T(8,128)(2,1)}) %all-gather.5.cloned.1.call-update) | async-done | bytes 8388624 | tf_op jit(solution)/shard_map/all_gather | solution.py:20
  120.6 7.0 %fusion.11 = (f32[128]{0:T(128)S(1)}, f32[128,512]{1,0:T(8,128)S(1)}) fusion(bf16[128,8192]{1,0:T(8,128)(2,1)} %all-gather.3.cloned.1.call-done, bf16[512,8192]{1,0:T(8,128)(2,1)} %all-gather.5.cloned.1.call-done), kind=kOutput, calls=%fused_computation.25 | convolution fusion | flops 1073807232 | bytes 10748416 | tf_op jit(solution)/shard_map/dot_general | solution.py:21
  127.6 21.4 %pmax.7 = f32[128]{0:T(128)S(1)} all-reduce(f32[128]{0:T(128)S(1)} %max.5), channel_id=1, replica_groups=mesh['vocab'=8,'tok'=4] {'vocab'}, use_global_device_ids=true, to_apply=%region_2.0 | all-reduce | flops 128 | bytes 1024 | tf_op jit(solution)/shard_map/pmax | solution.py:29
  149.0 0.2 fusion.1
  149.2 17.1 %psum.28 = f32[128]{0:T(128)S(1)} all-reduce(f32[128]{0:T(128)S(1)} %add.20), channel_id=1, replica_groups=mesh['vocab'=8,'tok'=4] {'vocab'}, use_global_device_ids=true, to_apply=%region_5.0 | all-reduce | flops 128 | bytes 1024 | tf_op jit(solution)/shard_map/psum | solution.py:33
  166.4 0.2 fusion.13
  166.6 34.9 %psum.29 = bf16[128,64]{0,1:T(8,128)(2,1)S(1)} all-reduce(f32[128,64]{0,1:T(8,128)S(1)} %fusion.13), channel_id=1, replica_groups=mesh['vocab'=8,'tok'=4] {'vocab'}, use_global_device_ids=true, to_apply=%region_7.0 | all-reduce | flops 8192 | bytes 49152 | tf_op jit(solution)/shard_map/psum | solution.py:48
  201.4 0.8 convolution_convert_fusion
  202.3 0.0 all-reduce.2.cloned.1.call-update
  202.3 0.0 reduce-scatter.2.cloned.1.call-start
  202.3 6.7 %convolution_bitcast_fusion = f32[8192,128]{0,1:T(8,128)} fusion(bf16[512,8192]{1,0:T(8,128)(2,1)} %all-gather.5.cloned.1.call-done, f32[128,512]{1,0:T(8,128)S(1)} %get-tuple-element.6, s32[128]{0:T(128)S(1)} %get-tuple-element.4, f32[128]{0:T(128)S(1)} %psum.28, f32[128]{0:T(128)S(1)} %pmax.7, f32[128]{0:T(128)S(1)} %convert_multiply_fusion), kind=kOutput, calls=%fused_computation | convolution fusion | flops 1074200576 | bytes 12847104 | tf_op jit(solution)/shard_map/dot_general | solution.py:50
  209.1 0.0 reduce-scatter.2.cloned.1.call-update
  209.1 0.1 convolution_convert_fusion.1
  209.2 10.2 %psum.30 = bf16[64,64]{1,0:T(8,128)(2,1)S(1)} all-reduce(bf16[64,64]{1,0:T(8,128)(2,1)S(1)} %convolution_convert_fusion.1), channel_id=1, replica_groups=mesh['vocab'=8,'tok'=4] {'tok'}, use_global_device_ids=true, to_apply=%region_8.0 | all-reduce | flops 4096 | bytes 16384 | tf_op jit(solution)/shard_map/psum | solution.py:66
  219.5 0.6 convert_element_type.45
  220.1 10.1 %all-reduce.2.cloned.1.call-done = bf16[64,1024]{1,0:T(8,128)(2,1)} async-done(((bf16[64,1024]{1,0:T(8,128)(2,1)}), bf16[64,1024]{1,0:T(8,128)(2,1)}) %all-reduce.2.cloned.1.call-update) | async-done | bytes 131088 | tf_op jit(solution)/shard_map/psum | solution.py:67
  230.2 1.6 convert_element_type.47
  231.8 90.8 %reduce-scatter.2.cloned.1.call-done = f32[1024,128]{0,1:T(8,128)} async-done(((f32[8192,128]{0,1:T(8,128)}), f32[1024,128]{0,1:T(8,128)}) %reduce-scatter.2.cloned.1.call-update) | async-done | bytes 524304 | tf_op jit(solution)/shard_map/reduce_scatter | solution.py:49
  322.6 2.0 fusion
  (7 shorter events, 0.1 us)
Async XLA Ops:
  7.2 55.0 %copy-start = (bf16[64,8192]{1,0:T(8,128)(2,1)S(1)}, bf16[64,8192]{1,0:T(8,128)(2,1)}, u32[]{:S(2)}) copy-start(bf16[64,8192]{1,0:T(8,128)(2,1)} %param.9) | copy-start | bytes 3145732
  7.2 57.5 %copy-start.2 = (bf16[64,64]{1,0:T(8,128)(2,1)S(1)}, bf16[64,64]{1,0:T(8,128)(2,1)}, u32[]{:S(2)}) copy-start(bf16[64,64]{1,0:T(8,128)(2,1)} %param.8) | copy-start | bytes 24580
  7.2 55.0 %all-gather.3.cloned.1.call-start = ((), (), s32[]{:S(2)}) async-start(), calls=%async_computation.1 | async-start | bytes 2359296 | tf_op jit(solution)/shard_map/all_gather | solution.py:19
  7.9 112.7 %all-gather.5.cloned.1.call-start = ((), (), s32[]{:S(2)}) async-start(), calls=%async_computation.2 | async-start | bytes 10485760 | tf_op jit(solution)/shard_map/all_gather | solution.py:20
  8.7 221.5 %all-reduce.2.cloned.1.call-start = ((), (), s32[]{:S(2)}) async-start(), calls=%async_computation.4 | async-start | bytes 262144 | tf_op jit(solution)/shard_map/psum | solution.py:67
  64.8 136.6 %copy-start.1 = (bf16[128,1024]{1,0:T(8,128)(2,1)S(1)}, bf16[128,1024]{1,0:T(8,128)(2,1)}, u32[]{:S(2)}) copy-start(bf16[128,1024]{1,0:T(8,128)(2,1)} %param.6) | copy-start | bytes 786436
  202.3 120.3 %reduce-scatter.2.cloned.1.call-start = ((), (), s32[]{:S(2)}) async-start(), calls=%async_computation.3 | async-start | bytes 4718592 | tf_op jit(solution)/shard_map/reduce_scatter | solution.py:49
Sparse Core Ops, SparseCore 0:
  10.2 51.9 all-gather.2
  63.8 56.7 all-gather.4
  202.4 27.7 all-reduce.1
  234.1 88.4 reduce-scatter.1
where the time goes:
time: 332 us; the launch traced here: 331 us
  waiting for transfers between devices  210 us (63%)
  blocking collectives  83.6 us (25%)
  matrix products  19.5 us (6%)
  between operations  13.8 us (4%)
  other arithmetic  3.82 us (1%)
    reduce_scatter x1, waiting for transfers between devices, on_device(): lax.psum_scatter(lax.dot_general(head_full, frozen_grad, contract_cross,...  90.8 us
    all_gather x1, waiting for transfers between devices, on_device(): head_full = lax.all_gather(head, 'tok', axis=0, tiled=True)  55.8 us
    all_gather x1, waiting for transfers between devices, on_device(): gathered = lax.all_gather(hidden, 'vocab', axis=1, tiled=True)  52.2 us
    psum x1, blocking collectives, on_device(): mix_total = lax.psum(mix_term, 'vocab').astype(jnp.bfloat16)  34.9 us
    pmax x1, blocking collectives, on_device(): row_top = lax.pmax(local_max, 'vocab')  21.4 us
    psum x1, blocking collectives, on_device(): sum_exp = lax.psum(local_sum, 'vocab')  17.1 us
    psum x1, blocking collectives, on_device(): lax.psum(rows_term.astype(jnp.bfloat16), 'tok').astype(jnp.float32)  10.2 us
    psum x1, waiting for transfers between devices, on_device(): lax.psum(basis_term.astype(jnp.bfloat16), 'tok').astype(jnp.float32)  10.1 us
  transfers between devices with their start and end apart: 4, of which 4 were waited for; matrix products, arithmetic and copies ran while one was open for 4% of the time, Pallas kernels for 0%

commit v1 on v0

v1 whole, which is shorter than its diff:
```python
import jax
import jax.numpy as jnp
from jax import lax
from jax.sharding import PartitionSpec as P

loss_scale = 64.0
f32 = jnp.float32
bf16 = jnp.bfloat16
contract_last = (((1,), (1,)), ((), ()))
contract_first = (((0,), (0,)), ((), ()))


def dot_last(a, b):
    return lax.dot_general(a, b, contract_last, preferred_element_type=f32)


def dot_first(a, b):
    return lax.dot_general(a, b, contract_first, preferred_element_type=f32)


def swap(value, axis, bit):
    size = lax.axis_size(axis)
    return lax.ppermute(value, axis, [(i, i ^ bit) for i in range(size)])


def swap_core(value):
    return swap(value, "tok", 1)


def swap_x(value):
    return swap(value, "tok", 2)


def swap_y(value):
    return swap(value, "vocab", 1)


def swap_z(value, step):
    return swap(value, "vocab", 2 * step)


def on_few(hidden, head, factor_rows, factor_basis, targets, loss_mask):
    n_z = lax.axis_size("vocab") // 2
    n_tok = lax.axis_size("tok")
    v = lax.axis_index("vocab")
    t = lax.axis_index("tok")
    toks, width = hidden.shape
    rows = head.shape[0]
    new_here = factor_rows.shape[0]
    half = width // 2

    head_other = swap_core(head)
    rows_all = lax.all_gather(factor_rows, "vocab", axis=0, tiled=True)
    token_info = jnp.stack([targets, loss_mask])
    token_info = jnp.concatenate([token_info, swap_x(token_info)], axis=1)
    shards = [hidden] + [swap_z(hidden, k) for k in range(1, n_z)]
    pieces = []
    for shard in shards:
        from_x = swap_x(shard)
        from_y = swap_y(shard)
        diag_a = swap_x(from_y[:, :half])
        diag_b = swap_y(from_x[:, half:])
        pieces.append((from_x, from_y, diag_a, diag_b))

    def weights(dy, dz):
        start = (v ^ (2 * dz + dy)) * width
        cut = lambda a: lax.dynamic_slice_in_dim(a, start, width, 1)
        return jnp.concatenate([cut(head), cut(head_other), cut(factor_basis)], axis=0)

    blocks = [[weights(dy, dz) for dy in range(2)] for dz in range(n_z)]

    own = jnp.zeros((2 * rows + factor_basis.shape[0], toks), f32)
    other = own
    for dz in range(n_z):
        from_x, from_y, diag_a, diag_b = pieces[dz]
        own = own + dot_last(blocks[dz][0], shards[dz])
        own = own + dot_last(blocks[dz][1], from_y)
        other = other + dot_last(blocks[dz][0], from_x)
        other = other + dot_last(blocks[dz][1][:, :half], diag_a)
        other = other + dot_last(blocks[dz][1][:, half:], diag_b)
    both = jnp.concatenate([own, other], axis=1)
    frozen = both[: 2 * rows]
    hidden_basis = both[2 * rows :].astype(bf16)

    def merge(stats):
        top = stats[0][0]
        for s in stats[1:]:
            top = jnp.maximum(top, s[0])
        total = stats[0][1] * jnp.exp(stats[0][0] - top)
        for s in stats[1:]:
            total = total + s[1] * jnp.exp(s[0] - top)
        return jnp.stack([top, total])

    def local(logits):
        top = jnp.max(logits, axis=0)
        return jnp.stack([top, jnp.sum(jnp.exp(logits - top[None, :]), axis=0)])

    def turn(stats):
        return jnp.concatenate([stats[:, toks:], stats[:, :toks]], axis=1)

    mine = local(frozen)
    stat_x = swap_x(mine)
    stat_y = swap_y(mine)
    stat_xy = swap_x(stat_y)
    plane = merge([mine, turn(stat_x), stat_y, turn(stat_xy)])
    fresh = lax.dot_general(
        rows_all, hidden_basis, (((1,), (0,)), ((), ())), preferred_element_type=f32
    )
    stats = merge([plane] + [swap_z(plane, k) for k in range(1, n_z)] + [local(fresh)])
    row_top, sum_exp = stats[0], stats[1]

    weight_row = loss_scale * token_info[1].astype(f32)
    scale_row = weight_row / sum_exp
    row_iota = lax.broadcasted_iota(jnp.int32, (rows, 1), 0)
    row_ids = jnp.concatenate(
        [row_iota + (v * n_tok + t) * rows, row_iota + (v * n_tok + (t ^ 1)) * rows], axis=0
    )
    hit = jnp.where(row_ids == token_info[0][None, :], weight_row[None, :], 0.0)
    grad = (jnp.exp(frozen - row_top[None, :]) * scale_row[None, :] - hit).astype(bf16)
    grad_own, grad_other = grad[:, :toks], grad[:, toks:]

    frozen_rows = rows * n_tok * lax.axis_size("vocab")
    fresh_ids = lax.broadcasted_iota(jnp.int32, (rows_all.shape[0], 1), 0) + frozen_rows
    fresh_hit = jnp.where(fresh_ids == targets[None, :], weight_row[None, :toks], 0.0)
    fresh_grad = (
        jnp.exp(fresh[:, :toks] - row_top[None, :toks]) * scale_row[None, :toks] - fresh_hit
    ).astype(bf16)
    mix_total = dot_first(rows_all, fresh_grad).astype(bf16)
    fresh_here = lax.dynamic_slice_in_dim(fresh_grad, v * new_here, new_here, 0)
    rows_part = dot_last(fresh_here, hidden_basis[:, :toks])
    basis_part = lax.reduce_precision(jnp.dot(mix_total, hidden, preferred_element_type=f32), 8, 7)

    def part(grads, dy, dz, cols=slice(None)):
        return dot_first(grads, blocks[dz][dy][: 2 * rows, cols])

    arrived = []
    for dz in range(n_z - 1, -1, -1):
        diag_a = swap_x(part(grad_other, 1, dz, slice(0, half)).astype(bf16))
        diag_b = swap_y(part(grad_other, 1, dz, slice(half, width)).astype(bf16))
        to_x = part(grad_other, 0, dz) + jnp.pad(diag_b.astype(f32), ((0, 0), (half, 0)))
        to_y = part(grad_own, 1, dz) + jnp.pad(diag_a.astype(f32), ((0, 0), (0, width - half)))
        from_x = swap_x(to_x.astype(bf16))
        from_y = swap_y(to_y.astype(bf16))
        here = part(grad_own, 0, dz) + from_x.astype(f32) + from_y.astype(f32)
        arrived.append(swap_z(here.astype(bf16), dz).astype(f32) if dz else here)

    basis_here = lax.dynamic_slice_in_dim(factor_basis, v * width, width, 1)
    hidden_grad = dot_first(mix_total, basis_here)
    for piece in arrived:
        hidden_grad = hidden_grad + piece
    hidden_grad = hidden_grad.astype(bf16)

    basis_two = basis_part + swap_x(basis_part.astype(bf16)).astype(f32)
    basis_grad = basis_two + swap_core(basis_two)
    rows_two = rows_part + swap_x(rows_part)
    rows_grad = rows_two + swap_core(rows_two)
    return hidden_grad, rows_grad, basis_grad


def on_many(hidden, head, factor_rows, factor_basis, targets, loss_mask):
    n_vocab = lax.axis_size("vocab")
    n_tok = lax.axis_size("tok")
    vocab_index = lax.axis_index("vocab")
    rows_here = head.shape[0] * n_tok
    new_here = factor_rows.shape[0]
    width_here = hidden.shape[1]
    gathered = lax.all_gather(hidden, "vocab", axis=1, tiled=True)
    head_full = lax.all_gather(head, "tok", axis=0, tiled=True)
    frozen = dot_last(gathered, head_full)
    hidden_basis = dot_last(gathered, factor_basis).astype(bf16)
    fresh_logits = dot_last(hidden_basis, factor_rows)
    local_max = jnp.maximum(jnp.max(frozen, axis=1), jnp.max(fresh_logits, axis=1))
    row_top = lax.pmax(local_max, "vocab")
    local_sum = jnp.sum(jnp.exp(frozen - row_top[:, None]), axis=1) + jnp.sum(
        jnp.exp(fresh_logits - row_top[:, None]), axis=1
    )
    sum_exp = lax.psum(local_sum, "vocab")
    frozen_prob = jnp.exp(frozen - row_top[:, None]) / sum_exp[:, None]
    fresh_prob = jnp.exp(fresh_logits - row_top[:, None]) / sum_exp[:, None]
    frozen_offset = targets - vocab_index * rows_here
    fresh_offset = targets - rows_here * n_vocab - vocab_index * new_here
    frozen_hit = (
        lax.broadcasted_iota(jnp.int32, frozen.shape, 1) == frozen_offset[:, None]
    ).astype(f32)
    fresh_hit = (
        lax.broadcasted_iota(jnp.int32, fresh_logits.shape, 1) == fresh_offset[:, None]
    ).astype(f32)
    weight_row = loss_scale * loss_mask.astype(f32)[:, None]
    frozen_grad = (weight_row * (frozen_prob - frozen_hit)).astype(bf16)
    fresh_grad = (weight_row * (fresh_prob - fresh_hit)).astype(bf16)
    mix_term = jnp.dot(fresh_grad, factor_rows, preferred_element_type=f32)
    mix_total = lax.psum(mix_term, "vocab").astype(bf16)
    grad_part = lax.psum_scatter(
        lax.dot_general(
            head_full, frozen_grad, (((0,), (1,)), ((), ())), preferred_element_type=f32
        ),
        "vocab",
        scatter_dimension=0,
        tiled=True,
    )
    basis_cols = lax.dynamic_slice_in_dim(factor_basis, vocab_index * width_here, width_here, 1)
    hidden_grad = (
        grad_part.T + jnp.dot(mix_total, basis_cols, preferred_element_type=f32)
    ).astype(bf16)
    rows_term = dot_first(fresh_grad, hidden_basis)
    basis_term = dot_first(mix_total, hidden)
    rows_grad, basis_grad = (
        lax.psum(rows_term.astype(bf16), "tok").astype(f32),
        lax.psum(basis_term.astype(bf16), "tok").astype(f32),
    )
    return hidden_grad, rows_grad, basis_grad


def solution(mesh):
    in_specs = (
        P("tok", "vocab"),
        P(("vocab", "tok"), None),
        P("vocab", None),
        P(),
        P("tok"),
        P("tok"),
    )
    out_specs = (P("tok", "vocab"), P("vocab", None), P(None, "vocab"))
    few = mesh.shape["vocab"] <= 16 and mesh.shape["tok"] == 4
    return jax.shard_map(
        on_few if few else on_many,
        mesh=mesh,
        in_specs=in_specs,
        out_specs=out_specs,
        check_vma=False,
    )
```

time: 332 us -> 174 us (0.52)
  waiting for transfers between devices: 210 us -> 53 us
  starting transfers between devices: 0.16 us -> 56.5 us
  blocking collectives: 83.6 us -> 30.7 us
  between operations: 13.8 us -> 1.43 us
  local copies, waits for them, and re-layouts: 0.02 us -> 8.61 us
    all_gather x2 -> x0, waiting for transfers between devices: 108 us -> none  [the longest x1 55.8 us: on_device(): head_full = lax.all_gather(head, 'tok', axis=0, tiled=True)]
    reduce_scatter x1 -> x0, waiting for transfers between devices: 90.8 us -> none  [on_device(): lax.psum_scatter(lax.dot_general(head_full, frozen_grad, contract_cross,...]
    psum x3 -> x0, blocking collectives: 62.2 us -> none  [the longest x1 34.9 us: on_device(): mix_total = lax.psum(mix_term, 'vocab').astype(jnp.bfloat16)]
    ppermute x0 -> x50, starting transfers between devices: none -> 56.5 us  [swap(): return lax.ppermute(value, axis, [(i, i ^ bit) for i in range(size)])]
    ppermute x0 -> x50, waiting for transfers between devices: none -> 53 us  [swap(): return lax.ppermute(value, axis, [(i, i ^ bit) for i in range(size)])]
    all_gather x0 -> x1, blocking collectives: none -> 30.7 us  [on_few(): rows_all = lax.all_gather(factor_rows, 'vocab', axis=0, tiled=True)]
    pmax x1 -> x0, blocking collectives: 21.4 us -> none  [on_device(): row_top = lax.pmax(local_max, 'vocab')]
    psum x1 -> x0, waiting for transfers between devices: 10.1 us -> none  [on_device(): lax.psum(basis_term.astype(jnp.bfloat16), 'tok').astype(jnp.float32)]
  transfers between devices with their start and end apart: 4 -> 50, of which waited for: 4 -> 17; matrix products, arithmetic and copies ran while one was open for 4% -> 14% of each run, Pallas kernels for 0% -> 0%
where the time goes in v1:
time: 174 us; the launch traced here: 173 us
  starting transfers between devices  56.5 us (32%)
  waiting for transfers between devices  53 us (30%)
  blocking collectives  30.7 us (18%)
  matrix products  19.3 us (11%)
  local copies, waits for them, and re-layouts  8.61 us (5%)
  other arithmetic  3.67 us (2%)
    ppermute x50, starting transfers between devices, swap(): return lax.ppermute(value, axis, [(i, i ^ bit) for i in range(size)])  56.5 us
    ppermute x50, waiting for transfers between devices, swap(): return lax.ppermute(value, axis, [(i, i ^ bit) for i in range(size)])  53 us
    all_gather x1, blocking collectives, on_few(): rows_all = lax.all_gather(factor_rows, 'vocab', axis=0, tiled=True)  30.7 us
    dot_general x21, matrix products, dot_last(): return lax.dot_general(a, b, contract_last, preferred_element_type=f32)  12.9 us
    dot_general x22, matrix products, dot_first(): return lax.dot_general(a, b, contract_first, preferred_element_type=f32)  5.92 us
    dynamic_slice x3, local copies, waits for them, and re-layouts, weights(): cut = lambda a: lax.dynamic_slice_in_dim(a, start, width, 1)  4.23 us
  transfers between devices with their start and end apart: 50, of which 17 were waited for; matrix products, arithmetic and copies ran while one was open for 14% of the time, Pallas kernels for 0%

profile of v1, /device:TPU:0, one launch (start us, length us, event | category | flops | bytes accessed | tf_op | source)
XLA Modules:
  0.0 173.3 jit_solution(3188251398518749451)
XLA Ops:
  1.1 2.6 %collective-permute-start.1 = (bf16[128,1024]{1,0:T(8,128)(2,1)}, bf16[128,1024]{1,0:T(8,128)(2,1)S(1)}, u32[]{:S(2)}, u32[]{:S(2)}) collective-permute-start(bf16[128,1024]{1,0:T(8,128)(2,1)} %param.6), channel_id=1, source_target_pairs={{0,4},{4,0},{8,12},{12,8},{16,20},{20,16},{24,28},{28,24},{1,5},{5... | collective-permute-start | bytes 786440 | tf_op jit(solution)/shard_map/ppermute | solution.py:23
  3.7 1.6 collective-permute-start.2
  5.3 2.6 %collective-permute-start.4 = (bf16[128,1024]{1,0:T(8,128)(2,1)}, bf16[128,1024]{1,0:T(8,128)(2,1)}, u32[]{:S(2)}, u32[]{:S(2)}) collective-permute-start(bf16[128,1024]{1,0:T(8,128)(2,1)} %param.6), channel_id=1, source_target_pairs={{0,16},{4,20},{8,24},{12,28},{16,0},{20,4},{24,8},{28,12},{1,17},{... | collective-permute-start | bytes 786440 | tf_op jit(solution)/shard_map/ppermute | solution.py:23
  8.6 1.5 collective-permute-start.26
  10.1 2.1 %collective-permute-done.26 = s32[2,128]{1,0:T(2,128)S(1)} collective-permute-done((s32[2,128]{1,0:T(2,128)S(1)}, s32[2,128]{1,0:T(2,128)S(1)}, u32[]{:S(2)}, u32[]{:S(2)}) %collective-permute-start.26) | collective-permute-done | bytes 1056 | tf_op jit(solution)/shard_map/ppermute | solution.py:23
  12.4 1.5 collective-permute-start.8
  13.9 3.7 %collective-permute-done.2 = bf16[128,1024]{1,0:T(8,128)(2,1)} collective-permute-done((bf16[128,1024]{1,0:T(8,128)(2,1)}, bf16[128,1024]{1,0:T(8,128)(2,1)}, u32[]{:S(2)}, u32[]{:S(2)}) %collective-permute-start.2) | collective-permute-done | bytes 262176 | tf_op jit(solution)/shard_map/ppermute | solution.py:23
  17.9 8.9 %collective-permute-done.4 = bf16[128,1024]{1,0:T(8,128)(2,1)} collective-permute-done((bf16[128,1024]{1,0:T(8,128)(2,1)}, bf16[128,1024]{1,0:T(8,128)(2,1)}, u32[]{:S(2)}, u32[]{:S(2)}) %collective-permute-start.4) | collective-permute-done | bytes 262176 | tf_op jit(solution)/shard_map/ppermute | solution.py:23
  26.8 1.5 collective-permute-start.11
  28.3 2.5 %constant_dynamic-slice_fusion.5 = (bf16[128,1024]{1,0:T(8,128)(2,1)}, bf16[128,1024]{1,0:T(8,128)(2,1)S(1)}, bf16[128,1024]{1,0:T(8,128)(2,1)}, bf16[128,1024]{...) fusion(bf16[128,8192]{1,0:T(8,128)(2,1)} %param.7, ...), kind=kLoop, calls=%fused_computation.147 | loop fusion | bytes 4194336 | tf_op jit(solution)/shard_map/dynamic_slice | solution.py:67
  32.0 1.5 collective-permute-start.7
  33.5 2.8 %collective-permute-done.11 = bf16[128,1024]{1,0:T(8,128)(2,1)S(1)} collective-permute-done((bf16[128,1024]{1,0:T(8,128)(2,1)}, bf16[128,1024]{1,0:T(8,128)(2,1)S(1)}, u32[]{:S(2)}, u32[]{:S(2)}) %collective-permute-start.11) | collective-permute-done | bytes 262176 | tf_op jit(solution)/shard_map/ppermute | solution.py:23
  36.3 1.5 collective-permute-start.17
  37.8 30.7 %all_gather.3 = bf16[512,64]{1,0:T(8,128)(2,1)S(1)} all-gather(bf16[64,64]{1,0:T(8,128)(2,1)S(1)} %copy-done.12), channel_id=1, replica_groups=mesh['vocab'=8,'tok'=4] {'vocab'}, dimensions={0}, use_global_device_ids=true | all-gather | bytes 73728 | tf_op jit(solution)/shard_map/all_gather | solution.py:53
  68.5 1.5 constant_dynamic-slice_fusion.3
  73.4 2.1 %collective-permute-start.13 = (bf16[128,512]{1,0:T(8,128)(2,1)S(1)}, bf16[128,512]{1,0:T(8,128)(2,1)S(1)}, u32[]{:S(2)}, u32[]{:S(2)}) collective-permute-start(bf16[128,512]{1,0:T(8,128)(2,1)S(1)} %slice.251), channel_id=1, source_target_pairs={{0,4},{4,0},{8,12},{12,8},{16,20},{20,16},{24,28},{28,24},{1,5},{5... | collective-permute-start | bytes 393224 | tf_op jit(solution)/shard_map/ppermute | solution.py:23
  76.4 1.5 collective-permute-start.12
  81.9 1.3 fusion.41
  87.0 1.5 collective-permute-start.18
  88.9 2.1 %collective-permute-start.19 = (bf16[128,512]{1,0:T(8,128)(2,1)S(1)}, bf16[128,512]{1,0:T(8,128)(2,1)S(1)}, u32[]{:S(2)}, u32[]{:S(2)}) collective-permute-start(bf16[128,512]{1,0:T(8,128)(2,1)S(1)} %slice.259), channel_id=1, source_target_pairs={{0,4},{4,0},{8,12},{12,8},{16,20},{20,16},{24,28},{28,24},{1,5},{5... | collective-permute-start | bytes 393224 | tf_op jit(solution)/shard_map/ppermute | solution.py:23
  97.8 2.1 %collective-permute-start.21 = (f32[2,256]{1,0:T(2,128)S(1)}, f32[2,256]{1,0:T(2,128)S(1)}, u32[]{:S(2)}, u32[]{:S(2)}) collective-permute-start(f32[2,256]{1,0:T(2,128)S(1)} %pad_maximum_fusion.39), channel_id=1, source_target_pairs={{0,4},{4,0},{8,12},{12,8},{16,20},{20,16},{24,28},{28,24},{1,5},{5... | collective-permute-start | bytes 6152 | tf_op jit(solution)/shard_map/ppermute | solution.py:23
  103.5 1.6 collective-permute-done.22
  105.2 2.2 %collective-permute-start.24 = (f32[2,256]{1,0:T(2,128)S(1)}, f32[2,256]{1,0:T(2,128)S(1)}, u32[]{:S(2)}, u32[]{:S(2)}) collective-permute-start(f32[2,256]{1,0:T(2,128)S(1)} %pad_maximum_fusion.40), channel_id=1, source_target_pairs={{0,16},{4,20},{8,24},{12,28},{16,0},{20,4},{24,8},{28,12},{1,17},{... | collective-permute-start | bytes 6152 | tf_op jit(solution)/shard_map/ppermute | solution.py:23
  107.4 2.2 %collective-permute-start.25 = (f32[2,256]{1,0:T(2,128)S(1)}, f32[2,256]{1,0:T(2,128)S(1)}, u32[]{:S(2)}, u32[]{:S(2)}) collective-permute-start(f32[2,256]{1,0:T(2,128)S(1)} %pad_maximum_fusion.40), channel_id=1, source_target_pairs={{0,24},{4,28},{8,16},{12,20},{16,8},{20,12},{24,0},{28,4},{1,25},{... | collective-permute-start | bytes 6152 | tf_op jit(solution)/shard_map/ppermute | solution.py:23
  109.8 3.0 %collective-permute-done.25 = f32[2,256]{1,0:T(2,128)S(1)} collective-permute-done((f32[2,256]{1,0:T(2,128)S(1)}, f32[2,256]{1,0:T(2,128)S(1)}, u32[]{:S(2)}, u32[]{:S(2)}) %collective-permute-start.25) | collective-permute-done | bytes 2080 | tf_op jit(solution)/shard_map/ppermute | solution.py:23
  132.6 3.8 %collective-permute-done.28 = bf16[128,1024]{1,0:T(8,128)(2,1)S(1)} collective-permute-done((bf16[128,1024]{1,0:T(8,128)(2,1)S(1)}, bf16[128,1024]{1,0:T(8,128)(2,1)S(1)}, u32[]{:S(2)}, u32[]{:S(2)}) %collective-permute-start.28) | collective-permute-done | bytes 262176 | tf_op jit(solution)/shard_map/ppermute | solution.py:23
  138.8 3.2 %collective-permute-done.33 = bf16[128,1024]{1,0:T(8,128)(2,1)S(1)} collective-permute-done((bf16[128,1024]{1,0:T(8,128)(2,1)S(1)}, bf16[128,1024]{1,0:T(8,128)(2,1)S(1)}, u32[]{:S(2)}, u32[]{:S(2)}) %collective-permute-start.33) | collective-permute-done | bytes 262176 | tf_op jit(solution)/shard_map/ppermute | solution.py:23
  142.0 1.3 collective-permute-done.35
  144.7 3.0 %collective-permute-done.38 = bf16[128,1024]{1,0:T(8,128)(2,1)S(1)} collective-permute-done((bf16[128,1024]{1,0:T(8,128)(2,1)S(1)}, bf16[128,1024]{1,0:T(8,128)(2,1)S(1)}, u32[]{:S(2)}, u32[]{:S(2)}) %collective-permute-start.38) | collective-permute-done | bytes 262176 | tf_op jit(solution)/shard_map/ppermute | solution.py:23
  148.4 3.5 %collective-permute-start.31 = (bf16[128,1024]{1,0:T(8,128)(2,1)S(1)}, bf16[128,1024]{1,0:T(8,128)(2,1)S(1)}, u32[]{:S(2)}, u32[]{:S(2)}) collective-permute-start(bf16[128,1024]{1,0:T(8,128)(2,1)S(1)} %fusion.4), channel_id=1, source_target_pairs={{0,24},{4,28},{8,16},{12,20},{16,8},{20,12},{24,0},{28,4},{1,25},{... | collective-permute-start | bytes 786440 | tf_op jit(solution)/shard_map/ppermute | solution.py:23
  155.4 4.2 %collective-permute-done.31 = bf16[128,1024]{1,0:T(8,128)(2,1)S(1)} collective-permute-done((bf16[128,1024]{1,0:T(8,128)(2,1)S(1)}, bf16[128,1024]{1,0:T(8,128)(2,1)S(1)}, u32[]{:S(2)}, u32[]{:S(2)}) %collective-permute-start.31) | collective-permute-done | bytes 262176 | tf_op jit(solution)/shard_map/ppermute | solution.py:23
  159.6 12.6 %collective-permute-done.36 = bf16[128,1024]{1,0:T(8,128)(2,1)S(1)} collective-permute-done((bf16[128,1024]{1,0:T(8,128)(2,1)S(1)}, bf16[128,1024]{1,0:T(8,128)(2,1)S(1)}, u32[]{:S(2)}, u32[]{:S(2)}) %collective-permute-start.36) | collective-permute-done | bytes 262176 | tf_op jit(solution)/shard_map/ppermute | solution.py:23
  (187 shorter events, 54.4 us)
Async XLA Ops:
  0.6 78.2 %collective-permute-start = (bf16[128,8192]{1,0:T(8,128)(2,1)}, bf16[128,8192]{1,0:T(8,128)(2,1)S(1)}, u32[]{:S(2)}, u32[]{:S(2)}) collective-permute-start(bf16[128,8192]{1,0:T(8,128)(2,1)} %param.7), channel_id=1, source_target_pairs={{0,1},{1,0},{2,3},{3,2},{4,5},{5,4},{6,7},{7,6},{8,9},{9,8},{10,11... | collective-permute-start | bytes 6291464 | tf_op jit(solution)/shard_map/ppermute | solution.py:23
  1.1 11.2 %collective-permute-start.1 = (bf16[128,1024]{1,0:T(8,128)(2,1)}, bf16[128,1024]{1,0:T(8,128)(2,1)S(1)}, u32[]{:S(2)}, u32[]{:S(2)}) collective-permute-start(bf16[128,1024]{1,0:T(8,128)(2,1)} %param.6), channel_id=1, source_target_pairs={{0,4},{4,0},{8,12},{12,8},{16,20},{20,16},{24,28},{28,24},{1,5},{5... | collective-permute-start | bytes 786440 | tf_op jit(solution)/shard_map/ppermute | solution.py:23
  3.7 13.8 %collective-permute-start.2 = (bf16[128,1024]{1,0:T(8,128)(2,1)}, bf16[128,1024]{1,0:T(8,128)(2,1)}, u32[]{:S(2)}, u32[]{:S(2)}) collective-permute-start(bf16[128,1024]{1,0:T(8,128)(2,1)} %param.6), channel_id=1, source_target_pairs={{0,8},{4,12},{8,0},{12,4},{16,24},{20,28},{24,16},{28,20},{1,9},{5... | collective-permute-start | bytes 786440 | tf_op jit(solution)/shard_map/ppermute | solution.py:23
  5.3 21.5 %collective-permute-start.4 = (bf16[128,1024]{1,0:T(8,128)(2,1)}, bf16[128,1024]{1,0:T(8,128)(2,1)}, u32[]{:S(2)}, u32[]{:S(2)}) collective-permute-start(bf16[128,1024]{1,0:T(8,128)(2,1)} %param.6), channel_id=1, source_target_pairs={{0,16},{4,20},{8,24},{12,28},{16,0},{20,4},{24,8},{28,12},{1,17},{... | collective-permute-start | bytes 786440 | tf_op jit(solution)/shard_map/ppermute | solution.py:23
  12.2 18.7 %collective-permute-start.6 = (bf16[128,1024]{1,0:T(8,128)(2,1)}, bf16[128,1024]{1,0:T(8,128)(2,1)}, u32[]{:S(2)}, u32[]{:S(2)}) collective-permute-start(bf16[128,1024]{1,0:T(8,128)(2,1)} %param.6), channel_id=1, source_target_pairs={{0,24},{4,28},{8,16},{12,20},{16,8},{20,12},{24,0},{28,4},{1,25},{... | collective-permute-start | bytes 786440 | tf_op jit(solution)/shard_map/ppermute | solution.py:23
  12.4 19.0 %collective-permute-start.8 = (bf16[128,1024]{1,0:T(8,128)(2,1)}, bf16[128,1024]{1,0:T(8,128)(2,1)S(1)}, u32[]{:S(2)}, u32[]{:S(2)}) collective-permute-start(bf16[128,1024]{1,0:T(8,128)(2,1)} %param.6), channel_id=1, source_target_pairs={{0,2},{1,3},{2,0},{3,1},{4,6},{5,7},{6,4},{7,5},{8,10},{9,11},{10,... | collective-permute-start | bytes 786440 | tf_op jit(solution)/shard_map/ppermute | solution.py:23
  17.5 14.4 %collective-permute-start.3 = (bf16[128,1024]{1,0:T(8,128)(2,1)}, bf16[128,1024]{1,0:T(8,128)(2,1)S(1)}, u32[]{:S(2)}, u32[]{:S(2)}) collective-permute-start(bf16[128,1024]{1,0:T(8,128)(2,1)} %collective-permute-done.2), channel_id=1, source_target_pairs={{0,4},{4,0},{8,12},{12,8},{16,20},{20,16},{24,28},{28,24},{1,5},{5... | collective-permute-start | bytes 786440 | tf_op jit(solution)/shard_map/ppermute | solution.py:23
  26.8 9.5 %collective-permute-start.11 = (bf16[128,1024]{1,0:T(8,128)(2,1)}, bf16[128,1024]{1,0:T(8,128)(2,1)S(1)}, u32[]{:S(2)}, u32[]{:S(2)}) collective-permute-start(bf16[128,1024]{1,0:T(8,128)(2,1)} %collective-permute-done.2), channel_id=1, source_target_pairs={{0,2},{1,3},{2,0},{3,1},{4,6},{5,7},{6,4},{7,5},{8,10},{9,11},{10,... | collective-permute-start | bytes 786440 | tf_op jit(solution)/shard_map/ppermute | solution.py:23
  30.9 41.0 %collective-permute-start.5 = (bf16[128,1024]{1,0:T(8,128)(2,1)}, bf16[128,1024]{1,0:T(8,128)(2,1)}, u32[]{:S(2)}, u32[]{:S(2)}) collective-permute-start(bf16[128,1024]{1,0:T(8,128)(2,1)} %collective-permute-done.4), channel_id=1, source_target_pairs={{0,4},{4,0},{8,12},{12,8},{16,20},{20,16},{24,28},{28,24},{1,5},{5... | collective-permute-start | bytes 786440 | tf_op jit(solution)/shard_map/ppermute | solution.py:23
  31.4 39.4 %collective-permute-start.14 = (bf16[128,1024]{1,0:T(8,128)(2,1)}, bf16[128,1024]{1,0:T(8,128)(2,1)}, u32[]{:S(2)}, u32[]{:S(2)}) collective-permute-start(bf16[128,1024]{1,0:T(8,128)(2,1)} %collective-permute-done.4), channel_id=1, source_target_pairs={{0,2},{1,3},{2,0},{3,1},{4,6},{5,7},{6,4},{7,5},{8,10},{9,11},{10,... | collective-permute-start | bytes 786440 | tf_op jit(solution)/shard_map/ppermute | solution.py:23
  32.0 41.4 %collective-permute-start.7 = (bf16[128,1024]{1,0:T(8,128)(2,1)}, bf16[128,1024]{1,0:T(8,128)(2,1)}, u32[]{:S(2)}, u32[]{:S(2)}) collective-permute-start(bf16[128,1024]{1,0:T(8,128)(2,1)} %collective-permute-done.6), channel_id=1, source_target_pairs={{0,4},{4,0},{8,12},{12,8},{16,20},{20,16},{24,28},{28,24},{1,5},{5... | collective-permute-start | bytes 786440 | tf_op jit(solution)/shard_map/ppermute | solution.py:23
  36.3 40.1 %collective-permute-start.17 = (bf16[128,1024]{1,0:T(8,128)(2,1)}, bf16[128,1024]{1,0:T(8,128)(2,1)}, u32[]{:S(2)}, u32[]{:S(2)}) collective-permute-start(bf16[128,1024]{1,0:T(8,128)(2,1)} %collective-permute-done.6), channel_id=1, source_target_pairs={{0,2},{1,3},{2,0},{3,1},{4,6},{5,7},{6,4},{7,5},{8,10},{9,11},{10,... | collective-permute-start | bytes 786440 | tf_op jit(solution)/shard_map/ppermute | solution.py:23
  70.8 15.3 %collective-permute-start.10 = (bf16[128,512]{1,0:T(8,128)(2,1)S(1)}, bf16[128,512]{1,0:T(8,128)(2,1)S(1)}, u32[]{:S(2)}, u32[]{:S(2)}) collective-permute-start(bf16[128,512]{1,0:T(8,128)(2,1)S(1)} %slice.247), channel_id=1, source_target_pairs={{0,4},{4,0},{8,12},{12,8},{16,20},{20,16},{24,28},{28,24},{1,5},{5... | collective-permute-start | bytes 393224 | tf_op jit(solution)/shard_map/ppermute | solution.py:23
  71.8 15.2 %collective-permute-start.9 = (bf16[128,512]{1,0:T(8,128)(2,1)S(1)}, bf16[128,512]{1,0:T(8,128)(2,1)S(1)}, u32[]{:S(2)}, u32[]{:S(2)}) collective-permute-start(bf16[128,512]{1,0:T(8,128)(2,1)S(1)} %slice.245), channel_id=1, source_target_pairs={{0,2},{1,3},{2,0},{3,1},{4,6},{5,7},{6,4},{7,5},{8,10},{9,11},{10,... | collective-permute-start | bytes 393224 | tf_op jit(solution)/shard_map/ppermute | solution.py:23
  73.4 15.4 %collective-permute-start.13 = (bf16[128,512]{1,0:T(8,128)(2,1)S(1)}, bf16[128,512]{1,0:T(8,128)(2,1)S(1)}, u32[]{:S(2)}, u32[]{:S(2)}) collective-permute-start(bf16[128,512]{1,0:T(8,128)(2,1)S(1)} %slice.251), channel_id=1, source_target_pairs={{0,4},{4,0},{8,12},{12,8},{16,20},{20,16},{24,28},{28,24},{1,5},{5... | collective-permute-start | bytes 393224 | tf_op jit(solution)/shard_map/ppermute | solution.py:23
  76.4 14.8 %collective-permute-start.12 = (bf16[128,512]{1,0:T(8,128)(2,1)S(1)}, bf16[128,512]{1,0:T(8,128)(2,1)S(1)}, u32[]{:S(2)}, u32[]{:S(2)}) collective-permute-start(bf16[128,512]{1,0:T(8,128)(2,1)S(1)} %slice.249), channel_id=1, source_target_pairs={{0,2},{1,3},{2,0},{3,1},{4,6},{5,7},{6,4},{7,5},{8,10},{9,11},{10,... | collective-permute-start | bytes 393224 | tf_op jit(solution)/shard_map/ppermute | solution.py:23
  78.8 12.6 %collective-permute-start.16 = (bf16[128,512]{1,0:T(8,128)(2,1)S(1)}, bf16[128,512]{1,0:T(8,128)(2,1)S(1)}, u32[]{:S(2)}, u32[]{:S(2)}) collective-permute-start(bf16[128,512]{1,0:T(8,128)(2,1)S(1)} %slice.255), channel_id=1, source_target_pairs={{0,4},{4,0},{8,12},{12,8},{16,20},{20,16},{24,28},{28,24},{1,5},{5... | collective-permute-start | bytes 393224 | tf_op jit(solution)/shard_map/ppermute | solution.py:23
  115.0 6.7 %collective-permute-start.48 = (bf16[64,1024]{1,0:T(8,128)(2,1)S(1)}, bf16[64,1024]{1,0:T(8,128)(2,1)S(1)}, u32[]{:S(2)}, u32[]{:S(2)}) collective-permute-start(bf16[64,1024]{1,0:T(8,128)(2,1)S(1)} %get-tuple-element.52), channel_id=1, source_target_pairs={{0,2},{1,3},{2,0},{3,1},{4,6},{5,7},{6,4},{7,5},{8,10},{9,11},{10,... | collective-permute-start | bytes 393224 | tf_op jit(solution)/shard_map/ppermute | solution.py:23
  120.6 6.2 %collective-permute-start.29 = (bf16[128,512]{1,0:T(8,128)(2,1)S(1)}, bf16[128,512]{1,0:T(8,128)(2,1)S(1)}, u32[]{:S(2)}, u32[]{:S(2)}) collective-permute-start(bf16[128,512]{1,0:T(8,128)(2,1)S(1)} %convolution_convert_fusion.6), channel_id=1, source_target_pairs={{0,2},{1,3},{2,0},{3,1},{4,6},{5,7},{6,4},{7,5},{8,10},{9,11},{10,... | collective-permute-start | bytes 393224 | tf_op jit(solution)/shard_map/ppermute | solution.py:23
  126.9 25.3 %collective-permute-start.47 = (f32[64,64]{1,0:T(8,128)S(1)}, f32[64,64]{1,0:T(8,128)S(1)}, u32[]{:S(2)}, u32[]{:S(2)}) collective-permute-start(f32[64,64]{1,0:T(8,128)S(1)} %add.345), channel_id=1, source_target_pairs={{0,1},{1,0},{2,3},{3,2},{4,5},{5,4},{6,7},{7,6},{8,9},{9,8},{10,11... | collective-permute-start | bytes 49160 | tf_op jit(solution)/shard_map/ppermute | solution.py:23
  127.2 9.2 %collective-permute-start.28 = (bf16[128,1024]{1,0:T(8,128)(2,1)S(1)}, bf16[128,1024]{1,0:T(8,128)(2,1)S(1)}, u32[]{:S(2)}, u32[]{:S(2)}) collective-permute-start(bf16[128,1024]{1,0:T(8,128)(2,1)S(1)} %fusion.7), channel_id=1, source_target_pairs={{0,2},{1,3},{2,0},{3,1},{4,6},{5,7},{6,4},{7,5},{8,10},{9,11},{10,... | collective-permute-start | bytes 786440 | tf_op jit(solution)/shard_map/ppermute | solution.py:23
  128.5 9.2 %collective-permute-start.30 = (bf16[128,1024]{1,0:T(8,128)(2,1)S(1)}, bf16[128,1024]{1,0:T(8,128)(2,1)S(1)}, u32[]{:S(2)}, u32[]{:S(2)}) collective-permute-start(bf16[128,1024]{1,0:T(8,128)(2,1)S(1)} %fusion.8), channel_id=1, source_target_pairs={{0,4},{4,0},{8,12},{12,8},{16,20},{20,16},{24,28},{28,24},{1,5},{5... | collective-permute-start | bytes 786440 | tf_op jit(solution)/shard_map/ppermute | solution.py:23
  129.6 12.4 %collective-permute-start.33 = (bf16[128,1024]{1,0:T(8,128)(2,1)S(1)}, bf16[128,1024]{1,0:T(8,128)(2,1)S(1)}, u32[]{:S(2)}, u32[]{:S(2)}) collective-permute-start(bf16[128,1024]{1,0:T(8,128)(2,1)S(1)} %fusion.9), channel_id=1, source_target_pairs={{0,2},{1,3},{2,0},{3,1},{4,6},{5,7},{6,4},{7,5},{8,10},{9,11},{10,... | collective-permute-start | bytes 786440 | tf_op jit(solution)/shard_map/ppermute | solution.py:23
  131.1 12.3 %collective-permute-start.35 = (bf16[128,1024]{1,0:T(8,128)(2,1)S(1)}, bf16[128,1024]{1,0:T(8,128)(2,1)S(1)}, u32[]{:S(2)}, u32[]{:S(2)}) collective-permute-start(bf16[128,1024]{1,0:T(8,128)(2,1)S(1)} %fusion.10), channel_id=1, source_target_pairs={{0,4},{4,0},{8,12},{12,8},{16,20},{20,16},{24,28},{28,24},{1,5},{5... | collective-permute-start | bytes 786440 | tf_op jit(solution)/shard_map/ppermute | solution.py:23
  136.4 11.2 %collective-permute-start.38 = (bf16[128,1024]{1,0:T(8,128)(2,1)S(1)}, bf16[128,1024]{1,0:T(8,128)(2,1)S(1)}, u32[]{:S(2)}, u32[]{:S(2)}) collective-permute-start(bf16[128,1024]{1,0:T(8,128)(2,1)S(1)} %fusion.11), channel_id=1, source_target_pairs={{0,2},{1,3},{2,0},{3,1},{4,6},{5,7},{6,4},{7,5},{8,10},{9,11},{10,... | collective-permute-start | bytes 786440 | tf_op jit(solution)/shard_map/ppermute | solution.py:23
  137.7 10.7 %collective-permute-start.40 = (bf16[128,1024]{1,0:T(8,128)(2,1)S(1)}, bf16[128,1024]{1,0:T(8,128)(2,1)S(1)}, u32[]{:S(2)}, u32[]{:S(2)}) collective-permute-start(bf16[128,1024]{1,0:T(8,128)(2,1)S(1)} %fusion.12), channel_id=1, source_target_pairs={{0,4},{4,0},{8,12},{12,8},{16,20},{20,16},{24,28},{28,24},{1,5},{5... | collective-permute-start | bytes 786440 | tf_op jit(solution)/shard_map/ppermute | solution.py:23
  142.0 10.2 %collective-permute-start.49 = (f32[64,1024]{1,0:T(8,128)S(1)}, f32[64,1024]{1,0:T(8,128)S(1)}, u32[]{:S(2)}, u32[]{:S(2)}) collective-permute-start(f32[64,1024]{1,0:T(8,128)S(1)} %convert_add_fusion), channel_id=1, source_target_pairs={{0,1},{1,0},{2,3},{3,2},{4,5},{5,4},{6,7},{7,6},{8,9},{9,8},{10,11... | collective-permute-start | bytes 786440 | tf_op jit(solution)/shard_map/ppermute | solution.py:23
  143.3 11.4 %collective-permute-start.43 = (bf16[128,1024]{1,0:T(8,128)(2,1)S(1)}, bf16[128,1024]{1,0:T(8,128)(2,1)S(1)}, u32[]{:S(2)}, u32[]{:S(2)}) collective-permute-start(bf16[128,1024]{1,0:T(8,128)(2,1)S(1)} %fusion.13), channel_id=1, source_target_pairs={{0,2},{1,3},{2,0},{3,1},{4,6},{5,7},{6,4},{7,5},{8,10},{9,11},{10,... | collective-permute-start | bytes 786440 | tf_op jit(solution)/shard_map/ppermute | solution.py:23
  147.6 7.8 %collective-permute-start.45 = (bf16[128,1024]{1,0:T(8,128)(2,1)S(1)}, bf16[128,1024]{1,0:T(8,128)(2,1)S(1)}, u32[]{:S(2)}, u32[]{:S(2)}) collective-permute-start(bf16[128,1024]{1,0:T(8,128)(2,1)S(1)} %fusion.14), channel_id=1, source_target_pairs={{0,4},{4,0},{8,12},{12,8},{16,20},{20,16},{24,28},{28,24},{1,5},{5... | collective-permute-start | bytes 786440 | tf_op jit(solution)/shard_map/ppermute | solution.py:23
  148.4 11.1 %collective-permute-start.31 = (bf16[128,1024]{1,0:T(8,128)(2,1)S(1)}, bf16[128,1024]{1,0:T(8,128)(2,1)S(1)}, u32[]{:S(2)}, u32[]{:S(2)}) collective-permute-start(bf16[128,1024]{1,0:T(8,128)(2,1)S(1)} %fusion.4), channel_id=1, source_target_pairs={{0,24},{4,28},{8,16},{12,20},{16,8},{20,12},{24,0},{28,4},{1,25},{... | collective-permute-start | bytes 786440 | tf_op jit(solution)/shard_map/ppermute | solution.py:23
  152.2 20.0 %collective-permute-start.36 = (bf16[128,1024]{1,0:T(8,128)(2,1)S(1)}, bf16[128,1024]{1,0:T(8,128)(2,1)S(1)}, u32[]{:S(2)}, u32[]{:S(2)}) collective-permute-start(bf16[128,1024]{1,0:T(8,128)(2,1)S(1)} %fusion.5), channel_id=1, source_target_pairs={{0,16},{4,20},{8,24},{12,28},{16,0},{20,4},{24,8},{28,12},{1,17},{... | collective-permute-start | bytes 786440 | tf_op jit(solution)/shard_map/ppermute | solution.py:23
  152.3 20.0 %collective-permute-start.41 = (bf16[128,1024]{1,0:T(8,128)(2,1)S(1)}, bf16[128,1024]{1,0:T(8,128)(2,1)S(1)}, u32[]{:S(2)}, u32[]{:S(2)}) collective-permute-start(bf16[128,1024]{1,0:T(8,128)(2,1)S(1)} %fusion.6), channel_id=1, source_target_pairs={{0,8},{4,12},{8,0},{12,4},{16,24},{20,28},{24,16},{28,20},{1,9},{5... | collective-permute-start | bytes 786440 | tf_op jit(solution)/shard_map/ppermute | solution.py:23
  (34 other events, 234.7 us)

commit v2 on v1

--- a/solution.py
+++ b/solution.py
@@ -50,7 +50,10 @@
     half = width // 2
 
     head_other = swap_core(head)
-    rows_all = lax.all_gather(factor_rows, "vocab", axis=0, tiled=True)
+    rows_all, row_blocks = factor_rows, [0]
+    for bit in [1 << b for b in range(1, n_z.bit_length() - 1 + 1)][::-1] + [1]:
+        rows_all = jnp.concatenate([rows_all, swap(rows_all, "vocab", bit)], axis=0)
+        row_blocks = row_blocks + [j ^ bit for j in row_blocks]
     token_info = jnp.stack([targets, loss_mask])
     token_info = jnp.concatenate([token_info, swap_x(token_info)], axis=1)
     shards = [hidden] + [swap_z(hidden, k) for k in range(1, n_z)]
@@ -98,15 +101,17 @@
     def turn(stats):
         return jnp.concatenate([stats[:, toks:], stats[:, :toks]], axis=1)
 
-    mine = local(frozen)
-    stat_x = swap_x(mine)
-    stat_y = swap_y(mine)
-    stat_xy = swap_x(stat_y)
-    plane = merge([mine, turn(stat_x), stat_y, turn(stat_xy)])
+    stats = local(frozen)
+    stats = merge([stats, turn(swap_x(stats))])
+    stats = merge([stats, swap_y(stats)])
+    step = 1
+    while step < n_z:
+        stats = merge([stats, swap_z(stats, step)])
+        step *= 2
     fresh = lax.dot_general(
         rows_all, hidden_basis, (((1,), (0,)), ((), ())), preferred_element_type=f32
     )
-    stats = merge([plane] + [swap_z(plane, k) for k in range(1, n_z)] + [local(fresh)])
+    stats = merge([stats, local(fresh)])
     row_top, sum_exp = stats[0], stats[1]
 
     weight_row = loss_scale * token_info[1].astype(f32)
@@ -120,23 +125,28 @@
     grad_own, grad_other = grad[:, :toks], grad[:, toks:]
 
     frozen_rows = rows * n_tok * lax.axis_size("vocab")
-    fresh_ids = lax.broadcasted_iota(jnp.int32, (rows_all.shape[0], 1), 0) + frozen_rows
+    new_iota = lax.broadcasted_iota(jnp.int32, (new_here, 1), 0) + frozen_rows
+    fresh_ids = jnp.concatenate([new_iota + (v ^ j) * new_here for j in row_blocks], axis=0)
     fresh_hit = jnp.where(fresh_ids == targets[None, :], weight_row[None, :toks], 0.0)
     fresh_grad = (
         jnp.exp(fresh[:, :toks] - row_top[None, :toks]) * scale_row[None, :toks] - fresh_hit
     ).astype(bf16)
     mix_total = dot_first(rows_all, fresh_grad).astype(bf16)
-    fresh_here = lax.dynamic_slice_in_dim(fresh_grad, v * new_here, new_here, 0)
-    rows_part = dot_last(fresh_here, hidden_basis[:, :toks])
+    rows_part = dot_last(fresh_grad[:new_here], hidden_basis[:, :toks])
     basis_part = lax.reduce_precision(jnp.dot(mix_total, hidden, preferred_element_type=f32), 8, 7)
 
     def part(grads, dy, dz, cols=slice(None)):
         return dot_first(grads, blocks[dz][dy][: 2 * rows, cols])
 
     arrived = []
+    diag_a = diag_b = None
     for dz in range(n_z - 1, -1, -1):
-        diag_a = swap_x(part(grad_other, 1, dz, slice(0, half)).astype(bf16))
-        diag_b = swap_y(part(grad_other, 1, dz, slice(half, width)).astype(bf16))
+        send_a = part(grad_other, 1, dz, slice(0, half)).astype(bf16)
+        send_b = part(grad_other, 1, dz, slice(half, width)).astype(bf16)
+        if diag_a is not None:
+            send_a, send_b, _, _ = lax.optimization_barrier((send_a, send_b, diag_a, diag_b))
+        diag_a = swap_x(send_a)
+        diag_b = swap_y(send_b)
         to_x = part(grad_other, 0, dz) + jnp.pad(diag_b.astype(f32), ((0, 0), (half, 0)))
         to_y = part(grad_own, 1, dz) + jnp.pad(diag_a.astype(f32), ((0, 0), (0, width - half)))
         from_x = swap_x(to_x.astype(bf16))

time: 174 us -> 156 us (0.90)
  blocking collectives: 30.7 us -> 0 us
  waiting for transfers between devices: 53 us -> 60.9 us
  other arithmetic: 3.67 us -> 7.84 us
  local copies, waits for them, and re-layouts: 8.61 us -> 12.6 us
  starting transfers between devices: 56.5 us -> 53 us
    all_gather x1 -> x0, blocking collectives: 30.7 us -> none  [on_few(): rows_all = lax.all_gather(factor_rows, 'vocab', axis=0, tiled=True)]
    ppermute x50 -> x51, waiting for transfers between devices: 53 us -> 60.9 us  [swap(): return lax.ppermute(value, axis, [(i, i ^ bit) for i in range(size)])]
    ppermute x50 -> x51, starting transfers between devices: 56.5 us -> 53 us  [swap(): return lax.ppermute(value, axis, [(i, i ^ bit) for i in range(size)])]
    unnamed x32 -> x25, local copies, waits for them, and re-layouts: 0.67 us -> 3.36 us
    add x1 -> x4, other arithmetic: 0.01 us -> 2.27 us  [on_few(): new_iota + (v ^ j) * new_here]
  transfers between devices with their start and end apart: 50 -> 51, of which waited for: 17 -> 28; matrix products, arithmetic and copies ran while one was open for 14% -> 23% of each run, Pallas kernels for 0% -> 0%
where the time goes in v2:
time: 156 us; the launch traced here: 155 us
  waiting for transfers between devices  60.9 us (39%)
  starting transfers between devices  53 us (34%)
  matrix products  19.2 us (12%)
  local copies, waits for them, and re-layouts  12.6 us (8%)
  other arithmetic  7.84 us (5%)
    ppermute x51, waiting for transfers between devices, swap(): return lax.ppermute(value, axis, [(i, i ^ bit) for i in range(size)])  60.9 us
    ppermute x51, starting transfers between devices, swap(): return lax.ppermute(value, axis, [(i, i ^ bit) for i in range(size)])  53 us
    dot_general x21, matrix products, dot_last(): return lax.dot_general(a, b, contract_last, preferred_element_type=f32)  12.8 us
    dot_general x22, matrix products, dot_first(): return lax.dot_general(a, b, contract_first, preferred_element_type=f32)  5.93 us
    dynamic_slice x3, local copies, waits for them, and re-layouts, weights(): cut = lambda a: lax.dynamic_slice_in_dim(a, start, width, 1)  4.12 us
    unnamed x25, local copies, waits for them, and re-layouts  3.36 us
  transfers between devices with their start and end apart: 51, of which 28 were waited for; matrix products, arithmetic and copies ran while one was open for 23% of the time, Pallas kernels for 0%

profile of v2, /device:TPU:0, one launch (start us, length us, event | category | flops | bytes accessed | tf_op | source)
XLA Modules:
  0.0 154.8 jit_solution(14480346090614530053)
XLA Ops:
  1.1 2.6 %collective-permute-start.4 = (bf16[128,1024]{1,0:T(8,128)(2,1)}, bf16[128,1024]{1,0:T(8,128)(2,1)}, u32[]{:S(2)}, u32[]{:S(2)}) collective-permute-start(bf16[128,1024]{1,0:T(8,128)(2,1)} %param.6), channel_id=1, source_target_pairs={{0,4},{4,0},{8,12},{12,8},{16,20},{20,16},{24,28},{28,24},{1,5},{5... | collective-permute-start | bytes 786440 | tf_op jit(solution)/shard_map/ppermute | solution.py:23
  3.7 1.6 %collective-permute-start.5 = (bf16[128,1024]{1,0:T(8,128)(2,1)}, bf16[128,1024]{1,0:T(8,128)(2,1)}, u32[]{:S(2)}, u32[]{:S(2)}) collective-permute-start(bf16[128,1024]{1,0:T(8,128)(2,1)} %param.6), channel_id=1, source_target_pairs={{0,8},{4,12},{8,0},{12,4},{16,24},{20,28},{24,16},{28,20},{1,9},{5... | collective-permute-start | bytes 786440 | tf_op jit(solution)/shard_map/ppermute | solution.py:23
  5.3 2.6 %collective-permute-start.7 = (bf16[128,1024]{1,0:T(8,128)(2,1)}, bf16[128,1024]{1,0:T(8,128)(2,1)}, u32[]{:S(2)}, u32[]{:S(2)}) collective-permute-start(bf16[128,1024]{1,0:T(8,128)(2,1)} %param.6), channel_id=1, source_target_pairs={{0,16},{4,20},{8,24},{12,28},{16,0},{20,4},{24,8},{28,12},{1,17},{... | collective-permute-start | bytes 786440 | tf_op jit(solution)/shard_map/ppermute | solution.py:23
  11.9 2.5 %constant_dynamic-slice_fusion.5 = (bf16[128,1024]{1,0:T(8,128)(2,1)}, bf16[128,1024]{1,0:T(8,128)(2,1)S(1)}, bf16[128,1024]{1,0:T(8,128)(2,1)}, bf16[128,1024]{...) fusion(bf16[128,8192]{1,0:T(8,128)(2,1)} %param.7, ...), kind=kLoop, calls=%fused_computation.152 | loop fusion | bytes 4194336 | tf_op jit(solution)/shard_map/dynamic_slice | solution.py:70
  15.0 6.0 %collective-permute-done = bf16[64,64]{1,0:T(8,128)(2,1)} collective-permute-done((bf16[64,64]{1,0:T(8,128)(2,1)}, bf16[64,64]{1,0:T(8,128)(2,1)}, u32[]{:S(2)}, u32[]{:S(2)}) %collective-permute-start) | collective-permute-done | bytes 8224 | tf_op jit(solution)/shard_map/ppermute | solution.py:23
  23.2 1.6 %collective-permute-done.27 = s32[2,128]{1,0:T(2,128)S(1)} collective-permute-done((s32[2,128]{1,0:T(2,128)}, s32[2,128]{1,0:T(2,128)S(1)}, u32[]{:S(2)}, u32[]{:S(2)}) %collective-permute-start.27) | collective-permute-done | bytes 1056 | tf_op jit(solution)/shard_map/ppermute | solution.py:23
  25.4 3.9 %collective-permute-done.1 = bf16[128,64]{1,0:T(8,128)(2,1)} collective-permute-done((bf16[128,64]{1,0:T(8,128)(2,1)S(1)}, bf16[128,64]{1,0:T(8,128)(2,1)}, u32[]{:S(2)}, u32[]{:S(2)}) %collective-permute-start.1) | collective-permute-done | bytes 16416 | tf_op jit(solution)/shard_map/ppermute | solution.py:23
  29.3 2.5 %collective-permute-start.9 = (bf16[128,1024]{1,0:T(8,128)(2,1)}, bf16[128,1024]{1,0:T(8,128)(2,1)}, u32[]{:S(2)}, u32[]{:S(2)}) collective-permute-start(bf16[128,1024]{1,0:T(8,128)(2,1)} %param.6), channel_id=1, source_target_pairs={{0,24},{4,28},{8,16},{12,20},{16,8},{20,12},{24,0},{28,4},{1,25},{... | collective-permute-start | bytes 786440 | tf_op jit(solution)/shard_map/ppermute | solution.py:23
  39.4 2.0 %collective-permute-done.11 = bf16[128,1024]{1,0:T(8,128)(2,1)} collective-permute-done((bf16[128,1024]{1,0:T(8,128)(2,1)}, bf16[128,1024]{1,0:T(8,128)(2,1)}, u32[]{:S(2)}, u32[]{:S(2)}) %collective-permute-start.11) | collective-permute-done | bytes 262176 | tf_op jit(solution)/shard_map/ppermute | solution.py:23
  43.4 3.6 %collective-permute-done.14 = bf16[128,1024]{1,0:T(8,128)(2,1)} collective-permute-done((bf16[128,1024]{1,0:T(8,128)(2,1)}, bf16[128,1024]{1,0:T(8,128)(2,1)}, u32[]{:S(2)}, u32[]{:S(2)}) %collective-permute-start.14) | collective-permute-done | bytes 262176 | tf_op jit(solution)/shard_map/ppermute | solution.py:23
  55.0 1.6 %collective-permute-start.13 = (bf16[128,512]{1,0:T(8,128)(2,1)S(1)}, bf16[128,512]{1,0:T(8,128)(2,1)S(1)}, u32[]{:S(2)}, u32[]{:S(2)}) collective-permute-start(bf16[128,512]{1,0:T(8,128)(2,1)S(1)} %slice.225), channel_id=1, source_target_pairs={{0,4},{4,0},{8,12},{12,8},{16,20},{20,16},{24,28},{28,24},{1,5},{5... | collective-permute-start | bytes 393224 | tf_op jit(solution)/shard_map/ppermute | solution.py:23
  57.8 1.6 %collective-permute-start.15 = (bf16[128,512]{1,0:T(8,128)(2,1)S(1)}, bf16[128,512]{1,0:T(8,128)(2,1)S(1)}, u32[]{:S(2)}, u32[]{:S(2)}) collective-permute-start(bf16[128,512]{1,0:T(8,128)(2,1)S(1)} %slice.227), channel_id=1, source_target_pairs={{0,2},{1,3},{2,0},{3,1},{4,6},{5,7},{6,4},{7,5},{8,10},{9,11},{10,... | collective-permute-start | bytes 393224 | tf_op jit(solution)/shard_map/ppermute | solution.py:23
  67.6 1.6 %collective-permute-start.19 = (bf16[128,512]{1,0:T(8,128)(2,1)S(1)}, bf16[128,512]{1,0:T(8,128)(2,1)S(1)}, u32[]{:S(2)}, u32[]{:S(2)}) collective-permute-start(bf16[128,512]{1,0:T(8,128)(2,1)S(1)} %slice.233), channel_id=1, source_target_pairs={{0,4},{4,0},{8,12},{12,8},{16,20},{20,16},{24,28},{28,24},{1,5},{5... | collective-permute-start | bytes 393224 | tf_op jit(solution)/shard_map/ppermute | solution.py:23
  71.1 1.6 %collective-permute-start.21 = (bf16[128,512]{1,0:T(8,128)(2,1)S(1)}, bf16[128,512]{1,0:T(8,128)(2,1)S(1)}, u32[]{:S(2)}, u32[]{:S(2)}) collective-permute-start(bf16[128,512]{1,0:T(8,128)(2,1)S(1)} %slice.235), channel_id=1, source_target_pairs={{0,2},{1,3},{2,0},{3,1},{4,6},{5,7},{6,4},{7,5},{8,10},{9,11},{10,... | collective-permute-start | bytes 393224 | tf_op jit(solution)/shard_map/ppermute | solution.py:23
  81.4 2.1 %collective-permute-done.23 = f32[2,256]{1,0:T(2,128)S(1)} collective-permute-done((f32[2,256]{1,0:T(2,128)S(1)}, f32[2,256]{1,0:T(2,128)S(1)}, u32[]{:S(2)}, u32[]{:S(2)}) %collective-permute-start.23) | collective-permute-done | bytes 2080 | tf_op jit(solution)/shard_map/ppermute | solution.py:23
  83.5 1.6 %collective-permute-start.24 = (f32[2,256]{1,0:T(2,128)S(1)}, f32[2,256]{1,0:T(2,128)S(1)}, u32[]{:S(2)}, u32[]{:S(2)}) collective-permute-start(f32[2,256]{1,0:T(2,128)S(1)} %pad_maximum_fusion.42), channel_id=1, source_target_pairs={{0,4},{4,0},{8,12},{12,8},{16,20},{20,16},{24,28},{28,24},{1,5},{5... | collective-permute-start | bytes 6152 | tf_op jit(solution)/shard_map/ppermute | solution.py:23
  85.1 2.0 %collective-permute-done.24 = f32[2,256]{1,0:T(2,128)S(1)} collective-permute-done((f32[2,256]{1,0:T(2,128)S(1)}, f32[2,256]{1,0:T(2,128)S(1)}, u32[]{:S(2)}, u32[]{:S(2)}) %collective-permute-start.24) | collective-permute-done | bytes 2080 | tf_op jit(solution)/shard_map/ppermute | solution.py:23
  87.5 3.3 %collective-permute-done.25 = f32[2,256]{1,0:T(2,128)S(1)} collective-permute-done((f32[2,256]{1,0:T(2,128)S(1)}, f32[2,256]{1,0:T(2,128)S(1)}, u32[]{:S(2)}, u32[]{:S(2)}) %collective-permute-start.25) | collective-permute-done | bytes 2080 | tf_op jit(solution)/shard_map/ppermute | solution.py:23
  91.1 4.3 %collective-permute-done.26 = f32[2,256]{1,0:T(2,128)S(1)} collective-permute-done((f32[2,256]{1,0:T(2,128)S(1)}, f32[2,256]{1,0:T(2,128)S(1)}, u32[]{:S(2)}, u32[]{:S(2)}) %collective-permute-start.26) | collective-permute-done | bytes 2080 | tf_op jit(solution)/shard_map/ppermute | solution.py:23
  97.9 1.6 %collective-permute-start.49 = (bf16[64,1024]{1,0:T(8,128)(2,1)S(1)}, bf16[64,1024]{1,0:T(8,128)(2,1)S(1)}, u32[]{:S(2)}, u32[]{:S(2)}) collective-permute-start(bf16[64,1024]{1,0:T(8,128)(2,1)S(1)} %get-tuple-element.66), channel_id=1, source_target_pairs={{0,2},{1,3},{2,0},{3,1},{4,6},{5,7},{6,4},{7,5},{8,10},{9,11},{10,... | collective-permute-start | bytes 393224 | tf_op jit(solution)/shard_map/ppermute | solution.py:23
  100.2 1.6 %collective-permute-start.28 = (bf16[128,512]{1,0:T(8,128)(2,1)S(1)}, bf16[128,512]{1,0:T(8,128)(2,1)S(1)}, u32[]{:S(2)}, u32[]{:S(2)}) collective-permute-start(bf16[128,512]{1,0:T(8,128)(2,1)S(1)} %convolution_convert_fusion.7), channel_id=1, source_target_pairs={{0,4},{4,0},{8,12},{12,8},{16,20},{20,16},{24,28},{28,24},{1,5},{5... | collective-permute-start | bytes 393224 | tf_op jit(solution)/shard_map/ppermute | solution.py:23
  109.8 3.1 %collective-permute-done.33 = bf16[128,512]{1,0:T(8,128)(2,1)S(1)} collective-permute-done((bf16[128,512]{1,0:T(8,128)(2,1)S(1)}, bf16[128,512]{1,0:T(8,128)(2,1)S(1)}, u32[]{:S(2)}, u32[]{:S(2)}) %collective-permute-start.33) | collective-permute-done | bytes 131104 | tf_op jit(solution)/shard_map/ppermute | solution.py:23
  118.0 1.8 %collective-permute-done.31 = bf16[128,1024]{1,0:T(8,128)(2,1)S(1)} collective-permute-done((bf16[128,1024]{1,0:T(8,128)(2,1)S(1)}, bf16[128,1024]{1,0:T(8,128)(2,1)S(1)}, u32[]{:S(2)}, u32[]{:S(2)}) %collective-permute-start.31) | collective-permute-done | bytes 262176 | tf_op jit(solution)/shard_map/ppermute | solution.py:23
  119.8 1.8 %collective-permute-start.34 = (bf16[128,1024]{1,0:T(8,128)(2,1)S(1)}, bf16[128,1024]{1,0:T(8,128)(2,1)S(1)}, u32[]{:S(2)}, u32[]{:S(2)}) collective-permute-start(bf16[128,1024]{1,0:T(8,128)(2,1)S(1)} %fusion.9), channel_id=1, source_target_pairs={{0,2},{1,3},{2,0},{3,1},{4,6},{5,7},{6,4},{7,5},{8,10},{9,11},{10,... | collective-permute-start | bytes 786440 | tf_op jit(solution)/shard_map/ppermute | solution.py:23
  122.6 2.0 %collective-permute-start.43 = (bf16[128,512]{1,0:T(8,128)(2,1)S(1)}, bf16[128,512]{1,0:T(8,128)(2,1)S(1)}, u32[]{:S(2)}, u32[]{:S(2)}) collective-permute-start(bf16[128,512]{1,0:T(8,128)(2,1)S(1)} %convolution_convert_fusion), channel_id=1, source_target_pairs={{0,4},{4,0},{8,12},{12,8},{16,20},{20,16},{24,28},{28,24},{1,5},{5... | collective-permute-start | bytes 393224 | tf_op jit(solution)/shard_map/ppermute | solution.py:23
  125.1 3.5 %collective-permute-done.34 = bf16[128,1024]{1,0:T(8,128)(2,1)S(1)} collective-permute-done((bf16[128,1024]{1,0:T(8,128)(2,1)S(1)}, bf16[128,1024]{1,0:T(8,128)(2,1)S(1)}, u32[]{:S(2)}, u32[]{:S(2)}) %collective-permute-start.34) | collective-permute-done | bytes 262176 | tf_op jit(solution)/shard_map/ppermute | solution.py:23
  128.6 2.1 %collective-permute-start.45 = (bf16[128,512]{1,0:T(8,128)(2,1)S(1)}, bf16[128,512]{1,0:T(8,128)(2,1)S(1)}, u32[]{:S(2)}, u32[]{:S(2)}) collective-permute-start(bf16[128,512]{1,0:T(8,128)(2,1)S(1)} %convolution_convert_fusion.1), channel_id=1, source_target_pairs={{0,2},{1,3},{2,0},{3,1},{4,6},{5,7},{6,4},{7,5},{8,10},{9,11},{10,... | collective-permute-start | bytes 393224 | tf_op jit(solution)/shard_map/ppermute | solution.py:23
  133.9 4.4 %collective-permute-done.39 = bf16[128,1024]{1,0:T(8,128)(2,1)S(1)} collective-permute-done((bf16[128,1024]{1,0:T(8,128)(2,1)S(1)}, bf16[128,1024]{1,0:T(8,128)(2,1)S(1)}, u32[]{:S(2)}, u32[]{:S(2)}) %collective-permute-start.39) | collective-permute-done | bytes 262176 | tf_op jit(solution)/shard_map/ppermute | solution.py:23
  138.3 2.8 %collective-permute-done.41 = bf16[128,1024]{1,0:T(8,128)(2,1)S(1)} collective-permute-done((bf16[128,1024]{1,0:T(8,128)(2,1)S(1)}, bf16[128,1024]{1,0:T(8,128)(2,1)S(1)}, u32[]{:S(2)}, u32[]{:S(2)}) %collective-permute-start.41) | collective-permute-done | bytes 262176 | tf_op jit(solution)/shard_map/ppermute | solution.py:23
  141.1 2.5 %collective-permute-start.44 = (bf16[128,1024]{1,0:T(8,128)(2,1)S(1)}, bf16[128,1024]{1,0:T(8,128)(2,1)S(1)}, u32[]{:S(2)}, u32[]{:S(2)}) collective-permute-start(bf16[128,1024]{1,0:T(8,128)(2,1)S(1)} %fusion.13), channel_id=1, source_target_pairs={{0,2},{1,3},{2,0},{3,1},{4,6},{5,7},{6,4},{7,5},{8,10},{9,11},{10,... | collective-permute-start | bytes 786440 | tf_op jit(solution)/shard_map/ppermute | solution.py:23
  145.8 5.4 %collective-permute-done.37 = bf16[128,1024]{1,0:T(8,128)(2,1)S(1)} collective-permute-done((bf16[128,1024]{1,0:T(8,128)(2,1)S(1)}, bf16[128,1024]{1,0:T(8,128)(2,1)S(1)}, u32[]{:S(2)}, u32[]{:S(2)}) %collective-permute-start.37) | collective-permute-done | bytes 262176 | tf_op jit(solution)/shard_map/ppermute | solution.py:23
  151.2 2.6 %collective-permute-done.42 = bf16[128,1024]{1,0:T(8,128)(2,1)S(1)} collective-permute-done((bf16[128,1024]{1,0:T(8,128)(2,1)S(1)}, bf16[128,1024]{1,0:T(8,128)(2,1)S(1)}, u32[]{:S(2)}, u32[]{:S(2)}) %collective-permute-start.42) | collective-permute-done | bytes 262176 | tf_op jit(solution)/shard_map/ppermute | solution.py:23
  (192 shorter events, 69.9 us)
Async XLA Ops:
  0.6 57.2 %collective-permute-start.3 = (bf16[128,8192]{1,0:T(8,128)(2,1)}, bf16[128,8192]{1,0:T(8,128)(2,1)S(1)}, u32[]{:S(2)}, u32[]{:S(2)}) collective-permute-start(bf16[128,8192]{1,0:T(8,128)(2,1)} %param.7), channel_id=1, source_target_pairs={{0,1},{1,0},{2,3},{3,2},{4,5},{5,4},{6,7},{7,6},{8,9},{9,8},{10,11... | collective-permute-start | bytes 6291464 | tf_op jit(solution)/shard_map/ppermute | solution.py:23
  1.1 30.7 %collective-permute-start.4 = (bf16[128,1024]{1,0:T(8,128)(2,1)}, bf16[128,1024]{1,0:T(8,128)(2,1)}, u32[]{:S(2)}, u32[]{:S(2)}) collective-permute-start(bf16[128,1024]{1,0:T(8,128)(2,1)} %param.6), channel_id=1, source_target_pairs={{0,4},{4,0},{8,12},{12,8},{16,20},{20,16},{24,28},{28,24},{1,5},{5... | collective-permute-start | bytes 786440 | tf_op jit(solution)/shard_map/ppermute | solution.py:23
  3.7 29.6 %collective-permute-start.5 = (bf16[128,1024]{1,0:T(8,128)(2,1)}, bf16[128,1024]{1,0:T(8,128)(2,1)}, u32[]{:S(2)}, u32[]{:S(2)}) collective-permute-start(bf16[128,1024]{1,0:T(8,128)(2,1)} %param.6), channel_id=1, source_target_pairs={{0,8},{4,12},{8,0},{12,4},{16,24},{20,28},{24,16},{28,20},{1,9},{5... | collective-permute-start | bytes 786440 | tf_op jit(solution)/shard_map/ppermute | solution.py:23
  5.3 28.5 %collective-permute-start.7 = (bf16[128,1024]{1,0:T(8,128)(2,1)}, bf16[128,1024]{1,0:T(8,128)(2,1)}, u32[]{:S(2)}, u32[]{:S(2)}) collective-permute-start(bf16[128,1024]{1,0:T(8,128)(2,1)} %param.6), channel_id=1, source_target_pairs={{0,16},{4,20},{8,24},{12,28},{16,0},{20,4},{24,8},{28,12},{1,17},{... | collective-permute-start | bytes 786440 | tf_op jit(solution)/shard_map/ppermute | solution.py:23
  7.9 13.1 %collective-permute-start = (bf16[64,64]{1,0:T(8,128)(2,1)}, bf16[64,64]{1,0:T(8,128)(2,1)}, u32[]{:S(2)}, u32[]{:S(2)}) collective-permute-start(bf16[64,64]{1,0:T(8,128)(2,1)} %param.8), channel_id=1, source_target_pairs={{0,16},{4,20},{8,24},{12,28},{16,0},{20,4},{24,8},{28,12},{1,17},{... | collective-permute-start | bytes 24584 | tf_op jit(solution)/shard_map/ppermute | solution.py:23
  29.3 8.6 %collective-permute-start.9 = (bf16[128,1024]{1,0:T(8,128)(2,1)}, bf16[128,1024]{1,0:T(8,128)(2,1)}, u32[]{:S(2)}, u32[]{:S(2)}) collective-permute-start(bf16[128,1024]{1,0:T(8,128)(2,1)} %param.6), channel_id=1, source_target_pairs={{0,24},{4,28},{8,16},{12,20},{16,8},{20,12},{24,0},{28,4},{1,25},{... | collective-permute-start | bytes 786440 | tf_op jit(solution)/shard_map/ppermute | solution.py:23
  31.8 9.6 %collective-permute-start.11 = (bf16[128,1024]{1,0:T(8,128)(2,1)}, bf16[128,1024]{1,0:T(8,128)(2,1)}, u32[]{:S(2)}, u32[]{:S(2)}) collective-permute-start(bf16[128,1024]{1,0:T(8,128)(2,1)} %param.6), channel_id=1, source_target_pairs={{0,2},{1,3},{2,0},{3,1},{4,6},{5,7},{6,4},{7,5},{8,10},{9,11},{10,... | collective-permute-start | bytes 786440 | tf_op jit(solution)/shard_map/ppermute | solution.py:23
  33.3 9.6 %collective-permute-start.6 = (bf16[128,1024]{1,0:T(8,128)(2,1)}, bf16[128,1024]{1,0:T(8,128)(2,1)}, u32[]{:S(2)}, u32[]{:S(2)}) collective-permute-start(bf16[128,1024]{1,0:T(8,128)(2,1)} %collective-permute-done.5), channel_id=1, source_target_pairs={{0,4},{4,0},{8,12},{12,8},{16,20},{20,16},{24,28},{28,24},{1,5},{5... | collective-permute-start | bytes 786440 | tf_op jit(solution)/shard_map/ppermute | solution.py:23
  33.8 13.2 %collective-permute-start.14 = (bf16[128,1024]{1,0:T(8,128)(2,1)}, bf16[128,1024]{1,0:T(8,128)(2,1)}, u32[]{:S(2)}, u32[]{:S(2)}) collective-permute-start(bf16[128,1024]{1,0:T(8,128)(2,1)} %collective-permute-done.5), channel_id=1, source_target_pairs={{0,2},{1,3},{2,0},{3,1},{4,6},{5,7},{6,4},{7,5},{8,10},{9,11},{10,... | collective-permute-start | bytes 786440 | tf_op jit(solution)/shard_map/ppermute | solution.py:23
  37.9 17.1 %collective-permute-start.8 = (bf16[128,1024]{1,0:T(8,128)(2,1)}, bf16[128,1024]{1,0:T(8,128)(2,1)S(1)}, u32[]{:S(2)}, u32[]{:S(2)}) collective-permute-start(bf16[128,1024]{1,0:T(8,128)(2,1)} %collective-permute-done.7), channel_id=1, source_target_pairs={{0,4},{4,0},{8,12},{12,8},{16,20},{20,16},{24,28},{28,24},{1,5},{5... | collective-permute-start | bytes 786440 | tf_op jit(solution)/shard_map/ppermute | solution.py:23
  41.4 13.1 %collective-permute-start.17 = (bf16[128,1024]{1,0:T(8,128)(2,1)}, bf16[128,1024]{1,0:T(8,128)(2,1)S(1)}, u32[]{:S(2)}, u32[]{:S(2)}) collective-permute-start(bf16[128,1024]{1,0:T(8,128)(2,1)} %collective-permute-done.7), channel_id=1, source_target_pairs={{0,2},{1,3},{2,0},{3,1},{4,6},{5,7},{6,4},{7,5},{8,10},{9,11},{10,... | collective-permute-start | bytes 786440 | tf_op jit(solution)/shard_map/ppermute | solution.py:23
  42.9 14.4 %collective-permute-start.10 = (bf16[128,1024]{1,0:T(8,128)(2,1)}, bf16[128,1024]{1,0:T(8,128)(2,1)S(1)}, u32[]{:S(2)}, u32[]{:S(2)}) collective-permute-start(bf16[128,1024]{1,0:T(8,128)(2,1)} %collective-permute-done.9), channel_id=1, source_target_pairs={{0,4},{4,0},{8,12},{12,8},{16,20},{20,16},{24,28},{28,24},{1,5},{5... | collective-permute-start | bytes 786440 | tf_op jit(solution)/shard_map/ppermute | solution.py:23
  47.0 9.6 %collective-permute-start.20 = (bf16[128,1024]{1,0:T(8,128)(2,1)}, bf16[128,1024]{1,0:T(8,128)(2,1)S(1)}, u32[]{:S(2)}, u32[]{:S(2)}) collective-permute-start(bf16[128,1024]{1,0:T(8,128)(2,1)} %collective-permute-done.9), channel_id=1, source_target_pairs={{0,2},{1,3},{2,0},{3,1},{4,6},{5,7},{6,4},{7,5},{8,10},{9,11},{10,... | collective-permute-start | bytes 786440 | tf_op jit(solution)/shard_map/ppermute | solution.py:23
  54.4 27.0 %collective-permute-start.2 = (bf16[256,64]{1,0:T(8,128)(2,1)S(1)}, bf16[256,64]{1,0:T(8,128)(2,1)S(1)}, u32[]{:S(2)}, u32[]{:S(2)}) collective-permute-start(bf16[256,64]{1,0:T(8,128)(2,1)S(1)} %pad_maximum_fusion.39), channel_id=1, source_target_pairs={{0,4},{4,0},{8,12},{12,8},{16,20},{20,16},{24,28},{28,24},{1,5},{5... | collective-permute-start | bytes 98312 | tf_op jit(solution)/shard_map/ppermute | solution.py:23
  55.0 12.5 %collective-permute-start.13 = (bf16[128,512]{1,0:T(8,128)(2,1)S(1)}, bf16[128,512]{1,0:T(8,128)(2,1)S(1)}, u32[]{:S(2)}, u32[]{:S(2)}) collective-permute-start(bf16[128,512]{1,0:T(8,128)(2,1)S(1)} %slice.225), channel_id=1, source_target_pairs={{0,4},{4,0},{8,12},{12,8},{16,20},{20,16},{24,28},{28,24},{1,5},{5... | collective-permute-start | bytes 393224 | tf_op jit(solution)/shard_map/ppermute | solution.py:23
  56.6 12.8 %collective-permute-start.12 = (bf16[128,512]{1,0:T(8,128)(2,1)S(1)}, bf16[128,512]{1,0:T(8,128)(2,1)S(1)}, u32[]{:S(2)}, u32[]{:S(2)}) collective-permute-start(bf16[128,512]{1,0:T(8,128)(2,1)S(1)} %slice.223), channel_id=1, source_target_pairs={{0,2},{1,3},{2,0},{3,1},{4,6},{5,7},{6,4},{7,5},{8,10},{9,11},{10,... | collective-permute-start | bytes 393224 | tf_op jit(solution)/shard_map/ppermute | solution.py:23
  57.3 13.1 %collective-permute-start.16 = (bf16[128,512]{1,0:T(8,128)(2,1)S(1)}, bf16[128,512]{1,0:T(8,128)(2,1)S(1)}, u32[]{:S(2)}, u32[]{:S(2)}) collective-permute-start(bf16[128,512]{1,0:T(8,128)(2,1)S(1)} %slice.229), channel_id=1, source_target_pairs={{0,4},{4,0},{8,12},{12,8},{16,20},{20,16},{24,28},{28,24},{1,5},{5... | collective-permute-start | bytes 393224 | tf_op jit(solution)/shard_map/ppermute | solution.py:23
  57.8 13.3 %collective-permute-start.15 = (bf16[128,512]{1,0:T(8,128)(2,1)S(1)}, bf16[128,512]{1,0:T(8,128)(2,1)S(1)}, u32[]{:S(2)}, u32[]{:S(2)}) collective-permute-start(bf16[128,512]{1,0:T(8,128)(2,1)S(1)} %slice.227), channel_id=1, source_target_pairs={{0,2},{1,3},{2,0},{3,1},{4,6},{5,7},{6,4},{7,5},{8,10},{9,11},{10,... | collective-permute-start | bytes 393224 | tf_op jit(solution)/shard_map/ppermute | solution.py:23
  103.3 40.5 %collective-permute-start.48 = (f32[64,64]{1,0:T(8,128)S(1)}, f32[64,64]{1,0:T(8,128)S(1)}, u32[]{:S(2)}, u32[]{:S(2)}) collective-permute-start(f32[64,64]{1,0:T(8,128)S(1)} %add.501), channel_id=1, source_target_pairs={{0,1},{1,0},{2,3},{3,2},{4,5},{5,4},{6,7},{7,6},{8,9},{9,8},{10,11... | collective-permute-start | bytes 49160 | tf_op jit(solution)/shard_map/ppermute | solution.py:23
  103.4 40.8 %collective-permute-start.50 = (f32[64,1024]{1,0:T(8,128)S(1)}, f32[64,1024]{1,0:T(8,128)S(1)}, u32[]{:S(2)}, u32[]{:S(2)}) collective-permute-start(f32[64,1024]{1,0:T(8,128)S(1)} %convert_add_fusion), channel_id=1, source_target_pairs={{0,1},{1,0},{2,3},{3,2},{4,5},{5,4},{6,7},{7,6},{8,9},{9,8},{10,11... | collective-permute-start | bytes 786440 | tf_op jit(solution)/shard_map/ppermute | solution.py:23
  109.0 7.5 %collective-permute-start.29 = (bf16[128,1024]{1,0:T(8,128)(2,1)S(1)}, bf16[128,1024]{1,0:T(8,128)(2,1)S(1)}, u32[]{:S(2)}, u32[]{:S(2)}) collective-permute-start(bf16[128,1024]{1,0:T(8,128)(2,1)S(1)} %fusion.7), channel_id=1, source_target_pairs={{0,2},{1,3},{2,0},{3,1},{4,6},{5,7},{6,4},{7,5},{8,10},{9,11},{10,... | collective-permute-start | bytes 786440 | tf_op jit(solution)/shard_map/ppermute | solution.py:23
  113.5 9.0 %collective-permute-start.38 = (bf16[128,512]{1,0:T(8,128)(2,1)S(1)}, bf16[128,512]{1,0:T(8,128)(2,1)S(1)}, u32[]{:S(2)}, u32[]{:S(2)}) collective-permute-start(bf16[128,512]{1,0:T(8,128)(2,1)S(1)} %convolution_convert_fusion.2), channel_id=1, source_target_pairs={{0,4},{4,0},{8,12},{12,8},{16,20},{20,16},{24,28},{28,24},{1,5},{5... | collective-permute-start | bytes 393224 | tf_op jit(solution)/shard_map/ppermute | solution.py:23
  119.8 8.9 %collective-permute-start.34 = (bf16[128,1024]{1,0:T(8,128)(2,1)S(1)}, bf16[128,1024]{1,0:T(8,128)(2,1)S(1)}, u32[]{:S(2)}, u32[]{:S(2)}) collective-permute-start(bf16[128,1024]{1,0:T(8,128)(2,1)S(1)} %fusion.9), channel_id=1, source_target_pairs={{0,2},{1,3},{2,0},{3,1},{4,6},{5,7},{6,4},{7,5},{8,10},{9,11},{10,... | collective-permute-start | bytes 786440 | tf_op jit(solution)/shard_map/ppermute | solution.py:23
  122.6 8.2 %collective-permute-start.36 = (bf16[128,1024]{1,0:T(8,128)(2,1)S(1)}, bf16[128,1024]{1,0:T(8,128)(2,1)S(1)}, u32[]{:S(2)}, u32[]{:S(2)}) collective-permute-start(bf16[128,1024]{1,0:T(8,128)(2,1)S(1)} %fusion.10), channel_id=1, source_target_pairs={{0,4},{4,0},{8,12},{12,8},{16,20},{20,16},{24,28},{28,24},{1,5},{5... | collective-permute-start | bytes 786440 | tf_op jit(solution)/shard_map/ppermute | solution.py:23
  122.6 10.4 %collective-permute-start.43 = (bf16[128,512]{1,0:T(8,128)(2,1)S(1)}, bf16[128,512]{1,0:T(8,128)(2,1)S(1)}, u32[]{:S(2)}, u32[]{:S(2)}) collective-permute-start(bf16[128,512]{1,0:T(8,128)(2,1)S(1)} %convolution_convert_fusion), channel_id=1, source_target_pairs={{0,4},{4,0},{8,12},{12,8},{16,20},{20,16},{24,28},{28,24},{1,5},{5... | collective-permute-start | bytes 393224 | tf_op jit(solution)/shard_map/ppermute | solution.py:23
  130.7 7.6 %collective-permute-start.39 = (bf16[128,1024]{1,0:T(8,128)(2,1)S(1)}, bf16[128,1024]{1,0:T(8,128)(2,1)S(1)}, u32[]{:S(2)}, u32[]{:S(2)}) collective-permute-start(bf16[128,1024]{1,0:T(8,128)(2,1)S(1)} %fusion.11), channel_id=1, source_target_pairs={{0,2},{1,3},{2,0},{3,1},{4,6},{5,7},{6,4},{7,5},{8,10},{9,11},{10,... | collective-permute-start | bytes 786440 | tf_op jit(solution)/shard_map/ppermute | solution.py:23
  133.0 8.1 %collective-permute-start.41 = (bf16[128,1024]{1,0:T(8,128)(2,1)S(1)}, bf16[128,1024]{1,0:T(8,128)(2,1)S(1)}, u32[]{:S(2)}, u32[]{:S(2)}) collective-permute-start(bf16[128,1024]{1,0:T(8,128)(2,1)S(1)} %fusion.12), channel_id=1, source_target_pairs={{0,4},{4,0},{8,12},{12,8},{16,20},{20,16},{24,28},{28,24},{1,5},{5... | collective-permute-start | bytes 786440 | tf_op jit(solution)/shard_map/ppermute | solution.py:23
  133.7 12.1 %collective-permute-start.32 = (bf16[128,1024]{1,0:T(8,128)(2,1)S(1)}, bf16[128,1024]{1,0:T(8,128)(2,1)S(1)}, u32[]{:S(2)}, u32[]{:S(2)}) collective-permute-start(bf16[128,1024]{1,0:T(8,128)(2,1)S(1)} %fusion.4), channel_id=1, source_target_pairs={{0,24},{4,28},{8,16},{12,20},{16,8},{20,12},{24,0},{28,4},{1,25},{... | collective-permute-start | bytes 786440 | tf_op jit(solution)/shard_map/ppermute | solution.py:23
  138.3 12.9 %collective-permute-start.37 = (bf16[128,1024]{1,0:T(8,128)(2,1)S(1)}, bf16[128,1024]{1,0:T(8,128)(2,1)S(1)}, u32[]{:S(2)}, u32[]{:S(2)}) collective-permute-start(bf16[128,1024]{1,0:T(8,128)(2,1)S(1)} %fusion.5), channel_id=1, source_target_pairs={{0,16},{4,20},{8,24},{12,28},{16,0},{20,4},{24,8},{28,12},{1,17},{... | collective-permute-start | bytes 786440 | tf_op jit(solution)/shard_map/ppermute | solution.py:23
  141.1 10.0 %collective-permute-start.44 = (bf16[128,1024]{1,0:T(8,128)(2,1)S(1)}, bf16[128,1024]{1,0:T(8,128)(2,1)S(1)}, u32[]{:S(2)}, u32[]{:S(2)}) collective-permute-start(bf16[128,1024]{1,0:T(8,128)(2,1)S(1)} %fusion.13), channel_id=1, source_target_pairs={{0,2},{1,3},{2,0},{3,1},{4,6},{5,7},{6,4},{7,5},{8,10},{9,11},{10,... | collective-permute-start | bytes 786440 | tf_op jit(solution)/shard_map/ppermute | solution.py:23
  143.9 7.3 %collective-permute-start.46 = (bf16[128,1024]{1,0:T(8,128)(2,1)S(1)}, bf16[128,1024]{1,0:T(8,128)(2,1)S(1)}, u32[]{:S(2)}, u32[]{:S(2)}) collective-permute-start(bf16[128,1024]{1,0:T(8,128)(2,1)S(1)} %fusion.14), channel_id=1, source_target_pairs={{0,4},{4,0},{8,12},{12,8},{16,20},{20,16},{24,28},{28,24},{1,5},{5... | collective-permute-start | bytes 786440 | tf_op jit(solution)/shard_map/ppermute | solution.py:23
  144.2 9.6 %collective-permute-start.42 = (bf16[128,1024]{1,0:T(8,128)(2,1)S(1)}, bf16[128,1024]{1,0:T(8,128)(2,1)S(1)}, u32[]{:S(2)}, u32[]{:S(2)}) collective-permute-start(bf16[128,1024]{1,0:T(8,128)(2,1)S(1)} %fusion.6), channel_id=1, source_target_pairs={{0,8},{4,12},{8,0},{12,4},{16,24},{20,28},{24,16},{28,20},{1,9},{5... | collective-permute-start | bytes 786440 | tf_op jit(solution)/shard_map/ppermute | solution.py:23
  (30 other events, 145.3 us)

commit v3 on v2

--- a/solution.py
+++ b/solution.py
@@ -42,87 +42,98 @@
 def on_few(hidden, head, factor_rows, factor_basis, targets, loss_mask):
     n_z = lax.axis_size("vocab") // 2
     n_tok = lax.axis_size("tok")
+    bits = [1 << b for b in range(n_z.bit_length() - 1)]
     v = lax.axis_index("vocab")
     t = lax.axis_index("tok")
+    y, z = v & 1, v >> 1
     toks, width = hidden.shape
     rows = head.shape[0]
     new_here = factor_rows.shape[0]
-    half = width // 2
-
-    head_other = swap_core(head)
-    rows_all, row_blocks = factor_rows, [0]
-    for bit in [1 << b for b in range(1, n_z.bit_length() - 1 + 1)][::-1] + [1]:
+    rank = factor_basis.shape[0]
+
+    def pack(array, which, blocks):
+        cuts = [
+            lax.dynamic_slice_in_dim(array, (2 * block + which) * width, width, 1)
+            for block in blocks
+        ]
+        return jnp.concatenate(cuts, axis=1) if len(cuts) > 1 else cuts[0]
+
+    first, last = list(range(n_z - 1)), [n_z - 1]
+    send_first, hidden = lax.optimization_barrier((pack(head, 1 - y, first), hidden))
+    beside_first = swap_y(send_first)
+
+    shards = {0: hidden}
+    for bit in reversed(bits):
+        for j in list(shards):
+            shards[j ^ bit] = swap_z(shards[j], bit)
+    cross = {j: swap_x(shards[j]) for j in shards}
+
+    beside_last = swap_y(pack(head, 1 - y, last))
+    kept = pack(head, y, range(n_z))
+    kept_core = swap_core(kept)
+    beside = jnp.concatenate([beside_first, beside_last], axis=1)
+    beside_core = jnp.concatenate([swap_core(beside_first), swap_core(beside_last)], axis=1)
+    basis_half = pack(factor_basis, y, range(n_z))
+
+    token_info, rows_all, _ = lax.optimization_barrier(
+        (jnp.stack([targets, loss_mask]), factor_rows, shards[bits[-1] if bits else 0])
+    )
+    row_blocks = [0]
+    for bit in [2 * b for b in reversed(bits)] + [1]:
         rows_all = jnp.concatenate([rows_all, swap(rows_all, "vocab", bit)], axis=0)
         row_blocks = row_blocks + [j ^ bit for j in row_blocks]
-    token_info = jnp.stack([targets, loss_mask])
     token_info = jnp.concatenate([token_info, swap_x(token_info)], axis=1)
-    shards = [hidden] + [swap_z(hidden, k) for k in range(1, n_z)]
-    pieces = []
-    for shard in shards:
-        from_x = swap_x(shard)
-        from_y = swap_y(shard)
-        diag_a = swap_x(from_y[:, :half])
-        diag_b = swap_y(from_x[:, half:])
-        pieces.append((from_x, from_y, diag_a, diag_b))
-
-    def weights(dy, dz):
-        start = (v ^ (2 * dz + dy)) * width
-        cut = lambda a: lax.dynamic_slice_in_dim(a, start, width, 1)
-        return jnp.concatenate([cut(head), cut(head_other), cut(factor_basis)], axis=0)
-
-    blocks = [[weights(dy, dz) for dy in range(2)] for dz in range(n_z)]
-
-    own = jnp.zeros((2 * rows + factor_basis.shape[0], toks), f32)
-    other = own
-    for dz in range(n_z):
-        from_x, from_y, diag_a, diag_b = pieces[dz]
-        own = own + dot_last(blocks[dz][0], shards[dz])
-        own = own + dot_last(blocks[dz][1], from_y)
-        other = other + dot_last(blocks[dz][0], from_x)
-        other = other + dot_last(blocks[dz][1][:, :half], diag_a)
-        other = other + dot_last(blocks[dz][1][:, half:], diag_b)
-    both = jnp.concatenate([own, other], axis=1)
-    frozen = both[: 2 * rows]
-    hidden_basis = both[2 * rows :].astype(bf16)
-
-    def merge(stats):
-        top = stats[0][0]
-        for s in stats[1:]:
-            top = jnp.maximum(top, s[0])
-        total = stats[0][1] * jnp.exp(stats[0][0] - top)
-        for s in stats[1:]:
-            total = total + s[1] * jnp.exp(s[0] - top)
-        return jnp.stack([top, total])
+
+    def in_order(parts):
+        whole = jnp.zeros((toks, n_z * width), bf16)
+        for j in sorted(parts):
+            whole = lax.dynamic_update_slice_in_dim(whole, parts[j], (z ^ j) * width, 1)
+        return whole
+
+    upper = jnp.concatenate([kept, kept_core, basis_half], axis=0)
+    lower = jnp.concatenate([beside, beside_core], axis=0)
+
+    def add_over_y(tokens):
+        up = dot_last(upper, tokens)
+        low = dot_last(lower, tokens)
+        mine = jnp.concatenate([up[: 2 * rows], low, up[2 * rows :]], axis=0)
+        theirs = swap_y(mine)
+        turned = jnp.concatenate(
+            [theirs[2 * rows : 4 * rows], theirs[: 2 * rows], theirs[4 * rows :]], axis=0
+        )
+        return mine + turned
+
+    both = jnp.concatenate([add_over_y(in_order(shards)), add_over_y(in_order(cross))], axis=1)
+    frozen = both[: 4 * rows]
+    hidden_basis = both[4 * rows :].astype(bf16)
+
+    def merge(a, b):
+        top = jnp.maximum(a[0], b[0])
+        return jnp.stack([top, a[1] * jnp.exp(a[0] - top) + b[1] * jnp.exp(b[0] - top)])
 
     def local(logits):
         top = jnp.max(logits, axis=0)
         return jnp.stack([top, jnp.sum(jnp.exp(logits - top[None, :]), axis=0)])
 
-    def turn(stats):
-        return jnp.concatenate([stats[:, toks:], stats[:, :toks]], axis=1)
-
     stats = local(frozen)
-    stats = merge([stats, turn(swap_x(stats))])
-    stats = merge([stats, swap_y(stats)])
-    step = 1
-    while step < n_z:
-        stats = merge([stats, swap_z(stats, step)])
-        step *= 2
+    turned = swap_x(stats)
+    stats = merge(stats, jnp.concatenate([turned[:, toks:], turned[:, :toks]], axis=1))
+    for bit in bits:
+        stats = merge(stats, swap_z(stats, bit))
     fresh = lax.dot_general(
         rows_all, hidden_basis, (((1,), (0,)), ((), ())), preferred_element_type=f32
     )
-    stats = merge([stats, local(fresh)])
+    stats = merge(stats, local(fresh))
     row_top, sum_exp = stats[0], stats[1]
 
     weight_row = loss_scale * token_info[1].astype(f32)
     scale_row = weight_row / sum_exp
     row_iota = lax.broadcasted_iota(jnp.int32, (rows, 1), 0)
     row_ids = jnp.concatenate(
-        [row_iota + (v * n_tok + t) * rows, row_iota + (v * n_tok + (t ^ 1)) * rows], axis=0
+        [row_iota + (vv * n_tok + tt) * rows for vv in (v, v ^ 1) for tt in (t, t ^ 1)], axis=0
     )
     hit = jnp.where(row_ids == token_info[0][None, :], weight_row[None, :], 0.0)
     grad = (jnp.exp(frozen - row_top[None, :]) * scale_row[None, :] - hit).astype(bf16)
-    grad_own, grad_other = grad[:, :toks], grad[:, toks:]
 
     frozen_rows = rows * n_tok * lax.axis_size("vocab")
     new_iota = lax.broadcasted_iota(jnp.int32, (new_here, 1), 0) + frozen_rows
@@ -135,30 +146,20 @@
     rows_part = dot_last(fresh_grad[:new_here], hidden_basis[:, :toks])
     basis_part = lax.reduce_precision(jnp.dot(mix_total, hidden, preferred_element_type=f32), 8, 7)
 
-    def part(grads, dy, dz, cols=slice(None)):
-        return dot_first(grads, blocks[dz][dy][: 2 * rows, cols])
-
-    arrived = []
-    diag_a = diag_b = None
-    for dz in range(n_z - 1, -1, -1):
-        send_a = part(grad_other, 1, dz, slice(0, half)).astype(bf16)
-        send_b = part(grad_other, 1, dz, slice(half, width)).astype(bf16)
-        if diag_a is not None:
-            send_a, send_b, _, _ = lax.optimization_barrier((send_a, send_b, diag_a, diag_b))
-        diag_a = swap_x(send_a)
-        diag_b = swap_y(send_b)
-        to_x = part(grad_other, 0, dz) + jnp.pad(diag_b.astype(f32), ((0, 0), (half, 0)))
-        to_y = part(grad_own, 1, dz) + jnp.pad(diag_a.astype(f32), ((0, 0), (0, width - half)))
-        from_x = swap_x(to_x.astype(bf16))
-        from_y = swap_y(to_y.astype(bf16))
-        here = part(grad_own, 0, dz) + from_x.astype(f32) + from_y.astype(f32)
-        arrived.append(swap_z(here.astype(bf16), dz).astype(f32) if dz else here)
-
+    weights = jnp.concatenate([upper[: 2 * rows], lower], axis=0)
+
+    def part(grads, j):
+        return dot_first(grads, lax.dynamic_slice_in_dim(weights, (z ^ j) * width, width, 1))
+
+    sums = {}
+    for j in reversed(range(n_z)):
+        from_x = swap_x(part(grad[:, toks:], j).astype(bf16))
+        sums[j] = part(grad[:, :toks], j) + from_x.astype(f32)
+    for bit in bits:
+        for j in [j for j in sorted(sums, reverse=True) if j & bit]:
+            sums[j ^ bit] = sums[j ^ bit] + swap_z(sums.pop(j).astype(bf16), bit).astype(f32)
     basis_here = lax.dynamic_slice_in_dim(factor_basis, v * width, width, 1)
-    hidden_grad = dot_first(mix_total, basis_here)
-    for piece in arrived:
-        hidden_grad = hidden_grad + piece
-    hidden_grad = hidden_grad.astype(bf16)
+    hidden_grad = (sums[0] + dot_first(mix_total, basis_here)).astype(bf16)
 
     basis_two = basis_part + swap_x(basis_part.astype(bf16)).astype(f32)
     basis_grad = basis_two + swap_core(basis_two)

time: 156 us -> 143 us (0.917)
  other arithmetic: 7.84 us -> 34.7 us
  starting transfers between devices: 53 us -> 33.7 us
  waiting for transfers between devices: 60.9 us -> 51.2 us
  matrix products: 19.2 us -> 9.88 us
    concatenate x6 -> x7, other arithmetic: 0.77 us -> 29.5 us  [the longest x1 19 us: on_few(): upper = jnp.concatenate([kept, kept_core, basis_half], axis=0)]
    ppermute x51 -> x32, starting transfers between devices: 53 us -> 33.7 us  [swap(): return lax.ppermute(value, axis, [(i, i ^ bit) for i in range(size)])]
    ppermute x51 -> x32, waiting for transfers between devices: 60.9 us -> 51.2 us  [swap(): return lax.ppermute(value, axis, [(i, i ^ bit) for i in range(size)])]
    dot_general x21 -> x5, matrix products: 12.8 us -> 3.44 us  [dot_last(): return lax.dot_general(a, b, contract_last, preferred_element_type=f32)]
    slice x9, local copies, waits for them, and re-layouts: 3.7 us -> 0.08 us  [the longest x2 0.04 us: add_over_y(): theirs[2 * rows:4 * rows]]
    dynamic_update_slice x0 -> x8, local copies, waits for them, and re-layouts: none -> 3.03 us  [in_order(): whole = lax.dynamic_update_slice_in_dim(whole, parts[j], (z ^ j) * width, 1)]
    unnamed x25 -> x28, local copies, waits for them, and re-layouts: 3.36 us -> 1.98 us
    dynamic_slice x3 -> x2, local copies, waits for them, and re-layouts: 4.12 us -> 4.31 us  [pack(): lax.dynamic_slice_in_dim(array, (2 * block + which) * width, width, 1)]
  transfers between devices with their start and end apart: 51 -> 32, of which waited for: 28 -> 16; matrix products, arithmetic and copies ran while one was open for 23% -> 33% of each run, Pallas kernels for 0% -> 0%
where the time goes in v3:
time: 143 us
  waiting for transfers between devices  51.2 us (36%)
  other arithmetic  34.7 us (24%)
  starting transfers between devices  33.7 us (24%)
  local copies, waits for them, and re-layouts  12 us (8%)
  matrix products  9.88 us (7%)
    ppermute x32, waiting for transfers between devices, swap(): return lax.ppermute(value, axis, [(i, i ^ bit) for i in range(size)])  51.2 us
    ppermute x32, starting transfers between devices, swap(): return lax.ppermute(value, axis, [(i, i ^ bit) for i in range(size)])  33.7 us
    concatenate x1, other arithmetic, on_few(): upper = jnp.concatenate([kept, kept_core, basis_half], axis=0)  19 us
    concatenate x1, other arithmetic, on_few(): weights = jnp.concatenate([upper[:2 * rows], lower], axis=0)  8.8 us
    dot_general x10, matrix products, dot_first(): return lax.dot_general(a, b, contract_first, preferred_element_type=f32)  6.02 us
    dynamic_slice x2, local copies, waits for them, and re-layouts, pack(): lax.dynamic_slice_in_dim(array, (2 * block + which) * width, width, 1)  4.31 us
    dot_general x5, matrix products, dot_last(): return lax.dot_general(a, b, contract_last, preferred_element_type=f32)  3.44 us
    dynamic_update_slice x8, local copies, waits for them, and re-layouts, in_order(): whole = lax.dynamic_update_slice_in_dim(whole, parts[j], (z ^ j) * width, 1)  3.03 us
  transfers between devices with their start and end apart: 32, of which 16 were waited for; matrix products, arithmetic and copies ran while one was open for 33% of the time, Pallas kernels for 0%

profile of v3, /device:TPU:0, one launch (start us, length us, event | category | flops | bytes accessed | tf_op | source)
XLA Modules:
  0.0 142.7 jit_solution(16767231874506436645)
XLA Ops:
  0.7 2.5 %constant_dynamic-slice_fusion = (bf16[128,1024]{1,0:T(8,128)(2,1)}, bf16[128,1024]{1,0:T(8,128)(2,1)S(1)}, bf16[128,1024]{1,0:T(8,128)(2,1)S(1)}, bf16[128,1024...) fusion(bf16[128,8192]{1,0:T(8,128)(2,1)} %param.7, ...), kind=kLoop, calls=%fused_computation.91 | loop fusion | bytes 4194336 | tf_op jit(solution)/shard_map/dynamic_slice | solution.py:56
  4.1 3.0 %collective-permute-start.1 = (bf16[128,1024]{1,0:T(8,128)(2,1)S(1)}, bf16[128,1024]{1,0:T(8,128)(2,1)}, u32[]{:S(2)}, u32[]{:S(2)}) collective-permute-start(bf16[128,1024]{1,0:T(8,128)(2,1)S(1)} %copy-done.1), channel_id=1, source_target_pairs={{0,8},{4,12},{8,0},{12,4},{16,24},{20,28},{24,16},{28,20},{1,9},{5... | collective-permute-start | bytes 786440 | tf_op jit(solution)/shard_map/ppermute | solution.py:23
  7.1 2.6 %collective-permute-start.2 = (bf16[128,1024]{1,0:T(8,128)(2,1)S(1)}, bf16[128,1024]{1,0:T(8,128)(2,1)}, u32[]{:S(2)}, u32[]{:S(2)}) collective-permute-start(bf16[128,1024]{1,0:T(8,128)(2,1)S(1)} %copy-done.1), channel_id=1, source_target_pairs={{0,16},{4,20},{8,24},{12,28},{16,0},{20,4},{24,8},{28,12},{1,17},{... | collective-permute-start | bytes 786440 | tf_op jit(solution)/shard_map/ppermute | solution.py:23
  9.7 1.5 %collective-permute-start.9 = (bf16[128,1024]{1,0:T(8,128)(2,1)S(1)}, bf16[128,1024]{1,0:T(8,128)(2,1)}, u32[]{:S(2)}, u32[]{:S(2)}) collective-permute-start(bf16[128,1024]{1,0:T(8,128)(2,1)S(1)} %copy-done.1), channel_id=1, source_target_pairs={{0,2},{1,3},{2,0},{3,1},{4,6},{5,7},{6,4},{7,5},{8,10},{9,11},{10,... | collective-permute-start | bytes 786440 | tf_op jit(solution)/shard_map/ppermute | solution.py:23
  11.2 1.5 %collective-permute-start.4 = (bf16[128,3072]{1,0:T(8,128)(2,1)}, bf16[128,3072]{1,0:T(8,128)(2,1)}, u32[]{:S(2)}, u32[]{:S(2)}) collective-permute-start(bf16[128,3072]{1,0:T(8,128)(2,1)} %pad_maximum_fusion.5), channel_id=1, source_target_pairs={{0,4},{4,0},{8,12},{12,8},{16,20},{20,16},{24,28},{28,24},{1,5},{5... | collective-permute-start | bytes 2359304 | tf_op jit(solution)/shard_map/ppermute | solution.py:23
  16.4 1.8 %constant_dynamic-slice_fusion.7 = (bf16[64,1024]{1,0:T(8,128)(2,1)S(1)}, bf16[64,1024]{1,0:T(8,128)(2,1)}, bf16[64,1024]{1,0:T(8,128)(2,1)}, bf16[64,1024]{1,0:T(8,128)(2,1)}) fusion(bf16[64,8192]{1,0:T(8,128)(2,1)} %param.9, s32[]{:T(128)S(6)} %select_n.63, s32[]{:T(128)S(6)} %select_n.65, s32[]{:T(128)S(6)} %select_n.64, s32[]{:T(128)S(6)} %select_n.66), kind=kLoop, calls=%fused_computation.102 | loop fusion | bytes 1048592 | tf_op jit(solution)/shard_map/dynamic_slice | solution.py:56
  18.9 1.4 concatenate.84
  22.6 1.5 %collective-permute-start.20 = (s32[2,128]{1,0:T(2,128)}, s32[2,128]{1,0:T(2,128)S(1)}, u32[]{:S(2)}, u32[]{:S(2)}) collective-permute-start(s32[2,128]{1,0:T(2,128)} %pad_add_fusion.1), channel_id=1, source_target_pairs={{0,2},{1,3},{2,0},{3,1},{4,6},{5,7},{6,4},{7,5},{8,10},{9,11},{10,... | collective-permute-start | bytes 3080 | tf_op jit(solution)/shard_map/ppermute | solution.py:23
  26.0 2.8 %collective-permute-start.3 = (bf16[128,1024]{1,0:T(8,128)(2,1)}, bf16[128,1024]{1,0:T(8,128)(2,1)S(1)}, u32[]{:S(2)}, u32[]{:S(2)}) collective-permute-start(bf16[128,1024]{1,0:T(8,128)(2,1)} %collective-permute-done.2), channel_id=1, source_target_pairs={{0,8},{4,12},{8,0},{12,4},{16,24},{20,28},{24,16},{28,20},{1,9},{5... | collective-permute-start | bytes 786440 | tf_op jit(solution)/shard_map/ppermute | solution.py:23
  30.7 3.8 %collective-permute-done.18 = bf16[128,64]{1,0:T(8,128)(2,1)S(1)} collective-permute-done((bf16[128,64]{1,0:T(8,128)(2,1)S(1)}, bf16[128,64]{1,0:T(8,128)(2,1)S(1)}, u32[]{:S(2)}, u32[]{:S(2)}) %collective-permute-start.18) | collective-permute-done | bytes 16416 | tf_op jit(solution)/shard_map/ppermute | solution.py:23
  34.5 1.6 %collective-permute-start.19 = (bf16[256,64]{1,0:T(8,128)(2,1)S(1)}, bf16[256,64]{1,0:T(8,128)(2,1)S(1)}, u32[]{:S(2)}, u32[]{:S(2)}) collective-permute-start(bf16[256,64]{1,0:T(8,128)(2,1)S(1)} %pad_maximum_fusion.9), channel_id=1, source_target_pairs={{0,4},{4,0},{8,12},{12,8},{16,20},{20,16},{24,28},{28,24},{1,5},{5... | collective-permute-start | bytes 98312 | tf_op jit(solution)/shard_map/ppermute | solution.py:23
  36.3 2.6 %collective-permute-done.19 = bf16[256,64]{1,0:T(8,128)(2,1)S(1)} collective-permute-done((bf16[256,64]{1,0:T(8,128)(2,1)S(1)}, bf16[256,64]{1,0:T(8,128)(2,1)S(1)}, u32[]{:S(2)}, u32[]{:S(2)}) %collective-permute-start.19) | collective-permute-done | bytes 32800 | tf_op jit(solution)/shard_map/ppermute | solution.py:23
  38.9 1.5 %collective-permute-start.11 = (bf16[128,1024]{1,0:T(8,128)(2,1)}, bf16[128,1024]{1,0:T(8,128)(2,1)S(1)}, u32[]{:S(2)}, u32[]{:S(2)}) collective-permute-start(bf16[128,1024]{1,0:T(8,128)(2,1)} %collective-permute-done.2), channel_id=1, source_target_pairs={{0,2},{1,3},{2,0},{3,1},{4,6},{5,7},{6,4},{7,5},{8,10},{9,11},{10,... | collective-permute-start | bytes 786440 | tf_op jit(solution)/shard_map/ppermute | solution.py:23
  41.1 6.9 %collective-permute-done.11 = bf16[128,1024]{1,0:T(8,128)(2,1)S(1)} collective-permute-done((bf16[128,1024]{1,0:T(8,128)(2,1)}, bf16[128,1024]{1,0:T(8,128)(2,1)S(1)}, u32[]{:S(2)}, u32[]{:S(2)}) %collective-permute-start.11) | collective-permute-done | bytes 262176 | tf_op jit(solution)/shard_map/ppermute | solution.py:23
  48.1 2.8 %collective-permute-done.12 = bf16[128,1024]{1,0:T(8,128)(2,1)S(1)} collective-permute-done((bf16[128,1024]{1,0:T(8,128)(2,1)S(1)}, bf16[128,1024]{1,0:T(8,128)(2,1)S(1)}, u32[]{:S(2)}, u32[]{:S(2)}) %collective-permute-start.12) | collective-permute-done | bytes 262176 | tf_op jit(solution)/shard_map/ppermute | solution.py:23
  53.2 19.0 %maximum_maximum_fusion = bf16[320,4096]{1,0:T(8,128)(2,1)S(1)} fusion(bf16[64,1024]{1,0:T(8,128)(2,1)S(1)} %copy-done.4, bf16[64,1024]{1,0:T(8,128)(2,1)S(1)} %copy-done.2, bf16[64,1024]{1,0:T(8,128)(2,1)S(1)} %copy-done.3, bf16[64,1024]{1,0:T(8,128)(2,1)S(1)} %get-tuple-element.30, bf16[128,4096]{1,0:T(8,128)(2,1)S(1)} %collective-permute-done, ...), kind=kLoop, calls=%fused_computation.1 | loop fusion | flops 23592960 | bytes 5242880 | tf_op jit(solution)/shard_map/concatenate | solution.py:93
  75.8 1.6 %collective-permute-start.8 = (f32[576,128]{1,0:T(8,128)S(1)}, f32[576,128]{1,0:T(8,128)S(1)}, u32[]{:S(2)}, u32[]{:S(2)}) collective-permute-start(f32[576,128]{1,0:T(8,128)S(1)} %pad_maximum_fusion.7), channel_id=1, source_target_pairs={{0,4},{4,0},{8,12},{12,8},{16,20},{20,16},{24,28},{28,24},{1,5},{5... | collective-permute-start | bytes 884744 | tf_op jit(solution)/shard_map/ppermute | solution.py:23
  77.9 8.8 %pad_maximum_fusion = bf16[512,4096]{1,0:T(8,128)(2,1)S(1)} fusion(bf16[128,4096]{1,0:T(8,128)(2,1)S(1)} %constant_dynamic-update-slice_fusion.2, bf16[128,4096]{1,0:T(8,128)(2,1)S(1)} %constant_dynamic-update-slice_fusion, bf16[128,4096]{1,0:T(8,128)(2,1)S(1)} %collective-permute-done, bf16[128,1024]{1,0:T(8,128)(2,1)S(1)} %get-tuple-element.25, ...), kind=kLoop, calls=%fused_computation | loop fusion | flops 29360128 | bytes 8388608 | tf_op jit(solution)/shard_map/concatenate | solution.py:149
  86.9 4.7 %collective-permute-done.13 = f32[576,128]{1,0:T(8,128)S(1)} collective-permute-done((f32[576,128]{1,0:T(8,128)S(1)}, f32[576,128]{1,0:T(8,128)S(1)}, u32[]{:S(2)}, u32[]{:S(2)}) %collective-permute-start.13) | collective-permute-done | bytes 294944 | tf_op jit(solution)/shard_map/ppermute | solution.py:23
  91.9 1.4 %collective-permute-start.14 = (f32[2,256]{1,0:T(2,128)S(1)}, f32[2,256]{1,0:T(2,128)S(1)}, u32[]{:S(2)}, u32[]{:S(2)}) collective-permute-start(f32[2,256]{1,0:T(2,128)S(1)} %pad_maximum_fusion.11), channel_id=1, source_target_pairs={{0,2},{1,3},{2,0},{3,1},{4,6},{5,7},{6,4},{7,5},{8,10},{9,11},{10,... | collective-permute-start | bytes 6152 | tf_op jit(solution)/shard_map/ppermute | solution.py:23
  93.4 2.2 %collective-permute-done.14 = f32[2,256]{1,0:T(2,128)S(1)} collective-permute-done((f32[2,256]{1,0:T(2,128)S(1)}, f32[2,256]{1,0:T(2,128)S(1)}, u32[]{:S(2)}, u32[]{:S(2)}) %collective-permute-start.14) | collective-permute-done | bytes 2080 | tf_op jit(solution)/shard_map/ppermute | solution.py:23
  97.0 2.2 %collective-permute-done.15 = f32[2,256]{1,0:T(2,128)S(1)} collective-permute-done((f32[2,256]{1,0:T(2,128)S(1)}, f32[2,256]{1,0:T(2,128)S(1)}, u32[]{:S(2)}, u32[]{:S(2)}) %collective-permute-start.15) | collective-permute-done | bytes 2080 | tf_op jit(solution)/shard_map/ppermute | solution.py:23
  100.5 3.3 %collective-permute-done.16 = f32[2,256]{1,0:T(2,128)S(1)} collective-permute-done((f32[2,256]{1,0:T(2,128)S(1)}, f32[2,256]{1,0:T(2,128)S(1)}, u32[]{:S(2)}, u32[]{:S(2)}) %collective-permute-start.16) | collective-permute-done | bytes 2080 | tf_op jit(solution)/shard_map/ppermute | solution.py:23
  105.3 1.4 %collective-permute-start.25 = (bf16[128,1024]{1,0:T(8,128)(2,1)S(1)}, bf16[128,1024]{1,0:T(8,128)(2,1)S(1)}, u32[]{:S(2)}, u32[]{:S(2)}) collective-permute-start(bf16[128,1024]{1,0:T(8,128)(2,1)S(1)} %convolution_convert_fusion), channel_id=1, source_target_pairs={{0,2},{1,3},{2,0},{3,1},{4,6},{5,7},{6,4},{7,5},{8,10},{9,11},{10,... | collective-permute-start | bytes 786440 | tf_op jit(solution)/shard_map/ppermute | solution.py:23
  107.8 1.4 collective-permute-start.21
  110.2 1.4 %collective-permute-start.24 = (bf16[128,1024]{1,0:T(8,128)(2,1)S(1)}, bf16[128,1024]{1,0:T(8,128)(2,1)S(1)}, u32[]{:S(2)}, u32[]{:S(2)}) collective-permute-start(bf16[128,1024]{1,0:T(8,128)(2,1)S(1)} %convolution_convert_fusion.1), channel_id=1, source_target_pairs={{0,2},{1,3},{2,0},{3,1},{4,6},{5,7},{6,4},{7,5},{8,10},{9,11},{10,... | collective-permute-start | bytes 786440 | tf_op jit(solution)/shard_map/ppermute | solution.py:23
  111.6 3.0 %collective-permute-done.25 = bf16[128,1024]{1,0:T(8,128)(2,1)S(1)} collective-permute-done((bf16[128,1024]{1,0:T(8,128)(2,1)S(1)}, bf16[128,1024]{1,0:T(8,128)(2,1)S(1)}, u32[]{:S(2)}, u32[]{:S(2)}) %collective-permute-start.25) | collective-permute-done | bytes 262176 | tf_op jit(solution)/shard_map/ppermute | solution.py:23
  117.5 9.2 %collective-permute-done.22 = bf16[128,1024]{1,0:T(8,128)(2,1)S(1)} collective-permute-done((bf16[128,1024]{1,0:T(8,128)(2,1)S(1)}, bf16[128,1024]{1,0:T(8,128)(2,1)S(1)}, u32[]{:S(2)}, u32[]{:S(2)}) %collective-permute-start.22) | collective-permute-done | bytes 262176 | tf_op jit(solution)/shard_map/ppermute | solution.py:23
  128.2 1.6 %collective-permute-done.24 = bf16[128,1024]{1,0:T(8,128)(2,1)S(1)} collective-permute-done((bf16[128,1024]{1,0:T(8,128)(2,1)S(1)}, bf16[128,1024]{1,0:T(8,128)(2,1)S(1)}, u32[]{:S(2)}, u32[]{:S(2)}) %collective-permute-start.24) | collective-permute-done | bytes 262176 | tf_op jit(solution)/shard_map/ppermute | solution.py:23
  131.8 3.2 %collective-permute-done.28 = f32[64,64]{1,0:T(8,128)S(1)} collective-permute-done((f32[64,64]{1,0:T(8,128)S(1)}, f32[64,64]{1,0:T(8,128)S(1)}, u32[]{:S(2)}, u32[]{:S(2)}) %collective-permute-start.28) | collective-permute-done | bytes 16416 | tf_op jit(solution)/shard_map/ppermute | solution.py:23
  137.6 2.8 %collective-permute-done.27 = bf16[128,1024]{1,0:T(8,128)(2,1)S(1)} collective-permute-done((bf16[128,1024]{1,0:T(8,128)(2,1)S(1)}, bf16[128,1024]{1,0:T(8,128)(2,1)S(1)}, u32[]{:S(2)}, u32[]{:S(2)}) %collective-permute-start.27) | collective-permute-done | bytes 262176 | tf_op jit(solution)/shard_map/ppermute | solution.py:23
  140.4 2.3 %fusion.6 = bf16[128,1024]{1,0:T(8,128)(2,1)} fusion(f32[128,1024]{1,0:T(8,128)S(1)} %fusion.24, bf16[512,4096]{1,0:T(8,128)(2,1)} %copy-done, s32[]{:T(128)S(6)} %select_n.70, bf16[128,1024]{1,0:T(8,128)(2,1)S(1)} %collective-permute-done.27, bf16[128,1024]{1,0:T(8,128)(2,1)S(1)} %collective-permute-done.23, ...), kind=kOutput, calls=%fused_computation.13 | convolution fusion | flops 135266304 | bytes 2752516 | tf_op jit(solution)/shard_map/dot_general | solution.py:18
  (143 shorter events, 34.0 us)
Async XLA Ops:
  4.1 18.5 %collective-permute-start.1 = (bf16[128,1024]{1,0:T(8,128)(2,1)S(1)}, bf16[128,1024]{1,0:T(8,128)(2,1)}, u32[]{:S(2)}, u32[]{:S(2)}) collective-permute-start(bf16[128,1024]{1,0:T(8,128)(2,1)S(1)} %copy-done.1), channel_id=1, source_target_pairs={{0,8},{4,12},{8,0},{12,4},{16,24},{20,28},{24,16},{28,20},{1,9},{5... | collective-permute-start | bytes 786440 | tf_op jit(solution)/shard_map/ppermute | solution.py:23
  7.1 14.4 %collective-permute-start.2 = (bf16[128,1024]{1,0:T(8,128)(2,1)S(1)}, bf16[128,1024]{1,0:T(8,128)(2,1)}, u32[]{:S(2)}, u32[]{:S(2)}) collective-permute-start(bf16[128,1024]{1,0:T(8,128)(2,1)S(1)} %copy-done.1), channel_id=1, source_target_pairs={{0,16},{4,20},{8,24},{12,28},{16,0},{20,4},{24,8},{28,12},{1,17},{... | collective-permute-start | bytes 786440 | tf_op jit(solution)/shard_map/ppermute | solution.py:23
  9.7 16.3 %collective-permute-start.9 = (bf16[128,1024]{1,0:T(8,128)(2,1)S(1)}, bf16[128,1024]{1,0:T(8,128)(2,1)}, u32[]{:S(2)}, u32[]{:S(2)}) collective-permute-start(bf16[128,1024]{1,0:T(8,128)(2,1)S(1)} %copy-done.1), channel_id=1, source_target_pairs={{0,2},{1,3},{2,0},{3,1},{4,6},{5,7},{6,4},{7,5},{8,10},{9,11},{10,... | collective-permute-start | bytes 786440 | tf_op jit(solution)/shard_map/ppermute | solution.py:23
  11.2 39.7 %collective-permute-start.4 = (bf16[128,3072]{1,0:T(8,128)(2,1)}, bf16[128,3072]{1,0:T(8,128)(2,1)}, u32[]{:S(2)}, u32[]{:S(2)}) collective-permute-start(bf16[128,3072]{1,0:T(8,128)(2,1)} %pad_maximum_fusion.5), channel_id=1, source_target_pairs={{0,4},{4,0},{8,12},{12,8},{16,20},{20,16},{24,28},{28,24},{1,5},{5... | collective-permute-start | bytes 2359304 | tf_op jit(solution)/shard_map/ppermute | solution.py:23
  12.7 23.6 %collective-permute-start.5 = (bf16[128,1024]{1,0:T(8,128)(2,1)}, bf16[128,1024]{1,0:T(8,128)(2,1)}, u32[]{:S(2)}, u32[]{:S(2)}) collective-permute-start(bf16[128,1024]{1,0:T(8,128)(2,1)} %get-tuple-element.22), channel_id=1, source_target_pairs={{0,4},{4,0},{8,12},{12,8},{16,20},{20,16},{24,28},{28,24},{1,5},{5... | collective-permute-start | bytes 786440 | tf_op jit(solution)/shard_map/ppermute | solution.py:23
  21.6 8.9 %collective-permute-start.17 = (bf16[64,64]{1,0:T(8,128)(2,1)S(1)}, bf16[64,64]{1,0:T(8,128)(2,1)S(1)}, u32[]{:S(2)}, u32[]{:S(2)}) collective-permute-start(bf16[64,64]{1,0:T(8,128)(2,1)S(1)} %copy-done.5), channel_id=1, source_target_pairs={{0,16},{4,20},{8,24},{12,28},{16,0},{20,4},{24,8},{28,12},{1,17},{... | collective-permute-start | bytes 24584 | tf_op jit(solution)/shard_map/ppermute | solution.py:23
  22.6 7.3 %collective-permute-start.20 = (s32[2,128]{1,0:T(2,128)}, s32[2,128]{1,0:T(2,128)S(1)}, u32[]{:S(2)}, u32[]{:S(2)}) collective-permute-start(s32[2,128]{1,0:T(2,128)} %pad_add_fusion.1), channel_id=1, source_target_pairs={{0,2},{1,3},{2,0},{3,1},{4,6},{5,7},{6,4},{7,5},{8,10},{9,11},{10,... | collective-permute-start | bytes 3080 | tf_op jit(solution)/shard_map/ppermute | solution.py:23
  26.0 14.3 %collective-permute-start.3 = (bf16[128,1024]{1,0:T(8,128)(2,1)}, bf16[128,1024]{1,0:T(8,128)(2,1)S(1)}, u32[]{:S(2)}, u32[]{:S(2)}) collective-permute-start(bf16[128,1024]{1,0:T(8,128)(2,1)} %collective-permute-done.2), channel_id=1, source_target_pairs={{0,8},{4,12},{8,0},{12,4},{16,24},{20,28},{24,16},{28,20},{1,9},{5... | collective-permute-start | bytes 786440 | tf_op jit(solution)/shard_map/ppermute | solution.py:23
  29.9 11.1 %collective-permute-start.10 = (bf16[128,1024]{1,0:T(8,128)(2,1)}, bf16[128,1024]{1,0:T(8,128)(2,1)S(1)}, u32[]{:S(2)}, u32[]{:S(2)}) collective-permute-start(bf16[128,1024]{1,0:T(8,128)(2,1)} %collective-permute-done.1), channel_id=1, source_target_pairs={{0,2},{1,3},{2,0},{3,1},{4,6},{5,7},{6,4},{7,5},{8,10},{9,11},{10,... | collective-permute-start | bytes 786440 | tf_op jit(solution)/shard_map/ppermute | solution.py:23
  30.5 4.0 %collective-permute-start.18 = (bf16[128,64]{1,0:T(8,128)(2,1)S(1)}, bf16[128,64]{1,0:T(8,128)(2,1)S(1)}, u32[]{:S(2)}, u32[]{:S(2)}) collective-permute-start(bf16[128,64]{1,0:T(8,128)(2,1)S(1)} %pad_maximum_fusion.10), channel_id=1, source_target_pairs={{0,8},{4,12},{8,0},{12,4},{16,24},{20,28},{24,16},{28,20},{1,9},{5... | collective-permute-start | bytes 49160 | tf_op jit(solution)/shard_map/ppermute | solution.py:23
  34.5 4.3 %collective-permute-start.19 = (bf16[256,64]{1,0:T(8,128)(2,1)S(1)}, bf16[256,64]{1,0:T(8,128)(2,1)S(1)}, u32[]{:S(2)}, u32[]{:S(2)}) collective-permute-start(bf16[256,64]{1,0:T(8,128)(2,1)S(1)} %pad_maximum_fusion.9), channel_id=1, source_target_pairs={{0,4},{4,0},{8,12},{12,8},{16,20},{20,16},{24,28},{28,24},{1,5},{5... | collective-permute-start | bytes 98312 | tf_op jit(solution)/shard_map/ppermute | solution.py:23
  36.3 16.8 %collective-permute-start = (bf16[128,4096]{1,0:T(8,128)(2,1)S(1)}, bf16[128,4096]{1,0:T(8,128)(2,1)S(1)}, u32[]{:S(2)}, u32[]{:S(2)}) collective-permute-start(bf16[128,4096]{1,0:T(8,128)(2,1)S(1)} %pad_maximum_fusion.4), channel_id=1, source_target_pairs={{0,1},{1,0},{2,3},{3,2},{4,5},{5,4},{6,7},{7,6},{8,9},{9,8},{10,11... | collective-permute-start | bytes 3145736 | tf_op jit(solution)/shard_map/ppermute | solution.py:23
  38.9 9.2 %collective-permute-start.11 = (bf16[128,1024]{1,0:T(8,128)(2,1)}, bf16[128,1024]{1,0:T(8,128)(2,1)S(1)}, u32[]{:S(2)}, u32[]{:S(2)}) collective-permute-start(bf16[128,1024]{1,0:T(8,128)(2,1)} %collective-permute-done.2), channel_id=1, source_target_pairs={{0,2},{1,3},{2,0},{3,1},{4,6},{5,7},{6,4},{7,5},{8,10},{9,11},{10,... | collective-permute-start | bytes 786440 | tf_op jit(solution)/shard_map/ppermute | solution.py:23
  40.4 10.5 %collective-permute-start.12 = (bf16[128,1024]{1,0:T(8,128)(2,1)S(1)}, bf16[128,1024]{1,0:T(8,128)(2,1)S(1)}, u32[]{:S(2)}, u32[]{:S(2)}) collective-permute-start(bf16[128,1024]{1,0:T(8,128)(2,1)S(1)} %collective-permute-done.3), channel_id=1, source_target_pairs={{0,2},{1,3},{2,0},{3,1},{4,6},{5,7},{6,4},{7,5},{8,10},{9,11},{10,... | collective-permute-start | bytes 786440 | tf_op jit(solution)/shard_map/ppermute | solution.py:23
  41.0 33.1 %collective-permute-start.7 = (bf16[128,1024]{1,0:T(8,128)(2,1)}, bf16[128,1024]{1,0:T(8,128)(2,1)S(1)}, u32[]{:S(2)}, u32[]{:S(2)}) collective-permute-start(bf16[128,1024]{1,0:T(8,128)(2,1)} %collective-permute-done.5), channel_id=1, source_target_pairs={{0,1},{1,0},{2,3},{3,2},{4,5},{5,4},{6,7},{7,6},{8,9},{9,8},{10,11... | collective-permute-start | bytes 786440 | tf_op jit(solution)/shard_map/ppermute | solution.py:23
  50.9 23.2 %collective-permute-start.6 = (bf16[128,3072]{1,0:T(8,128)(2,1)}, bf16[128,3072]{1,0:T(8,128)(2,1)S(1)}, u32[]{:S(2)}, u32[]{:S(2)}) collective-permute-start(bf16[128,3072]{1,0:T(8,128)(2,1)} %collective-permute-done.4), channel_id=1, source_target_pairs={{0,1},{1,0},{2,3},{3,2},{4,5},{5,4},{6,7},{7,6},{8,9},{9,8},{10,11... | collective-permute-start | bytes 2359304 | tf_op jit(solution)/shard_map/ppermute | solution.py:23
  75.8 11.0 %collective-permute-start.8 = (f32[576,128]{1,0:T(8,128)S(1)}, f32[576,128]{1,0:T(8,128)S(1)}, u32[]{:S(2)}, u32[]{:S(2)}) collective-permute-start(f32[576,128]{1,0:T(8,128)S(1)} %pad_maximum_fusion.7), channel_id=1, source_target_pairs={{0,4},{4,0},{8,12},{12,8},{16,20},{20,16},{24,28},{28,24},{1,5},{5... | collective-permute-start | bytes 884744 | tf_op jit(solution)/shard_map/ppermute | solution.py:23
  77.4 14.2 %collective-permute-start.13 = (f32[576,128]{1,0:T(8,128)S(1)}, f32[576,128]{1,0:T(8,128)S(1)}, u32[]{:S(2)}, u32[]{:S(2)}) collective-permute-start(f32[576,128]{1,0:T(8,128)S(1)} %pad_maximum_fusion.8), channel_id=1, source_target_pairs={{0,4},{4,0},{8,12},{12,8},{16,20},{20,16},{24,28},{28,24},{1,5},{5... | collective-permute-start | bytes 884744 | tf_op jit(solution)/shard_map/ppermute | solution.py:23
  91.9 3.6 %collective-permute-start.14 = (f32[2,256]{1,0:T(2,128)S(1)}, f32[2,256]{1,0:T(2,128)S(1)}, u32[]{:S(2)}, u32[]{:S(2)}) collective-permute-start(f32[2,256]{1,0:T(2,128)S(1)} %pad_maximum_fusion.11), channel_id=1, source_target_pairs={{0,2},{1,3},{2,0},{3,1},{4,6},{5,7},{6,4},{7,5},{8,10},{9,11},{10,... | collective-permute-start | bytes 6152 | tf_op jit(solution)/shard_map/ppermute | solution.py:23
  95.6 3.7 %collective-permute-start.15 = (f32[2,256]{1,0:T(2,128)S(1)}, f32[2,256]{1,0:T(2,128)S(1)}, u32[]{:S(2)}, u32[]{:S(2)}) collective-permute-start(f32[2,256]{1,0:T(2,128)S(1)} %pad_maximum_fusion.12), channel_id=1, source_target_pairs={{0,8},{4,12},{8,0},{12,4},{16,24},{20,28},{24,16},{28,20},{1,9},{5... | collective-permute-start | bytes 6152 | tf_op jit(solution)/shard_map/ppermute | solution.py:23
  99.2 4.5 %collective-permute-start.16 = (f32[2,256]{1,0:T(2,128)S(1)}, f32[2,256]{1,0:T(2,128)S(1)}, u32[]{:S(2)}, u32[]{:S(2)}) collective-permute-start(f32[2,256]{1,0:T(2,128)S(1)} %pad_maximum_fusion.13), channel_id=1, source_target_pairs={{0,16},{4,20},{8,24},{12,28},{16,0},{20,4},{24,8},{28,12},{1,17},{... | collective-permute-start | bytes 6152 | tf_op jit(solution)/shard_map/ppermute | solution.py:23
  105.3 9.3 %collective-permute-start.25 = (bf16[128,1024]{1,0:T(8,128)(2,1)S(1)}, bf16[128,1024]{1,0:T(8,128)(2,1)S(1)}, u32[]{:S(2)}, u32[]{:S(2)}) collective-permute-start(bf16[128,1024]{1,0:T(8,128)(2,1)S(1)} %convolution_convert_fusion), channel_id=1, source_target_pairs={{0,2},{1,3},{2,0},{3,1},{4,6},{5,7},{6,4},{7,5},{8,10},{9,11},{10,... | collective-permute-start | bytes 786440 | tf_op jit(solution)/shard_map/ppermute | solution.py:23
  107.1 10.3 %collective-permute-start.30 = (bf16[64,1024]{1,0:T(8,128)(2,1)S(1)}, bf16[64,1024]{1,0:T(8,128)(2,1)S(1)}, u32[]{:S(2)}, u32[]{:S(2)}) collective-permute-start(bf16[64,1024]{1,0:T(8,128)(2,1)S(1)} %get-tuple-element.49), channel_id=1, source_target_pairs={{0,2},{1,3},{2,0},{3,1},{4,6},{5,7},{6,4},{7,5},{8,10},{9,11},{10,... | collective-permute-start | bytes 393224 | tf_op jit(solution)/shard_map/ppermute | solution.py:23
  107.8 29.8 %collective-permute-start.21 = (bf16[128,1024]{1,0:T(8,128)(2,1)S(1)}, bf16[128,1024]{1,0:T(8,128)(2,1)S(1)}, u32[]{:S(2)}, u32[]{:S(2)}) collective-permute-start(bf16[128,1024]{1,0:T(8,128)(2,1)S(1)} %convolution_convert_fusion.3), channel_id=1, source_target_pairs={{0,2},{1,3},{2,0},{3,1},{4,6},{5,7},{6,4},{7,5},{8,10},{9,11},{10,... | collective-permute-start | bytes 786440 | tf_op jit(solution)/shard_map/ppermute | solution.py:23
  109.2 17.5 %collective-permute-start.22 = (bf16[128,1024]{1,0:T(8,128)(2,1)S(1)}, bf16[128,1024]{1,0:T(8,128)(2,1)S(1)}, u32[]{:S(2)}, u32[]{:S(2)}) collective-permute-start(bf16[128,1024]{1,0:T(8,128)(2,1)S(1)} %convolution_convert_fusion.2), channel_id=1, source_target_pairs={{0,2},{1,3},{2,0},{3,1},{4,6},{5,7},{6,4},{7,5},{8,10},{9,11},{10,... | collective-permute-start | bytes 786440 | tf_op jit(solution)/shard_map/ppermute | solution.py:23
  110.2 19.7 %collective-permute-start.24 = (bf16[128,1024]{1,0:T(8,128)(2,1)S(1)}, bf16[128,1024]{1,0:T(8,128)(2,1)S(1)}, u32[]{:S(2)}, u32[]{:S(2)}) collective-permute-start(bf16[128,1024]{1,0:T(8,128)(2,1)S(1)} %convolution_convert_fusion.1), channel_id=1, source_target_pairs={{0,2},{1,3},{2,0},{3,1},{4,6},{5,7},{6,4},{7,5},{8,10},{9,11},{10,... | collective-permute-start | bytes 786440 | tf_op jit(solution)/shard_map/ppermute | solution.py:23
  115.0 14.9 %collective-permute-start.26 = (bf16[128,1024]{1,0:T(8,128)(2,1)S(1)}, bf16[128,1024]{1,0:T(8,128)(2,1)S(1)}, u32[]{:S(2)}, u32[]{:S(2)}) collective-permute-start(bf16[128,1024]{1,0:T(8,128)(2,1)S(1)} %fusion.9), channel_id=1, source_target_pairs={{0,8},{4,12},{8,0},{12,4},{16,24},{20,28},{24,16},{28,20},{1,9},{5... | collective-permute-start | bytes 786440 | tf_op jit(solution)/shard_map/ppermute | solution.py:23
  117.5 19.4 %collective-permute-start.31 = (f32[64,1024]{1,0:T(8,128)S(1)}, f32[64,1024]{1,0:T(8,128)S(1)}, u32[]{:S(2)}, u32[]{:S(2)}) collective-permute-start(f32[64,1024]{1,0:T(8,128)S(1)} %convert_add_fusion), channel_id=1, source_target_pairs={{0,1},{1,0},{2,3},{3,2},{4,5},{5,4},{6,7},{7,6},{8,9},{9,8},{10,11... | collective-permute-start | bytes 786440 | tf_op jit(solution)/shard_map/ppermute | solution.py:23
  127.0 10.5 %collective-permute-start.23 = (bf16[128,1024]{1,0:T(8,128)(2,1)S(1)}, bf16[128,1024]{1,0:T(8,128)(2,1)S(1)}, u32[]{:S(2)}, u32[]{:S(2)}) collective-permute-start(bf16[128,1024]{1,0:T(8,128)(2,1)S(1)} %fusion.8), channel_id=1, source_target_pairs={{0,8},{4,12},{8,0},{12,4},{16,24},{20,28},{24,16},{28,20},{1,9},{5... | collective-permute-start | bytes 786440 | tf_op jit(solution)/shard_map/ppermute | solution.py:23
  130.2 10.1 %collective-permute-start.27 = (bf16[128,1024]{1,0:T(8,128)(2,1)S(1)}, bf16[128,1024]{1,0:T(8,128)(2,1)S(1)}, u32[]{:S(2)}, u32[]{:S(2)}) collective-permute-start(bf16[128,1024]{1,0:T(8,128)(2,1)S(1)} %fusion.7), channel_id=1, source_target_pairs={{0,16},{4,20},{8,24},{12,28},{16,0},{20,4},{24,8},{28,12},{1,17},{... | collective-permute-start | bytes 786440 | tf_op jit(solution)/shard_map/ppermute | solution.py:23
  131.1 3.9 %collective-permute-start.28 = (f32[64,64]{1,0:T(8,128)S(1)}, f32[64,64]{1,0:T(8,128)S(1)}, u32[]{:S(2)}, u32[]{:S(2)}) collective-permute-start(f32[64,64]{1,0:T(8,128)S(1)} %fusion.36), channel_id=1, source_target_pairs={{0,2},{1,3},{2,0},{3,1},{4,6},{5,7},{6,4},{7,5},{8,10},{9,11},{10,... | collective-permute-start | bytes 49160 | tf_op jit(solution)/shard_map/ppermute | solution.py:23
  135.0 1.2 collective-permute-start.29
  (11 other events, 232.6 us)

commit v4 on v3

--- a/solution.py
+++ b/solution.py
@@ -1,6 +1,8 @@
 import jax
 import jax.numpy as jnp
 from jax import lax
+from jax.experimental import pallas as pl
+from jax.experimental.pallas import tpu as pltpu
 from jax.sharding import PartitionSpec as P
 
 loss_scale = 64.0
@@ -37,6 +39,93 @@
 
 def swap_z(value, step):
     return swap(value, "vocab", 2 * step)
+
+
+anywhere = pl.BlockSpec(memory_space=pl.ANY)
+
+
+def copy_blocks(shapes, moves, *arrays):
+    def kernel(*refs):
+        ins, outs, sems = refs[: len(arrays)], refs[len(arrays) : -1], refs[-1]
+        copies = []
+        for n, (source, columns, target, row, column) in enumerate(moves()):
+            src, dst = ins[source], outs[target]
+            if columns is not None:
+                src = src.at[:, pl.ds(pl.multiple_of(columns[0], 128), columns[1])]
+            dst = dst.at[pl.ds(row, src.shape[0]), pl.ds(column, src.shape[1])]
+            copies.append(pltpu.make_async_copy(src, dst, sems.at[n]))
+        for copy in copies:
+            copy.start()
+        for copy in copies:
+            copy.wait()
+
+    size = sum(2 * shape[0] * shape[1] for shape in shapes)
+    return pl.pallas_call(
+        kernel,
+        out_shape=[jax.ShapeDtypeStruct(shape, bf16) for shape in shapes],
+        in_specs=[anywhere] * len(arrays),
+        out_specs=[anywhere] * len(shapes),
+        scratch_shapes=[pltpu.SemaphoreType.DMA((32,))],
+        cost_estimate=pl.CostEstimate(flops=0, bytes_accessed=2 * size, transcendentals=0),
+    )(*arrays)
+
+
+def partial_logits(groups, tokens):
+    heights = [group[0].shape[0] for group in groups]
+    depth = sum(a.shape[1] for a in tokens)
+    toks = tokens[0].shape[0]
+    flat = [a for group in groups for a in group]
+    n_flat = len(flat)
+
+    def kernel(*refs):
+        ins, out = refs[: n_flat + len(tokens)], refs[n_flat + len(tokens)]
+        weight, token, sems = refs[n_flat + len(tokens) + 1 :]
+        copies = []
+        at, row = 0, 0
+        for group, height in zip(groups, heights):
+            column = 0
+            for a in group:
+                dst = weight.at[pl.ds(row, height), pl.ds(column, a.shape[1])]
+                copies.append(pltpu.make_async_copy(ins[at], dst, sems.at[at]))
+                column += a.shape[1]
+                at += 1
+            row += height
+        column = 0
+        for a in tokens:
+            dst = token.at[:, pl.ds(column, a.shape[1])]
+            copies.append(pltpu.make_async_copy(ins[at], dst, sems.at[at]))
+            column += a.shape[1]
+            at += 1
+        for copy in copies:
+            copy.start()
+        for copy in copies[n_flat:]:
+            copy.wait()
+        at, row = 0, 0
+        for group, height in zip(groups, heights):
+            for _ in group:
+                copies[at].wait()
+                at += 1
+            out[row : row + height, :] = dot_last(weight[row : row + height, :], token[...])
+            row += height
+
+    total = sum(heights)
+    return pl.pallas_call(
+        kernel,
+        out_shape=jax.ShapeDtypeStruct((total, toks), f32),
+        in_specs=[anywhere] * (n_flat + len(tokens)),
+        out_specs=pl.BlockSpec(memory_space=pltpu.VMEM),
+        scratch_shapes=[
+            pltpu.VMEM((total, depth), bf16),
+            pltpu.VMEM((toks, depth), bf16),
+            pltpu.SemaphoreType.DMA((n_flat + len(tokens),)),
+        ],
+        compiler_params=pltpu.CompilerParams(vmem_limit_bytes=24 << 20),
+        cost_estimate=pl.CostEstimate(
+            flops=2 * total * depth * toks,
+            bytes_accessed=2 * (total + toks) * depth + 4 * total * toks,
+            transcendentals=0,
+        ),
+    )(*flat, *tokens)
 
 
 def on_few(hidden, head, factor_rows, factor_basis, targets, loss_mask):
@@ -45,79 +134,98 @@
     bits = [1 << b for b in range(n_z.bit_length() - 1)]
     v = lax.axis_index("vocab")
     t = lax.axis_index("tok")
-    y, z = v & 1, v >> 1
     toks, width = hidden.shape
     rows = head.shape[0]
     new_here = factor_rows.shape[0]
     rank = factor_basis.shape[0]
-
-    def pack(array, which, blocks):
-        cuts = [
-            lax.dynamic_slice_in_dim(array, (2 * block + which) * width, width, 1)
-            for block in blocks
-        ]
-        return jnp.concatenate(cuts, axis=1) if len(cuts) > 1 else cuts[0]
-
-    first, last = list(range(n_z - 1)), [n_z - 1]
-    send_first, hidden = lax.optimization_barrier((pack(head, 1 - y, first), hidden))
+    depth = n_z * width
+
+    def start_of(j, other):
+        return (lax.axis_index("vocab") ^ (2 * j + other)) * width
+
+    cut = (n_z - 1) * width
+    send_first, send_last = copy_blocks(
+        [(rows, cut), (rows, width)],
+        lambda: [(0, (start_of(j, 1), width), 0, 0, j * width) for j in range(n_z - 1)]
+        + [(0, (start_of(n_z - 1, 1), width), 1, 0, 0)],
+        head,
+    )
     beside_first = swap_y(send_first)
 
     shards = {0: hidden}
     for bit in reversed(bits):
-        for j in list(shards):
+        near = swap_z(hidden, bit)
+        for j in [j for j in shards if j]:
+            shards[j], _ = lax.optimization_barrier((shards[j], near))
             shards[j ^ bit] = swap_z(shards[j], bit)
-    cross = {j: swap_x(shards[j]) for j in shards}
-
-    beside_last = swap_y(pack(head, 1 - y, last))
-    kept = pack(head, y, range(n_z))
+        shards[bit] = near
+    cross = {}
+    for j in range(n_z):
+        sent = shards[j]
+        if j > 1:
+            sent, _ = lax.optimization_barrier((sent, cross[j - 2]))
+        cross[j] = swap_x(sent)
+
+    beside_last = swap_y(send_last)
+    head_after, basis_after, _ = lax.optimization_barrier(
+        (head, factor_basis, shards[n_z - 1])
+    )
+    kept, basis_half = copy_blocks(
+        [(rows, depth), (rank, depth)],
+        lambda: [
+            (a, (start_of(j, 0), width), a, 0, j * width) for j in range(n_z) for a in range(2)
+        ],
+        head_after,
+        basis_after,
+    )
     kept_core = swap_core(kept)
-    beside = jnp.concatenate([beside_first, beside_last], axis=1)
-    beside_core = jnp.concatenate([swap_core(beside_first), swap_core(beside_last)], axis=1)
-    basis_half = pack(factor_basis, y, range(n_z))
-
-    token_info, rows_all, _ = lax.optimization_barrier(
-        (jnp.stack([targets, loss_mask]), factor_rows, shards[bits[-1] if bits else 0])
-    )
-    row_blocks = [0]
-    for bit in [2 * b for b in reversed(bits)] + [1]:
+    beside = [beside_first, beside_last]
+    first_after, *_ = lax.optimization_barrier(
+        (beside_first, *[cross[j] for j in range(n_z - 1)])
+    )
+    last_after, _ = lax.optimization_barrier((beside_last, shards[n_z - 1]))
+    beside_core = [swap_core(first_after), swap_core(last_after)]
+
+    groups = [[kept], [kept_core], beside, beside_core, [basis_half]]
+    in_order = lambda parts: [parts[j] for j in range(n_z)]
+    mine_own = partial_logits(groups, in_order(shards))
+    mine_cross = partial_logits(groups, in_order(cross))
+    theirs_own, theirs_cross = swap_y(mine_own), swap_y(mine_cross)
+    mine = jnp.concatenate([mine_own, mine_cross], axis=1)
+    theirs = jnp.concatenate([theirs_own, theirs_cross], axis=1)
+    frozen_near = mine[: 2 * rows] + theirs[2 * rows : 4 * rows]
+    frozen_far = mine[2 * rows : 4 * rows] + theirs[: 2 * rows]
+    hidden_basis = (mine[4 * rows :] + theirs[4 * rows :]).astype(bf16)
+
+    near_rows, _ = lax.optimization_barrier((factor_rows, beside_core[1]))
+    rows_all = jnp.concatenate([factor_rows, swap_y(near_rows)], axis=0)
+    row_blocks = [0, 1]
+    rows_all, _ = lax.optimization_barrier((rows_all, mine_own))
+    for bit in [2 * b for b in reversed(bits)]:
         rows_all = jnp.concatenate([rows_all, swap(rows_all, "vocab", bit)], axis=0)
         row_blocks = row_blocks + [j ^ bit for j in row_blocks]
-    token_info = jnp.concatenate([token_info, swap_x(token_info)], axis=1)
-
-    def in_order(parts):
-        whole = jnp.zeros((toks, n_z * width), bf16)
-        for j in sorted(parts):
-            whole = lax.dynamic_update_slice_in_dim(whole, parts[j], (z ^ j) * width, 1)
-        return whole
-
-    upper = jnp.concatenate([kept, kept_core, basis_half], axis=0)
-    lower = jnp.concatenate([beside, beside_core], axis=0)
-
-    def add_over_y(tokens):
-        up = dot_last(upper, tokens)
-        low = dot_last(lower, tokens)
-        mine = jnp.concatenate([up[: 2 * rows], low, up[2 * rows :]], axis=0)
-        theirs = swap_y(mine)
-        turned = jnp.concatenate(
-            [theirs[2 * rows : 4 * rows], theirs[: 2 * rows], theirs[4 * rows :]], axis=0
-        )
-        return mine + turned
-
-    both = jnp.concatenate([add_over_y(in_order(shards)), add_over_y(in_order(cross))], axis=1)
-    frozen = both[: 4 * rows]
-    hidden_basis = both[4 * rows :].astype(bf16)
 
     def merge(a, b):
         top = jnp.maximum(a[0], b[0])
         return jnp.stack([top, a[1] * jnp.exp(a[0] - top) + b[1] * jnp.exp(b[0] - top)])
 
-    def local(logits):
-        top = jnp.max(logits, axis=0)
-        return jnp.stack([top, jnp.sum(jnp.exp(logits - top[None, :]), axis=0)])
-
-    stats = local(frozen)
-    turned = swap_x(stats)
-    stats = merge(stats, jnp.concatenate([turned[:, toks:], turned[:, :toks]], axis=1))
+    def local(*logits):
+        top = jnp.max(logits[0], axis=0)
+        for l in logits[1:]:
+            top = jnp.maximum(top, jnp.max(l, axis=0))
+        total = jnp.sum(jnp.exp(logits[0] - top[None, :]), axis=0)
+        for l in logits[1:]:
+            total = total + jnp.sum(jnp.exp(l - top[None, :]), axis=0)
+        return jnp.stack([top, total])
+
+    info = jnp.stack([targets.astype(f32), loss_mask.astype(f32)])
+    stats = local(frozen_near, frozen_far)
+    sent = jnp.concatenate([stats, jnp.concatenate([info, info], axis=1)], axis=0)
+    came = swap_x(sent)
+    stats = merge(stats, jnp.concatenate([came[:2, toks:], came[:2, :toks]], axis=1))
+    info = jnp.concatenate([info, came[2:, :toks]], axis=1)
+    target_row = info[0].astype(jnp.int32)
+    weight_row = loss_scale * info[1]
     for bit in bits:
         stats = merge(stats, swap_z(stats, bit))
     fresh = lax.dot_general(
@@ -125,15 +233,18 @@
     )
     stats = merge(stats, local(fresh))
     row_top, sum_exp = stats[0], stats[1]
-
-    weight_row = loss_scale * token_info[1].astype(f32)
     scale_row = weight_row / sum_exp
+
     row_iota = lax.broadcasted_iota(jnp.int32, (rows, 1), 0)
-    row_ids = jnp.concatenate(
-        [row_iota + (vv * n_tok + tt) * rows for vv in (v, v ^ 1) for tt in (t, t ^ 1)], axis=0
-    )
-    hit = jnp.where(row_ids == token_info[0][None, :], weight_row[None, :], 0.0)
-    grad = (jnp.exp(frozen - row_top[None, :]) * scale_row[None, :] - hit).astype(bf16)
+
+    def grad_of(frozen, vv):
+        row_ids = jnp.concatenate(
+            [row_iota + (vv * n_tok + tt) * rows for tt in (t, t ^ 1)], axis=0
+        )
+        hit = jnp.where(row_ids == target_row[None, :], weight_row[None, :], 0.0)
+        return (jnp.exp(frozen - row_top[None, :]) * scale_row[None, :] - hit).astype(bf16)
+
+    grad = jnp.concatenate([grad_of(frozen_near, v), grad_of(frozen_far, v ^ 1)], axis=0)
 
     frozen_rows = rows * n_tok * lax.axis_size("vocab")
     new_iota = lax.broadcasted_iota(jnp.int32, (new_here, 1), 0) + frozen_rows
@@ -146,21 +257,41 @@
     rows_part = dot_last(fresh_grad[:new_here], hidden_basis[:, :toks])
     basis_part = lax.reduce_precision(jnp.dot(mix_total, hidden, preferred_element_type=f32), 8, 7)
 
-    weights = jnp.concatenate([upper[: 2 * rows], lower], axis=0)
+    (weights,) = copy_blocks(
+        [(4 * rows, depth)],
+        lambda: [
+            (0, None, 0, 0, 0),
+            (1, None, 0, rows, 0),
+            (2, None, 0, 2 * rows, 0),
+            (3, None, 0, 2 * rows, cut),
+            (4, None, 0, 3 * rows, 0),
+            (5, None, 0, 3 * rows, cut),
+        ],
+        kept,
+        kept_core,
+        *beside,
+        *beside_core,
+    )
 
     def part(grads, j):
-        return dot_first(grads, lax.dynamic_slice_in_dim(weights, (z ^ j) * width, width, 1))
-
-    sums = {}
+        return dot_first(grads, weights[:, j * width : (j + 1) * width])
+
+    sums, from_x = {}, {}
     for j in reversed(range(n_z)):
-        from_x = swap_x(part(grad[:, toks:], j).astype(bf16))
-        sums[j] = part(grad[:, :toks], j) + from_x.astype(f32)
+        send = part(grad[:, toks:], j).astype(bf16)
+        if j + 2 in from_x:
+            send, _ = lax.optimization_barrier((send, from_x[j + 2]))
+        from_x[j] = swap_x(send)
+        sums[j] = part(grad[:, :toks], j) + from_x[j].astype(f32)
     for bit in bits:
         for j in [j for j in sorted(sums, reverse=True) if j & bit]:
             sums[j ^ bit] = sums[j ^ bit] + swap_z(sums.pop(j).astype(bf16), bit).astype(f32)
     basis_here = lax.dynamic_slice_in_dim(factor_basis, v * width, width, 1)
     hidden_grad = (sums[0] + dot_first(mix_total, basis_here)).astype(bf16)
 
+    basis_part, rows_part, _ = lax.optimization_barrier(
+        (basis_part, rows_part, from_x[min(1, n_z - 1)])
+    )
     basis_two = basis_part + swap_x(basis_part.astype(bf16)).astype(f32)
     basis_grad = basis_two + swap_core(basis_two)
     rows_two = rows_part + swap_x(rows_part)

time: 143 us -> 310 us (2.17)
  Pallas kernels: 0 us -> 219 us
  other arithmetic: 34.7 us -> 2.79 us
  waiting for transfers between devices: 51.2 us -> 36.5 us
  matrix products: 9.88 us -> 5.3 us
    pallas_call x0 -> x5, Pallas kernels: none -> 219 us  [the longest x3 211 us: copy_blocks(): pl.pallas_call(kernel, out_shape=[jax.ShapeDtypeStruct(shape, bf16) for s...]
    concatenate x7 -> x6, other arithmetic: 29.5 us -> 0.62 us  [the longest x2 0.57 us: grad_of(): jnp.concatenate([row_iota + (vv * n_tok + tt) * rows for tt in (t, t ^ 1)...]
    ppermute x32 -> x31, waiting for transfers between devices: 51.2 us -> 36.5 us  [swap(): return lax.ppermute(value, axis, [(i, i ^ bit) for i in range(size)])]
    unnamed x28 -> x57, local copies, waits for them, and re-layouts: 1.98 us -> 9.83 us
    dynamic_slice x2 -> x0, local copies, waits for them, and re-layouts: 4.31 us -> none  [pack(): lax.dynamic_slice_in_dim(array, (2 * block + which) * width, width, 1)]
    dot_general x5 -> x1, matrix products: 3.44 us -> 0.12 us  [dot_last(): return lax.dot_general(a, b, contract_last, preferred_element_type=f32)]
    ppermute x32 -> x31, starting transfers between devices: 33.7 us -> 34.2 us  [swap(): return lax.ppermute(value, axis, [(i, i ^ bit) for i in range(size)])]
  transfers between devices with their start and end apart: 32 -> 31, of which waited for: 16 -> 12; matrix products, arithmetic and copies ran while one was open for 33% -> 2% of each run, Pallas kernels for 0% -> 71%
where the time goes in v4:
time: 310 us
  Pallas kernels  219 us (71%)
  waiting for transfers between devices  36.5 us (12%)
  starting transfers between devices  34.2 us (11%)
  local copies, waits for them, and re-layouts  10.9 us (4%)
  matrix products  5.3 us (2%)
    pallas_call x3, Pallas kernels, copy_blocks(): pl.pallas_call(kernel, out_shape=[jax.ShapeDtypeStruct(shape, bf16) for s...  211 us
    ppermute x31, waiting for transfers between devices, swap(): return lax.ppermute(value, axis, [(i, i ^ bit) for i in range(size)])  36.5 us
    ppermute x31, starting transfers between devices, swap(): return lax.ppermute(value, axis, [(i, i ^ bit) for i in range(size)])  34.2 us
    unnamed x57, local copies, waits for them, and re-layouts  9.83 us
    pallas_call x2, Pallas kernels, partial_logits(): pl.pallas_call(kernel, out_shape=jax.ShapeDtypeStruct((total, toks), f32)...  8.29 us
  transfers between devices with their start and end apart: 31, of which 12 were waited for; matrix products, arithmetic and copies ran while one was open for 2% of the time, Pallas kernels for 71%

profile of v4, /device:TPU:0, one launch (start us, length us, event | category | flops | bytes accessed | tf_op | source)
XLA Modules:
  0.0 309.9 jit_solution(1864313043968404834)
XLA Ops:
  0.7 3.1 collective-permute-start.1
  3.8 2.6 collective-permute-start
  6.3 33.1 %shard_map.86 = (bf16[128,3072]{1,0:T(8,128)(2,1)}, bf16[128,1024]{1,0:T(8,128)(2,1)}) custom-call(bf16[128,8192]{1,0:T(8,128)(2,1)} %refs_0_.2), custom_call_target="tpu_custom_call" | custom-call | bytes 2097152 | tf_op jit(solution)/shard_map/pallas_call | solution.py:63
  39.5 1.6 collective-permute-start.4
  41.1 1.5 collective-permute-start.6
  43.6 4.9 %collective-permute-done.6.refs_7_ = bf16[128,1024]{1,0:T(8,128)(2,1)S(1)} collective-permute-done((bf16[128,1024]{1,0:T(8,128)(2,1)}, bf16[128,1024]{1,0:T(8,128)(2,1)S(1)}, u32[]{:S(2)}, u32[]{:S(2)}) %collective-permute-start.6) | collective-permute-done | bytes 262176 | tf_op jit(solution)/shard_map/ppermute | solution.py:25
  48.5 1.5 collective-permute-start.8
  50.5 49.0 %shard_map.85 = (bf16[128,4096]{1,0:T(8,128)(2,1)}, bf16[64,4096]{1,0:T(8,128)(2,1)}) custom-call(bf16[128,8192]{1,0:T(8,128)(2,1)} %refs_0_.2, bf16[64,8192]{1,0:T(8,128)(2,1)} %refs_1_), custom_call_target="tpu_custom_call" | custom-call | bytes 3145728 | tf_op jit(solution)/shard_map/pallas_call | solution.py:63
  101.8 2.1 collective-permute-done.10.refs_5_
  105.1 1.5 collective-permute-start.11
  107.8 1.9 copy-done
  113.6 4.6 %shard_map.87 = f32[576,128]{1,0:T(8,128)S(1)} custom-call(bf16[128,4096]{1,0:T(8,128)(2,1)S(1)} %copy-done, bf16[128,4096]{1,0:T(8,128)(2,1)S(1)} %collective-permute-done.3.refs_1_, bf16[128,3072]{1,0:T(8,128)(2,1)S(1)} %collective-permute-done.4.refs_2_, bf16[128,1024]{1,0:T(8,128)(2,1)S(1)} %collective-permute-done.5.refs_3_, ...), custom_call_target="tpu_custom_call" | custom-call | flops 603979776 | bytes 6062080 | tf_op jit(solution)/shard_map/pallas_call | solution.py:112
  120.7 3.7 %shard_map.88 = f32[576,128]{1,0:T(8,128)S(1)} custom-call(bf16[128,4096]{1,0:T(8,128)(2,1)S(1)} %copy-done, bf16[128,4096]{1,0:T(8,128)(2,1)S(1)} %collective-permute-done.3.refs_1_, bf16[128,3072]{1,0:T(8,128)(2,1)S(1)} %collective-permute-done.4.refs_2_, bf16[128,1024]{1,0:T(8,128)(2,1)S(1)} %collective-permute-done.5.refs_3_, ...), custom_call_target="tpu_custom_call" | custom-call | flops 603979776 | bytes 6062080 | tf_op jit(solution)/shard_map/pallas_call | solution.py:112
  124.4 1.6 collective-permute-start.13
  126.0 128.4 %shard_map.89 = bf16[512,4096]{1,0:T(8,128)(2,1)} custom-call(bf16[128,4096]{1,0:T(8,128)(2,1)} %get-tuple-element.23.refs_0_, bf16[128,4096]{1,0:T(8,128)(2,1)} %copy-done.1, bf16[128,3072]{1,0:T(8,128)(2,1)} %copy-done.2, bf16[128,1024]{1,0:T(8,128)(2,1)} %copy-done.4, bf16[128,3072]{1,0:T(8,128)(2,1)} %copy-done.3, bf16[128,1024]{1,0:T(8,128)(2,1)} %copy-done.5), custom_call_target="tpu_custom_call" | custom-call | bytes 8388608 | tf_op jit(solution)/shard_map/pallas_call | solution.py:63
  255.0 3.8 %collective-permute-done.19 = bf16[256,64]{1,0:T(8,128)(2,1)S(1)} collective-permute-done((bf16[256,64]{1,0:T(8,128)(2,1)S(1)}, bf16[256,64]{1,0:T(8,128)(2,1)S(1)}, u32[]{:S(2)}, u32[]{:S(2)}) %collective-permute-start.19) | collective-permute-done | bytes 32800 | tf_op jit(solution)/shard_map/ppermute | solution.py:25
  261.1 1.6 collective-permute-start.14
  262.9 1.9 collective-permute-done.14
  265.5 3.0 collective-permute-done.15
  268.5 2.7 collective-permute-start.16
  271.2 1.9 collective-permute-done.16
  274.4 1.6 collective-permute-start.22
  277.5 6.1 %collective-permute-done.22 = bf16[128,1024]{1,0:T(8,128)(2,1)S(1)} collective-permute-done((bf16[128,1024]{1,0:T(8,128)(2,1)S(1)}, bf16[128,1024]{1,0:T(8,128)(2,1)S(1)}, u32[]{:S(2)}, u32[]{:S(2)}) %collective-permute-start.22) | collective-permute-done | bytes 262176 | tf_op jit(solution)/shard_map/ppermute | solution.py:25
  283.7 1.5 collective-permute-start.23
  285.2 4.1 %collective-permute-done.20 = bf16[128,1024]{1,0:T(8,128)(2,1)S(1)} collective-permute-done((bf16[128,1024]{1,0:T(8,128)(2,1)S(1)}, bf16[128,1024]{1,0:T(8,128)(2,1)S(1)}, u32[]{:S(2)}, u32[]{:S(2)}) %collective-permute-start.20) | collective-permute-done | bytes 262176 | tf_op jit(solution)/shard_map/ppermute | solution.py:25
  289.3 1.5 collective-permute-start.21
  292.2 1.6 collective-permute-start.29
  295.7 1.8 collective-permute-done.25
  297.9 2.7 collective-permute-start.26
  300.7 1.2 fusion.25
  303.0 5.0 %collective-permute-done.26 = bf16[128,1024]{1,0:T(8,128)(2,1)S(1)} collective-permute-done((bf16[128,1024]{1,0:T(8,128)(2,1)S(1)}, bf16[128,1024]{1,0:T(8,128)(2,1)S(1)}, u32[]{:S(2)}, u32[]{:S(2)}) %collective-permute-start.26) | collective-permute-done | bytes 262176 | tf_op jit(solution)/shard_map/ppermute | solution.py:25
  308.1 1.1 fusion.4
  (146 shorter events, 24.6 us)
Async XLA Ops:
  0.7 41.9 %collective-permute-start.1 = (bf16[128,1024]{1,0:T(8,128)(2,1)}, bf16[128,1024]{1,0:T(8,128)(2,1)S(1)}, u32[]{:S(2)}, u32[]{:S(2)}) collective-permute-start(bf16[128,1024]{1,0:T(8,128)(2,1)} %refs_7_.1), channel_id=1, source_target_pairs={{0,8},{4,12},{8,0},{12,4},{16,24},{20,28},{24,16},{28,20},{1,9},{5... | collective-permute-start | bytes 786440 | tf_op jit(solution)/shard_map/ppermute | solution.py:25
  3.8 38.8 %collective-permute-start = (bf16[128,1024]{1,0:T(8,128)(2,1)}, bf16[128,1024]{1,0:T(8,128)(2,1)S(1)}, u32[]{:S(2)}, u32[]{:S(2)}) collective-permute-start(bf16[128,1024]{1,0:T(8,128)(2,1)} %refs_7_.1), channel_id=1, source_target_pairs={{0,16},{4,20},{8,24},{12,28},{16,0},{20,4},{24,8},{28,12},{1,17},{... | collective-permute-start | bytes 786440 | tf_op jit(solution)/shard_map/ppermute | solution.py:25
  39.5 61.7 %collective-permute-start.4 = (bf16[128,3072]{1,0:T(8,128)(2,1)}, bf16[128,3072]{1,0:T(8,128)(2,1)S(1)}, u32[]{:S(2)}, u32[]{:S(2)}) collective-permute-start(bf16[128,3072]{1,0:T(8,128)(2,1)} %get-tuple-element.24), channel_id=1, source_target_pairs={{0,4},{4,0},{8,12},{12,8},{16,20},{20,16},{24,28},{28,24},{1,5},{5... | collective-permute-start | bytes 2359304 | tf_op jit(solution)/shard_map/ppermute | solution.py:25
  41.1 7.4 %collective-permute-start.6 = (bf16[128,1024]{1,0:T(8,128)(2,1)}, bf16[128,1024]{1,0:T(8,128)(2,1)S(1)}, u32[]{:S(2)}, u32[]{:S(2)}) collective-permute-start(bf16[128,1024]{1,0:T(8,128)(2,1)} %refs_7_.1), channel_id=1, source_target_pairs={{0,2},{1,3},{2,0},{3,1},{4,6},{5,7},{6,4},{7,5},{8,10},{9,11},{10,... | collective-permute-start | bytes 786440 | tf_op jit(solution)/shard_map/ppermute | solution.py:25
  42.6 7.9 %collective-permute-start.2 = (bf16[128,1024]{1,0:T(8,128)(2,1)S(1)}, bf16[128,1024]{1,0:T(8,128)(2,1)}, u32[]{:S(2)}, u32[]{:S(2)}) collective-permute-start(bf16[128,1024]{1,0:T(8,128)(2,1)S(1)} %collective-permute-done.refs_9_), channel_id=1, source_target_pairs={{0,8},{4,12},{8,0},{12,4},{16,24},{20,28},{24,16},{28,20},{1,9},{5... | collective-permute-start | bytes 786440 | tf_op jit(solution)/shard_map/ppermute | solution.py:25
  43.1 58.6 %collective-permute-start.5 = (bf16[128,1024]{1,0:T(8,128)(2,1)}, bf16[128,1024]{1,0:T(8,128)(2,1)S(1)}, u32[]{:S(2)}, u32[]{:S(2)}) collective-permute-start(bf16[128,1024]{1,0:T(8,128)(2,1)} %get-tuple-element.25), channel_id=1, source_target_pairs={{0,4},{4,0},{8,12},{12,8},{16,20},{20,16},{24,28},{28,24},{1,5},{5... | collective-permute-start | bytes 786440 | tf_op jit(solution)/shard_map/ppermute | solution.py:25
  48.5 51.2 %collective-permute-start.8 = (bf16[128,1024]{1,0:T(8,128)(2,1)S(1)}, bf16[128,1024]{1,0:T(8,128)(2,1)S(1)}, u32[]{:S(2)}, u32[]{:S(2)}) collective-permute-start(bf16[128,1024]{1,0:T(8,128)(2,1)S(1)} %collective-permute-done.refs_9_), channel_id=1, source_target_pairs={{0,2},{1,3},{2,0},{3,1},{4,6},{5,7},{6,4},{7,5},{8,10},{9,11},{10,... | collective-permute-start | bytes 786440 | tf_op jit(solution)/shard_map/ppermute | solution.py:25
  50.0 50.5 %collective-permute-start.7 = (bf16[128,1024]{1,0:T(8,128)(2,1)S(1)}, bf16[128,1024]{1,0:T(8,128)(2,1)S(1)}, u32[]{:S(2)}, u32[]{:S(2)}) collective-permute-start(bf16[128,1024]{1,0:T(8,128)(2,1)S(1)} %collective-permute-done.1.refs_8_), channel_id=1, source_target_pairs={{0,2},{1,3},{2,0},{3,1},{4,6},{5,7},{6,4},{7,5},{8,10},{9,11},{10,... | collective-permute-start | bytes 786440 | tf_op jit(solution)/shard_map/ppermute | solution.py:25
  99.6 8.2 %collective-permute-start.3 = (bf16[128,4096]{1,0:T(8,128)(2,1)}, bf16[128,4096]{1,0:T(8,128)(2,1)S(1)}, u32[]{:S(2)}, u32[]{:S(2)}) collective-permute-start(bf16[128,4096]{1,0:T(8,128)(2,1)} %get-tuple-element.23.refs_0_), channel_id=1, source_target_pairs={{0,1},{1,0},{2,3},{3,2},{4,5},{5,4},{6,7},{7,6},{8,9},{9,8},{10,11... | collective-permute-start | bytes 3145736 | tf_op jit(solution)/shard_map/ppermute | solution.py:25
  101.2 6.6 %collective-permute-start.9 = (bf16[128,3072]{1,0:T(8,128)(2,1)S(1)}, bf16[128,3072]{1,0:T(8,128)(2,1)S(1)}, u32[]{:S(2)}, u32[]{:S(2)}) collective-permute-start(bf16[128,3072]{1,0:T(8,128)(2,1)S(1)} %collective-permute-done.4.refs_2_), channel_id=1, source_target_pairs={{0,1},{1,0},{2,3},{3,2},{4,5},{5,4},{6,7},{7,6},{8,9},{9,8},{10,11... | collective-permute-start | bytes 2359304 | tf_op jit(solution)/shard_map/ppermute | solution.py:25
  101.7 2.3 collective-permute-start.10
  104.0 3.8 %collective-permute-start.17 = (bf16[64,64]{1,0:T(8,128)(2,1)S(1)}, bf16[64,64]{1,0:T(8,128)(2,1)S(1)}, u32[]{:S(2)}, u32[]{:S(2)}) collective-permute-start(bf16[64,64]{1,0:T(8,128)(2,1)S(1)} %copy-done.22), channel_id=1, source_target_pairs={{0,4},{4,0},{8,12},{12,8},{16,20},{20,16},{24,28},{28,24},{1,5},{5... | collective-permute-start | bytes 24584 | tf_op jit(solution)/shard_map/ppermute | solution.py:25
  105.1 14.6 %collective-permute-start.11 = (bf16[128,1024]{1,0:T(8,128)(2,1)}, bf16[128,1024]{1,0:T(8,128)(2,1)S(1)}, u32[]{:S(2)}, u32[]{:S(2)}) collective-permute-start(bf16[128,1024]{1,0:T(8,128)(2,1)} %collective-permute-done.2.refs_10_), channel_id=1, source_target_pairs={{0,2},{1,3},{2,0},{3,1},{4,6},{5,7},{6,4},{7,5},{8,10},{9,11},{10,... | collective-permute-start | bytes 786440 | tf_op jit(solution)/shard_map/ppermute | solution.py:25
  118.2 140.7 %collective-permute-start.12 = (f32[576,128]{1,0:T(8,128)S(1)}, f32[576,128]{1,0:T(8,128)}, u32[]{:S(2)}, u32[]{:S(2)}) collective-permute-start(f32[576,128]{1,0:T(8,128)S(1)} %shard_map.87), channel_id=1, source_target_pairs={{0,4},{4,0},{8,12},{12,8},{16,20},{20,16},{24,28},{28,24},{1,5},{5... | collective-permute-start | bytes 884744 | tf_op jit(solution)/shard_map/ppermute | solution.py:25
  118.7 135.7 %collective-permute-start.18 = (bf16[128,64]{1,0:T(8,128)(2,1)S(1)}, bf16[128,64]{1,0:T(8,128)(2,1)S(1)}, u32[]{:S(2)}, u32[]{:S(2)}) collective-permute-start(bf16[128,64]{1,0:T(8,128)(2,1)S(1)} %pad_maximum_fusion.3), channel_id=1, source_target_pairs={{0,16},{4,20},{8,24},{12,28},{16,0},{20,4},{24,8},{28,12},{1,17},{... | collective-permute-start | bytes 49160 | tf_op jit(solution)/shard_map/ppermute | solution.py:25
  124.4 135.4 %collective-permute-start.13 = (f32[576,128]{1,0:T(8,128)S(1)}, f32[576,128]{1,0:T(8,128)}, u32[]{:S(2)}, u32[]{:S(2)}) collective-permute-start(f32[576,128]{1,0:T(8,128)S(1)} %shard_map.88), channel_id=1, source_target_pairs={{0,4},{4,0},{8,12},{12,8},{16,20},{20,16},{24,28},{28,24},{1,5},{5... | collective-permute-start | bytes 884744 | tf_op jit(solution)/shard_map/ppermute | solution.py:25
  126.0 129.0 %copy-start.21 = (bf16[512,64]{1,0:T(8,128)(2,1)S(1)}, bf16[512,64]{1,0:T(8,128)(2,1)}, u32[]{:S(2)}) copy-start(bf16[512,64]{1,0:T(8,128)(2,1)} %constant_dynamic-update-slice_fusion.4) | copy-start | bytes 196612
  254.5 4.3 %collective-permute-start.19 = (bf16[256,64]{1,0:T(8,128)(2,1)S(1)}, bf16[256,64]{1,0:T(8,128)(2,1)S(1)}, u32[]{:S(2)}, u32[]{:S(2)}) collective-permute-start(bf16[256,64]{1,0:T(8,128)(2,1)S(1)} %pad_maximum_fusion.2), channel_id=1, source_target_pairs={{0,8},{4,12},{8,0},{12,4},{16,24},{20,28},{24,16},{28,20},{1,9},{5... | collective-permute-start | bytes 98312 | tf_op jit(solution)/shard_map/ppermute | solution.py:25
  261.1 3.7 %collective-permute-start.14 = (f32[4,256]{1,0:T(4,128)S(1)}, f32[4,256]{1,0:T(4,128)S(1)}, u32[]{:S(2)}, u32[]{:S(2)}) collective-permute-start(f32[4,256]{1,0:T(4,128)S(1)} %maximum_maximum_fusion), channel_id=1, source_target_pairs={{0,2},{1,3},{2,0},{3,1},{4,6},{5,7},{6,4},{7,5},{8,10},{9,11},{10,... | collective-permute-start | bytes 12296 | tf_op jit(solution)/shard_map/ppermute | solution.py:25
  264.8 3.7 %collective-permute-start.15 = (f32[2,256]{1,0:T(2,128)S(1)}, f32[2,256]{1,0:T(2,128)S(1)}, u32[]{:S(2)}, u32[]{:S(2)}) collective-permute-start(f32[2,256]{1,0:T(2,128)S(1)} %pad_maximum_fusion.4), channel_id=1, source_target_pairs={{0,8},{4,12},{8,0},{12,4},{16,24},{20,28},{24,16},{28,20},{1,9},{5... | collective-permute-start | bytes 6152 | tf_op jit(solution)/shard_map/ppermute | solution.py:25
  268.5 4.5 %collective-permute-start.16 = (f32[2,256]{1,0:T(2,128)S(1)}, f32[2,256]{1,0:T(2,128)S(1)}, u32[]{:S(2)}, u32[]{:S(2)}) collective-permute-start(f32[2,256]{1,0:T(2,128)S(1)} %pad_maximum_fusion.5), channel_id=1, source_target_pairs={{0,16},{4,20},{8,24},{12,28},{16,0},{20,4},{24,8},{28,12},{1,17},{... | collective-permute-start | bytes 6152 | tf_op jit(solution)/shard_map/ppermute | solution.py:25
  274.4 9.3 %collective-permute-start.22 = (bf16[128,1024]{1,0:T(8,128)(2,1)S(1)}, bf16[128,1024]{1,0:T(8,128)(2,1)S(1)}, u32[]{:S(2)}, u32[]{:S(2)}) collective-permute-start(bf16[128,1024]{1,0:T(8,128)(2,1)S(1)} %convolution_convert_fusion), channel_id=1, source_target_pairs={{0,2},{1,3},{2,0},{3,1},{4,6},{5,7},{6,4},{7,5},{8,10},{9,11},{10,... | collective-permute-start | bytes 786440 | tf_op jit(solution)/shard_map/ppermute | solution.py:25
  276.5 12.8 %collective-permute-start.20 = (bf16[128,1024]{1,0:T(8,128)(2,1)S(1)}, bf16[128,1024]{1,0:T(8,128)(2,1)S(1)}, u32[]{:S(2)}, u32[]{:S(2)}) collective-permute-start(bf16[128,1024]{1,0:T(8,128)(2,1)S(1)} %convolution_convert_fusion.2), channel_id=1, source_target_pairs={{0,2},{1,3},{2,0},{3,1},{4,6},{5,7},{6,4},{7,5},{8,10},{9,11},{10,... | collective-permute-start | bytes 786440 | tf_op jit(solution)/shard_map/ppermute | solution.py:25
  283.7 8.5 %collective-permute-start.23 = (bf16[128,1024]{1,0:T(8,128)(2,1)S(1)}, bf16[128,1024]{1,0:T(8,128)(2,1)S(1)}, u32[]{:S(2)}, u32[]{:S(2)}) collective-permute-start(bf16[128,1024]{1,0:T(8,128)(2,1)S(1)} %convolution_convert_fusion.1), channel_id=1, source_target_pairs={{0,2},{1,3},{2,0},{3,1},{4,6},{5,7},{6,4},{7,5},{8,10},{9,11},{10,... | collective-permute-start | bytes 786440 | tf_op jit(solution)/shard_map/ppermute | solution.py:25
  289.3 13.7 %collective-permute-start.21 = (bf16[128,1024]{1,0:T(8,128)(2,1)S(1)}, bf16[128,1024]{1,0:T(8,128)(2,1)S(1)}, u32[]{:S(2)}, u32[]{:S(2)}) collective-permute-start(bf16[128,1024]{1,0:T(8,128)(2,1)S(1)} %convolution_convert_fusion.3), channel_id=1, source_target_pairs={{0,2},{1,3},{2,0},{3,1},{4,6},{5,7},{6,4},{7,5},{8,10},{9,11},{10,... | collective-permute-start | bytes 786440 | tf_op jit(solution)/shard_map/ppermute | solution.py:25
  291.1 6.4 %collective-permute-start.25 = (bf16[128,1024]{1,0:T(8,128)(2,1)S(1)}, bf16[128,1024]{1,0:T(8,128)(2,1)S(1)}, u32[]{:S(2)}, u32[]{:S(2)}) collective-permute-start(bf16[128,1024]{1,0:T(8,128)(2,1)S(1)} %fusion.7), channel_id=1, source_target_pairs={{0,8},{4,12},{8,0},{12,4},{16,24},{20,28},{24,16},{28,20},{1,9},{5... | collective-permute-start | bytes 786440 | tf_op jit(solution)/shard_map/ppermute | solution.py:25
  292.2 10.2 %collective-permute-start.29 = (bf16[64,1024]{1,0:T(8,128)(2,1)S(1)}, bf16[64,1024]{1,0:T(8,128)(2,1)S(1)}, u32[]{:S(2)}, u32[]{:S(2)}) collective-permute-start(bf16[64,1024]{1,0:T(8,128)(2,1)S(1)} %convert_element_type.99), channel_id=1, source_target_pairs={{0,2},{1,3},{2,0},{3,1},{4,6},{5,7},{6,4},{7,5},{8,10},{9,11},{10,... | collective-permute-start | bytes 393224 | tf_op jit(solution)/shard_map/ppermute | solution.py:25
  293.8 6.8 %collective-permute-start.27 = (f32[64,64]{1,0:T(8,128)S(1)}, f32[64,64]{1,0:T(8,128)S(1)}, u32[]{:S(2)}, u32[]{:S(2)}) collective-permute-start(f32[64,64]{1,0:T(8,128)S(1)} %fusion.28), channel_id=1, source_target_pairs={{0,2},{1,3},{2,0},{3,1},{4,6},{5,7},{6,4},{7,5},{8,10},{9,11},{10,... | collective-permute-start | bytes 49160 | tf_op jit(solution)/shard_map/ppermute | solution.py:25
  294.7 8.4 %collective-permute-start.24 = (bf16[128,1024]{1,0:T(8,128)(2,1)S(1)}, bf16[128,1024]{1,0:T(8,128)(2,1)S(1)}, u32[]{:S(2)}, u32[]{:S(2)}) collective-permute-start(bf16[128,1024]{1,0:T(8,128)(2,1)S(1)} %fusion.6), channel_id=1, source_target_pairs={{0,8},{4,12},{8,0},{12,4},{16,24},{20,28},{24,16},{28,20},{1,9},{5... | collective-permute-start | bytes 786440 | tf_op jit(solution)/shard_map/ppermute | solution.py:25
  297.9 10.1 %collective-permute-start.26 = (bf16[128,1024]{1,0:T(8,128)(2,1)S(1)}, bf16[128,1024]{1,0:T(8,128)(2,1)S(1)}, u32[]{:S(2)}, u32[]{:S(2)}) collective-permute-start(bf16[128,1024]{1,0:T(8,128)(2,1)S(1)} %fusion.5), channel_id=1, source_target_pairs={{0,16},{4,20},{8,24},{12,28},{16,0},{20,4},{24,8},{28,12},{1,17},{... | collective-permute-start | bytes 786440 | tf_op jit(solution)/shard_map/ppermute | solution.py:25
  300.6 1.3 collective-permute-start.28
  302.5 6.6 %collective-permute-start.30 = (f32[64,1024]{1,0:T(8,128)S(1)}, f32[64,1024]{1,0:T(8,128)S(1)}, u32[]{:S(2)}, u32[]{:S(2)}) collective-permute-start(f32[64,1024]{1,0:T(8,128)S(1)} %convert_add_fusion), channel_id=1, source_target_pairs={{0,1},{1,0},{2,3},{3,2},{4,5},{5,4},{6,7},{7,6},{8,9},{9,8},{10,11... | collective-permute-start | bytes 786440 | tf_op jit(solution)/shard_map/ppermute | solution.py:25
  (26 other events, 661.8 us)

commit v5 on v4

--- a/solution.py
+++ b/solution.py
@@ -42,6 +42,7 @@
 
 
 anywhere = pl.BlockSpec(memory_space=pl.ANY)
+in_vmem = pl.BlockSpec(memory_space=pltpu.VMEM)
 
 
 def copy_blocks(shapes, moves, *arrays):
@@ -64,68 +65,88 @@
         kernel,
         out_shape=[jax.ShapeDtypeStruct(shape, bf16) for shape in shapes],
         in_specs=[anywhere] * len(arrays),
-        out_specs=[anywhere] * len(shapes),
+        out_specs=[in_vmem] * len(shapes),
         scratch_shapes=[pltpu.SemaphoreType.DMA((32,))],
+        compiler_params=pltpu.CompilerParams(vmem_limit_bytes=4 << 20),
         cost_estimate=pl.CostEstimate(flops=0, bytes_accessed=2 * size, transcendentals=0),
     )(*arrays)
 
 
-def partial_logits(groups, tokens):
+def side_by_side(parts, into, row, sems, first):
+    copies, column = [], 0
+    for n, part in enumerate(parts):
+        dst = into.at[pl.ds(row, part.shape[0]), pl.ds(column, part.shape[1])]
+        copies.append(pltpu.make_async_copy(part, dst, sems.at[first + n]))
+        column += part.shape[1]
+    return copies
+
+
+def first_logits(groups, tokens):
     heights = [group[0].shape[0] for group in groups]
-    depth = sum(a.shape[1] for a in tokens)
+    sizes = [len(group) for group in groups]
+    total, depth = sum(heights), sum(a.shape[1] for a in tokens)
     toks = tokens[0].shape[0]
     flat = [a for group in groups for a in group]
-    n_flat = len(flat)
+    n_flat, n_all = len(flat), len(flat) + len(tokens)
 
     def kernel(*refs):
-        ins, out = refs[: n_flat + len(tokens)], refs[n_flat + len(tokens)]
-        weight, token, sems = refs[n_flat + len(tokens) + 1 :]
-        copies = []
-        at, row = 0, 0
-        for group, height in zip(groups, heights):
-            column = 0
-            for a in group:
-                dst = weight.at[pl.ds(row, height), pl.ds(column, a.shape[1])]
-                copies.append(pltpu.make_async_copy(ins[at], dst, sems.at[at]))
-                column += a.shape[1]
-                at += 1
-            row += height
-        column = 0
-        for a in tokens:
-            dst = token.at[:, pl.ds(column, a.shape[1])]
-            copies.append(pltpu.make_async_copy(ins[at], dst, sems.at[at]))
-            column += a.shape[1]
-            at += 1
-        for copy in copies:
+        out, weight, token, sems = refs[n_all:]
+        token_copies = side_by_side(refs[n_flat:n_all], token, 0, sems, n_flat)
+        row_copies, at, row = [], 0, 0
+        for size, height in zip(sizes, heights):
+            row_copies.append(side_by_side(refs[at : at + size], weight, row, sems, at))
+            at, row = at + size, row + height
+        for copy in token_copies + [copy for copies in row_copies for copy in copies]:
             copy.start()
-        for copy in copies[n_flat:]:
+        for copy in token_copies:
             copy.wait()
-        at, row = 0, 0
-        for group, height in zip(groups, heights):
-            for _ in group:
-                copies[at].wait()
-                at += 1
+        row = 0
+        for copies, height in zip(row_copies, heights):
+            for copy in copies:
+                copy.wait()
             out[row : row + height, :] = dot_last(weight[row : row + height, :], token[...])
             row += height
 
-    total = sum(heights)
+    return pl.pallas_call(
+        kernel,
+        out_shape=[
+            jax.ShapeDtypeStruct((total, toks), f32),
+            jax.ShapeDtypeStruct((total, depth), bf16),
+        ],
+        in_specs=[anywhere] * n_all,
+        out_specs=[in_vmem] * 2,
+        scratch_shapes=[pltpu.VMEM((toks, depth), bf16), pltpu.SemaphoreType.DMA((n_all,))],
+        compiler_params=pltpu.CompilerParams(vmem_limit_bytes=12 << 20),
+        cost_estimate=pl.CostEstimate(
+            flops=2 * total * depth * toks,
+            bytes_accessed=4 * (total + toks) * depth + 4 * total * toks,
+            transcendentals=0,
+        ),
+    )(*flat, *tokens)
+
+
+def second_logits(weight, tokens):
+    total, depth = weight.shape
+    toks, width = tokens[0].shape
+
+    def kernel(weight_ref, *refs):
+        out = refs[-1]
+        for j, token in enumerate(refs[:-1]):
+            part = dot_last(weight_ref[:, j * width : (j + 1) * width], token[...])
+            out[...] = part if j == 0 else out[...] + part
+
     return pl.pallas_call(
         kernel,
         out_shape=jax.ShapeDtypeStruct((total, toks), f32),
-        in_specs=[anywhere] * (n_flat + len(tokens)),
-        out_specs=pl.BlockSpec(memory_space=pltpu.VMEM),
-        scratch_shapes=[
-            pltpu.VMEM((total, depth), bf16),
-            pltpu.VMEM((toks, depth), bf16),
-            pltpu.SemaphoreType.DMA((n_flat + len(tokens),)),
-        ],
-        compiler_params=pltpu.CompilerParams(vmem_limit_bytes=24 << 20),
+        in_specs=[in_vmem] * (1 + len(tokens)),
+        out_specs=in_vmem,
+        compiler_params=pltpu.CompilerParams(vmem_limit_bytes=12 << 20),
         cost_estimate=pl.CostEstimate(
             flops=2 * total * depth * toks,
             bytes_accessed=2 * (total + toks) * depth + 4 * total * toks,
             transcendentals=0,
         ),
-    )(*flat, *tokens)
+    )(weight, *tokens)
 
 
 def on_few(hidden, head, factor_rows, factor_basis, targets, loss_mask):
@@ -188,8 +209,8 @@
 
     groups = [[kept], [kept_core], beside, beside_core, [basis_half]]
     in_order = lambda parts: [parts[j] for j in range(n_z)]
-    mine_own = partial_logits(groups, in_order(shards))
-    mine_cross = partial_logits(groups, in_order(cross))
+    mine_own, weights = first_logits(groups, in_order(shards))
+    mine_cross = second_logits(weights, in_order(cross))
     theirs_own, theirs_cross = swap_y(mine_own), swap_y(mine_cross)
     mine = jnp.concatenate([mine_own, mine_cross], axis=1)
     theirs = jnp.concatenate([theirs_own, theirs_cross], axis=1)
@@ -257,24 +278,8 @@
     rows_part = dot_last(fresh_grad[:new_here], hidden_basis[:, :toks])
     basis_part = lax.reduce_precision(jnp.dot(mix_total, hidden, preferred_element_type=f32), 8, 7)
 
-    (weights,) = copy_blocks(
-        [(4 * rows, depth)],
-        lambda: [
-            (0, None, 0, 0, 0),
-            (1, None, 0, rows, 0),
-            (2, None, 0, 2 * rows, 0),
-            (3, None, 0, 2 * rows, cut),
-            (4, None, 0, 3 * rows, 0),
-            (5, None, 0, 3 * rows, cut),
-        ],
-        kept,
-        kept_core,
-        *beside,
-        *beside_core,
-    )
-
     def part(grads, j):
-        return dot_first(grads, weights[:, j * width : (j + 1) * width])
+        return dot_first(grads, weights[: 4 * rows, j * width : (j + 1) * width])
 
     sums, from_x = {}, {}
     for j in reversed(range(n_z)):

time: 310 us -> 110 us (0.35)
  Pallas kernels: 219 us -> 8.62 us
  waiting for transfers between devices: 36.5 us -> 54.1 us
  starting transfers between devices: 34.2 us -> 30.6 us
    pallas_call x3 -> x2, Pallas kernels: 211 us -> 1.81 us  [copy_blocks(): pl.pallas_call(kernel, out_shape=[jax.ShapeDtypeStruct(shape, bf16) for s...]
    ppermute x31, waiting for transfers between devices: 36.5 us -> 54.1 us  [swap(): return lax.ppermute(value, axis, [(i, i ^ bit) for i in range(size)])]
    ppermute x31, starting transfers between devices: 34.2 us -> 30.6 us  [swap(): return lax.ppermute(value, axis, [(i, i ^ bit) for i in range(size)])]
    unnamed x57 -> x25, local copies, waits for them, and re-layouts: 9.83 us -> 7.94 us
  transfers between devices with their start and end apart: 31 -> 31, of which waited for: 12 -> 20; matrix products, arithmetic and copies ran while one was open for 2% -> 5% of each run, Pallas kernels for 71% -> 8%
where the time goes in v5:
time: 110 us
  waiting for transfers between devices  54.1 us (49%)
  starting transfers between devices  30.6 us (28%)
  Pallas kernels  8.62 us (8%)
  local copies, waits for them, and re-layouts  8.08 us (7%)
  matrix products  5.3 us (5%)
  other arithmetic  2.22 us (2%)
    ppermute x31, waiting for transfers between devices, swap(): return lax.ppermute(value, axis, [(i, i ^ bit) for i in range(size)])  54.1 us
    ppermute x31, starting transfers between devices, swap(): return lax.ppermute(value, axis, [(i, i ^ bit) for i in range(size)])  30.6 us
    unnamed x25, local copies, waits for them, and re-layouts  7.94 us
    dot_general x10, matrix products, dot_first(): return lax.dot_general(a, b, contract_first, preferred_element_type=f32)  4.78 us
    pallas_call x1, Pallas kernels, first_logits(): pl.pallas_call(kernel, out_shape=[jax.ShapeDtypeStruct((total, toks), f32...  4.41 us
    pallas_call x1, Pallas kernels, second_logits(): pl.pallas_call(kernel, out_shape=jax.ShapeDtypeStruct((total, toks), f32)...  2.41 us
  transfers between devices with their start and end apart: 31, of which 20 were waited for; matrix products, arithmetic and copies ran while one was open for 5% of the time, Pallas kernels for 8%

profile of v5, /device:TPU:0, one launch (start us, length us, event | category | flops | bytes accessed | tf_op | source)
XLA Modules:
  0.0 109.9 jit_solution(2430600954943525712)
XLA Ops:
  0.6 3.1 %collective-permute-start.1 = (bf16[128,1024]{1,0:T(8,128)(2,1)}, bf16[128,1024]{1,0:T(8,128)(2,1)}, u32[]{:S(2)}, u32[]{:S(2)}) collective-permute-start(bf16[128,1024]{1,0:T(8,128)(2,1)} %refs_7_.1), channel_id=1, source_target_pairs={{0,8},{4,12},{8,0},{12,4},{16,24},{20,28},{24,16},{28,20},{1,9},{5... | collective-permute-start | bytes 786440 | tf_op jit(solution)/shard_map/ppermute | solution.py:25
  3.7 2.6 %collective-permute-start = (bf16[128,1024]{1,0:T(8,128)(2,1)}, bf16[128,1024]{1,0:T(8,128)(2,1)}, u32[]{:S(2)}, u32[]{:S(2)}) collective-permute-start(bf16[128,1024]{1,0:T(8,128)(2,1)} %refs_7_.1), channel_id=1, source_target_pairs={{0,16},{4,20},{8,24},{12,28},{16,0},{20,4},{24,8},{28,12},{1,17},{... | collective-permute-start | bytes 786440 | tf_op jit(solution)/shard_map/ppermute | solution.py:25
  6.3 1.6 %copy-done = bf16[128,8192]{1,0:T(8,128)(2,1)S(1)} copy-done((bf16[128,8192]{1,0:T(8,128)(2,1)S(1)}, bf16[128,8192]{1,0:T(8,128)(2,1)}, u32[]{:S(2)}) %copy-start) | copy-done | bytes 2097176
  9.3 1.6 %collective-permute-start.4 = (bf16[128,3072]{1,0:T(8,128)(2,1)}, bf16[128,3072]{1,0:T(8,128)(2,1)S(1)}, u32[]{:S(2)}, u32[]{:S(2)}) collective-permute-start(bf16[128,3072]{1,0:T(8,128)(2,1)} %get-tuple-element.26), channel_id=1, source_target_pairs={{0,4},{4,0},{8,12},{12,8},{16,20},{20,16},{24,28},{28,24},{1,5},{5... | collective-permute-start | bytes 2359304 | tf_op jit(solution)/shard_map/ppermute | solution.py:25
  12.3 3.5 %collective-permute-done.1.refs_8_ = bf16[128,1024]{1,0:T(8,128)(2,1)} collective-permute-done((bf16[128,1024]{1,0:T(8,128)(2,1)}, bf16[128,1024]{1,0:T(8,128)(2,1)}, u32[]{:S(2)}, u32[]{:S(2)}) %collective-permute-start.1) | collective-permute-done | bytes 262176 | tf_op jit(solution)/shard_map/ppermute | solution.py:25
  15.8 2.5 %collective-permute-done.refs_9_ = bf16[128,1024]{1,0:T(8,128)(2,1)} collective-permute-done((bf16[128,1024]{1,0:T(8,128)(2,1)}, bf16[128,1024]{1,0:T(8,128)(2,1)}, u32[]{:S(2)}, u32[]{:S(2)}) %collective-permute-start) | collective-permute-done | bytes 262176 | tf_op jit(solution)/shard_map/ppermute | solution.py:25
  18.8 1.5 %collective-permute-start.5 = (bf16[128,1024]{1,0:T(8,128)(2,1)}, bf16[128,1024]{1,0:T(8,128)(2,1)}, u32[]{:S(2)}, u32[]{:S(2)}) collective-permute-start(bf16[128,1024]{1,0:T(8,128)(2,1)} %get-tuple-element.27), channel_id=1, source_target_pairs={{0,4},{4,0},{8,12},{12,8},{16,20},{20,16},{24,28},{28,24},{1,5},{5... | collective-permute-start | bytes 786440 | tf_op jit(solution)/shard_map/ppermute | solution.py:25
  20.3 1.5 %collective-permute-start.8 = (bf16[128,1024]{1,0:T(8,128)(2,1)}, bf16[128,1024]{1,0:T(8,128)(2,1)}, u32[]{:S(2)}, u32[]{:S(2)}) collective-permute-start(bf16[128,1024]{1,0:T(8,128)(2,1)} %collective-permute-done.refs_9_), channel_id=1, source_target_pairs={{0,2},{1,3},{2,0},{3,1},{4,6},{5,7},{6,4},{7,5},{8,10},{9,11},{10,... | collective-permute-start | bytes 786440 | tf_op jit(solution)/shard_map/ppermute | solution.py:25
  22.4 2.7 %collective-permute-done.2.refs_10_ = bf16[128,1024]{1,0:T(8,128)(2,1)} collective-permute-done((bf16[128,1024]{1,0:T(8,128)(2,1)}, bf16[128,1024]{1,0:T(8,128)(2,1)}, u32[]{:S(2)}, u32[]{:S(2)}) %collective-permute-start.2) | collective-permute-done | bytes 262176 | tf_op jit(solution)/shard_map/ppermute | solution.py:25
  25.1 1.6 %copy-done.1 = bf16[128,8192]{1,0:T(8,128)(2,1)S(1)} copy-done((bf16[128,8192]{1,0:T(8,128)(2,1)S(1)}, bf16[128,8192]{1,0:T(8,128)(2,1)}, u32[]{:S(2)}) %copy-start.1) | copy-done | bytes 2097176
  29.9 2.9 %collective-permute-done.7.refs_1_ = bf16[128,1024]{1,0:T(8,128)(2,1)} collective-permute-done((bf16[128,1024]{1,0:T(8,128)(2,1)}, bf16[128,1024]{1,0:T(8,128)(2,1)}, u32[]{:S(2)}, u32[]{:S(2)}) %collective-permute-start.7) | collective-permute-done | bytes 262176 | tf_op jit(solution)/shard_map/ppermute | solution.py:25
  34.0 1.7 %collective-permute-done.10.refs_5_ = bf16[128,1024]{1,0:T(8,128)(2,1)S(1)} collective-permute-done((bf16[128,1024]{1,0:T(8,128)(2,1)}, bf16[128,1024]{1,0:T(8,128)(2,1)S(1)}, u32[]{:S(2)}, u32[]{:S(2)}) %collective-permute-start.10) | collective-permute-done | bytes 262176 | tf_op jit(solution)/shard_map/ppermute | solution.py:25
  36.4 1.5 %collective-permute-start.17 = (bf16[64,64]{1,0:T(8,128)(2,1)S(1)}, bf16[64,64]{1,0:T(8,128)(2,1)S(1)}, u32[]{:S(2)}, u32[]{:S(2)}) collective-permute-start(bf16[64,64]{1,0:T(8,128)(2,1)S(1)} %copy-done.8), channel_id=1, source_target_pairs={{0,4},{4,0},{8,12},{12,8},{16,20},{20,16},{24,28},{28,24},{1,5},{5... | collective-permute-start | bytes 24584 | tf_op jit(solution)/shard_map/ppermute | solution.py:25
  38.1 1.5 %collective-permute-start.11 = (bf16[128,1024]{1,0:T(8,128)(2,1)}, bf16[128,1024]{1,0:T(8,128)(2,1)S(1)}, u32[]{:S(2)}, u32[]{:S(2)}) collective-permute-start(bf16[128,1024]{1,0:T(8,128)(2,1)} %collective-permute-done.2.refs_10_), channel_id=1, source_target_pairs={{0,2},{1,3},{2,0},{3,1},{4,6},{5,7},{6,4},{7,5},{8,10},{9,11},{10,... | collective-permute-start | bytes 786440 | tf_op jit(solution)/shard_map/ppermute | solution.py:25
  42.2 4.4 %shard_map.87 = (f32[576,128]{1,0:T(8,128)S(1)}, bf16[576,4096]{1,0:T(8,128)(2,1)S(1)}) custom-call(bf16[128,4096]{1,0:T(8,128)(2,1)S(1)} %get-tuple-element.25.refs_0_, bf16[128,4096]{1,0:T(8,128)(2,1)S(1)} %collective-permute-done.3.refs_1_, bf16[128,3072]{1,0:T(8,128)(2,1)S(1)} %collective-permute-done.4.refs_2_, ...), custom_call_target="tpu_custom_call" | custom-call | flops 603979776 | bytes 11829248 | tf_op jit(solution)/shard_map/pallas_call | solution.py:110
  46.6 1.6 %collective-permute-start.12 = (f32[576,128]{1,0:T(8,128)S(1)}, f32[576,128]{1,0:T(8,128)S(1)}, u32[]{:S(2)}, u32[]{:S(2)}) collective-permute-start(f32[576,128]{1,0:T(8,128)S(1)} %get-tuple-element.32), channel_id=1, source_target_pairs={{0,4},{4,0},{8,12},{12,8},{16,20},{20,16},{24,28},{28,24},{1,5},{5... | collective-permute-start | bytes 884744 | tf_op jit(solution)/shard_map/ppermute | solution.py:25
  48.6 2.4 %shard_map.88 = f32[576,128]{1,0:T(8,128)S(1)} custom-call(bf16[576,4096]{1,0:T(8,128)(2,1)S(1)} %get-tuple-element.33.weight_ref, bf16[128,1024]{1,0:T(8,128)(2,1)S(1)} %collective-permute-done.6.refs_0_, bf16[128,1024]{1,0:T(8,128)(2,1)} %collective-permute-done.7.refs_1_, bf16[128,1024]{1,0:T(8,128)(2,1)} %collective-permute-done.8.refs_2_, ...), custom_call_target="tpu_custom_call" | custom-call | flops 603979776 | bytes 6062080 | tf_op jit(solution)/shard_map/pallas_call | solution.py:138
  51.5 1.7 %collective-permute-done.18 = bf16[128,64]{1,0:T(8,128)(2,1)S(1)} collective-permute-done((bf16[128,64]{1,0:T(8,128)(2,1)S(1)}, bf16[128,64]{1,0:T(8,128)(2,1)S(1)}, u32[]{:S(2)}, u32[]{:S(2)}) %collective-permute-start.18) | collective-permute-done | bytes 16416 | tf_op jit(solution)/shard_map/ppermute | solution.py:25
  53.6 4.0 %collective-permute-done.19 = bf16[256,64]{1,0:T(8,128)(2,1)S(1)} collective-permute-done((bf16[256,64]{1,0:T(8,128)(2,1)S(1)}, bf16[256,64]{1,0:T(8,128)(2,1)S(1)}, u32[]{:S(2)}, u32[]{:S(2)}) %collective-permute-start.19) | collective-permute-done | bytes 32800 | tf_op jit(solution)/shard_map/ppermute | solution.py:25
  57.7 3.2 %collective-permute-done.13 = f32[576,128]{1,0:T(8,128)S(1)} collective-permute-done((f32[576,128]{1,0:T(8,128)S(1)}, f32[576,128]{1,0:T(8,128)S(1)}, u32[]{:S(2)}, u32[]{:S(2)}) %collective-permute-start.13) | collective-permute-done | bytes 294944 | tf_op jit(solution)/shard_map/ppermute | solution.py:25
  61.2 1.6 %collective-permute-start.14 = (f32[4,256]{1,0:T(4,128)S(1)}, f32[4,256]{1,0:T(4,128)S(1)}, u32[]{:S(2)}, u32[]{:S(2)}) collective-permute-start(f32[4,256]{1,0:T(4,128)S(1)} %maximum_maximum_fusion), channel_id=1, source_target_pairs={{0,2},{1,3},{2,0},{3,1},{4,6},{5,7},{6,4},{7,5},{8,10},{9,11},{10,... | collective-permute-start | bytes 12296 | tf_op jit(solution)/shard_map/ppermute | solution.py:25
  63.0 1.9 %collective-permute-done.14 = f32[4,256]{1,0:T(4,128)S(1)} collective-permute-done((f32[4,256]{1,0:T(4,128)S(1)}, f32[4,256]{1,0:T(4,128)S(1)}, u32[]{:S(2)}, u32[]{:S(2)}) %collective-permute-start.14) | collective-permute-done | bytes 4128 | tf_op jit(solution)/shard_map/ppermute | solution.py:25
  65.5 3.0 %collective-permute-done.15 = f32[2,256]{1,0:T(2,128)S(1)} collective-permute-done((f32[2,256]{1,0:T(2,128)S(1)}, f32[2,256]{1,0:T(2,128)S(1)}, u32[]{:S(2)}, u32[]{:S(2)}) %collective-permute-start.15) | collective-permute-done | bytes 2080 | tf_op jit(solution)/shard_map/ppermute | solution.py:25
  69.0 4.1 %collective-permute-done.16 = f32[2,256]{1,0:T(2,128)S(1)} collective-permute-done((f32[2,256]{1,0:T(2,128)S(1)}, f32[2,256]{1,0:T(2,128)S(1)}, u32[]{:S(2)}, u32[]{:S(2)}) %collective-permute-start.16) | collective-permute-done | bytes 2080 | tf_op jit(solution)/shard_map/ppermute | solution.py:25
  74.4 1.6 %collective-permute-start.22 = (bf16[128,1024]{1,0:T(8,128)(2,1)S(1)}, bf16[128,1024]{1,0:T(8,128)(2,1)S(1)}, u32[]{:S(2)}, u32[]{:S(2)}) collective-permute-start(bf16[128,1024]{1,0:T(8,128)(2,1)S(1)} %convolution_convert_fusion), channel_id=1, source_target_pairs={{0,2},{1,3},{2,0},{3,1},{4,6},{5,7},{6,4},{7,5},{8,10},{9,11},{10,... | collective-permute-start | bytes 786440 | tf_op jit(solution)/shard_map/ppermute | solution.py:25
  77.6 6.1 %collective-permute-done.22 = bf16[128,1024]{1,0:T(8,128)(2,1)S(1)} collective-permute-done((bf16[128,1024]{1,0:T(8,128)(2,1)S(1)}, bf16[128,1024]{1,0:T(8,128)(2,1)S(1)}, u32[]{:S(2)}, u32[]{:S(2)}) %collective-permute-start.22) | collective-permute-done | bytes 262176 | tf_op jit(solution)/shard_map/ppermute | solution.py:25
  83.7 1.5 %collective-permute-start.23 = (bf16[128,1024]{1,0:T(8,128)(2,1)S(1)}, bf16[128,1024]{1,0:T(8,128)(2,1)S(1)}, u32[]{:S(2)}, u32[]{:S(2)}) collective-permute-start(bf16[128,1024]{1,0:T(8,128)(2,1)S(1)} %convolution_convert_fusion.1), channel_id=1, source_target_pairs={{0,2},{1,3},{2,0},{3,1},{4,6},{5,7},{6,4},{7,5},{8,10},{9,11},{10,... | collective-permute-start | bytes 786440 | tf_op jit(solution)/shard_map/ppermute | solution.py:25
  85.2 4.1 %collective-permute-done.20 = bf16[128,1024]{1,0:T(8,128)(2,1)S(1)} collective-permute-done((bf16[128,1024]{1,0:T(8,128)(2,1)S(1)}, bf16[128,1024]{1,0:T(8,128)(2,1)S(1)}, u32[]{:S(2)}, u32[]{:S(2)}) %collective-permute-start.20) | collective-permute-done | bytes 262176 | tf_op jit(solution)/shard_map/ppermute | solution.py:25
  89.4 1.5 %collective-permute-start.21 = (bf16[128,1024]{1,0:T(8,128)(2,1)S(1)}, bf16[128,1024]{1,0:T(8,128)(2,1)S(1)}, u32[]{:S(2)}, u32[]{:S(2)}) collective-permute-start(bf16[128,1024]{1,0:T(8,128)(2,1)S(1)} %convolution_convert_fusion.3), channel_id=1, source_target_pairs={{0,2},{1,3},{2,0},{3,1},{4,6},{5,7},{6,4},{7,5},{8,10},{9,11},{10,... | collective-permute-start | bytes 786440 | tf_op jit(solution)/shard_map/ppermute | solution.py:25
  93.1 1.6 %collective-permute-start.29 = (bf16[64,1024]{1,0:T(8,128)(2,1)S(1)}, bf16[64,1024]{1,0:T(8,128)(2,1)S(1)}, u32[]{:S(2)}, u32[]{:S(2)}) collective-permute-start(bf16[64,1024]{1,0:T(8,128)(2,1)S(1)} %convert_element_type.99), channel_id=1, source_target_pairs={{0,2},{1,3},{2,0},{3,1},{4,6},{5,7},{6,4},{7,5},{8,10},{9,11},{10,... | collective-permute-start | bytes 393224 | tf_op jit(solution)/shard_map/ppermute | solution.py:25
  96.1 1.5 %collective-permute-done.25 = bf16[128,1024]{1,0:T(8,128)(2,1)S(1)} collective-permute-done((bf16[128,1024]{1,0:T(8,128)(2,1)S(1)}, bf16[128,1024]{1,0:T(8,128)(2,1)S(1)}, u32[]{:S(2)}, u32[]{:S(2)}) %collective-permute-start.25) | collective-permute-done | bytes 262176 | tf_op jit(solution)/shard_map/ppermute | solution.py:25
  102.0 6.0 %collective-permute-done.26 = bf16[128,1024]{1,0:T(8,128)(2,1)S(1)} collective-permute-done((bf16[128,1024]{1,0:T(8,128)(2,1)S(1)}, bf16[128,1024]{1,0:T(8,128)(2,1)S(1)}, u32[]{:S(2)}, u32[]{:S(2)}) %collective-permute-start.26) | collective-permute-done | bytes 262176 | tf_op jit(solution)/shard_map/ppermute | solution.py:25
  (113 shorter events, 27.1 us)
Async XLA Ops:
  0.6 15.2 %collective-permute-start.1 = (bf16[128,1024]{1,0:T(8,128)(2,1)}, bf16[128,1024]{1,0:T(8,128)(2,1)}, u32[]{:S(2)}, u32[]{:S(2)}) collective-permute-start(bf16[128,1024]{1,0:T(8,128)(2,1)} %refs_7_.1), channel_id=1, source_target_pairs={{0,8},{4,12},{8,0},{12,4},{16,24},{20,28},{24,16},{28,20},{1,9},{5... | collective-permute-start | bytes 786440 | tf_op jit(solution)/shard_map/ppermute | solution.py:25
  3.7 14.7 %collective-permute-start = (bf16[128,1024]{1,0:T(8,128)(2,1)}, bf16[128,1024]{1,0:T(8,128)(2,1)}, u32[]{:S(2)}, u32[]{:S(2)}) collective-permute-start(bf16[128,1024]{1,0:T(8,128)(2,1)} %refs_7_.1), channel_id=1, source_target_pairs={{0,16},{4,20},{8,24},{12,28},{16,0},{20,4},{24,8},{28,12},{1,17},{... | collective-permute-start | bytes 786440 | tf_op jit(solution)/shard_map/ppermute | solution.py:25
  7.9 32.3 %copy-start.3 = (bf16[128,1024]{1,0:T(8,128)(2,1)S(1)}, bf16[128,1024]{1,0:T(8,128)(2,1)}, u32[]{:S(2)}) copy-start(bf16[128,1024]{1,0:T(8,128)(2,1)} %refs_7_.1) | copy-start | bytes 786436
  9.3 23.6 %collective-permute-start.4 = (bf16[128,3072]{1,0:T(8,128)(2,1)}, bf16[128,3072]{1,0:T(8,128)(2,1)S(1)}, u32[]{:S(2)}, u32[]{:S(2)}) collective-permute-start(bf16[128,3072]{1,0:T(8,128)(2,1)} %get-tuple-element.26), channel_id=1, source_target_pairs={{0,4},{4,0},{8,12},{12,8},{16,20},{20,16},{24,28},{28,24},{1,5},{5... | collective-permute-start | bytes 2359304 | tf_op jit(solution)/shard_map/ppermute | solution.py:25
  10.8 9.5 %collective-permute-start.6 = (bf16[128,1024]{1,0:T(8,128)(2,1)}, bf16[128,1024]{1,0:T(8,128)(2,1)S(1)}, u32[]{:S(2)}, u32[]{:S(2)}) collective-permute-start(bf16[128,1024]{1,0:T(8,128)(2,1)} %refs_7_.1), channel_id=1, source_target_pairs={{0,2},{1,3},{2,0},{3,1},{4,6},{5,7},{6,4},{7,5},{8,10},{9,11},{10,... | collective-permute-start | bytes 786440 | tf_op jit(solution)/shard_map/ppermute | solution.py:25
  18.4 6.7 %collective-permute-start.2 = (bf16[128,1024]{1,0:T(8,128)(2,1)}, bf16[128,1024]{1,0:T(8,128)(2,1)}, u32[]{:S(2)}, u32[]{:S(2)}) collective-permute-start(bf16[128,1024]{1,0:T(8,128)(2,1)} %collective-permute-done.refs_9_), channel_id=1, source_target_pairs={{0,8},{4,12},{8,0},{12,4},{16,24},{20,28},{24,16},{28,20},{1,9},{5... | collective-permute-start | bytes 786440 | tf_op jit(solution)/shard_map/ppermute | solution.py:25
  18.8 15.2 %collective-permute-start.5 = (bf16[128,1024]{1,0:T(8,128)(2,1)}, bf16[128,1024]{1,0:T(8,128)(2,1)}, u32[]{:S(2)}, u32[]{:S(2)}) collective-permute-start(bf16[128,1024]{1,0:T(8,128)(2,1)} %get-tuple-element.27), channel_id=1, source_target_pairs={{0,4},{4,0},{8,12},{12,8},{16,20},{20,16},{24,28},{28,24},{1,5},{5... | collective-permute-start | bytes 786440 | tf_op jit(solution)/shard_map/ppermute | solution.py:25
  20.3 9.6 %collective-permute-start.8 = (bf16[128,1024]{1,0:T(8,128)(2,1)}, bf16[128,1024]{1,0:T(8,128)(2,1)}, u32[]{:S(2)}, u32[]{:S(2)}) collective-permute-start(bf16[128,1024]{1,0:T(8,128)(2,1)} %collective-permute-done.refs_9_), channel_id=1, source_target_pairs={{0,2},{1,3},{2,0},{3,1},{4,6},{5,7},{6,4},{7,5},{8,10},{9,11},{10,... | collective-permute-start | bytes 786440 | tf_op jit(solution)/shard_map/ppermute | solution.py:25
  21.8 11.0 %collective-permute-start.7 = (bf16[128,1024]{1,0:T(8,128)(2,1)}, bf16[128,1024]{1,0:T(8,128)(2,1)}, u32[]{:S(2)}, u32[]{:S(2)}) collective-permute-start(bf16[128,1024]{1,0:T(8,128)(2,1)} %collective-permute-done.1.refs_8_), channel_id=1, source_target_pairs={{0,2},{1,3},{2,0},{3,1},{4,6},{5,7},{6,4},{7,5},{8,10},{9,11},{10,... | collective-permute-start | bytes 786440 | tf_op jit(solution)/shard_map/ppermute | solution.py:25
  29.2 11.0 %collective-permute-start.3 = (bf16[128,4096]{1,0:T(8,128)(2,1)S(1)}, bf16[128,4096]{1,0:T(8,128)(2,1)S(1)}, u32[]{:S(2)}, u32[]{:S(2)}) collective-permute-start(bf16[128,4096]{1,0:T(8,128)(2,1)S(1)} %get-tuple-element.25.refs_0_), channel_id=1, source_target_pairs={{0,1},{1,0},{2,3},{3,2},{4,5},{5,4},{6,7},{7,6},{8,9},{9,8},{10,11... | collective-permute-start | bytes 3145736 | tf_op jit(solution)/shard_map/ppermute | solution.py:25
  32.8 7.4 %collective-permute-start.9 = (bf16[128,3072]{1,0:T(8,128)(2,1)S(1)}, bf16[128,3072]{1,0:T(8,128)(2,1)}, u32[]{:S(2)}, u32[]{:S(2)}) collective-permute-start(bf16[128,3072]{1,0:T(8,128)(2,1)S(1)} %collective-permute-done.4.refs_2_), channel_id=1, source_target_pairs={{0,1},{1,0},{2,3},{3,2},{4,5},{5,4},{6,7},{7,6},{8,9},{9,8},{10,11... | collective-permute-start | bytes 2359304 | tf_op jit(solution)/shard_map/ppermute | solution.py:25
  34.0 1.7 %collective-permute-start.10 = (bf16[128,1024]{1,0:T(8,128)(2,1)}, bf16[128,1024]{1,0:T(8,128)(2,1)S(1)}, u32[]{:S(2)}, u32[]{:S(2)}) collective-permute-start(bf16[128,1024]{1,0:T(8,128)(2,1)} %collective-permute-done.5.refs_3_), channel_id=1, source_target_pairs={{0,1},{1,0},{2,3},{3,2},{4,5},{5,4},{6,7},{7,6},{8,9},{9,8},{10,11... | collective-permute-start | bytes 786440 | tf_op jit(solution)/shard_map/ppermute | solution.py:25
  36.4 3.7 %collective-permute-start.17 = (bf16[64,64]{1,0:T(8,128)(2,1)S(1)}, bf16[64,64]{1,0:T(8,128)(2,1)S(1)}, u32[]{:S(2)}, u32[]{:S(2)}) collective-permute-start(bf16[64,64]{1,0:T(8,128)(2,1)S(1)} %copy-done.8), channel_id=1, source_target_pairs={{0,4},{4,0},{8,12},{12,8},{16,20},{20,16},{24,28},{28,24},{1,5},{5... | collective-permute-start | bytes 24584 | tf_op jit(solution)/shard_map/ppermute | solution.py:25
  38.1 10.5 %collective-permute-start.11 = (bf16[128,1024]{1,0:T(8,128)(2,1)}, bf16[128,1024]{1,0:T(8,128)(2,1)S(1)}, u32[]{:S(2)}, u32[]{:S(2)}) collective-permute-start(bf16[128,1024]{1,0:T(8,128)(2,1)} %collective-permute-done.2.refs_10_), channel_id=1, source_target_pairs={{0,2},{1,3},{2,0},{3,1},{4,6},{5,7},{6,4},{7,5},{8,10},{9,11},{10,... | collective-permute-start | bytes 786440 | tf_op jit(solution)/shard_map/ppermute | solution.py:25
  46.6 11.0 %collective-permute-start.12 = (f32[576,128]{1,0:T(8,128)S(1)}, f32[576,128]{1,0:T(8,128)S(1)}, u32[]{:S(2)}, u32[]{:S(2)}) collective-permute-start(f32[576,128]{1,0:T(8,128)S(1)} %get-tuple-element.32), channel_id=1, source_target_pairs={{0,4},{4,0},{8,12},{12,8},{16,20},{20,16},{24,28},{28,24},{1,5},{5... | collective-permute-start | bytes 884744 | tf_op jit(solution)/shard_map/ppermute | solution.py:25
  48.2 5.0 %collective-permute-start.18 = (bf16[128,64]{1,0:T(8,128)(2,1)S(1)}, bf16[128,64]{1,0:T(8,128)(2,1)S(1)}, u32[]{:S(2)}, u32[]{:S(2)}) collective-permute-start(bf16[128,64]{1,0:T(8,128)(2,1)S(1)} %pad_maximum_fusion.3), channel_id=1, source_target_pairs={{0,16},{4,20},{8,24},{12,28},{16,0},{20,4},{24,8},{28,12},{1,17},{... | collective-permute-start | bytes 49160 | tf_op jit(solution)/shard_map/ppermute | solution.py:25
  51.0 9.9 %collective-permute-start.13 = (f32[576,128]{1,0:T(8,128)S(1)}, f32[576,128]{1,0:T(8,128)S(1)}, u32[]{:S(2)}, u32[]{:S(2)}) collective-permute-start(f32[576,128]{1,0:T(8,128)S(1)} %shard_map.88), channel_id=1, source_target_pairs={{0,4},{4,0},{8,12},{12,8},{16,20},{20,16},{24,28},{28,24},{1,5},{5... | collective-permute-start | bytes 884744 | tf_op jit(solution)/shard_map/ppermute | solution.py:25
  53.3 4.3 %collective-permute-start.19 = (bf16[256,64]{1,0:T(8,128)(2,1)S(1)}, bf16[256,64]{1,0:T(8,128)(2,1)S(1)}, u32[]{:S(2)}, u32[]{:S(2)}) collective-permute-start(bf16[256,64]{1,0:T(8,128)(2,1)S(1)} %pad_maximum_fusion.2), channel_id=1, source_target_pairs={{0,8},{4,12},{8,0},{12,4},{16,24},{20,28},{24,16},{28,20},{1,9},{5... | collective-permute-start | bytes 98312 | tf_op jit(solution)/shard_map/ppermute | solution.py:25
  61.2 3.7 %collective-permute-start.14 = (f32[4,256]{1,0:T(4,128)S(1)}, f32[4,256]{1,0:T(4,128)S(1)}, u32[]{:S(2)}, u32[]{:S(2)}) collective-permute-start(f32[4,256]{1,0:T(4,128)S(1)} %maximum_maximum_fusion), channel_id=1, source_target_pairs={{0,2},{1,3},{2,0},{3,1},{4,6},{5,7},{6,4},{7,5},{8,10},{9,11},{10,... | collective-permute-start | bytes 12296 | tf_op jit(solution)/shard_map/ppermute | solution.py:25
  64.9 3.7 %collective-permute-start.15 = (f32[2,256]{1,0:T(2,128)S(1)}, f32[2,256]{1,0:T(2,128)S(1)}, u32[]{:S(2)}, u32[]{:S(2)}) collective-permute-start(f32[2,256]{1,0:T(2,128)S(1)} %pad_maximum_fusion.4), channel_id=1, source_target_pairs={{0,8},{4,12},{8,0},{12,4},{16,24},{20,28},{24,16},{28,20},{1,9},{5... | collective-permute-start | bytes 6152 | tf_op jit(solution)/shard_map/ppermute | solution.py:25
  68.6 4.5 %collective-permute-start.16 = (f32[2,256]{1,0:T(2,128)S(1)}, f32[2,256]{1,0:T(2,128)S(1)}, u32[]{:S(2)}, u32[]{:S(2)}) collective-permute-start(f32[2,256]{1,0:T(2,128)S(1)} %pad_maximum_fusion.5), channel_id=1, source_target_pairs={{0,16},{4,20},{8,24},{12,28},{16,0},{20,4},{24,8},{28,12},{1,17},{... | collective-permute-start | bytes 6152 | tf_op jit(solution)/shard_map/ppermute | solution.py:25
  74.4 9.3 %collective-permute-start.22 = (bf16[128,1024]{1,0:T(8,128)(2,1)S(1)}, bf16[128,1024]{1,0:T(8,128)(2,1)S(1)}, u32[]{:S(2)}, u32[]{:S(2)}) collective-permute-start(bf16[128,1024]{1,0:T(8,128)(2,1)S(1)} %convolution_convert_fusion), channel_id=1, source_target_pairs={{0,2},{1,3},{2,0},{3,1},{4,6},{5,7},{6,4},{7,5},{8,10},{9,11},{10,... | collective-permute-start | bytes 786440 | tf_op jit(solution)/shard_map/ppermute | solution.py:25
  76.5 12.8 %collective-permute-start.20 = (bf16[128,1024]{1,0:T(8,128)(2,1)S(1)}, bf16[128,1024]{1,0:T(8,128)(2,1)S(1)}, u32[]{:S(2)}, u32[]{:S(2)}) collective-permute-start(bf16[128,1024]{1,0:T(8,128)(2,1)S(1)} %convolution_convert_fusion.2), channel_id=1, source_target_pairs={{0,2},{1,3},{2,0},{3,1},{4,6},{5,7},{6,4},{7,5},{8,10},{9,11},{10,... | collective-permute-start | bytes 786440 | tf_op jit(solution)/shard_map/ppermute | solution.py:25
  83.7 9.4 %collective-permute-start.23 = (bf16[128,1024]{1,0:T(8,128)(2,1)S(1)}, bf16[128,1024]{1,0:T(8,128)(2,1)S(1)}, u32[]{:S(2)}, u32[]{:S(2)}) collective-permute-start(bf16[128,1024]{1,0:T(8,128)(2,1)S(1)} %convolution_convert_fusion.1), channel_id=1, source_target_pairs={{0,2},{1,3},{2,0},{3,1},{4,6},{5,7},{6,4},{7,5},{8,10},{9,11},{10,... | collective-permute-start | bytes 786440 | tf_op jit(solution)/shard_map/ppermute | solution.py:25
  89.4 11.8 %collective-permute-start.21 = (bf16[128,1024]{1,0:T(8,128)(2,1)S(1)}, bf16[128,1024]{1,0:T(8,128)(2,1)S(1)}, u32[]{:S(2)}, u32[]{:S(2)}) collective-permute-start(bf16[128,1024]{1,0:T(8,128)(2,1)S(1)} %convolution_convert_fusion.3), channel_id=1, source_target_pairs={{0,2},{1,3},{2,0},{3,1},{4,6},{5,7},{6,4},{7,5},{8,10},{9,11},{10,... | collective-permute-start | bytes 786440 | tf_op jit(solution)/shard_map/ppermute | solution.py:25
  91.2 6.4 %collective-permute-start.25 = (bf16[128,1024]{1,0:T(8,128)(2,1)S(1)}, bf16[128,1024]{1,0:T(8,128)(2,1)S(1)}, u32[]{:S(2)}, u32[]{:S(2)}) collective-permute-start(bf16[128,1024]{1,0:T(8,128)(2,1)S(1)} %fusion.7), channel_id=1, source_target_pairs={{0,8},{4,12},{8,0},{12,4},{16,24},{20,28},{24,16},{28,20},{1,9},{5... | collective-permute-start | bytes 786440 | tf_op jit(solution)/shard_map/ppermute | solution.py:25
  93.1 7.4 %collective-permute-start.29 = (bf16[64,1024]{1,0:T(8,128)(2,1)S(1)}, bf16[64,1024]{1,0:T(8,128)(2,1)S(1)}, u32[]{:S(2)}, u32[]{:S(2)}) collective-permute-start(bf16[64,1024]{1,0:T(8,128)(2,1)S(1)} %convert_element_type.99), channel_id=1, source_target_pairs={{0,2},{1,3},{2,0},{3,1},{4,6},{5,7},{6,4},{7,5},{8,10},{9,11},{10,... | collective-permute-start | bytes 393224 | tf_op jit(solution)/shard_map/ppermute | solution.py:25
  94.7 4.0 %collective-permute-start.27 = (f32[64,64]{1,0:T(8,128)S(1)}, f32[64,64]{1,0:T(8,128)S(1)}, u32[]{:S(2)}, u32[]{:S(2)}) collective-permute-start(f32[64,64]{1,0:T(8,128)S(1)} %fusion.28), channel_id=1, source_target_pairs={{0,2},{1,3},{2,0},{3,1},{4,6},{5,7},{6,4},{7,5},{8,10},{9,11},{10,... | collective-permute-start | bytes 49160 | tf_op jit(solution)/shard_map/ppermute | solution.py:25
  95.6 6.4 %collective-permute-start.24 = (bf16[128,1024]{1,0:T(8,128)(2,1)S(1)}, bf16[128,1024]{1,0:T(8,128)(2,1)S(1)}, u32[]{:S(2)}, u32[]{:S(2)}) collective-permute-start(bf16[128,1024]{1,0:T(8,128)(2,1)S(1)} %fusion.6), channel_id=1, source_target_pairs={{0,8},{4,12},{8,0},{12,4},{16,24},{20,28},{24,16},{28,20},{1,9},{5... | collective-permute-start | bytes 786440 | tf_op jit(solution)/shard_map/ppermute | solution.py:25
  98.0 10.1 %collective-permute-start.26 = (bf16[128,1024]{1,0:T(8,128)(2,1)S(1)}, bf16[128,1024]{1,0:T(8,128)(2,1)S(1)}, u32[]{:S(2)}, u32[]{:S(2)}) collective-permute-start(bf16[128,1024]{1,0:T(8,128)(2,1)S(1)} %fusion.5), channel_id=1, source_target_pairs={{0,16},{4,20},{8,24},{12,28},{16,0},{20,4},{24,8},{28,12},{1,17},{... | collective-permute-start | bytes 786440 | tf_op jit(solution)/shard_map/ppermute | solution.py:25
  98.7 1.3 %collective-permute-start.28 = (f32[64,64]{1,0:T(8,128)S(1)}, f32[64,64]{1,0:T(8,128)S(1)}, u32[]{:S(2)}, u32[]{:S(2)}) collective-permute-start(f32[64,64]{1,0:T(8,128)S(1)} %add.379), channel_id=1, source_target_pairs={{0,1},{1,0},{2,3},{3,2},{4,5},{5,4},{6,7},{7,6},{8,9},{9,8},{10,11... | collective-permute-start | bytes 49160 | tf_op jit(solution)/shard_map/ppermute | solution.py:25
  100.6 8.5 %collective-permute-start.30 = (f32[64,1024]{1,0:T(8,128)S(1)}, f32[64,1024]{1,0:T(8,128)S(1)}, u32[]{:S(2)}, u32[]{:S(2)}) collective-permute-start(f32[64,1024]{1,0:T(8,128)S(1)} %convert_add_fusion), channel_id=1, source_target_pairs={{0,1},{1,0},{2,3},{3,2},{4,5},{5,4},{6,7},{7,6},{8,9},{9,8},{10,11... | collective-permute-start | bytes 786440 | tf_op jit(solution)/shard_map/ppermute | solution.py:25
  (10 other events, 88.6 us)

commit v6 on v5

--- a/solution.py
+++ b/solution.py
@@ -41,16 +41,15 @@
     return swap(value, "vocab", 2 * step)
 
 
-anywhere = pl.BlockSpec(memory_space=pl.ANY)
 in_vmem = pl.BlockSpec(memory_space=pltpu.VMEM)
 
 
-def copy_blocks(shapes, moves, *arrays):
+def copy_blocks(shapes, moves, *arrays, source=pltpu.HBM):
     def kernel(*refs):
         ins, outs, sems = refs[: len(arrays)], refs[len(arrays) : -1], refs[-1]
         copies = []
-        for n, (source, columns, target, row, column) in enumerate(moves()):
-            src, dst = ins[source], outs[target]
+        for n, (origin, columns, target, row, column) in enumerate(moves()):
+            src, dst = ins[origin], outs[target]
             if columns is not None:
                 src = src.at[:, pl.ds(pl.multiple_of(columns[0], 128), columns[1])]
             dst = dst.at[pl.ds(row, src.shape[0]), pl.ds(column, src.shape[1])]
@@ -64,81 +63,39 @@
     return pl.pallas_call(
         kernel,
         out_shape=[jax.ShapeDtypeStruct(shape, bf16) for shape in shapes],
-        in_specs=[anywhere] * len(arrays),
+        in_specs=[pl.BlockSpec(memory_space=source)] * len(arrays),
         out_specs=[in_vmem] * len(shapes),
         scratch_shapes=[pltpu.SemaphoreType.DMA((32,))],
-        compiler_params=pltpu.CompilerParams(vmem_limit_bytes=4 << 20),
+        compiler_params=pltpu.CompilerParams(vmem_limit_bytes=12 << 20),
         cost_estimate=pl.CostEstimate(flops=0, bytes_accessed=2 * size, transcendentals=0),
     )(*arrays)
 
 
-def side_by_side(parts, into, row, sems, first):
-    copies, column = [], 0
-    for n, part in enumerate(parts):
-        dst = into.at[pl.ds(row, part.shape[0]), pl.ds(column, part.shape[1])]
-        copies.append(pltpu.make_async_copy(part, dst, sems.at[first + n]))
-        column += part.shape[1]
-    return copies
-
-
-def first_logits(groups, tokens):
+def logits_of(groups, tokens):
+    toks, width = tokens[0].shape
     heights = [group[0].shape[0] for group in groups]
-    sizes = [len(group) for group in groups]
-    total, depth = sum(heights), sum(a.shape[1] for a in tokens)
-    toks = tokens[0].shape[0]
+    total, depth = sum(heights), width * len(tokens)
     flat = [a for group in groups for a in group]
     n_flat, n_all = len(flat), len(flat) + len(tokens)
 
     def kernel(*refs):
-        out, weight, token, sems = refs[n_all:]
-        token_copies = side_by_side(refs[n_flat:n_all], token, 0, sems, n_flat)
-        row_copies, at, row = [], 0, 0
-        for size, height in zip(sizes, heights):
-            row_copies.append(side_by_side(refs[at : at + size], weight, row, sems, at))
-            at, row = at + size, row + height
-        for copy in token_copies + [copy for copies in row_copies for copy in copies]:
-            copy.start()
-        for copy in token_copies:
-            copy.wait()
-        row = 0
-        for copies, height in zip(row_copies, heights):
-            for copy in copies:
-                copy.wait()
-            out[row : row + height, :] = dot_last(weight[row : row + height, :], token[...])
+        out = refs[n_all]
+        at, row = 0, 0
+        for group, height in zip(groups, heights):
+            result, column = None, 0
+            for part in group:
+                for c in range(0, part.shape[1], width):
+                    token = refs[n_flat + (column + c) // width]
+                    term = dot_last(refs[at][:, c : c + width], token[...])
+                    result = term if result is None else result + term
+                at, column = at + 1, column + part.shape[1]
+            out[row : row + height, :] = result
             row += height
-
-    return pl.pallas_call(
-        kernel,
-        out_shape=[
-            jax.ShapeDtypeStruct((total, toks), f32),
-            jax.ShapeDtypeStruct((total, depth), bf16),
-        ],
-        in_specs=[anywhere] * n_all,
-        out_specs=[in_vmem] * 2,
-        scratch_shapes=[pltpu.VMEM((toks, depth), bf16), pltpu.SemaphoreType.DMA((n_all,))],
-        compiler_params=pltpu.CompilerParams(vmem_limit_bytes=12 << 20),
-        cost_estimate=pl.CostEstimate(
-            flops=2 * total * depth * toks,
-            bytes_accessed=4 * (total + toks) * depth + 4 * total * toks,
-            transcendentals=0,
-        ),
-    )(*flat, *tokens)
-
-
-def second_logits(weight, tokens):
-    total, depth = weight.shape
-    toks, width = tokens[0].shape
-
-    def kernel(weight_ref, *refs):
-        out = refs[-1]
-        for j, token in enumerate(refs[:-1]):
-            part = dot_last(weight_ref[:, j * width : (j + 1) * width], token[...])
-            out[...] = part if j == 0 else out[...] + part
 
     return pl.pallas_call(
         kernel,
         out_shape=jax.ShapeDtypeStruct((total, toks), f32),
-        in_specs=[in_vmem] * (1 + len(tokens)),
+        in_specs=[in_vmem] * n_all,
         out_specs=in_vmem,
         compiler_params=pltpu.CompilerParams(vmem_limit_bytes=12 << 20),
         cost_estimate=pl.CostEstimate(
@@ -146,7 +103,7 @@
             bytes_accessed=2 * (total + toks) * depth + 4 * total * toks,
             transcendentals=0,
         ),
-    )(weight, *tokens)
+    )(*flat, *tokens)
 
 
 def on_few(hidden, head, factor_rows, factor_basis, targets, loss_mask):
@@ -164,14 +121,22 @@
     def start_of(j, other):
         return (lax.axis_index("vocab") ^ (2 * j + other)) * width
 
-    cut = (n_z - 1) * width
-    send_first, send_last = copy_blocks(
-        [(rows, cut), (rows, width)],
-        lambda: [(0, (start_of(j, 1), width), 0, 0, j * width) for j in range(n_z - 1)]
-        + [(0, (start_of(n_z - 1, 1), width), 1, 0, 0)],
+    cuts = [0, n_z // 2, 3 * n_z // 4, n_z] if n_z > 2 else list(range(n_z + 1))
+    chunks = [range(a, b) for a, b in zip(cuts, cuts[1:])]
+    sends = copy_blocks(
+        [(rows, len(chunk) * width) for chunk in chunks],
+        lambda: [
+            (0, (start_of(j, 1), width), n, 0, (j - chunk[0]) * width)
+            for n, chunk in enumerate(chunks)
+            for j in chunk
+        ],
         head,
     )
-    beside_first = swap_y(send_first)
+    beside = []
+    for n, send in enumerate(sends):
+        if n > 1:
+            send, _ = lax.optimization_barrier((send, beside[0]))
+        beside.append(swap_y(send))
 
     shards = {0: hidden}
     for bit in reversed(bits):
@@ -187,9 +152,8 @@
             sent, _ = lax.optimization_barrier((sent, cross[j - 2]))
         cross[j] = swap_x(sent)
 
-    beside_last = swap_y(send_last)
     head_after, basis_after, _ = lax.optimization_barrier(
-        (head, factor_basis, shards[n_z - 1])
+        (head, factor_basis, cross[0])
     )
     kept, basis_half = copy_blocks(
         [(rows, depth), (rank, depth)],
@@ -200,28 +164,38 @@
         basis_after,
     )
     kept_core = swap_core(kept)
-    beside = [beside_first, beside_last]
-    first_after, *_ = lax.optimization_barrier(
-        (beside_first, *[cross[j] for j in range(n_z - 1)])
-    )
-    last_after, _ = lax.optimization_barrier((beside_last, shards[n_z - 1]))
-    beside_core = [swap_core(first_after), swap_core(last_after)]
-
-    groups = [[kept], [kept_core], beside, beside_core, [basis_half]]
+    beside_core = []
+    for n, came in enumerate(beside):
+        after = shards[n_z - 1] if n else cross[min(1, n_z - 1)]
+        came, _ = lax.optimization_barrier((came, after))
+        beside_core.append(swap_core(came))
+
     in_order = lambda parts: [parts[j] for j in range(n_z)]
-    mine_own, weights = first_logits(groups, in_order(shards))
-    mine_cross = second_logits(weights, in_order(cross))
-    theirs_own, theirs_cross = swap_y(mine_own), swap_y(mine_cross)
-    mine = jnp.concatenate([mine_own, mine_cross], axis=1)
-    theirs = jnp.concatenate([theirs_own, theirs_cross], axis=1)
-    frozen_near = mine[: 2 * rows] + theirs[2 * rows : 4 * rows]
-    frozen_far = mine[2 * rows : 4 * rows] + theirs[: 2 * rows]
-    hidden_basis = (mine[4 * rows :] + theirs[4 * rows :]).astype(bf16)
-
-    near_rows, _ = lax.optimization_barrier((factor_rows, beside_core[1]))
-    rows_all = jnp.concatenate([factor_rows, swap_y(near_rows)], axis=0)
+    upper = [[kept], [kept_core], [basis_half]]
+    upper_own = logits_of(upper, in_order(shards))
+    beside_core[-1], _ = lax.optimization_barrier((beside_core[-1], upper_own))
+    lower_own = logits_of([beside, beside_core], in_order(shards))
+    both_cross = logits_of(upper + [beside, beside_core], in_order(cross))
+    n_up = 2 * rows + rank
+
+    def add_over_y(up, low, up_came, low_came):
+        near = up[: 2 * rows] + low_came
+        far = low + up_came[: 2 * rows]
+        return near, far, (up[2 * rows :] + up_came[2 * rows :]).astype(bf16)
+
+    upper_came, lower_came = swap_y(upper_own), swap_y(lower_own)
+    cross_came = swap_y(both_cross)
+    near_own, far_own, basis_own = add_over_y(upper_own, lower_own, upper_came, lower_came)
+    near_cross, far_cross, basis_cross = add_over_y(
+        both_cross[:n_up], both_cross[n_up:], cross_came[:n_up], cross_came[n_up:]
+    )
+    hidden_basis = jnp.concatenate([basis_own, basis_cross], axis=1)
+
+    near_rows, _ = lax.optimization_barrier((factor_rows, beside[-1]))
+    rows_came = swap_y(near_rows)
     row_blocks = [0, 1]
-    rows_all, _ = lax.optimization_barrier((rows_all, mine_own))
+    rows_came, _ = lax.optimization_barrier((rows_came, upper_own))
+    rows_all = jnp.concatenate([factor_rows, rows_came], axis=0)
     for bit in [2 * b for b in reversed(bits)]:
         rows_all = jnp.concatenate([rows_all, swap(rows_all, "vocab", bit)], axis=0)
         row_blocks = row_blocks + [j ^ bit for j in row_blocks]
@@ -240,7 +214,7 @@
         return jnp.stack([top, total])
 
     info = jnp.stack([targets.astype(f32), loss_mask.astype(f32)])
-    stats = local(frozen_near, frozen_far)
+    stats = jnp.concatenate([local(near_own, far_own), local(near_cross, far_cross)], axis=1)
     sent = jnp.concatenate([stats, jnp.concatenate([info, info], axis=1)], axis=0)
     came = swap_x(sent)
     stats = merge(stats, jnp.concatenate([came[:2, toks:], came[:2, :toks]], axis=1))
@@ -258,15 +232,44 @@
 
     row_iota = lax.broadcasted_iota(jnp.int32, (rows, 1), 0)
 
-    def grad_of(frozen, vv):
+    def grad_of(frozen, vv, cols):
         row_ids = jnp.concatenate(
             [row_iota + (vv * n_tok + tt) * rows for tt in (t, t ^ 1)], axis=0
         )
-        hit = jnp.where(row_ids == target_row[None, :], weight_row[None, :], 0.0)
-        return (jnp.exp(frozen - row_top[None, :]) * scale_row[None, :] - hit).astype(bf16)
-
-    grad = jnp.concatenate([grad_of(frozen_near, v), grad_of(frozen_far, v ^ 1)], axis=0)
-
+        hit = jnp.where(row_ids == target_row[None, cols], weight_row[None, cols], 0.0)
+        return (jnp.exp(frozen - row_top[None, cols]) * scale_row[None, cols] - hit).astype(bf16)
+
+    at_own, at_cross = slice(0, toks), slice(toks, 2 * toks)
+    grad_cross = (grad_of(near_cross, v, at_cross), grad_of(far_cross, v ^ 1, at_cross))
+    grad_own = (grad_of(near_own, v, at_own), grad_of(far_own, v ^ 1, at_own))
+
+    laid = [kept, kept_core] + beside + beside_core
+    laid[0], _ = lax.optimization_barrier((kept, both_cross))
+    places, row = [], 0
+    for group in ([kept], [kept_core], beside, beside_core):
+        column = 0
+        for array in group:
+            places.append((len(places), None, 0, row, column))
+            column += array.shape[1]
+        row += rows
+    (weights,) = copy_blocks([(4 * rows, depth)], lambda: places, *laid, source=pltpu.VMEM)
+
+    def part(grads, j):
+        return dot_first(grads, weights[:, j * width : (j + 1) * width])
+
+    grad_cross = jnp.concatenate(grad_cross, axis=0)
+    grad_own = jnp.concatenate(grad_own, axis=0)
+    sums, from_x, first_z = {}, {}, None
+    for j in reversed(range(n_z)):
+        send = part(grad_cross, j).astype(bf16)
+        if j + 2 in from_x:
+            send, _, _ = lax.optimization_barrier((send, from_x[j + 2], first_z))
+        first_send = send if j == n_z - 1 else first_send
+        from_x[j] = swap_x(send)
+        sums[j] = part(grad_own, j) + from_x[j].astype(f32)
+        if first_z is None:
+            first_z = sums[j].astype(bf16)
+    fresh, _ = lax.optimization_barrier((fresh, first_send))
     frozen_rows = rows * n_tok * lax.axis_size("vocab")
     new_iota = lax.broadcasted_iota(jnp.int32, (new_here, 1), 0) + frozen_rows
     fresh_ids = jnp.concatenate([new_iota + (v ^ j) * new_here for j in row_blocks], axis=0)
@@ -276,31 +279,23 @@
     ).astype(bf16)
     mix_total = dot_first(rows_all, fresh_grad).astype(bf16)
     rows_part = dot_last(fresh_grad[:new_here], hidden_basis[:, :toks])
-    basis_part = lax.reduce_precision(jnp.dot(mix_total, hidden, preferred_element_type=f32), 8, 7)
-
-    def part(grads, j):
-        return dot_first(grads, weights[: 4 * rows, j * width : (j + 1) * width])
-
-    sums, from_x = {}, {}
-    for j in reversed(range(n_z)):
-        send = part(grad[:, toks:], j).astype(bf16)
-        if j + 2 in from_x:
-            send, _ = lax.optimization_barrier((send, from_x[j + 2]))
-        from_x[j] = swap_x(send)
-        sums[j] = part(grad[:, :toks], j) + from_x[j].astype(f32)
+    basis_part = jnp.dot(mix_total, hidden, preferred_element_type=f32)
+
     for bit in bits:
         for j in [j for j in sorted(sums, reverse=True) if j & bit]:
-            sums[j ^ bit] = sums[j ^ bit] + swap_z(sums.pop(j).astype(bf16), bit).astype(f32)
+            total = sums.pop(j)
+            send = first_z if j == n_z - 1 else total.astype(bf16)
+            sums[j ^ bit] = sums[j ^ bit] + swap_z(send, bit).astype(f32)
     basis_here = lax.dynamic_slice_in_dim(factor_basis, v * width, width, 1)
     hidden_grad = (sums[0] + dot_first(mix_total, basis_here)).astype(bf16)
 
-    basis_part, rows_part, _ = lax.optimization_barrier(
-        (basis_part, rows_part, from_x[min(1, n_z - 1)])
-    )
-    basis_two = basis_part + swap_x(basis_part.astype(bf16)).astype(f32)
-    basis_grad = basis_two + swap_core(basis_two)
-    rows_two = rows_part + swap_x(rows_part)
-    rows_grad = rows_two + swap_core(rows_two)
+    basis_two = lax.reduce_precision(basis_part + swap_core(basis_part), 8, 7)
+    rows_two = rows_part + swap_core(rows_part)
+    basis_two, rows_two, _ = lax.optimization_barrier(
+        (basis_two, rows_two, from_x[min(1, n_z - 1)])
+    )
+    basis_grad = basis_two + swap_x(basis_two.astype(bf16)).astype(f32)
+    rows_grad = rows_two + swap_x(rows_two)
     return hidden_grad, rows_grad, basis_grad
 
 

time: 110 us -> 123 us (1.12)
  starting transfers between devices: 30.6 us -> 38.6 us
  waiting for transfers between devices: 54.1 us -> 49.6 us
  other arithmetic: 2.22 us -> 6.38 us
  local copies, waits for them, and re-layouts: 8.08 us -> 11.2 us
  Pallas kernels: 8.62 us -> 10.3 us
    ppermute x31 -> x34, starting transfers between devices: 30.6 us -> 38.6 us  [swap(): return lax.ppermute(value, axis, [(i, i ^ bit) for i in range(size)])]
    ppermute x31 -> x34, waiting for transfers between devices: 54.1 us -> 49.6 us  [swap(): return lax.ppermute(value, axis, [(i, i ^ bit) for i in range(size)])]
    add x4, other arithmetic: 0.02 us -> 2.26 us  [on_few(): new_iota + (v ^ j) * new_here]
    unnamed x25 -> x41, local copies, waits for them, and re-layouts: 7.94 us -> 9.86 us
    pallas_call x2 -> x3, Pallas kernels: 1.81 us -> 3.39 us  [copy_blocks(): pl.pallas_call(kernel, out_shape=[jax.ShapeDtypeStruct(shape, bf16) for s...]
    concatenate x1, local copies, waits for them, and re-layouts: 0.1 us -> 1.36 us  [on_few(): jnp.concatenate([new_iota + (v ^ j) * new_here for j in row_blocks], axis=0)]
    pallas_call x2 -> x3, Pallas kernels: 6.82 us -> 6.9 us  [logits_of(): pl.pallas_call(kernel, out_shape=jax.ShapeDtypeStruct((total, toks), f32)...]
  transfers between devices with their start and end apart: 31 -> 34, of which waited for: 20 -> 17; matrix products, arithmetic and copies ran while one was open for 5% -> 9% of each run, Pallas kernels for 8% -> 8%
where the time goes in v6:
time: 123 us
  waiting for transfers between devices  49.6 us (40%)
  starting transfers between devices  38.6 us (31%)
  local copies, waits for them, and re-layouts  11.2 us (9%)
  Pallas kernels  10.3 us (8%)
  other arithmetic  6.38 us (5%)
  matrix products  5.31 us (4%)
    ppermute x34, waiting for transfers between devices, swap(): return lax.ppermute(value, axis, [(i, i ^ bit) for i in range(size)])  49.6 us
    ppermute x34, starting transfers between devices, swap(): return lax.ppermute(value, axis, [(i, i ^ bit) for i in range(size)])  38.6 us
    unnamed x41, local copies, waits for them, and re-layouts  9.86 us
    pallas_call x3, Pallas kernels, logits_of(): pl.pallas_call(kernel, out_shape=jax.ShapeDtypeStruct((total, toks), f32)...  6.9 us
    dot_general x10, matrix products, dot_first(): return lax.dot_general(a, b, contract_first, preferred_element_type=f32)  4.77 us
    pallas_call x3, Pallas kernels, copy_blocks(): pl.pallas_call(kernel, out_shape=[jax.ShapeDtypeStruct(shape, bf16) for s...  3.39 us
  transfers between devices with their start and end apart: 34, of which 17 were waited for; matrix products, arithmetic and copies ran while one was open for 9% of the time, Pallas kernels for 8%

profile of v6, /device:TPU:0, one launch (start us, length us, event | category | flops | bytes accessed | tf_op | source)
XLA Modules:
  0.0 122.5 jit_solution(10104880371650598850)
XLA Ops:
  0.6 3.0 %collective-permute-start = (bf16[128,1024]{1,0:T(8,128)(2,1)}, bf16[128,1024]{1,0:T(8,128)(2,1)S(1)}, u32[]{:S(2)}, u32[]{:S(2)}) collective-permute-start(bf16[128,1024]{1,0:T(8,128)(2,1)} %refs_6_.1), channel_id=1, source_target_pairs={{0,2},{1,3},{2,0},{3,1},{4,6},{5,7},{6,4},{7,5},{8,10},{9,11},{10,... | collective-permute-start | bytes 786440 | tf_op jit(solution)/shard_map/ppermute | solution.py:25
  3.6 6.5 %collective-permute-done.refs_9_ = bf16[128,1024]{1,0:T(8,128)(2,1)S(1)} collective-permute-done((bf16[128,1024]{1,0:T(8,128)(2,1)}, bf16[128,1024]{1,0:T(8,128)(2,1)S(1)}, u32[]{:S(2)}, u32[]{:S(2)}) %collective-permute-start) | collective-permute-done | bytes 262176 | tf_op jit(solution)/shard_map/ppermute | solution.py:25
  10.9 1.6 %copy-done = bf16[128,8192]{1,0:T(8,128)(2,1)S(1)} copy-done((bf16[128,8192]{1,0:T(8,128)(2,1)S(1)}, bf16[128,8192]{1,0:T(8,128)(2,1)}, u32[]{:S(2)}) %copy-start) | copy-done | bytes 2097176
  14.3 2.9 %collective-permute-start.3 = (bf16[128,1024]{1,0:T(8,128)(2,1)}, bf16[128,1024]{1,0:T(8,128)(2,1)}, u32[]{:S(2)}, u32[]{:S(2)}) collective-permute-start(bf16[128,1024]{1,0:T(8,128)(2,1)} %refs_6_.1), channel_id=1, source_target_pairs={{0,16},{4,20},{8,24},{12,28},{16,0},{20,4},{24,8},{28,12},{1,17},{... | collective-permute-start | bytes 786440 | tf_op jit(solution)/shard_map/ppermute | solution.py:25
  17.2 1.6 %collective-permute-start.2 = (bf16[128,1024]{1,0:T(8,128)(2,1)}, bf16[128,1024]{1,0:T(8,128)(2,1)S(1)}, u32[]{:S(2)}, u32[]{:S(2)}) collective-permute-start(bf16[128,1024]{1,0:T(8,128)(2,1)} %refs_6_.1), channel_id=1, source_target_pairs={{0,8},{4,12},{8,0},{12,4},{16,24},{20,28},{24,16},{28,20},{1,9},{5... | collective-permute-start | bytes 786440 | tf_op jit(solution)/shard_map/ppermute | solution.py:25
  20.0 1.6 %collective-permute-start.6 = (bf16[128,1024]{1,0:T(8,128)(2,1)}, bf16[128,1024]{1,0:T(8,128)(2,1)S(1)}, u32[]{:S(2)}, u32[]{:S(2)}) collective-permute-start(bf16[128,1024]{1,0:T(8,128)(2,1)} %get-tuple-element.32), channel_id=1, source_target_pairs={{0,4},{4,0},{8,12},{12,8},{16,20},{20,16},{24,28},{28,24},{1,5},{5... | collective-permute-start | bytes 786440 | tf_op jit(solution)/shard_map/ppermute | solution.py:25
  22.8 7.4 %collective-permute-done.2.refs_4_.refs_7_ = bf16[128,1024]{1,0:T(8,128)(2,1)S(1)} collective-permute-done((bf16[128,1024]{1,0:T(8,128)(2,1)}, bf16[128,1024]{1,0:T(8,128)(2,1)S(1)}, u32[]{:S(2)}, u32[]{:S(2)}) %collective-permute-start.2) | collective-permute-done | bytes 262176 | tf_op jit(solution)/shard_map/ppermute | solution.py:25
  30.2 1.6 %collective-permute-start.8 = (bf16[128,1024]{1,0:T(8,128)(2,1)S(1)}, bf16[128,1024]{1,0:T(8,128)(2,1)S(1)}, u32[]{:S(2)}, u32[]{:S(2)}) collective-permute-start(bf16[128,1024]{1,0:T(8,128)(2,1)S(1)} %collective-permute-done.2.refs_4_.refs_7_), channel_id=1, source_target_pairs={{0,2},{1,3},{2,0},{3,1},{4,6},{5,7},{6,4},{7,5},{8,10},{9,11},{10,... | collective-permute-start | bytes 786440 | tf_op jit(solution)/shard_map/ppermute | solution.py:25
  35.0 4.6 %collective-permute-done.5.refs_0_.refs_3_.refs_2_ = bf16[128,2048]{1,0:T(8,128)(2,1)S(1)} collective-permute-done((bf16[128,2048]{1,0:T(8,128)(2,1)}, bf16[128,2048]{1,0:T(8,128)(2,1)S(1)}, u32[]{:S(2)}, u32[]{:S(2)}) %collective-permute-start.5) | collective-permute-done | bytes 524320 | tf_op jit(solution)/shard_map/ppermute | solution.py:25
  43.0 1.6 %collective-permute-start.14 = (bf16[128,1024]{1,0:T(8,128)(2,1)}, bf16[128,1024]{1,0:T(8,128)(2,1)}, u32[]{:S(2)}, u32[]{:S(2)}) collective-permute-start(bf16[128,1024]{1,0:T(8,128)(2,1)} %collective-permute-done.3.refs_5_.refs_8_), channel_id=1, source_target_pairs={{0,2},{1,3},{2,0},{3,1},{4,6},{5,7},{6,4},{7,5},{8,10},{9,11},{10,... | collective-permute-start | bytes 786440 | tf_op jit(solution)/shard_map/ppermute | solution.py:25
  45.1 2.1 %collective-permute-done.7.refs_2_.refs_5_.refs_4_ = bf16[128,1024]{1,0:T(8,128)(2,1)} collective-permute-done((bf16[128,1024]{1,0:T(8,128)(2,1)}, bf16[128,1024]{1,0:T(8,128)(2,1)}, u32[]{:S(2)}, u32[]{:S(2)}) %collective-permute-start.7) | collective-permute-done | bytes 262176 | tf_op jit(solution)/shard_map/ppermute | solution.py:25
  53.3 2.1 %shard_map.86 = f32[320,128]{1,0:T(8,128)S(1)} custom-call(bf16[128,4096]{1,0:T(8,128)(2,1)S(1)} %get-tuple-element.43.refs_0_, bf16[128,4096]{1,0:T(8,128)(2,1)S(1)} %collective-permute-done.1.refs_1_, bf16[64,4096]{1,0:T(8,128)(2,1)S(1)} %copy-done.4, bf16[128,1024]{1,0:T(8,128)(2,1)S(1)} %copy-done.1, bf16[128,1024]{1,0:T(8,128)(2,1)S(1)} %copy-done.7, ...), custom_call_target="tpu_custom_call" | custom-call | flops 335544320 | bytes 3833856 | tf_op jit(solution)/shard_map/pallas_call | solution.py:95
  55.4 1.6 %collective-permute-start.20 = (bf16[64,64]{1,0:T(8,128)(2,1)S(1)}, bf16[64,64]{1,0:T(8,128)(2,1)S(1)}, u32[]{:S(2)}, u32[]{:S(2)}) collective-permute-start(bf16[64,64]{1,0:T(8,128)(2,1)S(1)} %copy-done.14), channel_id=1, source_target_pairs={{0,4},{4,0},{8,12},{12,8},{16,20},{20,16},{24,28},{28,24},{1,5},{5... | collective-permute-start | bytes 24584 | tf_op jit(solution)/shard_map/ppermute | solution.py:25
  59.6 2.8 %shard_map.89 = f32[576,128]{1,0:T(8,128)S(1)} custom-call(bf16[128,4096]{1,0:T(8,128)(2,1)S(1)} %get-tuple-element.43.refs_0_, bf16[128,4096]{1,0:T(8,128)(2,1)S(1)} %collective-permute-done.1.refs_1_, bf16[64,4096]{1,0:T(8,128)(2,1)S(1)} %copy-done.4, bf16[128,2048]{1,0:T(8,128)(2,1)S(1)} %collective-permute-done.5.refs_0_.refs_3_.refs_2_, ...), custom_call_target="tpu_custom_call" | custom-call | flops 603979776 | bytes 6062080 | tf_op jit(solution)/shard_map/pallas_call | solution.py:95
  64.3 2.0 %shard_map.88 = f32[256,128]{1,0:T(8,128)S(1)} custom-call(bf16[128,2048]{1,0:T(8,128)(2,1)S(1)} %collective-permute-done.5.refs_0_.refs_3_.refs_2_, bf16[128,1024]{1,0:T(8,128)(2,1)S(1)} %collective-permute-done.6.refs_1_.refs_4_.refs_3_, bf16[128,1024]{1,0:T(8,128)(2,1)} %collective-permute-done.7.refs_2_.refs_5_.refs_4_, ...), custom_call_target="tpu_custom_call" | custom-call | flops 268435456 | bytes 3276800 | tf_op jit(solution)/shard_map/pallas_call | solution.py:95
  67.1 1.7 %shard_map.90 = bf16[512,4096]{1,0:T(8,128)(2,1)S(1)} custom-call(bf16[128,4096]{1,0:T(8,128)(2,1)S(1)} %get-tuple-element.43.refs_0_, bf16[128,4096]{1,0:T(8,128)(2,1)S(1)} %collective-permute-done.1.refs_1_, bf16[128,2048]{1,0:T(8,128)(2,1)S(1)} %collective-permute-done.5.refs_0_.refs_3_.refs_2_, ...), custom_call_target="tpu_custom_call" | custom-call | bytes 8388608 | tf_op jit(solution)/shard_map/pallas_call | solution.py:63
  69.4 4.0 %collective-permute-done.22 = bf16[256,64]{1,0:T(8,128)(2,1)S(1)} collective-permute-done((bf16[256,64]{1,0:T(8,128)(2,1)S(1)}, bf16[256,64]{1,0:T(8,128)(2,1)S(1)}, u32[]{:S(2)}, u32[]{:S(2)}) %collective-permute-start.22) | collective-permute-done | bytes 32800 | tf_op jit(solution)/shard_map/ppermute | solution.py:25
  74.4 1.6 %collective-permute-start.17 = (f32[4,256]{1,0:T(4,128)S(1)}, f32[4,256]{1,0:T(4,128)S(1)}, u32[]{:S(2)}, u32[]{:S(2)}) collective-permute-start(f32[4,256]{1,0:T(4,128)S(1)} %maximum_maximum_fusion), channel_id=1, source_target_pairs={{0,2},{1,3},{2,0},{3,1},{4,6},{5,7},{6,4},{7,5},{8,10},{9,11},{10,... | collective-permute-start | bytes 12296 | tf_op jit(solution)/shard_map/ppermute | solution.py:25
  76.3 1.7 %collective-permute-done.17 = f32[4,256]{1,0:T(4,128)S(1)} collective-permute-done((f32[4,256]{1,0:T(4,128)S(1)}, f32[4,256]{1,0:T(4,128)S(1)}, u32[]{:S(2)}, u32[]{:S(2)}) %collective-permute-start.17) | collective-permute-done | bytes 4128 | tf_op jit(solution)/shard_map/ppermute | solution.py:25
  78.6 3.1 %collective-permute-done.18 = f32[2,256]{1,0:T(2,128)S(1)} collective-permute-done((f32[2,256]{1,0:T(2,128)S(1)}, f32[2,256]{1,0:T(2,128)S(1)}, u32[]{:S(2)}, u32[]{:S(2)}) %collective-permute-start.18) | collective-permute-done | bytes 2080 | tf_op jit(solution)/shard_map/ppermute | solution.py:25
  81.8 1.8 %collective-permute-start.19 = (f32[2,256]{1,0:T(2,128)S(1)}, f32[2,256]{1,0:T(2,128)S(1)}, u32[]{:S(2)}, u32[]{:S(2)}) collective-permute-start(f32[2,256]{1,0:T(2,128)S(1)} %pad_maximum_fusion.5), channel_id=1, source_target_pairs={{0,16},{4,20},{8,24},{12,28},{16,0},{20,4},{24,8},{28,12},{1,17},{... | collective-permute-start | bytes 6152 | tf_op jit(solution)/shard_map/ppermute | solution.py:25
  83.7 2.7 %collective-permute-done.19 = f32[2,256]{1,0:T(2,128)S(1)} collective-permute-done((f32[2,256]{1,0:T(2,128)S(1)}, f32[2,256]{1,0:T(2,128)S(1)}, u32[]{:S(2)}, u32[]{:S(2)}) %collective-permute-start.19) | collective-permute-done | bytes 2080 | tf_op jit(solution)/shard_map/ppermute | solution.py:25
  87.8 1.6 %collective-permute-start.24 = (bf16[128,1024]{1,0:T(8,128)(2,1)S(1)}, bf16[128,1024]{1,0:T(8,128)(2,1)S(1)}, u32[]{:S(2)}, u32[]{:S(2)}) collective-permute-start(bf16[128,1024]{1,0:T(8,128)(2,1)S(1)} %convolution_convert_fusion.1), channel_id=1, source_target_pairs={{0,2},{1,3},{2,0},{3,1},{4,6},{5,7},{6,4},{7,5},{8,10},{9,11},{10,... | collective-permute-start | bytes 786440 | tf_op jit(solution)/shard_map/ppermute | solution.py:25
  90.7 5.0 %collective-permute-done.24 = bf16[128,1024]{1,0:T(8,128)(2,1)S(1)} collective-permute-done((bf16[128,1024]{1,0:T(8,128)(2,1)S(1)}, bf16[128,1024]{1,0:T(8,128)(2,1)S(1)}, u32[]{:S(2)}, u32[]{:S(2)}) %collective-permute-start.24) | collective-permute-done | bytes 262176 | tf_op jit(solution)/shard_map/ppermute | solution.py:25
  96.1 2.5 %collective-permute-start.26 = (bf16[128,1024]{1,0:T(8,128)(2,1)S(1)}, bf16[128,1024]{1,0:T(8,128)(2,1)S(1)}, u32[]{:S(2)}, u32[]{:S(2)}) collective-permute-start(bf16[128,1024]{1,0:T(8,128)(2,1)S(1)} %convolution_convert_fusion), channel_id=1, source_target_pairs={{0,2},{1,3},{2,0},{3,1},{4,6},{5,7},{6,4},{7,5},{8,10},{9,11},{10,... | collective-permute-start | bytes 786440 | tf_op jit(solution)/shard_map/ppermute | solution.py:25
  99.5 1.9 %collective-permute-done.23 = bf16[128,1024]{1,0:T(8,128)(2,1)S(1)} collective-permute-done((bf16[128,1024]{1,0:T(8,128)(2,1)S(1)}, bf16[128,1024]{1,0:T(8,128)(2,1)S(1)}, u32[]{:S(2)}, u32[]{:S(2)}) %collective-permute-start.23) | collective-permute-done | bytes 262176 | tf_op jit(solution)/shard_map/ppermute | solution.py:25
  101.4 2.5 %collective-permute-start.25 = (bf16[128,1024]{1,0:T(8,128)(2,1)S(1)}, bf16[128,1024]{1,0:T(8,128)(2,1)S(1)}, u32[]{:S(2)}, u32[]{:S(2)}) collective-permute-start(bf16[128,1024]{1,0:T(8,128)(2,1)S(1)} %convolution_convert_fusion.3), channel_id=1, source_target_pairs={{0,2},{1,3},{2,0},{3,1},{4,6},{5,7},{6,4},{7,5},{8,10},{9,11},{10,... | collective-permute-start | bytes 786440 | tf_op jit(solution)/shard_map/ppermute | solution.py:25
  103.9 3.1 %collective-permute-done.26 = bf16[128,1024]{1,0:T(8,128)(2,1)S(1)} collective-permute-done((bf16[128,1024]{1,0:T(8,128)(2,1)S(1)}, bf16[128,1024]{1,0:T(8,128)(2,1)S(1)}, u32[]{:S(2)}, u32[]{:S(2)}) %collective-permute-start.26) | collective-permute-done | bytes 262176 | tf_op jit(solution)/shard_map/ppermute | solution.py:25
  107.0 2.5 %collective-permute-start.32 = (f32[64,64]{1,0:T(8,128)S(1)}, f32[64,64]{1,0:T(8,128)S(1)}, u32[]{:S(2)}, u32[]{:S(2)}) collective-permute-start(f32[64,64]{1,0:T(8,128)S(1)} %add.406), channel_id=1, source_target_pairs={{0,2},{1,3},{2,0},{3,1},{4,6},{5,7},{6,4},{7,5},{8,10},{9,11},{10,... | collective-permute-start | bytes 49160 | tf_op jit(solution)/shard_map/ppermute | solution.py:25
  110.8 1.8 %collective-permute-start.29 = (bf16[128,1024]{1,0:T(8,128)(2,1)S(1)}, bf16[128,1024]{1,0:T(8,128)(2,1)S(1)}, u32[]{:S(2)}, u32[]{:S(2)}) collective-permute-start(bf16[128,1024]{1,0:T(8,128)(2,1)S(1)} %fusion.5), channel_id=1, source_target_pairs={{0,16},{4,20},{8,24},{12,28},{16,0},{20,4},{24,8},{28,12},{1,17},{... | collective-permute-start | bytes 786440 | tf_op jit(solution)/shard_map/ppermute | solution.py:25
  115.3 4.3 %collective-permute-done.27 = bf16[128,1024]{1,0:T(8,128)(2,1)S(1)} collective-permute-done((bf16[128,1024]{1,0:T(8,128)(2,1)S(1)}, bf16[128,1024]{1,0:T(8,128)(2,1)S(1)}, u32[]{:S(2)}, u32[]{:S(2)}) %collective-permute-start.27) | collective-permute-done | bytes 262176 | tf_op jit(solution)/shard_map/ppermute | solution.py:25
  119.7 1.8 %collective-permute-done.29 = bf16[128,1024]{1,0:T(8,128)(2,1)S(1)} collective-permute-done((bf16[128,1024]{1,0:T(8,128)(2,1)S(1)}, bf16[128,1024]{1,0:T(8,128)(2,1)S(1)}, u32[]{:S(2)}, u32[]{:S(2)}) %collective-permute-start.29) | collective-permute-done | bytes 262176 | tf_op jit(solution)/shard_map/ppermute | solution.py:25
  (143 shorter events, 35.0 us)
Async XLA Ops:
  0.6 9.5 %collective-permute-start = (bf16[128,1024]{1,0:T(8,128)(2,1)}, bf16[128,1024]{1,0:T(8,128)(2,1)S(1)}, u32[]{:S(2)}, u32[]{:S(2)}) collective-permute-start(bf16[128,1024]{1,0:T(8,128)(2,1)} %refs_6_.1), channel_id=1, source_target_pairs={{0,2},{1,3},{2,0},{3,1},{4,6},{5,7},{6,4},{7,5},{8,10},{9,11},{10,... | collective-permute-start | bytes 786440 | tf_op jit(solution)/shard_map/ppermute | solution.py:25
  14.2 33.1 %collective-permute-start.1 = (bf16[128,4096]{1,0:T(8,128)(2,1)S(1)}, bf16[128,4096]{1,0:T(8,128)(2,1)S(1)}, u32[]{:S(2)}, u32[]{:S(2)}) collective-permute-start(bf16[128,4096]{1,0:T(8,128)(2,1)S(1)} %get-tuple-element.43.refs_0_), channel_id=1, source_target_pairs={{0,1},{1,0},{2,3},{3,2},{4,5},{5,4},{6,7},{7,6},{8,9},{9,8},{10,11... | collective-permute-start | bytes 3145736 | tf_op jit(solution)/shard_map/ppermute | solution.py:25
  14.3 19.3 %collective-permute-start.3 = (bf16[128,1024]{1,0:T(8,128)(2,1)}, bf16[128,1024]{1,0:T(8,128)(2,1)}, u32[]{:S(2)}, u32[]{:S(2)}) collective-permute-start(bf16[128,1024]{1,0:T(8,128)(2,1)} %refs_6_.1), channel_id=1, source_target_pairs={{0,16},{4,20},{8,24},{12,28},{16,0},{20,4},{24,8},{28,12},{1,17},{... | collective-permute-start | bytes 786440 | tf_op jit(solution)/shard_map/ppermute | solution.py:25
  17.2 13.0 %collective-permute-start.2 = (bf16[128,1024]{1,0:T(8,128)(2,1)}, bf16[128,1024]{1,0:T(8,128)(2,1)S(1)}, u32[]{:S(2)}, u32[]{:S(2)}) collective-permute-start(bf16[128,1024]{1,0:T(8,128)(2,1)} %refs_6_.1), channel_id=1, source_target_pairs={{0,8},{4,12},{8,0},{12,4},{16,24},{20,28},{24,16},{28,20},{1,9},{5... | collective-permute-start | bytes 786440 | tf_op jit(solution)/shard_map/ppermute | solution.py:25
  20.0 24.6 %collective-permute-start.6 = (bf16[128,1024]{1,0:T(8,128)(2,1)}, bf16[128,1024]{1,0:T(8,128)(2,1)S(1)}, u32[]{:S(2)}, u32[]{:S(2)}) collective-permute-start(bf16[128,1024]{1,0:T(8,128)(2,1)} %get-tuple-element.32), channel_id=1, source_target_pairs={{0,4},{4,0},{8,12},{12,8},{16,20},{20,16},{24,28},{28,24},{1,5},{5... | collective-permute-start | bytes 786440 | tf_op jit(solution)/shard_map/ppermute | solution.py:25
  21.6 18.0 %collective-permute-start.5 = (bf16[128,2048]{1,0:T(8,128)(2,1)}, bf16[128,2048]{1,0:T(8,128)(2,1)S(1)}, u32[]{:S(2)}, u32[]{:S(2)}) collective-permute-start(bf16[128,2048]{1,0:T(8,128)(2,1)} %get-tuple-element.31), channel_id=1, source_target_pairs={{0,4},{4,0},{8,12},{12,8},{16,20},{20,16},{24,28},{28,24},{1,5},{5... | collective-permute-start | bytes 1572872 | tf_op jit(solution)/shard_map/ppermute | solution.py:25
  30.2 11.5 %collective-permute-start.8 = (bf16[128,1024]{1,0:T(8,128)(2,1)S(1)}, bf16[128,1024]{1,0:T(8,128)(2,1)S(1)}, u32[]{:S(2)}, u32[]{:S(2)}) collective-permute-start(bf16[128,1024]{1,0:T(8,128)(2,1)S(1)} %collective-permute-done.2.refs_4_.refs_7_), channel_id=1, source_target_pairs={{0,2},{1,3},{2,0},{3,1},{4,6},{5,7},{6,4},{7,5},{8,10},{9,11},{10,... | collective-permute-start | bytes 786440 | tf_op jit(solution)/shard_map/ppermute | solution.py:25
  33.6 9.4 %collective-permute-start.4 = (bf16[128,1024]{1,0:T(8,128)(2,1)}, bf16[128,1024]{1,0:T(8,128)(2,1)}, u32[]{:S(2)}, u32[]{:S(2)}) collective-permute-start(bf16[128,1024]{1,0:T(8,128)(2,1)} %collective-permute-done.3.refs_5_.refs_8_), channel_id=1, source_target_pairs={{0,8},{4,12},{8,0},{12,4},{16,24},{20,28},{24,16},{28,20},{1,9},{5... | collective-permute-start | bytes 786440 | tf_op jit(solution)/shard_map/ppermute | solution.py:25
  39.6 7.7 %collective-permute-start.7 = (bf16[128,1024]{1,0:T(8,128)(2,1)}, bf16[128,1024]{1,0:T(8,128)(2,1)}, u32[]{:S(2)}, u32[]{:S(2)}) collective-permute-start(bf16[128,1024]{1,0:T(8,128)(2,1)} %copy-done.13), channel_id=1, source_target_pairs={{0,4},{4,0},{8,12},{12,8},{16,20},{20,16},{24,28},{28,24},{1,5},{5... | collective-permute-start | bytes 786440 | tf_op jit(solution)/shard_map/ppermute | solution.py:25
  42.4 15.3 %collective-permute-start.9 = (bf16[128,2048]{1,0:T(8,128)(2,1)S(1)}, bf16[128,2048]{1,0:T(8,128)(2,1)S(1)}, u32[]{:S(2)}, u32[]{:S(2)}) collective-permute-start(bf16[128,2048]{1,0:T(8,128)(2,1)S(1)} %collective-permute-done.5.refs_0_.refs_3_.refs_2_), channel_id=1, source_target_pairs={{0,1},{1,0},{2,3},{3,2},{4,5},{5,4},{6,7},{7,6},{8,9},{9,8},{10,11... | collective-permute-start | bytes 1572872 | tf_op jit(solution)/shard_map/ppermute | solution.py:25
  43.0 14.0 %collective-permute-start.14 = (bf16[128,1024]{1,0:T(8,128)(2,1)}, bf16[128,1024]{1,0:T(8,128)(2,1)}, u32[]{:S(2)}, u32[]{:S(2)}) collective-permute-start(bf16[128,1024]{1,0:T(8,128)(2,1)} %collective-permute-done.3.refs_5_.refs_8_), channel_id=1, source_target_pairs={{0,2},{1,3},{2,0},{3,1},{4,6},{5,7},{6,4},{7,5},{8,10},{9,11},{10,... | collective-permute-start | bytes 786440 | tf_op jit(solution)/shard_map/ppermute | solution.py:25
  44.6 13.2 %collective-permute-start.15 = (bf16[128,1024]{1,0:T(8,128)(2,1)}, bf16[128,1024]{1,0:T(8,128)(2,1)}, u32[]{:S(2)}, u32[]{:S(2)}) collective-permute-start(bf16[128,1024]{1,0:T(8,128)(2,1)} %collective-permute-done.4.refs_6_.refs_9_), channel_id=1, source_target_pairs={{0,2},{1,3},{2,0},{3,1},{4,6},{5,7},{6,4},{7,5},{8,10},{9,11},{10,... | collective-permute-start | bytes 786440 | tf_op jit(solution)/shard_map/ppermute | solution.py:25
  47.3 10.5 %collective-permute-start.10 = (bf16[128,1024]{1,0:T(8,128)(2,1)S(1)}, bf16[128,1024]{1,0:T(8,128)(2,1)}, u32[]{:S(2)}, u32[]{:S(2)}) collective-permute-start(bf16[128,1024]{1,0:T(8,128)(2,1)S(1)} %collective-permute-done.6.refs_1_.refs_4_.refs_3_), channel_id=1, source_target_pairs={{0,1},{1,0},{2,3},{3,2},{4,5},{5,4},{6,7},{7,6},{8,9},{9,8},{10,11... | collective-permute-start | bytes 786440 | tf_op jit(solution)/shard_map/ppermute | solution.py:25
  47.3 8.1 %collective-permute-start.11 = (bf16[128,1024]{1,0:T(8,128)(2,1)}, bf16[128,1024]{1,0:T(8,128)(2,1)}, u32[]{:S(2)}, u32[]{:S(2)}) collective-permute-start(bf16[128,1024]{1,0:T(8,128)(2,1)} %collective-permute-done.7.refs_2_.refs_5_.refs_4_), channel_id=1, source_target_pairs={{0,1},{1,0},{2,3},{3,2},{4,5},{5,4},{6,7},{7,6},{8,9},{9,8},{10,11... | collective-permute-start | bytes 786440 | tf_op jit(solution)/shard_map/ppermute | solution.py:25
  55.4 8.4 %collective-permute-start.20 = (bf16[64,64]{1,0:T(8,128)(2,1)S(1)}, bf16[64,64]{1,0:T(8,128)(2,1)S(1)}, u32[]{:S(2)}, u32[]{:S(2)}) collective-permute-start(bf16[64,64]{1,0:T(8,128)(2,1)S(1)} %copy-done.14), channel_id=1, source_target_pairs={{0,4},{4,0},{8,12},{12,8},{16,20},{20,16},{24,28},{28,24},{1,5},{5... | collective-permute-start | bytes 24584 | tf_op jit(solution)/shard_map/ppermute | solution.py:25
  57.0 17.1 %collective-permute-start.13 = (f32[320,128]{1,0:T(8,128)S(1)}, f32[320,128]{1,0:T(8,128)S(1)}, u32[]{:S(2)}, u32[]{:S(2)}) collective-permute-start(f32[320,128]{1,0:T(8,128)S(1)} %shard_map.86), channel_id=1, source_target_pairs={{0,4},{4,0},{8,12},{12,8},{16,20},{20,16},{24,28},{28,24},{1,5},{5... | collective-permute-start | bytes 491528 | tf_op jit(solution)/shard_map/ppermute | solution.py:25
  62.5 11.7 %collective-permute-start.16 = (f32[576,128]{1,0:T(8,128)S(1)}, f32[576,128]{1,0:T(8,128)S(1)}, u32[]{:S(2)}, u32[]{:S(2)}) collective-permute-start(f32[576,128]{1,0:T(8,128)S(1)} %shard_map.89), channel_id=1, source_target_pairs={{0,4},{4,0},{8,12},{12,8},{16,20},{20,16},{24,28},{28,24},{1,5},{5... | collective-permute-start | bytes 884744 | tf_op jit(solution)/shard_map/ppermute | solution.py:25
  63.9 5.1 %collective-permute-start.21 = (bf16[128,64]{1,0:T(8,128)(2,1)S(1)}, bf16[128,64]{1,0:T(8,128)(2,1)S(1)}, u32[]{:S(2)}, u32[]{:S(2)}) collective-permute-start(bf16[128,64]{1,0:T(8,128)(2,1)S(1)} %pad_maximum_fusion.3), channel_id=1, source_target_pairs={{0,16},{4,20},{8,24},{12,28},{16,0},{20,4},{24,8},{28,12},{1,17},{... | collective-permute-start | bytes 49160 | tf_op jit(solution)/shard_map/ppermute | solution.py:25
  66.3 7.7 %collective-permute-start.12 = (f32[256,128]{1,0:T(8,128)S(1)}, f32[256,128]{1,0:T(8,128)S(1)}, u32[]{:S(2)}, u32[]{:S(2)}) collective-permute-start(f32[256,128]{1,0:T(8,128)S(1)} %shard_map.88), channel_id=1, source_target_pairs={{0,4},{4,0},{8,12},{12,8},{16,20},{20,16},{24,28},{28,24},{1,5},{5... | collective-permute-start | bytes 393224 | tf_op jit(solution)/shard_map/ppermute | solution.py:25
  69.0 4.3 %collective-permute-start.22 = (bf16[256,64]{1,0:T(8,128)(2,1)S(1)}, bf16[256,64]{1,0:T(8,128)(2,1)S(1)}, u32[]{:S(2)}, u32[]{:S(2)}) collective-permute-start(bf16[256,64]{1,0:T(8,128)(2,1)S(1)} %pad_maximum_fusion.2), channel_id=1, source_target_pairs={{0,8},{4,12},{8,0},{12,4},{16,24},{20,28},{24,16},{28,20},{1,9},{5... | collective-permute-start | bytes 98312 | tf_op jit(solution)/shard_map/ppermute | solution.py:25
  81.8 4.5 %collective-permute-start.19 = (f32[2,256]{1,0:T(2,128)S(1)}, f32[2,256]{1,0:T(2,128)S(1)}, u32[]{:S(2)}, u32[]{:S(2)}) collective-permute-start(f32[2,256]{1,0:T(2,128)S(1)} %pad_maximum_fusion.5), channel_id=1, source_target_pairs={{0,16},{4,20},{8,24},{12,28},{16,0},{20,4},{24,8},{28,12},{1,17},{... | collective-permute-start | bytes 6152 | tf_op jit(solution)/shard_map/ppermute | solution.py:25
  87.8 7.9 %collective-permute-start.24 = (bf16[128,1024]{1,0:T(8,128)(2,1)S(1)}, bf16[128,1024]{1,0:T(8,128)(2,1)S(1)}, u32[]{:S(2)}, u32[]{:S(2)}) collective-permute-start(bf16[128,1024]{1,0:T(8,128)(2,1)S(1)} %convolution_convert_fusion.1), channel_id=1, source_target_pairs={{0,2},{1,3},{2,0},{3,1},{4,6},{5,7},{6,4},{7,5},{8,10},{9,11},{10,... | collective-permute-start | bytes 786440 | tf_op jit(solution)/shard_map/ppermute | solution.py:25
  89.4 9.6 %collective-permute-start.31 = (f32[64,64]{1,0:T(8,128)S(1)}, f32[64,64]{1,0:T(8,128)S(1)}, u32[]{:S(2)}, u32[]{:S(2)}) collective-permute-start(f32[64,64]{1,0:T(8,128)S(1)} %fusion.24), channel_id=1, source_target_pairs={{0,1},{1,0},{2,3},{3,2},{4,5},{5,4},{6,7},{7,6},{8,9},{9,8},{10,11... | collective-permute-start | bytes 49160 | tf_op jit(solution)/shard_map/ppermute | solution.py:25
  89.5 11.8 %collective-permute-start.23 = (bf16[128,1024]{1,0:T(8,128)(2,1)S(1)}, bf16[128,1024]{1,0:T(8,128)(2,1)S(1)}, u32[]{:S(2)}, u32[]{:S(2)}) collective-permute-start(bf16[128,1024]{1,0:T(8,128)(2,1)S(1)} %convolution_convert_fusion.2), channel_id=1, source_target_pairs={{0,2},{1,3},{2,0},{3,1},{4,6},{5,7},{6,4},{7,5},{8,10},{9,11},{10,... | collective-permute-start | bytes 786440 | tf_op jit(solution)/shard_map/ppermute | solution.py:25
  90.1 13.7 %collective-permute-start.30 = (f32[64,1024]{1,0:T(8,128)S(1)}, f32[64,1024]{1,0:T(8,128)S(1)}, u32[]{:S(2)}, u32[]{:S(2)}) collective-permute-start(f32[64,1024]{1,0:T(8,128)S(1)} %fusion.48), channel_id=1, source_target_pairs={{0,1},{1,0},{2,3},{3,2},{4,5},{5,4},{6,7},{7,6},{8,9},{9,8},{10,11... | collective-permute-start | bytes 786440 | tf_op jit(solution)/shard_map/ppermute | solution.py:25
  96.1 10.9 %collective-permute-start.26 = (bf16[128,1024]{1,0:T(8,128)(2,1)S(1)}, bf16[128,1024]{1,0:T(8,128)(2,1)S(1)}, u32[]{:S(2)}, u32[]{:S(2)}) collective-permute-start(bf16[128,1024]{1,0:T(8,128)(2,1)S(1)} %convolution_convert_fusion), channel_id=1, source_target_pairs={{0,2},{1,3},{2,0},{3,1},{4,6},{5,7},{6,4},{7,5},{8,10},{9,11},{10,... | collective-permute-start | bytes 786440 | tf_op jit(solution)/shard_map/ppermute | solution.py:25
  99.0 11.4 %collective-permute-start.28 = (bf16[128,1024]{1,0:T(8,128)(2,1)S(1)}, bf16[128,1024]{1,0:T(8,128)(2,1)S(1)}, u32[]{:S(2)}, u32[]{:S(2)}) collective-permute-start(bf16[128,1024]{1,0:T(8,128)(2,1)S(1)} %fusion.6), channel_id=1, source_target_pairs={{0,8},{4,12},{8,0},{12,4},{16,24},{20,28},{24,16},{28,20},{1,9},{5... | collective-permute-start | bytes 786440 | tf_op jit(solution)/shard_map/ppermute | solution.py:25
  101.4 14.0 %collective-permute-start.25 = (bf16[128,1024]{1,0:T(8,128)(2,1)S(1)}, bf16[128,1024]{1,0:T(8,128)(2,1)S(1)}, u32[]{:S(2)}, u32[]{:S(2)}) collective-permute-start(bf16[128,1024]{1,0:T(8,128)(2,1)S(1)} %convolution_convert_fusion.3), channel_id=1, source_target_pairs={{0,2},{1,3},{2,0},{3,1},{4,6},{5,7},{6,4},{7,5},{8,10},{9,11},{10,... | collective-permute-start | bytes 786440 | tf_op jit(solution)/shard_map/ppermute | solution.py:25
  107.0 6.8 %collective-permute-start.32 = (f32[64,64]{1,0:T(8,128)S(1)}, f32[64,64]{1,0:T(8,128)S(1)}, u32[]{:S(2)}, u32[]{:S(2)}) collective-permute-start(f32[64,64]{1,0:T(8,128)S(1)} %add.406), channel_id=1, source_target_pairs={{0,2},{1,3},{2,0},{3,1},{4,6},{5,7},{6,4},{7,5},{8,10},{9,11},{10,... | collective-permute-start | bytes 49160 | tf_op jit(solution)/shard_map/ppermute | solution.py:25
  109.5 5.1 %collective-permute-start.33 = (bf16[64,1024]{1,0:T(8,128)(2,1)S(1)}, bf16[64,1024]{1,0:T(8,128)(2,1)S(1)}, u32[]{:S(2)}, u32[]{:S(2)}) collective-permute-start(bf16[64,1024]{1,0:T(8,128)(2,1)S(1)} %convert_element_type.111), channel_id=1, source_target_pairs={{0,2},{1,3},{2,0},{3,1},{4,6},{5,7},{6,4},{7,5},{8,10},{9,11},{10,... | collective-permute-start | bytes 393224 | tf_op jit(solution)/shard_map/ppermute | solution.py:25
  109.9 9.8 %collective-permute-start.27 = (bf16[128,1024]{1,0:T(8,128)(2,1)S(1)}, bf16[128,1024]{1,0:T(8,128)(2,1)S(1)}, u32[]{:S(2)}, u32[]{:S(2)}) collective-permute-start(bf16[128,1024]{1,0:T(8,128)(2,1)S(1)} %fusion.7), channel_id=1, source_target_pairs={{0,8},{4,12},{8,0},{12,4},{16,24},{20,28},{24,16},{28,20},{1,9},{5... | collective-permute-start | bytes 786440 | tf_op jit(solution)/shard_map/ppermute | solution.py:25
  110.8 10.7 %collective-permute-start.29 = (bf16[128,1024]{1,0:T(8,128)(2,1)S(1)}, bf16[128,1024]{1,0:T(8,128)(2,1)S(1)}, u32[]{:S(2)}, u32[]{:S(2)}) collective-permute-start(bf16[128,1024]{1,0:T(8,128)(2,1)S(1)} %fusion.5), channel_id=1, source_target_pairs={{0,16},{4,20},{8,24},{12,28},{16,0},{20,4},{24,8},{28,12},{1,17},{... | collective-permute-start | bytes 786440 | tf_op jit(solution)/shard_map/ppermute | solution.py:25
  (21 other events, 154.2 us)

commit v7 on v6

--- a/solution.py
+++ b/solution.py
@@ -107,8 +107,8 @@
 
 
 def on_few(hidden, head, factor_rows, factor_basis, targets, loss_mask):
-    n_z = lax.axis_size("vocab") // 2
-    n_tok = lax.axis_size("tok")
+    n_vocab, n_tok = lax.axis_size("vocab"), lax.axis_size("tok")
+    n_z = n_vocab // 2
     bits = [1 << b for b in range(n_z.bit_length() - 1)]
     v = lax.axis_index("vocab")
     t = lax.axis_index("tok")
@@ -117,6 +117,14 @@
     new_here = factor_rows.shape[0]
     rank = factor_basis.shape[0]
     depth = n_z * width
+
+    near_first = v * (n_tok * rows) + (t >> 1) * (2 * rows)
+    far_first = (v ^ 1) * (n_tok * rows) + (t >> 1) * (2 * rows)
+    turn = (t & 1) * rows
+    new_first = v * new_here
+    hidden, head, near_first, far_first, turn, new_first = lax.optimization_barrier(
+        (hidden, head, near_first, far_first, turn, new_first)
+    )
 
     def start_of(j, other):
         return (lax.axis_index("vocab") ^ (2 * j + other)) * width
@@ -132,29 +140,9 @@
         ],
         head,
     )
-    beside = []
-    for n, send in enumerate(sends):
-        if n > 1:
-            send, _ = lax.optimization_barrier((send, beside[0]))
-        beside.append(swap_y(send))
-
-    shards = {0: hidden}
-    for bit in reversed(bits):
-        near = swap_z(hidden, bit)
-        for j in [j for j in shards if j]:
-            shards[j], _ = lax.optimization_barrier((shards[j], near))
-            shards[j ^ bit] = swap_z(shards[j], bit)
-        shards[bit] = near
-    cross = {}
-    for j in range(n_z):
-        sent = shards[j]
-        if j > 1:
-            sent, _ = lax.optimization_barrier((sent, cross[j - 2]))
-        cross[j] = swap_x(sent)
-
-    head_after, basis_after, _ = lax.optimization_barrier(
-        (head, factor_basis, cross[0])
-    )
+    beside = [swap_y(sends[0])]
+
+    head_after, basis_after, _ = lax.optimization_barrier((head, factor_basis, sends[0]))
     kept, basis_half = copy_blocks(
         [(rows, depth), (rank, depth)],
         lambda: [
@@ -163,15 +151,38 @@
         head_after,
         basis_after,
     )
+
+    hidden, _ = lax.optimization_barrier((hidden, kept))
+    shards, cross = {0: hidden}, {0: swap_x(hidden)}
+    for bit in reversed(bits):
+        near = swap_z(hidden, bit)
+        for j in [j for j in shards if j]:
+            shards[j], _, _ = lax.optimization_barrier((shards[j], near, cross[0]))
+            shards[j ^ bit] = swap_z(shards[j], bit)
+        shards[bit] = near
+    for n, send in list(enumerate(sends))[1:]:
+        send, _ = lax.optimization_barrier((send, shards[bits[0]] if n == 1 else beside[n - 2]))
+        beside.append(swap_y(send))
+    for j in range(1, n_z):
+        sent = shards[j]
+        if j > 1:
+            sent, _, _ = lax.optimization_barrier((sent, cross[j - 2], beside[j // 2 - 1]))
+        cross[j] = swap_x(sent)
+
     kept_core = swap_core(kept)
     beside_core = []
     for n, came in enumerate(beside):
-        after = shards[n_z - 1] if n else cross[min(1, n_z - 1)]
-        came, _ = lax.optimization_barrier((came, after))
+        if n < len(beside) - 1:
+            came, _ = lax.optimization_barrier((came, cross[max(0, n_z - 2)]))
         beside_core.append(swap_core(came))
 
+    rows_all, _ = lax.optimization_barrier((factor_rows, shards[n_z - 1]))
+    for bit in bits:
+        rows_all = jnp.concatenate([rows_all, swap_z(rows_all, bit)], axis=0)
+    basis_ready, _, _ = lax.optimization_barrier((basis_half, rows_all, cross[n_z - 1]))
+
     in_order = lambda parts: [parts[j] for j in range(n_z)]
-    upper = [[kept], [kept_core], [basis_half]]
+    upper = [[kept], [kept_core], [basis_ready]]
     upper_own = logits_of(upper, in_order(shards))
     beside_core[-1], _ = lax.optimization_barrier((beside_core[-1], upper_own))
     lower_own = logits_of([beside, beside_core], in_order(shards))
@@ -191,14 +202,8 @@
     )
     hidden_basis = jnp.concatenate([basis_own, basis_cross], axis=1)
 
-    near_rows, _ = lax.optimization_barrier((factor_rows, beside[-1]))
-    rows_came = swap_y(near_rows)
-    row_blocks = [0, 1]
-    rows_came, _ = lax.optimization_barrier((rows_came, upper_own))
-    rows_all = jnp.concatenate([factor_rows, rows_came], axis=0)
-    for bit in [2 * b for b in reversed(bits)]:
-        rows_all = jnp.concatenate([rows_all, swap(rows_all, "vocab", bit)], axis=0)
-        row_blocks = row_blocks + [j ^ bit for j in row_blocks]
+    rows_after, _ = lax.optimization_barrier((rows_all, upper_own))
+    rows_all = jnp.concatenate([rows_all, swap_y(rows_after)], axis=0)
 
     def merge(a, b):
         top = jnp.maximum(a[0], b[0])
@@ -230,18 +235,14 @@
     row_top, sum_exp = stats[0], stats[1]
     scale_row = weight_row / sum_exp
 
-    row_iota = lax.broadcasted_iota(jnp.int32, (rows, 1), 0)
-
-    def grad_of(frozen, vv, cols):
-        row_ids = jnp.concatenate(
-            [row_iota + (vv * n_tok + tt) * rows for tt in (t, t ^ 1)], axis=0
-        )
+    def grad_of(frozen, first, cols):
+        row_ids = (lax.broadcasted_iota(jnp.int32, frozen.shape, 0) ^ turn) + first
         hit = jnp.where(row_ids == target_row[None, cols], weight_row[None, cols], 0.0)
         return (jnp.exp(frozen - row_top[None, cols]) * scale_row[None, cols] - hit).astype(bf16)
 
     at_own, at_cross = slice(0, toks), slice(toks, 2 * toks)
-    grad_cross = (grad_of(near_cross, v, at_cross), grad_of(far_cross, v ^ 1, at_cross))
-    grad_own = (grad_of(near_own, v, at_own), grad_of(far_own, v ^ 1, at_own))
+    grad_cross = (grad_of(near_cross, near_first, at_cross), grad_of(far_cross, far_first, at_cross))
+    grad_own = (grad_of(near_own, near_first, at_own), grad_of(far_own, far_first, at_own))
 
     laid = [kept, kept_core] + beside + beside_core
     laid[0], _ = lax.optimization_barrier((kept, both_cross))
@@ -269,10 +270,12 @@
         sums[j] = part(grad_own, j) + from_x[j].astype(f32)
         if first_z is None:
             first_z = sums[j].astype(bf16)
-    fresh, _ = lax.optimization_barrier((fresh, first_send))
-    frozen_rows = rows * n_tok * lax.axis_size("vocab")
-    new_iota = lax.broadcasted_iota(jnp.int32, (new_here, 1), 0) + frozen_rows
-    fresh_ids = jnp.concatenate([new_iota + (v ^ j) * new_here for j in row_blocks], axis=0)
+    fresh, _ = lax.optimization_barrier((fresh, from_x[max(0, n_z - 2)]))
+    fresh_iota = lax.broadcasted_iota(jnp.int32, (n_vocab * new_here, toks), 0)
+    in_block = fresh_iota & (new_here - 1)
+    from_block = fresh_iota - in_block
+    from_block = ((from_block & (n_z * new_here - 1)) << 1) + (from_block & (n_z * new_here)) // n_z
+    fresh_ids = ((from_block + in_block) ^ new_first) + rows * n_tok * n_vocab
     fresh_hit = jnp.where(fresh_ids == targets[None, :], weight_row[None, :toks], 0.0)
     fresh_grad = (
         jnp.exp(fresh[:, :toks] - row_top[None, :toks]) * scale_row[None, :toks] - fresh_hit
@@ -281,13 +284,17 @@
     rows_part = dot_last(fresh_grad[:new_here], hidden_basis[:, :toks])
     basis_part = jnp.dot(mix_total, hidden, preferred_element_type=f32)
 
+    came_z = None
     for bit in bits:
         for j in [j for j in sorted(sums, reverse=True) if j & bit]:
             total = sums.pop(j)
             send = first_z if j == n_z - 1 else total.astype(bf16)
-            sums[j ^ bit] = sums[j ^ bit] + swap_z(send, bit).astype(f32)
-    basis_here = lax.dynamic_slice_in_dim(factor_basis, v * width, width, 1)
-    hidden_grad = (sums[0] + dot_first(mix_total, basis_here)).astype(bf16)
+            if bit == bits[0] and came_z is not None:
+                send, _ = lax.optimization_barrier((send, came_z))
+            came = swap_z(send, bit)
+            came_z = came if came_z is None else came_z
+            sums[j ^ bit] = sums[j ^ bit] + came.astype(f32)
+    hidden_grad = (sums[0] + dot_first(mix_total, basis_half[:, :width])).astype(bf16)
 
     basis_two = lax.reduce_precision(basis_part + swap_core(basis_part), 8, 7)
     rows_two = rows_part + swap_core(rows_part)
@@ -363,11 +370,12 @@
         P("tok"),
     )
     out_specs = (P("tok", "vocab"), P("vocab", None), P(None, "vocab"))
-    few = mesh.shape["vocab"] <= 16 and mesh.shape["tok"] == 4
+
+    def on_device(hidden, head, factor_rows, *rest):
+        even = [n & (n - 1) == 0 for n in (mesh.shape["vocab"], head.shape[0], factor_rows.shape[0])]
+        few = 2 <= mesh.shape["vocab"] <= 16 and mesh.shape["tok"] == 4 and all(even)
+        return (on_few if few else on_many)(hidden, head, factor_rows, *rest)
+
     return jax.shard_map(
-        on_few if few else on_many,
-        mesh=mesh,
-        in_specs=in_specs,
-        out_specs=out_specs,
-        check_vma=False,
-    )
+        on_device, mesh=mesh, in_specs=in_specs, out_specs=out_specs, check_vma=False
+    )

time: 123 us -> 109 us (0.89)
  waiting for transfers between devices: 49.6 us -> 58.3 us
  local copies, waits for them, and re-layouts: 11.2 us -> 2.89 us
  Pallas kernels: 10.3 us -> 4.71 us
  starting transfers between devices: 38.6 us -> 34.6 us
  other arithmetic: 6.38 us -> 2.77 us
    ppermute x34, waiting for transfers between devices: 49.6 us -> 58.3 us  [swap(): return lax.ppermute(value, axis, [(i, i ^ bit) for i in range(size)])]
    unnamed x41 -> x14, local copies, waits for them, and re-layouts: 9.86 us -> 2.84 us
    ppermute x34, starting transfers between devices: 38.6 us -> 34.6 us  [swap(): return lax.ppermute(value, axis, [(i, i ^ bit) for i in range(size)])]
    pallas_call x3, Pallas kernels: 6.9 us -> 3.3 us  [logits_of(): pl.pallas_call(kernel, out_shape=jax.ShapeDtypeStruct((total, toks), f32)...]
    add x6 -> x1, other arithmetic: 2.27 us -> 0.01 us  [grad_of(): row_ids = (lax.broadcasted_iota(jnp.int32, frozen.shape, 0) ^ turn) + first]
    pallas_call x3, Pallas kernels: 3.39 us -> 1.41 us  [copy_blocks(): pl.pallas_call(kernel, out_shape=[jax.ShapeDtypeStruct(shape, bf16) for s...]
    concatenate x2, local copies, waits for them, and re-layouts: 1.37 us -> 0.03 us  [the longest x1 0.01 us: on_few(): rows_all = jnp.concatenate([rows_all, swap_z(rows_all, bit)], axis=0)]
  transfers between devices with their start and end apart: 34 -> 34, of which waited for: 17 -> 22; matrix products, arithmetic and copies ran while one was open for 9% -> 5% of each run, Pallas kernels for 8% -> 3%
where the time goes in v7:
time: 109 us
  waiting for transfers between devices  58.3 us (53%)
  starting transfers between devices  34.6 us (32%)
  Pallas kernels  4.71 us (4%)
  matrix products  4.39 us (4%)
  local copies, waits for them, and re-layouts  2.89 us (3%)
  other arithmetic  2.77 us (3%)
    ppermute x34, waiting for transfers between devices, swap(): return lax.ppermute(value, axis, [(i, i ^ bit) for i in range(size)])  58.3 us
    ppermute x34, starting transfers between devices, swap(): return lax.ppermute(value, axis, [(i, i ^ bit) for i in range(size)])  34.6 us
    dot_general x10, matrix products, dot_first(): return lax.dot_general(a, b, contract_first, preferred_element_type=f32)  3.85 us
    pallas_call x3, Pallas kernels, logits_of(): pl.pallas_call(kernel, out_shape=jax.ShapeDtypeStruct((total, toks), f32)...  3.3 us
    unnamed x14, local copies, waits for them, and re-layouts  2.84 us
  transfers between devices with their start and end apart: 34, of which 22 were waited for; matrix products, arithmetic and copies ran while one was open for 5% of the time, Pallas kernels for 3%

profile of v7, /device:TPU:0, one launch (start us, length us, event | category | flops | bytes accessed | tf_op | source)
XLA Modules:
  0.0 108.6 jit_solution(13067717003231467694)
XLA Ops:
  0.7 1.6 %copy-done = bf16[128,8192]{1,0:T(8,128)(2,1)S(1)} copy-done((bf16[128,8192]{1,0:T(8,128)(2,1)S(1)}, bf16[128,8192]{1,0:T(8,128)(2,1)}, u32[]{:S(2)}) %copy-start) | copy-done | bytes 2097176
  2.6 3.0 %collective-permute-start.8 = (bf16[128,2048]{1,0:T(8,128)(2,1)S(1)}, bf16[128,2048]{1,0:T(8,128)(2,1)S(1)}, u32[]{:S(2)}, u32[]{:S(2)}) collective-permute-start(bf16[128,2048]{1,0:T(8,128)(2,1)S(1)} %get-tuple-element.36), channel_id=1, source_target_pairs={{0,4},{4,0},{8,12},{12,8},{16,20},{20,16},{24,28},{28,24},{1,5},{5... | collective-permute-start | bytes 1572872 | tf_op jit(solution)/shard_map/ppermute | solution.py:25
  7.4 1.6 %collective-permute-start.3 = (bf16[128,1024]{1,0:T(8,128)(2,1)S(1)}, bf16[128,1024]{1,0:T(8,128)(2,1)S(1)}, u32[]{:S(2)}, u32[]{:S(2)}) collective-permute-start(bf16[128,1024]{1,0:T(8,128)(2,1)S(1)} %copy-done.1), channel_id=1, source_target_pairs={{0,2},{1,3},{2,0},{3,1},{4,6},{5,7},{6,4},{7,5},{8,10},{9,11},{10,... | collective-permute-start | bytes 786440 | tf_op jit(solution)/shard_map/ppermute | solution.py:25
  8.9 1.6 %collective-permute-start.2 = (bf16[128,1024]{1,0:T(8,128)(2,1)S(1)}, bf16[128,1024]{1,0:T(8,128)(2,1)S(1)}, u32[]{:S(2)}, u32[]{:S(2)}) collective-permute-start(bf16[128,1024]{1,0:T(8,128)(2,1)S(1)} %copy-done.1), channel_id=1, source_target_pairs={{0,8},{4,12},{8,0},{12,4},{16,24},{20,28},{24,16},{28,20},{1,9},{5... | collective-permute-start | bytes 786440 | tf_op jit(solution)/shard_map/ppermute | solution.py:25
  10.5 2.6 %collective-permute-start.1 = (bf16[128,1024]{1,0:T(8,128)(2,1)S(1)}, bf16[128,1024]{1,0:T(8,128)(2,1)S(1)}, u32[]{:S(2)}, u32[]{:S(2)}) collective-permute-start(bf16[128,1024]{1,0:T(8,128)(2,1)S(1)} %copy-done.1), channel_id=1, source_target_pairs={{0,16},{4,20},{8,24},{12,28},{16,0},{20,4},{24,8},{28,12},{1,17},{... | collective-permute-start | bytes 786440 | tf_op jit(solution)/shard_map/ppermute | solution.py:25
  13.1 2.1 %collective-permute-done.3.refs_9_ = bf16[128,1024]{1,0:T(8,128)(2,1)S(1)} collective-permute-done((bf16[128,1024]{1,0:T(8,128)(2,1)S(1)}, bf16[128,1024]{1,0:T(8,128)(2,1)S(1)}, u32[]{:S(2)}, u32[]{:S(2)}) %collective-permute-start.3) | collective-permute-done | bytes 262176 | tf_op jit(solution)/shard_map/ppermute | solution.py:25
  15.2 6.7 %collective-permute-done.2.refs_4_.refs_7_ = bf16[128,1024]{1,0:T(8,128)(2,1)S(1)} collective-permute-done((bf16[128,1024]{1,0:T(8,128)(2,1)S(1)}, bf16[128,1024]{1,0:T(8,128)(2,1)S(1)}, u32[]{:S(2)}, u32[]{:S(2)}) %collective-permute-start.2) | collective-permute-done | bytes 262176 | tf_op jit(solution)/shard_map/ppermute | solution.py:25
  21.9 2.5 %collective-permute-done.1.refs_5_.refs_8_ = bf16[128,1024]{1,0:T(8,128)(2,1)S(1)} collective-permute-done((bf16[128,1024]{1,0:T(8,128)(2,1)S(1)}, bf16[128,1024]{1,0:T(8,128)(2,1)S(1)}, u32[]{:S(2)}, u32[]{:S(2)}) %collective-permute-start.1) | collective-permute-done | bytes 262176 | tf_op jit(solution)/shard_map/ppermute | solution.py:25
  25.8 1.5 %collective-permute-start.12 = (bf16[128,1024]{1,0:T(8,128)(2,1)S(1)}, bf16[128,1024]{1,0:T(8,128)(2,1)S(1)}, u32[]{:S(2)}, u32[]{:S(2)}) collective-permute-start(bf16[128,1024]{1,0:T(8,128)(2,1)S(1)} %collective-permute-done.1.refs_5_.refs_8_), channel_id=1, source_target_pairs={{0,2},{1,3},{2,0},{3,1},{4,6},{5,7},{6,4},{7,5},{8,10},{9,11},{10,... | collective-permute-start | bytes 786440 | tf_op jit(solution)/shard_map/ppermute | solution.py:25
  27.3 3.7 %collective-permute-done.4.refs_6_.refs_9_ = bf16[128,1024]{1,0:T(8,128)(2,1)S(1)} collective-permute-done((bf16[128,1024]{1,0:T(8,128)(2,1)S(1)}, bf16[128,1024]{1,0:T(8,128)(2,1)S(1)}, u32[]{:S(2)}, u32[]{:S(2)}) %collective-permute-start.4) | collective-permute-done | bytes 262176 | tf_op jit(solution)/shard_map/ppermute | solution.py:25
  31.2 2.7 %collective-permute-done.7.refs_10_ = bf16[128,1024]{1,0:T(8,128)(2,1)S(1)} collective-permute-done((bf16[128,1024]{1,0:T(8,128)(2,1)S(1)}, bf16[128,1024]{1,0:T(8,128)(2,1)S(1)}, u32[]{:S(2)}, u32[]{:S(2)}) %collective-permute-start.7) | collective-permute-done | bytes 262176 | tf_op jit(solution)/shard_map/ppermute | solution.py:25
  36.4 3.0 %collective-permute-done.12.refs_11_ = bf16[128,1024]{1,0:T(8,128)(2,1)S(1)} collective-permute-done((bf16[128,1024]{1,0:T(8,128)(2,1)S(1)}, bf16[128,1024]{1,0:T(8,128)(2,1)S(1)}, u32[]{:S(2)}, u32[]{:S(2)}) %collective-permute-start.12) | collective-permute-done | bytes 262176 | tf_op jit(solution)/shard_map/ppermute | solution.py:25
  40.2 2.0 %collective-permute-done.9.refs_12_ = bf16[128,1024]{1,0:T(8,128)(2,1)S(1)} collective-permute-done((bf16[128,1024]{1,0:T(8,128)(2,1)S(1)}, bf16[128,1024]{1,0:T(8,128)(2,1)S(1)}, u32[]{:S(2)}, u32[]{:S(2)}) %collective-permute-start.9) | collective-permute-done | bytes 262176 | tf_op jit(solution)/shard_map/ppermute | solution.py:25
  43.8 1.5 %collective-permute-start.22 = (bf16[256,64]{1,0:T(8,128)(2,1)S(1)}, bf16[256,64]{1,0:T(8,128)(2,1)S(1)}, u32[]{:S(2)}, u32[]{:S(2)}) collective-permute-start(bf16[256,64]{1,0:T(8,128)(2,1)S(1)} %get-tuple-element.55), channel_id=1, source_target_pairs={{0,4},{4,0},{8,12},{12,8},{16,20},{20,16},{24,28},{28,24},{1,5},{5... | collective-permute-start | bytes 98312 | tf_op jit(solution)/shard_map/ppermute | solution.py:25
  45.4 4.0 %collective-permute-done.22 = bf16[256,64]{1,0:T(8,128)(2,1)S(1)} collective-permute-done((bf16[256,64]{1,0:T(8,128)(2,1)S(1)}, bf16[256,64]{1,0:T(8,128)(2,1)S(1)}, u32[]{:S(2)}, u32[]{:S(2)}) %collective-permute-start.22) | collective-permute-done | bytes 32800 | tf_op jit(solution)/shard_map/ppermute | solution.py:25
  50.1 1.3 %collective-permute-start.16 = (f32[256,128]{1,0:T(8,128)S(1)}, f32[256,128]{1,0:T(8,128)S(1)}, u32[]{:S(2)}, u32[]{:S(2)}) collective-permute-start(f32[256,128]{1,0:T(8,128)S(1)} %shard_map.88), channel_id=1, source_target_pairs={{0,4},{4,0},{8,12},{12,8},{16,20},{20,16},{24,28},{28,24},{1,5},{5... | collective-permute-start | bytes 393224 | tf_op jit(solution)/shard_map/ppermute | solution.py:25
  51.4 1.6 %shard_map.89 = f32[576,128]{1,0:T(8,128)S(1)} custom-call(bf16[128,4096]{1,0:T(8,128)(2,1)S(1)} %get-tuple-element.59.refs_0_, bf16[128,4096]{1,0:T(8,128)(2,1)S(1)} %collective-permute-done.refs_1_, bf16[64,4096]{1,0:T(8,128)(2,1)S(1)} %get-tuple-element.46.refs_2_, bf16[128,2048]{1,0:T(8,128)(2,1)S(1)} %collective-permute-done.8.refs_0_.refs_3_.refs_2_, ...), custom_call_target="tpu_custom_call" | custom-call | flops 603979776 | bytes 6062080 | tf_op jit(solution)/shard_map/pallas_call | solution.py:95
  54.5 2.1 %collective-permute-done.16 = f32[256,128]{1,0:T(8,128)S(1)} collective-permute-done((f32[256,128]{1,0:T(8,128)S(1)}, f32[256,128]{1,0:T(8,128)S(1)}, u32[]{:S(2)}, u32[]{:S(2)}) %collective-permute-start.16) | collective-permute-done | bytes 131104 | tf_op jit(solution)/shard_map/ppermute | solution.py:25
  56.7 4.8 %collective-permute-done.18 = f32[576,128]{1,0:T(8,128)S(1)} collective-permute-done((f32[576,128]{1,0:T(8,128)S(1)}, f32[576,128]{1,0:T(8,128)S(1)}, u32[]{:S(2)}, u32[]{:S(2)}) %collective-permute-start.18) | collective-permute-done | bytes 294944 | tf_op jit(solution)/shard_map/ppermute | solution.py:25
  61.6 1.8 %collective-permute-start.19 = (f32[4,256]{1,0:T(4,128)S(1)}, f32[4,256]{1,0:T(4,128)S(1)}, u32[]{:S(2)}, u32[]{:S(2)}) collective-permute-start(f32[4,256]{1,0:T(4,128)S(1)} %maximum_maximum_fusion), channel_id=1, source_target_pairs={{0,2},{1,3},{2,0},{3,1},{4,6},{5,7},{6,4},{7,5},{8,10},{9,11},{10,... | collective-permute-start | bytes 12296 | tf_op jit(solution)/shard_map/ppermute | solution.py:25
  63.8 1.4 %collective-permute-done.19 = f32[4,256]{1,0:T(4,128)S(1)} collective-permute-done((f32[4,256]{1,0:T(4,128)S(1)}, f32[4,256]{1,0:T(4,128)S(1)}, u32[]{:S(2)}, u32[]{:S(2)}) %collective-permute-start.19) | collective-permute-done | bytes 4128 | tf_op jit(solution)/shard_map/ppermute | solution.py:25
  65.6 3.4 %collective-permute-done.20 = f32[2,256]{1,0:T(2,128)S(1)} collective-permute-done((f32[2,256]{1,0:T(2,128)S(1)}, f32[2,256]{1,0:T(2,128)S(1)}, u32[]{:S(2)}, u32[]{:S(2)}) %collective-permute-start.20) | collective-permute-done | bytes 2080 | tf_op jit(solution)/shard_map/ppermute | solution.py:25
  70.2 3.3 %collective-permute-done.21 = f32[2,256]{1,0:T(2,128)S(1)} collective-permute-done((f32[2,256]{1,0:T(2,128)S(1)}, f32[2,256]{1,0:T(2,128)S(1)}, u32[]{:S(2)}, u32[]{:S(2)}) %collective-permute-start.21) | collective-permute-done | bytes 2080 | tf_op jit(solution)/shard_map/ppermute | solution.py:25
  74.5 1.8 %collective-permute-start.24 = (bf16[128,1024]{1,0:T(8,128)(2,1)S(1)}, bf16[128,1024]{1,0:T(8,128)(2,1)S(1)}, u32[]{:S(2)}, u32[]{:S(2)}) collective-permute-start(bf16[128,1024]{1,0:T(8,128)(2,1)S(1)} %convolution_convert_fusion.1), channel_id=1, source_target_pairs={{0,2},{1,3},{2,0},{3,1},{4,6},{5,7},{6,4},{7,5},{8,10},{9,11},{10,... | collective-permute-start | bytes 786440 | tf_op jit(solution)/shard_map/ppermute | solution.py:25
  77.3 6.1 %collective-permute-done.24 = bf16[128,1024]{1,0:T(8,128)(2,1)S(1)} collective-permute-done((bf16[128,1024]{1,0:T(8,128)(2,1)S(1)}, bf16[128,1024]{1,0:T(8,128)(2,1)S(1)}, u32[]{:S(2)}, u32[]{:S(2)}) %collective-permute-start.24) | collective-permute-done | bytes 262176 | tf_op jit(solution)/shard_map/ppermute | solution.py:25
  83.9 1.8 %collective-permute-start.26 = (bf16[128,1024]{1,0:T(8,128)(2,1)S(1)}, bf16[128,1024]{1,0:T(8,128)(2,1)S(1)}, u32[]{:S(2)}, u32[]{:S(2)}) collective-permute-start(bf16[128,1024]{1,0:T(8,128)(2,1)S(1)} %convolution_convert_fusion), channel_id=1, source_target_pairs={{0,2},{1,3},{2,0},{3,1},{4,6},{5,7},{6,4},{7,5},{8,10},{9,11},{10,... | collective-permute-start | bytes 786440 | tf_op jit(solution)/shard_map/ppermute | solution.py:25
  88.3 1.7 %collective-permute-start.25 = (bf16[128,1024]{1,0:T(8,128)(2,1)S(1)}, bf16[128,1024]{1,0:T(8,128)(2,1)S(1)}, u32[]{:S(2)}, u32[]{:S(2)}) collective-permute-start(bf16[128,1024]{1,0:T(8,128)(2,1)S(1)} %convolution_convert_fusion.3), channel_id=1, source_target_pairs={{0,2},{1,3},{2,0},{3,1},{4,6},{5,7},{6,4},{7,5},{8,10},{9,11},{10,... | collective-permute-start | bytes 786440 | tf_op jit(solution)/shard_map/ppermute | solution.py:25
  90.6 2.2 %collective-permute-start.28 = (bf16[128,1024]{1,0:T(8,128)(2,1)S(1)}, bf16[128,1024]{1,0:T(8,128)(2,1)S(1)}, u32[]{:S(2)}, u32[]{:S(2)}) collective-permute-start(bf16[128,1024]{1,0:T(8,128)(2,1)S(1)} %fusion.7), channel_id=1, source_target_pairs={{0,8},{4,12},{8,0},{12,4},{16,24},{20,28},{24,16},{28,20},{1,9},{5... | collective-permute-start | bytes 786440 | tf_op jit(solution)/shard_map/ppermute | solution.py:25
  92.9 2.0 %collective-permute-start.32 = (f32[64,64]{1,0:T(8,128)S(1)}, f32[64,64]{1,0:T(8,128)S(1)}, u32[]{:S(2)}, u32[]{:S(2)}) collective-permute-start(f32[64,64]{1,0:T(8,128)S(1)} %add.172), channel_id=1, source_target_pairs={{0,2},{1,3},{2,0},{3,1},{4,6},{5,7},{6,4},{7,5},{8,10},{9,11},{10,... | collective-permute-start | bytes 49160 | tf_op jit(solution)/shard_map/ppermute | solution.py:25
  95.4 2.2 %collective-permute-start.29 = (bf16[128,1024]{1,0:T(8,128)(2,1)S(1)}, bf16[128,1024]{1,0:T(8,128)(2,1)S(1)}, u32[]{:S(2)}, u32[]{:S(2)}) collective-permute-start(bf16[128,1024]{1,0:T(8,128)(2,1)S(1)} %fusion.5), channel_id=1, source_target_pairs={{0,16},{4,20},{8,24},{12,28},{16,0},{20,4},{24,8},{28,12},{1,17},{... | collective-permute-start | bytes 786440 | tf_op jit(solution)/shard_map/ppermute | solution.py:25
  98.8 1.3 %collective-permute-done.33 = bf16[64,1024]{1,0:T(8,128)(2,1)S(1)} collective-permute-done((bf16[64,1024]{1,0:T(8,128)(2,1)S(1)}, bf16[64,1024]{1,0:T(8,128)(2,1)S(1)}, u32[]{:S(2)}, u32[]{:S(2)}) %collective-permute-start.33) | collective-permute-done | bytes 131104 | tf_op jit(solution)/shard_map/ppermute | solution.py:25
  101.0 6.5 %collective-permute-done.29 = bf16[128,1024]{1,0:T(8,128)(2,1)S(1)} collective-permute-done((bf16[128,1024]{1,0:T(8,128)(2,1)S(1)}, bf16[128,1024]{1,0:T(8,128)(2,1)S(1)}, u32[]{:S(2)}, u32[]{:S(2)}) %collective-permute-start.29) | collective-permute-done | bytes 262176 | tf_op jit(solution)/shard_map/ppermute | solution.py:25
  (111 shorter events, 22.2 us)
Async XLA Ops:
  2.6 22.6 %collective-permute-start.8 = (bf16[128,2048]{1,0:T(8,128)(2,1)S(1)}, bf16[128,2048]{1,0:T(8,128)(2,1)S(1)}, u32[]{:S(2)}, u32[]{:S(2)}) collective-permute-start(bf16[128,2048]{1,0:T(8,128)(2,1)S(1)} %get-tuple-element.36), channel_id=1, source_target_pairs={{0,4},{4,0},{8,12},{12,8},{16,20},{20,16},{24,28},{28,24},{1,5},{5... | collective-permute-start | bytes 1572872 | tf_op jit(solution)/shard_map/ppermute | solution.py:25
  7.4 7.8 %collective-permute-start.3 = (bf16[128,1024]{1,0:T(8,128)(2,1)S(1)}, bf16[128,1024]{1,0:T(8,128)(2,1)S(1)}, u32[]{:S(2)}, u32[]{:S(2)}) collective-permute-start(bf16[128,1024]{1,0:T(8,128)(2,1)S(1)} %copy-done.1), channel_id=1, source_target_pairs={{0,2},{1,3},{2,0},{3,1},{4,6},{5,7},{6,4},{7,5},{8,10},{9,11},{10,... | collective-permute-start | bytes 786440 | tf_op jit(solution)/shard_map/ppermute | solution.py:25
  8.9 13.0 %collective-permute-start.2 = (bf16[128,1024]{1,0:T(8,128)(2,1)S(1)}, bf16[128,1024]{1,0:T(8,128)(2,1)S(1)}, u32[]{:S(2)}, u32[]{:S(2)}) collective-permute-start(bf16[128,1024]{1,0:T(8,128)(2,1)S(1)} %copy-done.1), channel_id=1, source_target_pairs={{0,8},{4,12},{8,0},{12,4},{16,24},{20,28},{24,16},{28,20},{1,9},{5... | collective-permute-start | bytes 786440 | tf_op jit(solution)/shard_map/ppermute | solution.py:25
  10.5 13.9 %collective-permute-start.1 = (bf16[128,1024]{1,0:T(8,128)(2,1)S(1)}, bf16[128,1024]{1,0:T(8,128)(2,1)S(1)}, u32[]{:S(2)}, u32[]{:S(2)}) collective-permute-start(bf16[128,1024]{1,0:T(8,128)(2,1)S(1)} %copy-done.1), channel_id=1, source_target_pairs={{0,16},{4,20},{8,24},{12,28},{16,0},{20,4},{24,8},{28,12},{1,17},{... | collective-permute-start | bytes 786440 | tf_op jit(solution)/shard_map/ppermute | solution.py:25
  13.1 29.1 %collective-permute-start = (bf16[128,4096]{1,0:T(8,128)(2,1)S(1)}, bf16[128,4096]{1,0:T(8,128)(2,1)S(1)}, u32[]{:S(2)}, u32[]{:S(2)}) collective-permute-start(bf16[128,4096]{1,0:T(8,128)(2,1)S(1)} %get-tuple-element.59.refs_0_), channel_id=1, source_target_pairs={{0,1},{1,0},{2,3},{3,2},{4,5},{5,4},{6,7},{7,6},{8,9},{9,8},{10,11... | collective-permute-start | bytes 3145736 | tf_op jit(solution)/shard_map/ppermute | solution.py:25
  24.4 6.5 %collective-permute-start.4 = (bf16[128,1024]{1,0:T(8,128)(2,1)S(1)}, bf16[128,1024]{1,0:T(8,128)(2,1)S(1)}, u32[]{:S(2)}, u32[]{:S(2)}) collective-permute-start(bf16[128,1024]{1,0:T(8,128)(2,1)S(1)} %collective-permute-done.1.refs_5_.refs_8_), channel_id=1, source_target_pairs={{0,8},{4,12},{8,0},{12,4},{16,24},{20,28},{24,16},{28,20},{1,9},{5... | collective-permute-start | bytes 786440 | tf_op jit(solution)/shard_map/ppermute | solution.py:25
  24.7 9.2 %collective-permute-start.7 = (bf16[128,1024]{1,0:T(8,128)(2,1)S(1)}, bf16[128,1024]{1,0:T(8,128)(2,1)S(1)}, u32[]{:S(2)}, u32[]{:S(2)}) collective-permute-start(bf16[128,1024]{1,0:T(8,128)(2,1)S(1)} %collective-permute-done.2.refs_4_.refs_7_), channel_id=1, source_target_pairs={{0,2},{1,3},{2,0},{3,1},{4,6},{5,7},{6,4},{7,5},{8,10},{9,11},{10,... | collective-permute-start | bytes 786440 | tf_op jit(solution)/shard_map/ppermute | solution.py:25
  25.3 9.9 %collective-permute-start.11 = (bf16[128,1024]{1,0:T(8,128)(2,1)S(1)}, bf16[128,1024]{1,0:T(8,128)(2,1)S(1)}, u32[]{:S(2)}, u32[]{:S(2)}) collective-permute-start(bf16[128,1024]{1,0:T(8,128)(2,1)S(1)} %get-tuple-element.50), channel_id=1, source_target_pairs={{0,4},{4,0},{8,12},{12,8},{16,20},{20,16},{24,28},{28,24},{1,5},{5... | collective-permute-start | bytes 786440 | tf_op jit(solution)/shard_map/ppermute | solution.py:25
  25.8 13.6 %collective-permute-start.12 = (bf16[128,1024]{1,0:T(8,128)(2,1)S(1)}, bf16[128,1024]{1,0:T(8,128)(2,1)S(1)}, u32[]{:S(2)}, u32[]{:S(2)}) collective-permute-start(bf16[128,1024]{1,0:T(8,128)(2,1)S(1)} %collective-permute-done.1.refs_5_.refs_8_), channel_id=1, source_target_pairs={{0,2},{1,3},{2,0},{3,1},{4,6},{5,7},{6,4},{7,5},{8,10},{9,11},{10,... | collective-permute-start | bytes 786440 | tf_op jit(solution)/shard_map/ppermute | solution.py:25
  30.9 3.7 %collective-permute-start.5 = (bf16[64,64]{1,0:T(8,128)(2,1)S(1)}, bf16[64,64]{1,0:T(8,128)(2,1)S(1)}, u32[]{:S(2)}, u32[]{:S(2)}) collective-permute-start(bf16[64,64]{1,0:T(8,128)(2,1)S(1)} %copy-done.3), channel_id=1, source_target_pairs={{0,8},{4,12},{8,0},{12,4},{16,24},{20,28},{24,16},{28,20},{1,9},{5... | collective-permute-start | bytes 24584 | tf_op jit(solution)/shard_map/ppermute | solution.py:25
  34.0 11.4 %collective-permute-start.10 = (bf16[128,1024]{1,0:T(8,128)(2,1)S(1)}, bf16[128,1024]{1,0:T(8,128)(2,1)S(1)}, u32[]{:S(2)}, u32[]{:S(2)}) collective-permute-start(bf16[128,1024]{1,0:T(8,128)(2,1)S(1)} %get-tuple-element.48), channel_id=1, source_target_pairs={{0,4},{4,0},{8,12},{12,8},{16,20},{20,16},{24,28},{28,24},{1,5},{5... | collective-permute-start | bytes 786440 | tf_op jit(solution)/shard_map/ppermute | solution.py:25
  34.7 7.5 %collective-permute-start.9 = (bf16[128,1024]{1,0:T(8,128)(2,1)S(1)}, bf16[128,1024]{1,0:T(8,128)(2,1)S(1)}, u32[]{:S(2)}, u32[]{:S(2)}) collective-permute-start(bf16[128,1024]{1,0:T(8,128)(2,1)S(1)} %collective-permute-done.4.refs_6_.refs_9_), channel_id=1, source_target_pairs={{0,2},{1,3},{2,0},{3,1},{4,6},{5,7},{6,4},{7,5},{8,10},{9,11},{10,... | collective-permute-start | bytes 786440 | tf_op jit(solution)/shard_map/ppermute | solution.py:25
  35.2 5.0 %collective-permute-start.6 = (bf16[128,64]{1,0:T(8,128)(2,1)S(1)}, bf16[128,64]{1,0:T(8,128)(2,1)S(1)}, u32[]{:S(2)}, u32[]{:S(2)}) collective-permute-start(bf16[128,64]{1,0:T(8,128)(2,1)S(1)} %pad_maximum_fusion.2), channel_id=1, source_target_pairs={{0,16},{4,20},{8,24},{12,28},{16,0},{20,4},{24,8},{28,12},{1,17},{... | collective-permute-start | bytes 49160 | tf_op jit(solution)/shard_map/ppermute | solution.py:25
  39.4 6.0 %collective-permute-start.15 = (bf16[128,1024]{1,0:T(8,128)(2,1)S(1)}, bf16[128,1024]{1,0:T(8,128)(2,1)S(1)}, u32[]{:S(2)}, u32[]{:S(2)}) collective-permute-start(bf16[128,1024]{1,0:T(8,128)(2,1)S(1)} %collective-permute-done.11.refs_2_.refs_5_.refs_4_), channel_id=1, source_target_pairs={{0,1},{1,0},{2,3},{3,2},{4,5},{5,4},{6,7},{7,6},{8,9},{9,8},{10,11... | collective-permute-start | bytes 786440 | tf_op jit(solution)/shard_map/ppermute | solution.py:25
  40.2 9.2 %collective-permute-start.13 = (bf16[128,2048]{1,0:T(8,128)(2,1)S(1)}, bf16[128,2048]{1,0:T(8,128)(2,1)S(1)}, u32[]{:S(2)}, u32[]{:S(2)}) collective-permute-start(bf16[128,2048]{1,0:T(8,128)(2,1)S(1)} %collective-permute-done.8.refs_0_.refs_3_.refs_2_), channel_id=1, source_target_pairs={{0,1},{1,0},{2,3},{3,2},{4,5},{5,4},{6,7},{7,6},{8,9},{9,8},{10,11... | collective-permute-start | bytes 1572872 | tf_op jit(solution)/shard_map/ppermute | solution.py:25
  43.2 6.1 %collective-permute-start.17 = (f32[320,128]{1,0:T(8,128)S(1)}, f32[320,128]{1,0:T(8,128)S(1)}, u32[]{:S(2)}, u32[]{:S(2)}) collective-permute-start(f32[320,128]{1,0:T(8,128)S(1)} %shard_map.87), channel_id=1, source_target_pairs={{0,4},{4,0},{8,12},{12,8},{16,20},{20,16},{24,28},{28,24},{1,5},{5... | collective-permute-start | bytes 491528 | tf_op jit(solution)/shard_map/ppermute | solution.py:25
  43.8 5.6 %collective-permute-start.22 = (bf16[256,64]{1,0:T(8,128)(2,1)S(1)}, bf16[256,64]{1,0:T(8,128)(2,1)S(1)}, u32[]{:S(2)}, u32[]{:S(2)}) collective-permute-start(bf16[256,64]{1,0:T(8,128)(2,1)S(1)} %get-tuple-element.55), channel_id=1, source_target_pairs={{0,4},{4,0},{8,12},{12,8},{16,20},{20,16},{24,28},{28,24},{1,5},{5... | collective-permute-start | bytes 98312 | tf_op jit(solution)/shard_map/ppermute | solution.py:25
  45.3 4.1 %collective-permute-start.14 = (bf16[128,1024]{1,0:T(8,128)(2,1)S(1)}, bf16[128,1024]{1,0:T(8,128)(2,1)S(1)}, u32[]{:S(2)}, u32[]{:S(2)}) collective-permute-start(bf16[128,1024]{1,0:T(8,128)(2,1)S(1)} %collective-permute-done.10.refs_1_.refs_4_.refs_3_), channel_id=1, source_target_pairs={{0,1},{1,0},{2,3},{3,2},{4,5},{5,4},{6,7},{7,6},{8,9},{9,8},{10,11... | collective-permute-start | bytes 786440 | tf_op jit(solution)/shard_map/ppermute | solution.py:25
  50.1 6.4 %collective-permute-start.16 = (f32[256,128]{1,0:T(8,128)S(1)}, f32[256,128]{1,0:T(8,128)S(1)}, u32[]{:S(2)}, u32[]{:S(2)}) collective-permute-start(f32[256,128]{1,0:T(8,128)S(1)} %shard_map.88), channel_id=1, source_target_pairs={{0,4},{4,0},{8,12},{12,8},{16,20},{20,16},{24,28},{28,24},{1,5},{5... | collective-permute-start | bytes 393224 | tf_op jit(solution)/shard_map/ppermute | solution.py:25
  53.0 8.4 %collective-permute-start.18 = (f32[576,128]{1,0:T(8,128)S(1)}, f32[576,128]{1,0:T(8,128)S(1)}, u32[]{:S(2)}, u32[]{:S(2)}) collective-permute-start(f32[576,128]{1,0:T(8,128)S(1)} %shard_map.89), channel_id=1, source_target_pairs={{0,4},{4,0},{8,12},{12,8},{16,20},{20,16},{24,28},{28,24},{1,5},{5... | collective-permute-start | bytes 884744 | tf_op jit(solution)/shard_map/ppermute | solution.py:25
  61.6 3.7 %collective-permute-start.19 = (f32[4,256]{1,0:T(4,128)S(1)}, f32[4,256]{1,0:T(4,128)S(1)}, u32[]{:S(2)}, u32[]{:S(2)}) collective-permute-start(f32[4,256]{1,0:T(4,128)S(1)} %maximum_maximum_fusion), channel_id=1, source_target_pairs={{0,2},{1,3},{2,0},{3,1},{4,6},{5,7},{6,4},{7,5},{8,10},{9,11},{10,... | collective-permute-start | bytes 12296 | tf_op jit(solution)/shard_map/ppermute | solution.py:25
  69.0 4.5 %collective-permute-start.21 = (f32[2,256]{1,0:T(2,128)S(1)}, f32[2,256]{1,0:T(2,128)S(1)}, u32[]{:S(2)}, u32[]{:S(2)}) collective-permute-start(f32[2,256]{1,0:T(2,128)S(1)} %pad_maximum_fusion.4), channel_id=1, source_target_pairs={{0,16},{4,20},{8,24},{12,28},{16,0},{20,4},{24,8},{28,12},{1,17},{... | collective-permute-start | bytes 6152 | tf_op jit(solution)/shard_map/ppermute | solution.py:25
  74.5 8.9 %collective-permute-start.24 = (bf16[128,1024]{1,0:T(8,128)(2,1)S(1)}, bf16[128,1024]{1,0:T(8,128)(2,1)S(1)}, u32[]{:S(2)}, u32[]{:S(2)}) collective-permute-start(bf16[128,1024]{1,0:T(8,128)(2,1)S(1)} %convolution_convert_fusion.1), channel_id=1, source_target_pairs={{0,2},{1,3},{2,0},{3,1},{4,6},{5,7},{6,4},{7,5},{8,10},{9,11},{10,... | collective-permute-start | bytes 786440 | tf_op jit(solution)/shard_map/ppermute | solution.py:25
  76.7 9.9 %collective-permute-start.23 = (bf16[128,1024]{1,0:T(8,128)(2,1)S(1)}, bf16[128,1024]{1,0:T(8,128)(2,1)S(1)}, u32[]{:S(2)}, u32[]{:S(2)}) collective-permute-start(bf16[128,1024]{1,0:T(8,128)(2,1)S(1)} %convolution_convert_fusion.2), channel_id=1, source_target_pairs={{0,2},{1,3},{2,0},{3,1},{4,6},{5,7},{6,4},{7,5},{8,10},{9,11},{10,... | collective-permute-start | bytes 786440 | tf_op jit(solution)/shard_map/ppermute | solution.py:25
  83.8 6.9 %collective-permute-start.27 = (bf16[128,1024]{1,0:T(8,128)(2,1)S(1)}, bf16[128,1024]{1,0:T(8,128)(2,1)S(1)}, u32[]{:S(2)}, u32[]{:S(2)}) collective-permute-start(bf16[128,1024]{1,0:T(8,128)(2,1)S(1)} %fusion.6), channel_id=1, source_target_pairs={{0,8},{4,12},{8,0},{12,4},{16,24},{20,28},{24,16},{28,20},{1,9},{5... | collective-permute-start | bytes 786440 | tf_op jit(solution)/shard_map/ppermute | solution.py:25
  83.9 6.4 %collective-permute-start.26 = (bf16[128,1024]{1,0:T(8,128)(2,1)S(1)}, bf16[128,1024]{1,0:T(8,128)(2,1)S(1)}, u32[]{:S(2)}, u32[]{:S(2)}) collective-permute-start(bf16[128,1024]{1,0:T(8,128)(2,1)S(1)} %convolution_convert_fusion), channel_id=1, source_target_pairs={{0,2},{1,3},{2,0},{3,1},{4,6},{5,7},{6,4},{7,5},{8,10},{9,11},{10,... | collective-permute-start | bytes 786440 | tf_op jit(solution)/shard_map/ppermute | solution.py:25
  87.8 5.1 %collective-permute-start.30 = (f32[64,1024]{1,0:T(8,128)S(1)}, f32[64,1024]{1,0:T(8,128)S(1)}, u32[]{:S(2)}, u32[]{:S(2)}) collective-permute-start(f32[64,1024]{1,0:T(8,128)S(1)} %fusion.45), channel_id=1, source_target_pairs={{0,1},{1,0},{2,3},{3,2},{4,5},{5,4},{6,7},{7,6},{8,9},{9,8},{10,11... | collective-permute-start | bytes 786440 | tf_op jit(solution)/shard_map/ppermute | solution.py:25
  88.3 12.5 %collective-permute-start.25 = (bf16[128,1024]{1,0:T(8,128)(2,1)S(1)}, bf16[128,1024]{1,0:T(8,128)(2,1)S(1)}, u32[]{:S(2)}, u32[]{:S(2)}) collective-permute-start(bf16[128,1024]{1,0:T(8,128)(2,1)S(1)} %convolution_convert_fusion.3), channel_id=1, source_target_pairs={{0,2},{1,3},{2,0},{3,1},{4,6},{5,7},{6,4},{7,5},{8,10},{9,11},{10,... | collective-permute-start | bytes 786440 | tf_op jit(solution)/shard_map/ppermute | solution.py:25
  90.6 10.4 %collective-permute-start.28 = (bf16[128,1024]{1,0:T(8,128)(2,1)S(1)}, bf16[128,1024]{1,0:T(8,128)(2,1)S(1)}, u32[]{:S(2)}, u32[]{:S(2)}) collective-permute-start(bf16[128,1024]{1,0:T(8,128)(2,1)S(1)} %fusion.7), channel_id=1, source_target_pairs={{0,8},{4,12},{8,0},{12,4},{16,24},{20,28},{24,16},{28,20},{1,9},{5... | collective-permute-start | bytes 786440 | tf_op jit(solution)/shard_map/ppermute | solution.py:25
  92.9 5.3 %collective-permute-start.32 = (f32[64,64]{1,0:T(8,128)S(1)}, f32[64,64]{1,0:T(8,128)S(1)}, u32[]{:S(2)}, u32[]{:S(2)}) collective-permute-start(f32[64,64]{1,0:T(8,128)S(1)} %add.172), channel_id=1, source_target_pairs={{0,2},{1,3},{2,0},{3,1},{4,6},{5,7},{6,4},{7,5},{8,10},{9,11},{10,... | collective-permute-start | bytes 49160 | tf_op jit(solution)/shard_map/ppermute | solution.py:25
  94.9 5.2 %collective-permute-start.33 = (bf16[64,1024]{1,0:T(8,128)(2,1)S(1)}, bf16[64,1024]{1,0:T(8,128)(2,1)S(1)}, u32[]{:S(2)}, u32[]{:S(2)}) collective-permute-start(bf16[64,1024]{1,0:T(8,128)(2,1)S(1)} %convert_element_type.111), channel_id=1, source_target_pairs={{0,2},{1,3},{2,0},{3,1},{4,6},{5,7},{6,4},{7,5},{8,10},{9,11},{10,... | collective-permute-start | bytes 393224 | tf_op jit(solution)/shard_map/ppermute | solution.py:25
  95.4 12.1 %collective-permute-start.29 = (bf16[128,1024]{1,0:T(8,128)(2,1)S(1)}, bf16[128,1024]{1,0:T(8,128)(2,1)S(1)}, u32[]{:S(2)}, u32[]{:S(2)}) collective-permute-start(bf16[128,1024]{1,0:T(8,128)(2,1)S(1)} %fusion.5), channel_id=1, source_target_pairs={{0,16},{4,20},{8,24},{12,28},{16,0},{20,4},{24,8},{28,12},{1,17},{... | collective-permute-start | bytes 786440 | tf_op jit(solution)/shard_map/ppermute | solution.py:25
  (8 other events, 69.3 us)

commit v8 on v7

--- a/solution.py
+++ b/solution.py
@@ -44,7 +44,7 @@
 in_vmem = pl.BlockSpec(memory_space=pltpu.VMEM)
 
 
-def copy_blocks(shapes, moves, *arrays, source=pltpu.HBM):
+def copy_blocks(shapes, moves, *arrays, source=pltpu.HBM, limit=12):
     def kernel(*refs):
         ins, outs, sems = refs[: len(arrays)], refs[len(arrays) : -1], refs[-1]
         copies = []
@@ -66,7 +66,7 @@
         in_specs=[pl.BlockSpec(memory_space=source)] * len(arrays),
         out_specs=[in_vmem] * len(shapes),
         scratch_shapes=[pltpu.SemaphoreType.DMA((32,))],
-        compiler_params=pltpu.CompilerParams(vmem_limit_bytes=12 << 20),
+        compiler_params=pltpu.CompilerParams(vmem_limit_bytes=limit << 20),
         cost_estimate=pl.CostEstimate(flops=0, bytes_accessed=2 * size, transcendentals=0),
     )(*arrays)
 
@@ -129,8 +129,8 @@
     def start_of(j, other):
         return (lax.axis_index("vocab") ^ (2 * j + other)) * width
 
-    cuts = [0, n_z // 2, 3 * n_z // 4, n_z] if n_z > 2 else list(range(n_z + 1))
-    chunks = [range(a, b) for a, b in zip(cuts, cuts[1:])]
+    cuts = [0, n_z]
+    chunks = [range(a, b) for a, b in zip(cuts, cuts[1:]) if a < b]
     sends = copy_blocks(
         [(rows, len(chunk) * width) for chunk in chunks],
         lambda: [
@@ -139,53 +139,50 @@
             for j in chunk
         ],
         head,
+        limit=56,
     )
     beside = [swap_y(sends[0])]
 
-    head_after, basis_after, _ = lax.optimization_barrier((head, factor_basis, sends[0]))
-    kept, basis_half = copy_blocks(
-        [(rows, depth), (rank, depth)],
-        lambda: [
-            (a, (start_of(j, 0), width), a, 0, j * width) for j in range(n_z) for a in range(2)
-        ],
-        head_after,
-        basis_after,
-    )
-
-    hidden, _ = lax.optimization_barrier((hidden, kept))
-    shards, cross = {0: hidden}, {0: swap_x(hidden)}
+    def half(array, after):
+        array, _ = lax.optimization_barrier((array, after))
+        moves = lambda: [(0, (start_of(j, 0), width), 0, 0, j * width) for j in range(n_z)]
+        return copy_blocks([(array.shape[0], depth)], moves, array)[0]
+
+    kept = half(head, sends[0])
+    kept_core = swap_core(kept)
+
+    z_hidden, _ = lax.optimization_barrier((hidden, sends[0]))
+    x_hidden, _ = lax.optimization_barrier((hidden, sends[0]))
+    shards, cross = {0: hidden}, {0: swap_x(x_hidden)}
     for bit in reversed(bits):
-        near = swap_z(hidden, bit)
+        near = swap_z(z_hidden, bit)
         for j in [j for j in shards if j]:
-            shards[j], _, _ = lax.optimization_barrier((shards[j], near, cross[0]))
+            shards[j], *_ = lax.optimization_barrier((shards[j], near, cross[0], kept_core))
             shards[j ^ bit] = swap_z(shards[j], bit)
         shards[bit] = near
-    for n, send in list(enumerate(sends))[1:]:
-        send, _ = lax.optimization_barrier((send, shards[bits[0]] if n == 1 else beside[n - 2]))
+    waits = []
+    for send, wait in zip(sends[1:], waits):
+        send, _ = lax.optimization_barrier((send, wait))
         beside.append(swap_y(send))
     for j in range(1, n_z):
         sent = shards[j]
         if j > 1:
-            sent, _, _ = lax.optimization_barrier((sent, cross[j - 2], beside[j // 2 - 1]))
+            sent, *_ = lax.optimization_barrier((sent, cross[j - 2], kept_core))
         cross[j] = swap_x(sent)
-
-    kept_core = swap_core(kept)
+    basis_half = half(factor_basis, shards[n_z // 2])
+
     beside_core = []
     for n, came in enumerate(beside):
-        if n < len(beside) - 1:
-            came, _ = lax.optimization_barrier((came, cross[max(0, n_z - 2)]))
+        came, *_ = lax.optimization_barrier((came, cross[1], cross[n_z - 2], shards[n_z - 1]))
         beside_core.append(swap_core(came))
 
-    rows_all, _ = lax.optimization_barrier((factor_rows, shards[n_z - 1]))
-    for bit in bits:
-        rows_all = jnp.concatenate([rows_all, swap_z(rows_all, bit)], axis=0)
-    basis_ready, _, _ = lax.optimization_barrier((basis_half, rows_all, cross[n_z - 1]))
-
     in_order = lambda parts: [parts[j] for j in range(n_z)]
+    basis_ready, *_ = lax.optimization_barrier((basis_half, cross[n_z - 2], shards[n_z - 1]))
     upper = [[kept], [kept_core], [basis_ready]]
     upper_own = logits_of(upper, in_order(shards))
-    beside_core[-1], _ = lax.optimization_barrier((beside_core[-1], upper_own))
+    beside_core[-1], *_ = lax.optimization_barrier((beside_core[-1], upper_own, cross[n_z - 1]))
     lower_own = logits_of([beside, beside_core], in_order(shards))
+    cross[0], _ = lax.optimization_barrier((cross[0], lower_own))
     both_cross = logits_of(upper + [beside, beside_core], in_order(cross))
     n_up = 2 * rows + rank
 
@@ -202,8 +199,10 @@
     )
     hidden_basis = jnp.concatenate([basis_own, basis_cross], axis=1)
 
-    rows_after, _ = lax.optimization_barrier((rows_all, upper_own))
-    rows_all = jnp.concatenate([rows_all, swap_y(rows_after)], axis=0)
+    rows_all, _ = lax.optimization_barrier((factor_rows, both_cross))
+    for bit in bits:
+        rows_all = jnp.concatenate([rows_all, swap_z(rows_all, bit)], axis=0)
+    rows_all = jnp.concatenate([rows_all, swap_y(rows_all)], axis=0)
 
     def merge(a, b):
         top = jnp.maximum(a[0], b[0])
@@ -296,13 +295,11 @@
             sums[j ^ bit] = sums[j ^ bit] + came.astype(f32)
     hidden_grad = (sums[0] + dot_first(mix_total, basis_half[:, :width])).astype(bf16)
 
-    basis_two = lax.reduce_precision(basis_part + swap_core(basis_part), 8, 7)
-    rows_two = rows_part + swap_core(rows_part)
-    basis_two, rows_two, _ = lax.optimization_barrier(
-        (basis_two, rows_two, from_x[min(1, n_z - 1)])
-    )
-    basis_grad = basis_two + swap_x(basis_two.astype(bf16)).astype(f32)
-    rows_grad = rows_two + swap_x(rows_two)
+    factor_part = jnp.concatenate([basis_part, rows_part], axis=1)
+    factor_two = lax.reduce_precision(factor_part + swap_core(factor_part), 8, 7)
+    factor_two, _ = lax.optimization_barrier((factor_two, from_x[min(1, n_z - 1)]))
+    factor_grad = factor_two + swap_x(factor_two.astype(bf16)).astype(f32)
+    basis_grad, rows_grad = factor_grad[:, :width], factor_grad[:, width:]
     return hidden_grad, rows_grad, basis_grad
 
 

time: 109 us -> 111 us (1.018)
  waiting for transfers between devices: 58.3 us -> 62.4 us
  Pallas kernels: 4.71 us -> 7.3 us
  starting transfers between devices: 34.6 us -> 33.1 us
  local copies, waits for them, and re-layouts: 2.89 us -> 1.41 us
  other arithmetic: 2.77 us -> 1.5 us
    ppermute x34 -> x28, waiting for transfers between devices: 58.3 us -> 62.4 us  [swap(): return lax.ppermute(value, axis, [(i, i ^ bit) for i in range(size)])]
    unnamed x14 -> x15, local copies, waits for them, and re-layouts: 2.84 us -> 0.04 us
    pallas_call x3 -> x4, Pallas kernels: 1.41 us -> 3.99 us  [copy_blocks(): pl.pallas_call(kernel, out_shape=[jax.ShapeDtypeStruct(shape, bf16) for s...]
    ppermute x34 -> x28, starting transfers between devices: 34.6 us -> 33.1 us  [swap(): return lax.ppermute(value, axis, [(i, i ^ bit) for i in range(size)])]
    slice x0 -> x2, local copies, waits for them, and re-layouts: none -> 1.34 us  [on_few(): basis_grad, rows_grad = (factor_grad[:, :width], factor_grad[:, width:])]
    add x3 -> x1, other arithmetic: 1.35 us -> 0.03 us  [on_few(): factor_grad = factor_two + swap_x(factor_two.astype(bf16)).astype(f32)]
  transfers between devices with their start and end apart: 34 -> 28, of which waited for: 22 -> 18; matrix products, arithmetic and copies ran while one was open for 5% -> 4% of each run, Pallas kernels for 3% -> 3%
where the time goes in v8:
time: 111 us
  waiting for transfers between devices  62.4 us (56%)
  starting transfers between devices  33.1 us (30%)
  Pallas kernels  7.3 us (7%)
  matrix products  4.38 us (4%)
  other arithmetic  1.5 us (1%)
  local copies, waits for them, and re-layouts  1.41 us (1%)
    ppermute x28, waiting for transfers between devices, swap(): return lax.ppermute(value, axis, [(i, i ^ bit) for i in range(size)])  62.4 us
    ppermute x28, starting transfers between devices, swap(): return lax.ppermute(value, axis, [(i, i ^ bit) for i in range(size)])  33.1 us
    pallas_call x4, Pallas kernels, copy_blocks(): pl.pallas_call(kernel, out_shape=[jax.ShapeDtypeStruct(shape, bf16) for s...  3.99 us
    dot_general x10, matrix products, dot_first(): return lax.dot_general(a, b, contract_first, preferred_element_type=f32)  3.86 us
    pallas_call x3, Pallas kernels, logits_of(): pl.pallas_call(kernel, out_shape=jax.ShapeDtypeStruct((total, toks), f32)...  3.31 us
  transfers between devices with their start and end apart: 28, of which 18 were waited for; matrix products, arithmetic and copies ran while one was open for 4% of the time, Pallas kernels for 3%

profile of v8, /device:TPU:0, one launch (start us, length us, event | category | flops | bytes accessed | tf_op | source)
XLA Modules:
  0.0 111.1 jit_solution(8937832640723248123)
XLA Ops:
  0.7 2.6 %shard_map.85 = bf16[128,4096]{1,0:T(8,128)(2,1)} custom-call(bf16[128,8192]{1,0:T(8,128)(2,1)} %refs_0_.1), custom_call_target="tpu_custom_call" | custom-call | bytes 2097152 | tf_op jit(solution)/shard_map/pallas_call | solution.py:63
  4.3 2.6 %collective-permute-start.6 = (bf16[128,4096]{1,0:T(8,128)(2,1)}, bf16[128,4096]{1,0:T(8,128)(2,1)S(1)}, u32[]{:S(2)}, u32[]{:S(2)}) collective-permute-start(bf16[128,4096]{1,0:T(8,128)(2,1)} %shard_map.85), channel_id=1, source_target_pairs={{0,4},{4,0},{8,12},{12,8},{16,20},{20,16},{24,28},{28,24},{1,5},{5... | collective-permute-start | bytes 3145736 | tf_op jit(solution)/shard_map/ppermute | solution.py:25
  6.9 1.6 %collective-permute-start.2 = (bf16[128,1024]{1,0:T(8,128)(2,1)S(1)}, bf16[128,1024]{1,0:T(8,128)(2,1)S(1)}, u32[]{:S(2)}, u32[]{:S(2)}) collective-permute-start(bf16[128,1024]{1,0:T(8,128)(2,1)S(1)} %copy-done.1), channel_id=1, source_target_pairs={{0,8},{4,12},{8,0},{12,4},{16,24},{20,28},{24,16},{28,20},{1,9},{5... | collective-permute-start | bytes 786440 | tf_op jit(solution)/shard_map/ppermute | solution.py:25
  9.9 2.6 %collective-permute-start.1 = (bf16[128,1024]{1,0:T(8,128)(2,1)S(1)}, bf16[128,1024]{1,0:T(8,128)(2,1)S(1)}, u32[]{:S(2)}, u32[]{:S(2)}) collective-permute-start(bf16[128,1024]{1,0:T(8,128)(2,1)S(1)} %copy-done.1), channel_id=1, source_target_pairs={{0,16},{4,20},{8,24},{12,28},{16,0},{20,4},{24,8},{28,12},{1,17},{... | collective-permute-start | bytes 786440 | tf_op jit(solution)/shard_map/ppermute | solution.py:25
  12.5 7.0 %collective-permute-done.2.refs_4_.refs_3_ = bf16[128,1024]{1,0:T(8,128)(2,1)S(1)} collective-permute-done((bf16[128,1024]{1,0:T(8,128)(2,1)S(1)}, bf16[128,1024]{1,0:T(8,128)(2,1)S(1)}, u32[]{:S(2)}, u32[]{:S(2)}) %collective-permute-start.2) | collective-permute-done | bytes 262176 | tf_op jit(solution)/shard_map/ppermute | solution.py:25
  19.5 2.5 %collective-permute-start.7 = (bf16[128,1024]{1,0:T(8,128)(2,1)S(1)}, bf16[128,1024]{1,0:T(8,128)(2,1)S(1)}, u32[]{:S(2)}, u32[]{:S(2)}) collective-permute-start(bf16[128,1024]{1,0:T(8,128)(2,1)S(1)} %collective-permute-done.2.refs_4_.refs_3_), channel_id=1, source_target_pairs={{0,2},{1,3},{2,0},{3,1},{4,6},{5,7},{6,4},{7,5},{8,10},{9,11},{10,... | collective-permute-start | bytes 786440 | tf_op jit(solution)/shard_map/ppermute | solution.py:25
  22.0 2.3 %collective-permute-done.1.refs_5_.refs_4_ = bf16[128,1024]{1,0:T(8,128)(2,1)S(1)} collective-permute-done((bf16[128,1024]{1,0:T(8,128)(2,1)S(1)}, bf16[128,1024]{1,0:T(8,128)(2,1)S(1)}, u32[]{:S(2)}, u32[]{:S(2)}) %collective-permute-start.1) | collective-permute-done | bytes 262176 | tf_op jit(solution)/shard_map/ppermute | solution.py:25
  25.0 4.1 %collective-permute-done.7.refs_6_ = bf16[128,1024]{1,0:T(8,128)(2,1)S(1)} collective-permute-done((bf16[128,1024]{1,0:T(8,128)(2,1)S(1)}, bf16[128,1024]{1,0:T(8,128)(2,1)S(1)}, u32[]{:S(2)}, u32[]{:S(2)}) %collective-permute-start.7) | collective-permute-done | bytes 262176 | tf_op jit(solution)/shard_map/ppermute | solution.py:25
  29.2 1.6 %collective-permute-done.6.refs_0_.refs_3_.refs_2_ = bf16[128,4096]{1,0:T(8,128)(2,1)S(1)} collective-permute-done((bf16[128,4096]{1,0:T(8,128)(2,1)}, bf16[128,4096]{1,0:T(8,128)(2,1)S(1)}, u32[]{:S(2)}, u32[]{:S(2)}) %collective-permute-start.6) | collective-permute-done | bytes 1048608 | tf_op jit(solution)/shard_map/ppermute | solution.py:25
  30.8 2.6 %collective-permute-done.4.refs_7_ = bf16[128,1024]{1,0:T(8,128)(2,1)S(1)} collective-permute-done((bf16[128,1024]{1,0:T(8,128)(2,1)S(1)}, bf16[128,1024]{1,0:T(8,128)(2,1)S(1)}, u32[]{:S(2)}, u32[]{:S(2)}) %collective-permute-start.4) | collective-permute-done | bytes 262176 | tf_op jit(solution)/shard_map/ppermute | solution.py:25
  35.5 1.7 %collective-permute-start.9 = (bf16[128,1024]{1,0:T(8,128)(2,1)S(1)}, bf16[128,1024]{1,0:T(8,128)(2,1)S(1)}, u32[]{:S(2)}, u32[]{:S(2)}) collective-permute-start(bf16[128,1024]{1,0:T(8,128)(2,1)S(1)} %collective-permute-done.5.refs_6_.refs_5_), channel_id=1, source_target_pairs={{0,2},{1,3},{2,0},{3,1},{4,6},{5,7},{6,4},{7,5},{8,10},{9,11},{10,... | collective-permute-start | bytes 786440 | tf_op jit(solution)/shard_map/ppermute | solution.py:25
  37.2 4.4 %collective-permute-done.11 = f32[320,128]{1,0:T(8,128)S(1)} collective-permute-done((f32[320,128]{1,0:T(8,128)S(1)}, f32[320,128]{1,0:T(8,128)S(1)}, u32[]{:S(2)}, u32[]{:S(2)}) %collective-permute-start.11) | collective-permute-done | bytes 163872 | tf_op jit(solution)/shard_map/ppermute | solution.py:25
  41.6 2.3 %collective-permute-done.9.refs_8_ = bf16[128,1024]{1,0:T(8,128)(2,1)S(1)} collective-permute-done((bf16[128,1024]{1,0:T(8,128)(2,1)S(1)}, bf16[128,1024]{1,0:T(8,128)(2,1)S(1)}, u32[]{:S(2)}, u32[]{:S(2)}) %collective-permute-start.9) | collective-permute-done | bytes 262176 | tf_op jit(solution)/shard_map/ppermute | solution.py:25
  44.6 1.6 %collective-permute-start.10 = (f32[256,128]{1,0:T(8,128)S(1)}, f32[256,128]{1,0:T(8,128)S(1)}, u32[]{:S(2)}, u32[]{:S(2)}) collective-permute-start(f32[256,128]{1,0:T(8,128)S(1)} %shard_map.89), channel_id=1, source_target_pairs={{0,4},{4,0},{8,12},{12,8},{16,20},{20,16},{24,28},{28,24},{1,5},{5... | collective-permute-start | bytes 393224 | tf_op jit(solution)/shard_map/ppermute | solution.py:25
  46.2 1.6 %shard_map.90 = f32[576,128]{1,0:T(8,128)S(1)} custom-call(bf16[128,4096]{1,0:T(8,128)(2,1)S(1)} %shard_map.86.refs_0_, bf16[128,4096]{1,0:T(8,128)(2,1)S(1)} %collective-permute-done.refs_1_, bf16[64,4096]{1,0:T(8,128)(2,1)S(1)} %shard_map.87.refs_2_, bf16[128,4096]{1,0:T(8,128)(2,1)S(1)} %collective-permute-done.6.refs_0_.refs_3_.refs_2_, ...), custom_call_target="tpu_custom_call" | custom-call | flops 603979776 | bytes 6062080 | tf_op jit(solution)/shard_map/pallas_call | solution.py:95
  49.3 2.9 %collective-permute-done.16 = bf16[64,64]{1,0:T(8,128)(2,1)S(1)} collective-permute-done((bf16[64,64]{1,0:T(8,128)(2,1)S(1)}, bf16[64,64]{1,0:T(8,128)(2,1)S(1)}, u32[]{:S(2)}, u32[]{:S(2)}) %collective-permute-start.16) | collective-permute-done | bytes 8224 | tf_op jit(solution)/shard_map/ppermute | solution.py:25
  53.5 3.6 %collective-permute-done.17 = bf16[128,64]{1,0:T(8,128)(2,1)S(1)} collective-permute-done((bf16[128,64]{1,0:T(8,128)(2,1)S(1)}, bf16[128,64]{1,0:T(8,128)(2,1)S(1)}, u32[]{:S(2)}, u32[]{:S(2)}) %collective-permute-start.17) | collective-permute-done | bytes 16416 | tf_op jit(solution)/shard_map/ppermute | solution.py:25
  57.1 1.5 %collective-permute-start.18 = (bf16[256,64]{1,0:T(8,128)(2,1)S(1)}, bf16[256,64]{1,0:T(8,128)(2,1)S(1)}, u32[]{:S(2)}, u32[]{:S(2)}) collective-permute-start(bf16[256,64]{1,0:T(8,128)(2,1)S(1)} %pad_maximum_fusion.3), channel_id=1, source_target_pairs={{0,4},{4,0},{8,12},{12,8},{16,20},{20,16},{24,28},{28,24},{1,5},{5... | collective-permute-start | bytes 98312 | tf_op jit(solution)/shard_map/ppermute | solution.py:25
  58.6 2.8 %collective-permute-done.18 = bf16[256,64]{1,0:T(8,128)(2,1)S(1)} collective-permute-done((bf16[256,64]{1,0:T(8,128)(2,1)S(1)}, bf16[256,64]{1,0:T(8,128)(2,1)S(1)}, u32[]{:S(2)}, u32[]{:S(2)}) %collective-permute-start.18) | collective-permute-done | bytes 32800 | tf_op jit(solution)/shard_map/ppermute | solution.py:25
  61.7 1.8 %collective-permute-start.13 = (f32[4,256]{1,0:T(4,128)S(1)}, f32[4,256]{1,0:T(4,128)S(1)}, u32[]{:S(2)}, u32[]{:S(2)}) collective-permute-start(f32[4,256]{1,0:T(4,128)S(1)} %maximum_maximum_fusion), channel_id=1, source_target_pairs={{0,2},{1,3},{2,0},{3,1},{4,6},{5,7},{6,4},{7,5},{8,10},{9,11},{10,... | collective-permute-start | bytes 12296 | tf_op jit(solution)/shard_map/ppermute | solution.py:25
  63.9 1.5 %collective-permute-done.13 = f32[4,256]{1,0:T(4,128)S(1)} collective-permute-done((f32[4,256]{1,0:T(4,128)S(1)}, f32[4,256]{1,0:T(4,128)S(1)}, u32[]{:S(2)}, u32[]{:S(2)}) %collective-permute-start.13) | collective-permute-done | bytes 4128 | tf_op jit(solution)/shard_map/ppermute | solution.py:25
  65.7 3.4 %collective-permute-done.14 = f32[2,256]{1,0:T(2,128)S(1)} collective-permute-done((f32[2,256]{1,0:T(2,128)S(1)}, f32[2,256]{1,0:T(2,128)S(1)}, u32[]{:S(2)}, u32[]{:S(2)}) %collective-permute-start.14) | collective-permute-done | bytes 2080 | tf_op jit(solution)/shard_map/ppermute | solution.py:25
  70.4 3.3 %collective-permute-done.15 = f32[2,256]{1,0:T(2,128)S(1)} collective-permute-done((f32[2,256]{1,0:T(2,128)S(1)}, f32[2,256]{1,0:T(2,128)S(1)}, u32[]{:S(2)}, u32[]{:S(2)}) %collective-permute-start.15) | collective-permute-done | bytes 2080 | tf_op jit(solution)/shard_map/ppermute | solution.py:25
  74.6 1.8 %collective-permute-start.19 = (bf16[128,1024]{1,0:T(8,128)(2,1)S(1)}, bf16[128,1024]{1,0:T(8,128)(2,1)S(1)}, u32[]{:S(2)}, u32[]{:S(2)}) collective-permute-start(bf16[128,1024]{1,0:T(8,128)(2,1)S(1)} %convolution_convert_fusion.2), channel_id=1, source_target_pairs={{0,2},{1,3},{2,0},{3,1},{4,6},{5,7},{6,4},{7,5},{8,10},{9,11},{10,... | collective-permute-start | bytes 786440 | tf_op jit(solution)/shard_map/ppermute | solution.py:25
  77.4 6.3 %collective-permute-done.19 = bf16[128,1024]{1,0:T(8,128)(2,1)S(1)} collective-permute-done((bf16[128,1024]{1,0:T(8,128)(2,1)S(1)}, bf16[128,1024]{1,0:T(8,128)(2,1)S(1)}, u32[]{:S(2)}, u32[]{:S(2)}) %collective-permute-start.19) | collective-permute-done | bytes 262176 | tf_op jit(solution)/shard_map/ppermute | solution.py:25
  84.7 1.9 %collective-permute-done.20 = bf16[128,1024]{1,0:T(8,128)(2,1)S(1)} collective-permute-done((bf16[128,1024]{1,0:T(8,128)(2,1)S(1)}, bf16[128,1024]{1,0:T(8,128)(2,1)S(1)}, u32[]{:S(2)}, u32[]{:S(2)}) %collective-permute-start.20) | collective-permute-done | bytes 262176 | tf_op jit(solution)/shard_map/ppermute | solution.py:25
  87.3 1.6 %collective-permute-start.22 = (bf16[128,1024]{1,0:T(8,128)(2,1)S(1)}, bf16[128,1024]{1,0:T(8,128)(2,1)S(1)}, u32[]{:S(2)}, u32[]{:S(2)}) collective-permute-start(bf16[128,1024]{1,0:T(8,128)(2,1)S(1)} %convolution_convert_fusion), channel_id=1, source_target_pairs={{0,2},{1,3},{2,0},{3,1},{4,6},{5,7},{6,4},{7,5},{8,10},{9,11},{10,... | collective-permute-start | bytes 786440 | tf_op jit(solution)/shard_map/ppermute | solution.py:25
  89.9 5.2 %collective-permute-done.22 = bf16[128,1024]{1,0:T(8,128)(2,1)S(1)} collective-permute-done((bf16[128,1024]{1,0:T(8,128)(2,1)S(1)}, bf16[128,1024]{1,0:T(8,128)(2,1)S(1)}, u32[]{:S(2)}, u32[]{:S(2)}) %collective-permute-start.22) | collective-permute-done | bytes 262176 | tf_op jit(solution)/shard_map/ppermute | solution.py:25
  95.4 2.0 %collective-permute-start.24 = (bf16[128,1024]{1,0:T(8,128)(2,1)S(1)}, bf16[128,1024]{1,0:T(8,128)(2,1)S(1)}, u32[]{:S(2)}, u32[]{:S(2)}) collective-permute-start(bf16[128,1024]{1,0:T(8,128)(2,1)S(1)} %fusion.7), channel_id=1, source_target_pairs={{0,8},{4,12},{8,0},{12,4},{16,24},{20,28},{24,16},{28,20},{1,9},{5... | collective-permute-start | bytes 786440 | tf_op jit(solution)/shard_map/ppermute | solution.py:25
  97.4 2.5 %collective-permute-start.27 = (bf16[64,1088]{1,0:T(8,128)(2,1)S(1)}, bf16[64,1088]{1,0:T(8,128)(2,1)S(1)}, u32[]{:S(2)}, u32[]{:S(2)}) collective-permute-start(bf16[64,1088]{1,0:T(8,128)(2,1)S(1)} %convert_element_type.111), channel_id=1, source_target_pairs={{0,2},{1,3},{2,0},{3,1},{4,6},{5,7},{6,4},{7,5},{8,10},{9,11},{10,... | collective-permute-start | bytes 417800 | tf_op jit(solution)/shard_map/ppermute | solution.py:25
  101.4 1.7 %collective-permute-done.27 = bf16[64,1088]{1,0:T(8,128)(2,1)S(1)} collective-permute-done((bf16[64,1088]{1,0:T(8,128)(2,1)S(1)}, bf16[64,1088]{1,0:T(8,128)(2,1)S(1)}, u32[]{:S(2)}, u32[]{:S(2)}) %collective-permute-start.27) | collective-permute-done | bytes 139296 | tf_op jit(solution)/shard_map/ppermute | solution.py:25
  104.5 5.6 %collective-permute-done.25 = bf16[128,1024]{1,0:T(8,128)(2,1)S(1)} collective-permute-done((bf16[128,1024]{1,0:T(8,128)(2,1)S(1)}, bf16[128,1024]{1,0:T(8,128)(2,1)S(1)}, u32[]{:S(2)}, u32[]{:S(2)}) %collective-permute-start.25) | collective-permute-done | bytes 262176 | tf_op jit(solution)/shard_map/ppermute | solution.py:25
  (102 shorter events, 19.9 us)
Async XLA Ops:
  0.7 32.8 %copy-start.4 = (s32[128]{0:T(128)S(1)}, s32[128]{0:T(128)}, u32[]{:S(2)}) copy-start(s32[128]{0:T(128)} %param.10) | copy-start | bytes 1540
  0.7 32.8 %copy-start.5 = (s32[128]{0:T(128)S(1)}, s32[128]{0:T(128)}, u32[]{:S(2)}) copy-start(s32[128]{0:T(128)} %param.11) | copy-start | bytes 1540
  0.7 32.8 %copy-start.2 = (bf16[64,8192]{1,0:T(8,128)(2,1)S(1)}, bf16[64,8192]{1,0:T(8,128)(2,1)}, u32[]{:S(2)}) copy-start(bf16[64,8192]{1,0:T(8,128)(2,1)} %refs_0_.2) | copy-start | bytes 3145732
  3.7 20.6 %collective-permute-start = (bf16[128,4096]{1,0:T(8,128)(2,1)S(1)}, bf16[128,4096]{1,0:T(8,128)(2,1)S(1)}, u32[]{:S(2)}, u32[]{:S(2)}) collective-permute-start(bf16[128,4096]{1,0:T(8,128)(2,1)S(1)} %shard_map.86.refs_0_), channel_id=1, source_target_pairs={{0,1},{1,0},{2,3},{3,2},{4,5},{5,4},{6,7},{7,6},{8,9},{9,8},{10,11... | collective-permute-start | bytes 3145736 | tf_op jit(solution)/shard_map/ppermute | solution.py:25
  4.3 26.6 %collective-permute-start.6 = (bf16[128,4096]{1,0:T(8,128)(2,1)}, bf16[128,4096]{1,0:T(8,128)(2,1)S(1)}, u32[]{:S(2)}, u32[]{:S(2)}) collective-permute-start(bf16[128,4096]{1,0:T(8,128)(2,1)} %shard_map.85), channel_id=1, source_target_pairs={{0,4},{4,0},{8,12},{12,8},{16,20},{20,16},{24,28},{28,24},{1,5},{5... | collective-permute-start | bytes 3145736 | tf_op jit(solution)/shard_map/ppermute | solution.py:25
  6.9 12.7 %collective-permute-start.2 = (bf16[128,1024]{1,0:T(8,128)(2,1)S(1)}, bf16[128,1024]{1,0:T(8,128)(2,1)S(1)}, u32[]{:S(2)}, u32[]{:S(2)}) collective-permute-start(bf16[128,1024]{1,0:T(8,128)(2,1)S(1)} %copy-done.1), channel_id=1, source_target_pairs={{0,8},{4,12},{8,0},{12,4},{16,24},{20,28},{24,16},{28,20},{1,9},{5... | collective-permute-start | bytes 786440 | tf_op jit(solution)/shard_map/ppermute | solution.py:25
  8.4 13.5 %collective-permute-start.3 = (bf16[128,1024]{1,0:T(8,128)(2,1)S(1)}, bf16[128,1024]{1,0:T(8,128)(2,1)S(1)}, u32[]{:S(2)}, u32[]{:S(2)}) collective-permute-start(bf16[128,1024]{1,0:T(8,128)(2,1)S(1)} %copy-done.1), channel_id=1, source_target_pairs={{0,2},{1,3},{2,0},{3,1},{4,6},{5,7},{6,4},{7,5},{8,10},{9,11},{10,... | collective-permute-start | bytes 786440 | tf_op jit(solution)/shard_map/ppermute | solution.py:25
  9.9 14.4 %collective-permute-start.1 = (bf16[128,1024]{1,0:T(8,128)(2,1)S(1)}, bf16[128,1024]{1,0:T(8,128)(2,1)S(1)}, u32[]{:S(2)}, u32[]{:S(2)}) collective-permute-start(bf16[128,1024]{1,0:T(8,128)(2,1)S(1)} %copy-done.1), channel_id=1, source_target_pairs={{0,16},{4,20},{8,24},{12,28},{16,0},{20,4},{24,8},{28,12},{1,17},{... | collective-permute-start | bytes 786440 | tf_op jit(solution)/shard_map/ppermute | solution.py:25
  19.5 9.7 %collective-permute-start.7 = (bf16[128,1024]{1,0:T(8,128)(2,1)S(1)}, bf16[128,1024]{1,0:T(8,128)(2,1)S(1)}, u32[]{:S(2)}, u32[]{:S(2)}) collective-permute-start(bf16[128,1024]{1,0:T(8,128)(2,1)S(1)} %collective-permute-done.2.refs_4_.refs_3_), channel_id=1, source_target_pairs={{0,2},{1,3},{2,0},{3,1},{4,6},{5,7},{6,4},{7,5},{8,10},{9,11},{10,... | collective-permute-start | bytes 786440 | tf_op jit(solution)/shard_map/ppermute | solution.py:25
  24.3 9.1 %collective-permute-start.4 = (bf16[128,1024]{1,0:T(8,128)(2,1)S(1)}, bf16[128,1024]{1,0:T(8,128)(2,1)S(1)}, u32[]{:S(2)}, u32[]{:S(2)}) collective-permute-start(bf16[128,1024]{1,0:T(8,128)(2,1)S(1)} %collective-permute-done.1.refs_5_.refs_4_), channel_id=1, source_target_pairs={{0,2},{1,3},{2,0},{3,1},{4,6},{5,7},{6,4},{7,5},{8,10},{9,11},{10,... | collective-permute-start | bytes 786440 | tf_op jit(solution)/shard_map/ppermute | solution.py:25
  24.8 8.6 %collective-permute-start.5 = (bf16[128,1024]{1,0:T(8,128)(2,1)S(1)}, bf16[128,1024]{1,0:T(8,128)(2,1)S(1)}, u32[]{:S(2)}, u32[]{:S(2)}) collective-permute-start(bf16[128,1024]{1,0:T(8,128)(2,1)S(1)} %collective-permute-done.1.refs_5_.refs_4_), channel_id=1, source_target_pairs={{0,8},{4,12},{8,0},{12,4},{16,24},{20,28},{24,16},{28,20},{1,9},{5... | collective-permute-start | bytes 786440 | tf_op jit(solution)/shard_map/ppermute | solution.py:25
  33.4 10.5 %collective-permute-start.8 = (bf16[128,4096]{1,0:T(8,128)(2,1)S(1)}, bf16[128,4096]{1,0:T(8,128)(2,1)S(1)}, u32[]{:S(2)}, u32[]{:S(2)}) collective-permute-start(bf16[128,4096]{1,0:T(8,128)(2,1)S(1)} %collective-permute-done.6.refs_0_.refs_3_.refs_2_), channel_id=1, source_target_pairs={{0,1},{1,0},{2,3},{3,2},{4,5},{5,4},{6,7},{7,6},{8,9},{9,8},{10,11... | collective-permute-start | bytes 3145736 | tf_op jit(solution)/shard_map/ppermute | solution.py:25
  34.9 6.7 %collective-permute-start.11 = (f32[320,128]{1,0:T(8,128)S(1)}, f32[320,128]{1,0:T(8,128)S(1)}, u32[]{:S(2)}, u32[]{:S(2)}) collective-permute-start(f32[320,128]{1,0:T(8,128)S(1)} %shard_map.88), channel_id=1, source_target_pairs={{0,4},{4,0},{8,12},{12,8},{16,20},{20,16},{24,28},{28,24},{1,5},{5... | collective-permute-start | bytes 491528 | tf_op jit(solution)/shard_map/ppermute | solution.py:25
  35.5 8.4 %collective-permute-start.9 = (bf16[128,1024]{1,0:T(8,128)(2,1)S(1)}, bf16[128,1024]{1,0:T(8,128)(2,1)S(1)}, u32[]{:S(2)}, u32[]{:S(2)}) collective-permute-start(bf16[128,1024]{1,0:T(8,128)(2,1)S(1)} %collective-permute-done.5.refs_6_.refs_5_), channel_id=1, source_target_pairs={{0,2},{1,3},{2,0},{3,1},{4,6},{5,7},{6,4},{7,5},{8,10},{9,11},{10,... | collective-permute-start | bytes 786440 | tf_op jit(solution)/shard_map/ppermute | solution.py:25
  41.6 6.8 %copy-start.3 = (bf16[64,64]{1,0:T(8,128)(2,1)S(1)}, bf16[64,64]{1,0:T(8,128)(2,1)}, u32[]{:S(2)}) copy-start(bf16[64,64]{1,0:T(8,128)(2,1)} %param.8) | copy-start | bytes 24580
  44.6 16.8 %collective-permute-start.10 = (f32[256,128]{1,0:T(8,128)S(1)}, f32[256,128]{1,0:T(8,128)S(1)}, u32[]{:S(2)}, u32[]{:S(2)}) collective-permute-start(f32[256,128]{1,0:T(8,128)S(1)} %shard_map.89), channel_id=1, source_target_pairs={{0,4},{4,0},{8,12},{12,8},{16,20},{20,16},{24,28},{28,24},{1,5},{5... | collective-permute-start | bytes 393224 | tf_op jit(solution)/shard_map/ppermute | solution.py:25
  47.8 13.8 %collective-permute-start.12 = (f32[576,128]{1,0:T(8,128)S(1)}, f32[576,128]{1,0:T(8,128)S(1)}, u32[]{:S(2)}, u32[]{:S(2)}) collective-permute-start(f32[576,128]{1,0:T(8,128)S(1)} %shard_map.90), channel_id=1, source_target_pairs={{0,4},{4,0},{8,12},{12,8},{16,20},{20,16},{24,28},{28,24},{1,5},{5... | collective-permute-start | bytes 884744 | tf_op jit(solution)/shard_map/ppermute | solution.py:25
  48.4 3.7 %collective-permute-start.16 = (bf16[64,64]{1,0:T(8,128)(2,1)S(1)}, bf16[64,64]{1,0:T(8,128)(2,1)S(1)}, u32[]{:S(2)}, u32[]{:S(2)}) collective-permute-start(bf16[64,64]{1,0:T(8,128)(2,1)S(1)} %copy-done.3), channel_id=1, source_target_pairs={{0,8},{4,12},{8,0},{12,4},{16,24},{20,28},{24,16},{28,20},{1,9},{5... | collective-permute-start | bytes 24584 | tf_op jit(solution)/shard_map/ppermute | solution.py:25
  52.1 4.9 %collective-permute-start.17 = (bf16[128,64]{1,0:T(8,128)(2,1)S(1)}, bf16[128,64]{1,0:T(8,128)(2,1)S(1)}, u32[]{:S(2)}, u32[]{:S(2)}) collective-permute-start(bf16[128,64]{1,0:T(8,128)(2,1)S(1)} %pad_maximum_fusion.4), channel_id=1, source_target_pairs={{0,16},{4,20},{8,24},{12,28},{16,0},{20,4},{24,8},{28,12},{1,17},{... | collective-permute-start | bytes 49160 | tf_op jit(solution)/shard_map/ppermute | solution.py:25
  57.1 4.3 %collective-permute-start.18 = (bf16[256,64]{1,0:T(8,128)(2,1)S(1)}, bf16[256,64]{1,0:T(8,128)(2,1)S(1)}, u32[]{:S(2)}, u32[]{:S(2)}) collective-permute-start(bf16[256,64]{1,0:T(8,128)(2,1)S(1)} %pad_maximum_fusion.3), channel_id=1, source_target_pairs={{0,4},{4,0},{8,12},{12,8},{16,20},{20,16},{24,28},{28,24},{1,5},{5... | collective-permute-start | bytes 98312 | tf_op jit(solution)/shard_map/ppermute | solution.py:25
  61.7 3.7 %collective-permute-start.13 = (f32[4,256]{1,0:T(4,128)S(1)}, f32[4,256]{1,0:T(4,128)S(1)}, u32[]{:S(2)}, u32[]{:S(2)}) collective-permute-start(f32[4,256]{1,0:T(4,128)S(1)} %maximum_maximum_fusion), channel_id=1, source_target_pairs={{0,2},{1,3},{2,0},{3,1},{4,6},{5,7},{6,4},{7,5},{8,10},{9,11},{10,... | collective-permute-start | bytes 12296 | tf_op jit(solution)/shard_map/ppermute | solution.py:25
  65.5 3.7 %collective-permute-start.14 = (f32[2,256]{1,0:T(2,128)S(1)}, f32[2,256]{1,0:T(2,128)S(1)}, u32[]{:S(2)}, u32[]{:S(2)}) collective-permute-start(f32[2,256]{1,0:T(2,128)S(1)} %pad_maximum_fusion.5), channel_id=1, source_target_pairs={{0,8},{4,12},{8,0},{12,4},{16,24},{20,28},{24,16},{28,20},{1,9},{5... | collective-permute-start | bytes 6152 | tf_op jit(solution)/shard_map/ppermute | solution.py:25
  69.1 4.5 %collective-permute-start.15 = (f32[2,256]{1,0:T(2,128)S(1)}, f32[2,256]{1,0:T(2,128)S(1)}, u32[]{:S(2)}, u32[]{:S(2)}) collective-permute-start(f32[2,256]{1,0:T(2,128)S(1)} %pad_maximum_fusion.6), channel_id=1, source_target_pairs={{0,16},{4,20},{8,24},{12,28},{16,0},{20,4},{24,8},{28,12},{1,17},{... | collective-permute-start | bytes 6152 | tf_op jit(solution)/shard_map/ppermute | solution.py:25
  74.6 9.1 %collective-permute-start.19 = (bf16[128,1024]{1,0:T(8,128)(2,1)S(1)}, bf16[128,1024]{1,0:T(8,128)(2,1)S(1)}, u32[]{:S(2)}, u32[]{:S(2)}) collective-permute-start(bf16[128,1024]{1,0:T(8,128)(2,1)S(1)} %convolution_convert_fusion.2), channel_id=1, source_target_pairs={{0,2},{1,3},{2,0},{3,1},{4,6},{5,7},{6,4},{7,5},{8,10},{9,11},{10,... | collective-permute-start | bytes 786440 | tf_op jit(solution)/shard_map/ppermute | solution.py:25
  76.7 9.8 %collective-permute-start.20 = (bf16[128,1024]{1,0:T(8,128)(2,1)S(1)}, bf16[128,1024]{1,0:T(8,128)(2,1)S(1)}, u32[]{:S(2)}, u32[]{:S(2)}) collective-permute-start(bf16[128,1024]{1,0:T(8,128)(2,1)S(1)} %convolution_convert_fusion.1), channel_id=1, source_target_pairs={{0,2},{1,3},{2,0},{3,1},{4,6},{5,7},{6,4},{7,5},{8,10},{9,11},{10,... | collective-permute-start | bytes 786440 | tf_op jit(solution)/shard_map/ppermute | solution.py:25
  86.9 8.5 %collective-permute-start.23 = (bf16[128,1024]{1,0:T(8,128)(2,1)S(1)}, bf16[128,1024]{1,0:T(8,128)(2,1)S(1)}, u32[]{:S(2)}, u32[]{:S(2)}) collective-permute-start(bf16[128,1024]{1,0:T(8,128)(2,1)S(1)} %fusion.6), channel_id=1, source_target_pairs={{0,8},{4,12},{8,0},{12,4},{16,24},{20,28},{24,16},{28,20},{1,9},{5... | collective-permute-start | bytes 786440 | tf_op jit(solution)/shard_map/ppermute | solution.py:25
  87.3 7.8 %collective-permute-start.22 = (bf16[128,1024]{1,0:T(8,128)(2,1)S(1)}, bf16[128,1024]{1,0:T(8,128)(2,1)S(1)}, u32[]{:S(2)}, u32[]{:S(2)}) collective-permute-start(bf16[128,1024]{1,0:T(8,128)(2,1)S(1)} %convolution_convert_fusion), channel_id=1, source_target_pairs={{0,2},{1,3},{2,0},{3,1},{4,6},{5,7},{6,4},{7,5},{8,10},{9,11},{10,... | collective-permute-start | bytes 786440 | tf_op jit(solution)/shard_map/ppermute | solution.py:25
  89.1 8.3 %collective-permute-start.26 = (f32[64,1088]{1,0:T(8,128)S(1)}, f32[64,1088]{1,0:T(8,128)S(1)}, u32[]{:S(2)}, u32[]{:S(2)}) collective-permute-start(f32[64,1088]{1,0:T(8,128)S(1)} %pad_maximum_fusion), channel_id=1, source_target_pairs={{0,1},{1,0},{2,3},{3,2},{4,5},{5,4},{6,7},{7,6},{8,9},{9,8},{10,11... | collective-permute-start | bytes 835592 | tf_op jit(solution)/shard_map/ppermute | solution.py:25
  89.4 15.1 %collective-permute-start.21 = (bf16[128,1024]{1,0:T(8,128)(2,1)S(1)}, bf16[128,1024]{1,0:T(8,128)(2,1)S(1)}, u32[]{:S(2)}, u32[]{:S(2)}) collective-permute-start(bf16[128,1024]{1,0:T(8,128)(2,1)S(1)} %convolution_convert_fusion.3), channel_id=1, source_target_pairs={{0,2},{1,3},{2,0},{3,1},{4,6},{5,7},{6,4},{7,5},{8,10},{9,11},{10,... | collective-permute-start | bytes 786440 | tf_op jit(solution)/shard_map/ppermute | solution.py:25
  95.4 9.1 %collective-permute-start.24 = (bf16[128,1024]{1,0:T(8,128)(2,1)S(1)}, bf16[128,1024]{1,0:T(8,128)(2,1)S(1)}, u32[]{:S(2)}, u32[]{:S(2)}) collective-permute-start(bf16[128,1024]{1,0:T(8,128)(2,1)S(1)} %fusion.7), channel_id=1, source_target_pairs={{0,8},{4,12},{8,0},{12,4},{16,24},{20,28},{24,16},{28,20},{1,9},{5... | collective-permute-start | bytes 786440 | tf_op jit(solution)/shard_map/ppermute | solution.py:25
  97.4 5.7 %collective-permute-start.27 = (bf16[64,1088]{1,0:T(8,128)(2,1)S(1)}, bf16[64,1088]{1,0:T(8,128)(2,1)S(1)}, u32[]{:S(2)}, u32[]{:S(2)}) collective-permute-start(bf16[64,1088]{1,0:T(8,128)(2,1)S(1)} %convert_element_type.111), channel_id=1, source_target_pairs={{0,2},{1,3},{2,0},{3,1},{4,6},{5,7},{6,4},{7,5},{8,10},{9,11},{10,... | collective-permute-start | bytes 417800 | tf_op jit(solution)/shard_map/ppermute | solution.py:25
  100.3 9.7 %collective-permute-start.25 = (bf16[128,1024]{1,0:T(8,128)(2,1)S(1)}, bf16[128,1024]{1,0:T(8,128)(2,1)S(1)}, u32[]{:S(2)}, u32[]{:S(2)}) collective-permute-start(bf16[128,1024]{1,0:T(8,128)(2,1)S(1)} %fusion.5), channel_id=1, source_target_pairs={{0,16},{4,20},{8,24},{12,28},{16,0},{20,4},{24,8},{28,12},{1,17},{... | collective-permute-start | bytes 786440 | tf_op jit(solution)/shard_map/ppermute | solution.py:25
  (2 other events, 8.9 us)

commit v9 on v8

--- a/solution.py
+++ b/solution.py
@@ -44,7 +44,7 @@
 in_vmem = pl.BlockSpec(memory_space=pltpu.VMEM)
 
 
-def copy_blocks(shapes, moves, *arrays, source=pltpu.HBM, limit=12):
+def copy_blocks(shapes, moves, *arrays, source=pltpu.HBM):
     def kernel(*refs):
         ins, outs, sems = refs[: len(arrays)], refs[len(arrays) : -1], refs[-1]
         copies = []
@@ -66,17 +66,19 @@
         in_specs=[pl.BlockSpec(memory_space=source)] * len(arrays),
         out_specs=[in_vmem] * len(shapes),
         scratch_shapes=[pltpu.SemaphoreType.DMA((32,))],
-        compiler_params=pltpu.CompilerParams(vmem_limit_bytes=limit << 20),
+        compiler_params=pltpu.CompilerParams(vmem_limit_bytes=12 << 20),
         cost_estimate=pl.CostEstimate(flops=0, bytes_accessed=2 * size, transcendentals=0),
     )(*arrays)
 
 
-def logits_of(groups, tokens):
+def logits_of(groups, tokens, rider=None):
     toks, width = tokens[0].shape
     heights = [group[0].shape[0] for group in groups]
     total, depth = sum(heights), width * len(tokens)
     flat = [a for group in groups for a in group]
-    n_flat, n_all = len(flat), len(flat) + len(tokens)
+    riders = [] if rider is None else [rider]
+    extra = 0 if rider is None else rider.shape[0] // 2
+    n_flat, n_all = len(flat), len(flat) + len(tokens) + len(riders)
 
     def kernel(*refs):
         out = refs[n_all]
@@ -91,10 +93,13 @@
                 at, column = at + 1, column + part.shape[1]
             out[row : row + height, :] = result
             row += height
+        if extra:
+            wide = refs[n_all - 1][...].astype(f32)
+            out[row:, :] = jnp.concatenate([wide[:extra], wide[extra:]], axis=1)
 
     return pl.pallas_call(
         kernel,
-        out_shape=jax.ShapeDtypeStruct((total, toks), f32),
+        out_shape=jax.ShapeDtypeStruct((total + extra, toks), f32),
         in_specs=[in_vmem] * n_all,
         out_specs=in_vmem,
         compiler_params=pltpu.CompilerParams(vmem_limit_bytes=12 << 20),
@@ -103,7 +108,7 @@
             bytes_accessed=2 * (total + toks) * depth + 4 * total * toks,
             transcendentals=0,
         ),
-    )(*flat, *tokens)
+    )(*flat, *tokens, *riders)
 
 
 def on_few(hidden, head, factor_rows, factor_basis, targets, loss_mask):
@@ -129,7 +134,7 @@
     def start_of(j, other):
         return (lax.axis_index("vocab") ^ (2 * j + other)) * width
 
-    cuts = [0, n_z]
+    cuts = [0, 1, n_z]
     chunks = [range(a, b) for a, b in zip(cuts, cuts[1:]) if a < b]
     sends = copy_blocks(
         [(rows, len(chunk) * width) for chunk in chunks],
@@ -139,35 +144,31 @@
             for j in chunk
         ],
         head,
-        limit=56,
-    )
-    beside = [swap_y(sends[0])]
+    )
+    beside = [swap_y(send) for send in sends]
 
     def half(array, after):
         array, _ = lax.optimization_barrier((array, after))
         moves = lambda: [(0, (start_of(j, 0), width), 0, 0, j * width) for j in range(n_z)]
         return copy_blocks([(array.shape[0], depth)], moves, array)[0]
 
-    kept = half(head, sends[0])
+    kept = half(head, beside[0])
     kept_core = swap_core(kept)
 
-    z_hidden, _ = lax.optimization_barrier((hidden, sends[0]))
-    x_hidden, _ = lax.optimization_barrier((hidden, sends[0]))
-    shards, cross = {0: hidden}, {0: swap_x(x_hidden)}
+    later, _ = lax.optimization_barrier((hidden, sends[0]))
+    shards, cross = {0: hidden}, {0: swap_x(later)}
     for bit in reversed(bits):
-        near = swap_z(z_hidden, bit)
+        near = swap_z(hidden if bit == bits[-1] else later, bit)
         for j in [j for j in shards if j]:
-            shards[j], *_ = lax.optimization_barrier((shards[j], near, cross[0], kept_core))
+            shards[j], *_ = lax.optimization_barrier((shards[j], near, beside[0]))
             shards[j ^ bit] = swap_z(shards[j], bit)
         shards[bit] = near
-    waits = []
-    for send, wait in zip(sends[1:], waits):
-        send, _ = lax.optimization_barrier((send, wait))
-        beside.append(swap_y(send))
     for j in range(1, n_z):
         sent = shards[j]
+        if j == 1:
+            sent, *_ = lax.optimization_barrier((sent, shards[n_z // 2]))
         if j > 1:
-            sent, *_ = lax.optimization_barrier((sent, cross[j - 2], kept_core))
+            sent, *_ = lax.optimization_barrier((sent, cross[j - 2]))
         cross[j] = swap_x(sent)
     basis_half = half(factor_basis, shards[n_z // 2])
 
@@ -180,10 +181,13 @@
     basis_ready, *_ = lax.optimization_barrier((basis_half, cross[n_z - 2], shards[n_z - 1]))
     upper = [[kept], [kept_core], [basis_ready]]
     upper_own = logits_of(upper, in_order(shards))
-    beside_core[-1], *_ = lax.optimization_barrier((beside_core[-1], upper_own, cross[n_z - 1]))
+    beside_core[-1], *_ = lax.optimization_barrier((beside_core[-1], upper_own))
     lower_own = logits_of([beside, beside_core], in_order(shards))
     cross[0], _ = lax.optimization_barrier((cross[0], lower_own))
-    both_cross = logits_of(upper + [beside, beside_core], in_order(cross))
+    rows_all, _ = lax.optimization_barrier((factor_rows, shards[n_z - 1]))
+    for bit in bits:
+        rows_all = jnp.concatenate([rows_all, swap_z(rows_all, bit)], axis=0)
+    both_cross = logits_of(upper + [beside, beside_core], in_order(cross), rows_all)
     n_up = 2 * rows + rank
 
     def add_over_y(up, low, up_came, low_came):
@@ -193,16 +197,16 @@
 
     upper_came, lower_came = swap_y(upper_own), swap_y(lower_own)
     cross_came = swap_y(both_cross)
+    upper_came, _ = lax.optimization_barrier((upper_came, both_cross))
     near_own, far_own, basis_own = add_over_y(upper_own, lower_own, upper_came, lower_came)
     near_cross, far_cross, basis_cross = add_over_y(
-        both_cross[:n_up], both_cross[n_up:], cross_came[:n_up], cross_came[n_up:]
+        both_cross[:n_up], both_cross[n_up : n_up + 2 * rows], cross_came[:n_up], cross_came[n_up : n_up + 2 * rows]
     )
     hidden_basis = jnp.concatenate([basis_own, basis_cross], axis=1)
 
-    rows_all, _ = lax.optimization_barrier((factor_rows, both_cross))
-    for bit in bits:
-        rows_all = jnp.concatenate([rows_all, swap_z(rows_all, bit)], axis=0)
-    rows_all = jnp.concatenate([rows_all, swap_y(rows_all)], axis=0)
+    n_rows = n_up + 2 * rows
+    rows_came = cross_came[n_rows:].astype(bf16)
+    rows_all = jnp.concatenate([rows_all, rows_came[:, :rank], rows_came[:, rank:]], axis=0)
 
     def merge(a, b):
         top = jnp.maximum(a[0], b[0])
@@ -371,6 +375,7 @@
     def on_device(hidden, head, factor_rows, *rest):
         even = [n & (n - 1) == 0 for n in (mesh.shape["vocab"], head.shape[0], factor_rows.shape[0])]
         few = 2 <= mesh.shape["vocab"] <= 16 and mesh.shape["tok"] == 4 and all(even)
+        few = few and hidden.shape[0] == 2 * factor_rows.shape[1]
         return (on_few if few else on_many)(hidden, head, factor_rows, *rest)
 
     return jax.shard_map(

time: 111 us -> 121 us (1.090)
  waiting for transfers between devices: 62.4 us -> 67.9 us
  starting transfers between devices: 33.1 us -> 37.4 us
  Pallas kernels: 7.3 us -> 5 us
  local copies, waits for them, and re-layouts: 1.41 us -> 3.08 us
    ppermute x28 -> x29, waiting for transfers between devices: 62.4 us -> 67.9 us  [swap(): return lax.ppermute(value, axis, [(i, i ^ bit) for i in range(size)])]
    ppermute x28 -> x29, starting transfers between devices: 33.1 us -> 37.4 us  [swap(): return lax.ppermute(value, axis, [(i, i ^ bit) for i in range(size)])]
    pallas_call x4, Pallas kernels: 3.99 us -> 1.71 us  [copy_blocks(): pl.pallas_call(kernel, out_shape=[jax.ShapeDtypeStruct(shape, bf16) for s...]
    unnamed x15 -> x16, local copies, waits for them, and re-layouts: 0.04 us -> 1.64 us
  transfers between devices with their start and end apart: 28 -> 29, of which waited for: 18 -> 16; matrix products, arithmetic and copies ran while one was open for 4% -> 4% of each run, Pallas kernels for 3% -> 4%
where the time goes in v9:
time: 121 us; the launch traced here: 120 us
  waiting for transfers between devices  67.9 us (56%)
  starting transfers between devices  37.4 us (31%)
  Pallas kernels  5 us (4%)
  matrix products  4.38 us (4%)
  local copies, waits for them, and re-layouts  3.08 us (3%)
  other arithmetic  1.53 us (1%)
    ppermute x29, waiting for transfers between devices, swap(): return lax.ppermute(value, axis, [(i, i ^ bit) for i in range(size)])  67.9 us
    ppermute x29, starting transfers between devices, swap(): return lax.ppermute(value, axis, [(i, i ^ bit) for i in range(size)])  37.4 us
    dot_general x10, matrix products, dot_first(): return lax.dot_general(a, b, contract_first, preferred_element_type=f32)  3.86 us
    pallas_call x3, Pallas kernels, logits_of(): pl.pallas_call(kernel, out_shape=jax.ShapeDtypeStruct((total + extra, tok...  3.29 us
  transfers between devices with their start and end apart: 29, of which 16 were waited for; matrix products, arithmetic and copies ran while one was open for 4% of the time, Pallas kernels for 4%

profile of v9, /device:TPU:0, one launch (start us, length us, event | category | flops | bytes accessed | tf_op | source)
XLA Modules:
  0.0 120.4 jit_solution(1938960854032149685)
XLA Ops:
  0.7 1.6 %copy-done = bf16[128,8192]{1,0:T(8,128)(2,1)S(1)} copy-done((bf16[128,8192]{1,0:T(8,128)(2,1)S(1)}, bf16[128,8192]{1,0:T(8,128)(2,1)}, u32[]{:S(2)}) %copy-start) | copy-done | bytes 2097176
  2.6 3.0 %collective-permute-start.7 = (bf16[128,3072]{1,0:T(8,128)(2,1)S(1)}, bf16[128,3072]{1,0:T(8,128)(2,1)S(1)}, u32[]{:S(2)}, u32[]{:S(2)}) collective-permute-start(bf16[128,3072]{1,0:T(8,128)(2,1)S(1)} %get-tuple-element.40), channel_id=1, source_target_pairs={{0,4},{4,0},{8,12},{12,8},{16,20},{20,16},{24,28},{28,24},{1,5},{5... | collective-permute-start | bytes 2359304 | tf_op jit(solution)/shard_map/ppermute | solution.py:25
  5.8 3.0 %collective-permute-start.2 = (bf16[128,1024]{1,0:T(8,128)(2,1)}, bf16[128,1024]{1,0:T(8,128)(2,1)S(1)}, u32[]{:S(2)}, u32[]{:S(2)}) collective-permute-start(bf16[128,1024]{1,0:T(8,128)(2,1)} %refs_4_), channel_id=1, source_target_pairs={{0,16},{4,20},{8,24},{12,28},{16,0},{20,4},{24,8},{28,12},{1,17},{... | collective-permute-start | bytes 786440 | tf_op jit(solution)/shard_map/ppermute | solution.py:25
  8.8 1.6 %collective-permute-start.3 = (bf16[128,1024]{1,0:T(8,128)(2,1)}, bf16[128,1024]{1,0:T(8,128)(2,1)S(1)}, u32[]{:S(2)}, u32[]{:S(2)}) collective-permute-start(bf16[128,1024]{1,0:T(8,128)(2,1)} %refs_4_), channel_id=1, source_target_pairs={{0,8},{4,12},{8,0},{12,4},{16,24},{20,28},{24,16},{28,20},{1,9},{5... | collective-permute-start | bytes 786440 | tf_op jit(solution)/shard_map/ppermute | solution.py:25
  10.4 1.5 %collective-permute-start.4 = (bf16[128,1024]{1,0:T(8,128)(2,1)}, bf16[128,1024]{1,0:T(8,128)(2,1)S(1)}, u32[]{:S(2)}, u32[]{:S(2)}) collective-permute-start(bf16[128,1024]{1,0:T(8,128)(2,1)} %refs_4_), channel_id=1, source_target_pairs={{0,2},{1,3},{2,0},{3,1},{4,6},{5,7},{6,4},{7,5},{8,10},{9,11},{10,... | collective-permute-start | bytes 786440 | tf_op jit(solution)/shard_map/ppermute | solution.py:25
  11.8 17.0 %collective-permute-done.refs_0_.refs_3_.refs_2_ = bf16[128,1024]{1,0:T(8,128)(2,1)S(1)} collective-permute-done((bf16[128,1024]{1,0:T(8,128)(2,1)S(1)}, bf16[128,1024]{1,0:T(8,128)(2,1)S(1)}, u32[]{:S(2)}, u32[]{:S(2)}) %collective-permute-start) | collective-permute-done | bytes 262176 | tf_op jit(solution)/shard_map/ppermute | solution.py:25
  29.3 1.9 %collective-permute-start.6 = (bf16[128,1024]{1,0:T(8,128)(2,1)S(1)}, bf16[128,1024]{1,0:T(8,128)(2,1)S(1)}, u32[]{:S(2)}, u32[]{:S(2)}) collective-permute-start(bf16[128,1024]{1,0:T(8,128)(2,1)S(1)} %collective-permute-done.2.refs_5_.refs_6_), channel_id=1, source_target_pairs={{0,8},{4,12},{8,0},{12,4},{16,24},{20,28},{24,16},{28,20},{1,9},{5... | collective-permute-start | bytes 786440 | tf_op jit(solution)/shard_map/ppermute | solution.py:25
  31.2 1.5 %collective-permute-start.5 = (bf16[128,1024]{1,0:T(8,128)(2,1)S(1)}, bf16[128,1024]{1,0:T(8,128)(2,1)S(1)}, u32[]{:S(2)}, u32[]{:S(2)}) collective-permute-start(bf16[128,1024]{1,0:T(8,128)(2,1)S(1)} %collective-permute-done.2.refs_5_.refs_6_), channel_id=1, source_target_pairs={{0,2},{1,3},{2,0},{3,1},{4,6},{5,7},{6,4},{7,5},{8,10},{9,11},{10,... | collective-permute-start | bytes 786440 | tf_op jit(solution)/shard_map/ppermute | solution.py:25
  33.2 7.1 %collective-permute-done.5.refs_9_ = bf16[128,1024]{1,0:T(8,128)(2,1)S(1)} collective-permute-done((bf16[128,1024]{1,0:T(8,128)(2,1)S(1)}, bf16[128,1024]{1,0:T(8,128)(2,1)S(1)}, u32[]{:S(2)}, u32[]{:S(2)}) %collective-permute-start.5) | collective-permute-done | bytes 262176 | tf_op jit(solution)/shard_map/ppermute | solution.py:25
  40.3 4.9 %collective-permute-done.8.refs_8_ = bf16[128,1024]{1,0:T(8,128)(2,1)S(1)} collective-permute-done((bf16[128,1024]{1,0:T(8,128)(2,1)S(1)}, bf16[128,1024]{1,0:T(8,128)(2,1)S(1)}, u32[]{:S(2)}, u32[]{:S(2)}) %collective-permute-start.8) | collective-permute-done | bytes 262176 | tf_op jit(solution)/shard_map/ppermute | solution.py:25
  46.3 1.6 %collective-permute-start.13 = (bf16[128,1024]{1,0:T(8,128)(2,1)S(1)}, bf16[128,1024]{1,0:T(8,128)(2,1)S(1)}, u32[]{:S(2)}, u32[]{:S(2)}) collective-permute-start(bf16[128,1024]{1,0:T(8,128)(2,1)S(1)} %collective-permute-done.6.refs_6_.refs_7_), channel_id=1, source_target_pairs={{0,2},{1,3},{2,0},{3,1},{4,6},{5,7},{6,4},{7,5},{8,10},{9,11},{10,... | collective-permute-start | bytes 786440 | tf_op jit(solution)/shard_map/ppermute | solution.py:25
  47.9 1.6 %collective-permute-done.14 = bf16[64,64]{1,0:T(8,128)(2,1)S(1)} collective-permute-done((bf16[64,64]{1,0:T(8,128)(2,1)S(1)}, bf16[64,64]{1,0:T(8,128)(2,1)S(1)}, u32[]{:S(2)}, u32[]{:S(2)}) %collective-permute-start.14) | collective-permute-done | bytes 8224 | tf_op jit(solution)/shard_map/ppermute | solution.py:25
  49.5 2.7 %collective-permute-start.15 = (bf16[128,64]{1,0:T(8,128)(2,1)S(1)}, bf16[128,64]{1,0:T(8,128)(2,1)S(1)}, u32[]{:S(2)}, u32[]{:S(2)}) collective-permute-start(bf16[128,64]{1,0:T(8,128)(2,1)S(1)} %pad_maximum_fusion.4), channel_id=1, source_target_pairs={{0,16},{4,20},{8,24},{12,28},{16,0},{20,4},{24,8},{28,12},{1,17},{... | collective-permute-start | bytes 49160 | tf_op jit(solution)/shard_map/ppermute | solution.py:25
  52.2 2.4 %collective-permute-done.15 = bf16[128,64]{1,0:T(8,128)(2,1)S(1)} collective-permute-done((bf16[128,64]{1,0:T(8,128)(2,1)S(1)}, bf16[128,64]{1,0:T(8,128)(2,1)S(1)}, u32[]{:S(2)}, u32[]{:S(2)}) %collective-permute-start.15) | collective-permute-done | bytes 16416 | tf_op jit(solution)/shard_map/ppermute | solution.py:25
  55.6 1.7 %collective-permute-start.12 = (f32[320,128]{1,0:T(8,128)S(1)}, f32[320,128]{1,0:T(8,128)S(1)}, u32[]{:S(2)}, u32[]{:S(2)}) collective-permute-start(f32[320,128]{1,0:T(8,128)S(1)} %shard_map.88), channel_id=1, source_target_pairs={{0,4},{4,0},{8,12},{12,8},{16,20},{20,16},{24,28},{28,24},{1,5},{5... | collective-permute-start | bytes 491528 | tf_op jit(solution)/shard_map/ppermute | solution.py:25
  58.5 1.6 %shard_map.90 = f32[704,128]{1,0:T(8,128)S(1)} custom-call(bf16[128,4096]{1,0:T(8,128)(2,1)S(1)} %shard_map.86.refs_0_, bf16[128,4096]{1,0:T(8,128)(2,1)S(1)} %collective-permute-done.1.refs_1_, bf16[64,4096]{1,0:T(8,128)(2,1)S(1)} %shard_map.87.refs_2_, bf16[128,1024]{1,0:T(8,128)(2,1)S(1)} %collective-permute-done.refs_0_.refs_3_.refs_2_, ...), custom_call_target="tpu_custom_call" | custom-call | flops 603979776 | bytes 6062080 | tf_op jit(solution)/shard_map/pallas_call | solution.py:100
  60.1 1.7 %collective-permute-start.16 = (f32[704,128]{1,0:T(8,128)S(1)}, f32[704,128]{1,0:T(8,128)S(1)}, u32[]{:S(2)}, u32[]{:S(2)}) collective-permute-start(f32[704,128]{1,0:T(8,128)S(1)} %shard_map.90), channel_id=1, source_target_pairs={{0,4},{4,0},{8,12},{12,8},{16,20},{20,16},{24,28},{28,24},{1,5},{5... | collective-permute-start | bytes 1081352 | tf_op jit(solution)/shard_map/ppermute | solution.py:25
  63.3 2.2 %collective-permute-done.11 = f32[256,128]{1,0:T(8,128)S(1)} collective-permute-done((f32[256,128]{1,0:T(8,128)S(1)}, f32[256,128]{1,0:T(8,128)S(1)}, u32[]{:S(2)}, u32[]{:S(2)}) %collective-permute-start.11) | collective-permute-done | bytes 131104 | tf_op jit(solution)/shard_map/ppermute | solution.py:25
  65.6 5.4 %collective-permute-done.16 = f32[704,128]{1,0:T(8,128)S(1)} collective-permute-done((f32[704,128]{1,0:T(8,128)S(1)}, f32[704,128]{1,0:T(8,128)S(1)}, u32[]{:S(2)}, u32[]{:S(2)}) %collective-permute-start.16) | collective-permute-done | bytes 360480 | tf_op jit(solution)/shard_map/ppermute | solution.py:25
  71.2 1.5 %collective-permute-start.17 = (f32[4,256]{1,0:T(4,128)S(1)}, f32[4,256]{1,0:T(4,128)S(1)}, u32[]{:S(2)}, u32[]{:S(2)}) collective-permute-start(f32[4,256]{1,0:T(4,128)S(1)} %maximum_maximum_fusion), channel_id=1, source_target_pairs={{0,2},{1,3},{2,0},{3,1},{4,6},{5,7},{6,4},{7,5},{8,10},{9,11},{10,... | collective-permute-start | bytes 12296 | tf_op jit(solution)/shard_map/ppermute | solution.py:25
  73.1 1.7 %collective-permute-done.17 = f32[4,256]{1,0:T(4,128)S(1)} collective-permute-done((f32[4,256]{1,0:T(4,128)S(1)}, f32[4,256]{1,0:T(4,128)S(1)}, u32[]{:S(2)}, u32[]{:S(2)}) %collective-permute-start.17) | collective-permute-done | bytes 4128 | tf_op jit(solution)/shard_map/ppermute | solution.py:25
  75.4 3.2 %collective-permute-done.18 = f32[2,256]{1,0:T(2,128)S(1)} collective-permute-done((f32[2,256]{1,0:T(2,128)S(1)}, f32[2,256]{1,0:T(2,128)S(1)}, u32[]{:S(2)}, u32[]{:S(2)}) %collective-permute-start.18) | collective-permute-done | bytes 2080 | tf_op jit(solution)/shard_map/ppermute | solution.py:25
  78.6 2.3 %collective-permute-start.19 = (f32[2,256]{1,0:T(2,128)S(1)}, f32[2,256]{1,0:T(2,128)S(1)}, u32[]{:S(2)}, u32[]{:S(2)}) collective-permute-start(f32[2,256]{1,0:T(2,128)S(1)} %pad_maximum_fusion.6), channel_id=1, source_target_pairs={{0,16},{4,20},{8,24},{12,28},{16,0},{20,4},{24,8},{28,12},{1,17},{... | collective-permute-start | bytes 6152 | tf_op jit(solution)/shard_map/ppermute | solution.py:25
  80.9 2.2 %collective-permute-done.19 = f32[2,256]{1,0:T(2,128)S(1)} collective-permute-done((f32[2,256]{1,0:T(2,128)S(1)}, f32[2,256]{1,0:T(2,128)S(1)}, u32[]{:S(2)}, u32[]{:S(2)}) %collective-permute-start.19) | collective-permute-done | bytes 2080 | tf_op jit(solution)/shard_map/ppermute | solution.py:25
  84.0 1.4 %collective-permute-start.20 = (bf16[128,1024]{1,0:T(8,128)(2,1)S(1)}, bf16[128,1024]{1,0:T(8,128)(2,1)S(1)}, u32[]{:S(2)}, u32[]{:S(2)}) collective-permute-start(bf16[128,1024]{1,0:T(8,128)(2,1)S(1)} %convolution_convert_fusion.2), channel_id=1, source_target_pairs={{0,2},{1,3},{2,0},{3,1},{4,6},{5,7},{6,4},{7,5},{8,10},{9,11},{10,... | collective-permute-start | bytes 786440 | tf_op jit(solution)/shard_map/ppermute | solution.py:25
  86.9 4.2 %collective-permute-done.20 = bf16[128,1024]{1,0:T(8,128)(2,1)S(1)} collective-permute-done((bf16[128,1024]{1,0:T(8,128)(2,1)S(1)}, bf16[128,1024]{1,0:T(8,128)(2,1)S(1)}, u32[]{:S(2)}, u32[]{:S(2)}) %collective-permute-start.20) | collective-permute-done | bytes 262176 | tf_op jit(solution)/shard_map/ppermute | solution.py:25
  92.0 4.1 %collective-permute-done.21 = bf16[128,1024]{1,0:T(8,128)(2,1)S(1)} collective-permute-done((bf16[128,1024]{1,0:T(8,128)(2,1)S(1)}, bf16[128,1024]{1,0:T(8,128)(2,1)S(1)}, u32[]{:S(2)}, u32[]{:S(2)}) %collective-permute-start.21) | collective-permute-done | bytes 262176 | tf_op jit(solution)/shard_map/ppermute | solution.py:25
  99.2 5.0 %collective-permute-done.23 = bf16[128,1024]{1,0:T(8,128)(2,1)S(1)} collective-permute-done((bf16[128,1024]{1,0:T(8,128)(2,1)S(1)}, bf16[128,1024]{1,0:T(8,128)(2,1)S(1)}, u32[]{:S(2)}, u32[]{:S(2)}) %collective-permute-start.23) | collective-permute-done | bytes 262176 | tf_op jit(solution)/shard_map/ppermute | solution.py:25
  104.5 2.0 %collective-permute-start.25 = (bf16[128,1024]{1,0:T(8,128)(2,1)S(1)}, bf16[128,1024]{1,0:T(8,128)(2,1)S(1)}, u32[]{:S(2)}, u32[]{:S(2)}) collective-permute-start(bf16[128,1024]{1,0:T(8,128)(2,1)S(1)} %fusion.7), channel_id=1, source_target_pairs={{0,8},{4,12},{8,0},{12,4},{16,24},{20,28},{24,16},{28,20},{1,9},{5... | collective-permute-start | bytes 786440 | tf_op jit(solution)/shard_map/ppermute | solution.py:25
  106.6 2.3 %collective-permute-start.28 = (bf16[64,1088]{1,0:T(8,128)(2,1)S(1)}, bf16[64,1088]{1,0:T(8,128)(2,1)S(1)}, u32[]{:S(2)}, u32[]{:S(2)}) collective-permute-start(bf16[64,1088]{1,0:T(8,128)(2,1)S(1)} %convert_element_type.112), channel_id=1, source_target_pairs={{0,2},{1,3},{2,0},{3,1},{4,6},{5,7},{6,4},{7,5},{8,10},{9,11},{10,... | collective-permute-start | bytes 417800 | tf_op jit(solution)/shard_map/ppermute | solution.py:25
  109.3 2.5 %collective-permute-start.26 = (bf16[128,1024]{1,0:T(8,128)(2,1)S(1)}, bf16[128,1024]{1,0:T(8,128)(2,1)S(1)}, u32[]{:S(2)}, u32[]{:S(2)}) collective-permute-start(bf16[128,1024]{1,0:T(8,128)(2,1)S(1)} %fusion.5), channel_id=1, source_target_pairs={{0,16},{4,20},{8,24},{12,28},{16,0},{20,4},{24,8},{28,12},{1,17},{... | collective-permute-start | bytes 786440 | tf_op jit(solution)/shard_map/ppermute | solution.py:25
  113.4 5.9 %collective-permute-done.26 = bf16[128,1024]{1,0:T(8,128)(2,1)S(1)} collective-permute-done((bf16[128,1024]{1,0:T(8,128)(2,1)S(1)}, bf16[128,1024]{1,0:T(8,128)(2,1)S(1)}, u32[]{:S(2)}, u32[]{:S(2)}) %collective-permute-start.26) | collective-permute-done | bytes 262176 | tf_op jit(solution)/shard_map/ppermute | solution.py:25
  (106 shorter events, 17.3 us)
Async XLA Ops:
  0.6 44.6 %copy-start.4 = (s32[128]{0:T(128)S(1)}, s32[128]{0:T(128)}, u32[]{:S(2)}) copy-start(s32[128]{0:T(128)} %param.10) | copy-start | bytes 1540
  0.7 45.0 %copy-start.3 = (bf16[64,64]{1,0:T(8,128)(2,1)S(1)}, bf16[64,64]{1,0:T(8,128)(2,1)}, u32[]{:S(2)}) copy-start(bf16[64,64]{1,0:T(8,128)(2,1)} %param.8) | copy-start | bytes 24580
  2.3 52.3 %copy-start.1 = (bf16[128,1024]{1,0:T(8,128)(2,1)S(1)}, bf16[128,1024]{1,0:T(8,128)(2,1)}, u32[]{:S(2)}) copy-start(bf16[128,1024]{1,0:T(8,128)(2,1)} %refs_4_) | copy-start | bytes 786436
  2.6 42.6 %collective-permute-start.7 = (bf16[128,3072]{1,0:T(8,128)(2,1)S(1)}, bf16[128,3072]{1,0:T(8,128)(2,1)S(1)}, u32[]{:S(2)}, u32[]{:S(2)}) collective-permute-start(bf16[128,3072]{1,0:T(8,128)(2,1)S(1)} %get-tuple-element.40), channel_id=1, source_target_pairs={{0,4},{4,0},{8,12},{12,8},{16,20},{20,16},{24,28},{28,24},{1,5},{5... | collective-permute-start | bytes 2359304 | tf_op jit(solution)/shard_map/ppermute | solution.py:25
  5.7 23.2 %collective-permute-start = (bf16[128,1024]{1,0:T(8,128)(2,1)S(1)}, bf16[128,1024]{1,0:T(8,128)(2,1)S(1)}, u32[]{:S(2)}, u32[]{:S(2)}) collective-permute-start(bf16[128,1024]{1,0:T(8,128)(2,1)S(1)} %get-tuple-element.32), channel_id=1, source_target_pairs={{0,4},{4,0},{8,12},{12,8},{16,20},{20,16},{24,28},{28,24},{1,5},{5... | collective-permute-start | bytes 786440 | tf_op jit(solution)/shard_map/ppermute | solution.py:25
  5.8 23.6 %collective-permute-start.2 = (bf16[128,1024]{1,0:T(8,128)(2,1)}, bf16[128,1024]{1,0:T(8,128)(2,1)S(1)}, u32[]{:S(2)}, u32[]{:S(2)}) collective-permute-start(bf16[128,1024]{1,0:T(8,128)(2,1)} %refs_4_), channel_id=1, source_target_pairs={{0,16},{4,20},{8,24},{12,28},{16,0},{20,4},{24,8},{28,12},{1,17},{... | collective-permute-start | bytes 786440 | tf_op jit(solution)/shard_map/ppermute | solution.py:25
  8.8 20.5 %collective-permute-start.3 = (bf16[128,1024]{1,0:T(8,128)(2,1)}, bf16[128,1024]{1,0:T(8,128)(2,1)S(1)}, u32[]{:S(2)}, u32[]{:S(2)}) collective-permute-start(bf16[128,1024]{1,0:T(8,128)(2,1)} %refs_4_), channel_id=1, source_target_pairs={{0,8},{4,12},{8,0},{12,4},{16,24},{20,28},{24,16},{28,20},{1,9},{5... | collective-permute-start | bytes 786440 | tf_op jit(solution)/shard_map/ppermute | solution.py:25
  10.4 20.8 %collective-permute-start.4 = (bf16[128,1024]{1,0:T(8,128)(2,1)}, bf16[128,1024]{1,0:T(8,128)(2,1)S(1)}, u32[]{:S(2)}, u32[]{:S(2)}) collective-permute-start(bf16[128,1024]{1,0:T(8,128)(2,1)} %refs_4_), channel_id=1, source_target_pairs={{0,2},{1,3},{2,0},{3,1},{4,6},{5,7},{6,4},{7,5},{8,10},{9,11},{10,... | collective-permute-start | bytes 786440 | tf_op jit(solution)/shard_map/ppermute | solution.py:25
  29.2 25.4 %collective-permute-start.1 = (bf16[128,4096]{1,0:T(8,128)(2,1)S(1)}, bf16[128,4096]{1,0:T(8,128)(2,1)S(1)}, u32[]{:S(2)}, u32[]{:S(2)}) collective-permute-start(bf16[128,4096]{1,0:T(8,128)(2,1)S(1)} %shard_map.86.refs_0_), channel_id=1, source_target_pairs={{0,1},{1,0},{2,3},{3,2},{4,5},{5,4},{6,7},{7,6},{8,9},{9,8},{10,11... | collective-permute-start | bytes 3145736 | tf_op jit(solution)/shard_map/ppermute | solution.py:25
  29.3 15.9 %collective-permute-start.6 = (bf16[128,1024]{1,0:T(8,128)(2,1)S(1)}, bf16[128,1024]{1,0:T(8,128)(2,1)S(1)}, u32[]{:S(2)}, u32[]{:S(2)}) collective-permute-start(bf16[128,1024]{1,0:T(8,128)(2,1)S(1)} %collective-permute-done.2.refs_5_.refs_6_), channel_id=1, source_target_pairs={{0,8},{4,12},{8,0},{12,4},{16,24},{20,28},{24,16},{28,20},{1,9},{5... | collective-permute-start | bytes 786440 | tf_op jit(solution)/shard_map/ppermute | solution.py:25
  31.2 9.1 %collective-permute-start.5 = (bf16[128,1024]{1,0:T(8,128)(2,1)S(1)}, bf16[128,1024]{1,0:T(8,128)(2,1)S(1)}, u32[]{:S(2)}, u32[]{:S(2)}) collective-permute-start(bf16[128,1024]{1,0:T(8,128)(2,1)S(1)} %collective-permute-done.2.refs_5_.refs_6_), channel_id=1, source_target_pairs={{0,2},{1,3},{2,0},{3,1},{4,6},{5,7},{6,4},{7,5},{8,10},{9,11},{10,... | collective-permute-start | bytes 786440 | tf_op jit(solution)/shard_map/ppermute | solution.py:25
  32.7 12.5 %collective-permute-start.8 = (bf16[128,1024]{1,0:T(8,128)(2,1)S(1)}, bf16[128,1024]{1,0:T(8,128)(2,1)S(1)}, u32[]{:S(2)}, u32[]{:S(2)}) collective-permute-start(bf16[128,1024]{1,0:T(8,128)(2,1)S(1)} %collective-permute-done.3.refs_4_.refs_5_), channel_id=1, source_target_pairs={{0,2},{1,3},{2,0},{3,1},{4,6},{5,7},{6,4},{7,5},{8,10},{9,11},{10,... | collective-permute-start | bytes 786440 | tf_op jit(solution)/shard_map/ppermute | solution.py:25
  45.2 12.1 %collective-permute-start.10 = (bf16[128,3072]{1,0:T(8,128)(2,1)S(1)}, bf16[128,3072]{1,0:T(8,128)(2,1)S(1)}, u32[]{:S(2)}, u32[]{:S(2)}) collective-permute-start(bf16[128,3072]{1,0:T(8,128)(2,1)S(1)} %collective-permute-done.7.refs_1_.refs_4_.refs_3_), channel_id=1, source_target_pairs={{0,1},{1,0},{2,3},{3,2},{4,5},{5,4},{6,7},{7,6},{8,9},{9,8},{10,11... | collective-permute-start | bytes 2359304 | tf_op jit(solution)/shard_map/ppermute | solution.py:25
  45.7 3.8 %collective-permute-start.14 = (bf16[64,64]{1,0:T(8,128)(2,1)S(1)}, bf16[64,64]{1,0:T(8,128)(2,1)S(1)}, u32[]{:S(2)}, u32[]{:S(2)}) collective-permute-start(bf16[64,64]{1,0:T(8,128)(2,1)S(1)} %copy-done.3), channel_id=1, source_target_pairs={{0,8},{4,12},{8,0},{12,4},{16,24},{20,28},{24,16},{28,20},{1,9},{5... | collective-permute-start | bytes 24584 | tf_op jit(solution)/shard_map/ppermute | solution.py:25
  46.1 11.2 %collective-permute-start.9 = (bf16[128,1024]{1,0:T(8,128)(2,1)S(1)}, bf16[128,1024]{1,0:T(8,128)(2,1)S(1)}, u32[]{:S(2)}, u32[]{:S(2)}) collective-permute-start(bf16[128,1024]{1,0:T(8,128)(2,1)S(1)} %collective-permute-done.refs_0_.refs_3_.refs_2_), channel_id=1, source_target_pairs={{0,1},{1,0},{2,3},{3,2},{4,5},{5,4},{6,7},{7,6},{8,9},{9,8},{10,11... | collective-permute-start | bytes 786440 | tf_op jit(solution)/shard_map/ppermute | solution.py:25
  46.3 12.2 %collective-permute-start.13 = (bf16[128,1024]{1,0:T(8,128)(2,1)S(1)}, bf16[128,1024]{1,0:T(8,128)(2,1)S(1)}, u32[]{:S(2)}, u32[]{:S(2)}) collective-permute-start(bf16[128,1024]{1,0:T(8,128)(2,1)S(1)} %collective-permute-done.6.refs_6_.refs_7_), channel_id=1, source_target_pairs={{0,2},{1,3},{2,0},{3,1},{4,6},{5,7},{6,4},{7,5},{8,10},{9,11},{10,... | collective-permute-start | bytes 786440 | tf_op jit(solution)/shard_map/ppermute | solution.py:25
  49.5 5.0 %collective-permute-start.15 = (bf16[128,64]{1,0:T(8,128)(2,1)S(1)}, bf16[128,64]{1,0:T(8,128)(2,1)S(1)}, u32[]{:S(2)}, u32[]{:S(2)}) collective-permute-start(bf16[128,64]{1,0:T(8,128)(2,1)S(1)} %pad_maximum_fusion.4), channel_id=1, source_target_pairs={{0,16},{4,20},{8,24},{12,28},{16,0},{20,4},{24,8},{28,12},{1,17},{... | collective-permute-start | bytes 49160 | tf_op jit(solution)/shard_map/ppermute | solution.py:25
  55.6 7.1 %collective-permute-start.12 = (f32[320,128]{1,0:T(8,128)S(1)}, f32[320,128]{1,0:T(8,128)S(1)}, u32[]{:S(2)}, u32[]{:S(2)}) collective-permute-start(f32[320,128]{1,0:T(8,128)S(1)} %shard_map.88), channel_id=1, source_target_pairs={{0,4},{4,0},{8,12},{12,8},{16,20},{20,16},{24,28},{28,24},{1,5},{5... | collective-permute-start | bytes 491528 | tf_op jit(solution)/shard_map/ppermute | solution.py:25
  58.0 7.5 %collective-permute-start.11 = (f32[256,128]{1,0:T(8,128)S(1)}, f32[256,128]{1,0:T(8,128)S(1)}, u32[]{:S(2)}, u32[]{:S(2)}) collective-permute-start(f32[256,128]{1,0:T(8,128)S(1)} %shard_map.89), channel_id=1, source_target_pairs={{0,4},{4,0},{8,12},{12,8},{16,20},{20,16},{24,28},{28,24},{1,5},{5... | collective-permute-start | bytes 393224 | tf_op jit(solution)/shard_map/ppermute | solution.py:25
  60.1 10.9 %collective-permute-start.16 = (f32[704,128]{1,0:T(8,128)S(1)}, f32[704,128]{1,0:T(8,128)S(1)}, u32[]{:S(2)}, u32[]{:S(2)}) collective-permute-start(f32[704,128]{1,0:T(8,128)S(1)} %shard_map.90), channel_id=1, source_target_pairs={{0,4},{4,0},{8,12},{12,8},{16,20},{20,16},{24,28},{28,24},{1,5},{5... | collective-permute-start | bytes 1081352 | tf_op jit(solution)/shard_map/ppermute | solution.py:25
  71.2 3.7 %collective-permute-start.17 = (f32[4,256]{1,0:T(4,128)S(1)}, f32[4,256]{1,0:T(4,128)S(1)}, u32[]{:S(2)}, u32[]{:S(2)}) collective-permute-start(f32[4,256]{1,0:T(4,128)S(1)} %maximum_maximum_fusion), channel_id=1, source_target_pairs={{0,2},{1,3},{2,0},{3,1},{4,6},{5,7},{6,4},{7,5},{8,10},{9,11},{10,... | collective-permute-start | bytes 12296 | tf_op jit(solution)/shard_map/ppermute | solution.py:25
  74.9 3.7 %collective-permute-start.18 = (f32[2,256]{1,0:T(2,128)S(1)}, f32[2,256]{1,0:T(2,128)S(1)}, u32[]{:S(2)}, u32[]{:S(2)}) collective-permute-start(f32[2,256]{1,0:T(2,128)S(1)} %pad_maximum_fusion.5), channel_id=1, source_target_pairs={{0,8},{4,12},{8,0},{12,4},{16,24},{20,28},{24,16},{28,20},{1,9},{5... | collective-permute-start | bytes 6152 | tf_op jit(solution)/shard_map/ppermute | solution.py:25
  78.6 4.5 %collective-permute-start.19 = (f32[2,256]{1,0:T(2,128)S(1)}, f32[2,256]{1,0:T(2,128)S(1)}, u32[]{:S(2)}, u32[]{:S(2)}) collective-permute-start(f32[2,256]{1,0:T(2,128)S(1)} %pad_maximum_fusion.6), channel_id=1, source_target_pairs={{0,16},{4,20},{8,24},{12,28},{16,0},{20,4},{24,8},{28,12},{1,17},{... | collective-permute-start | bytes 6152 | tf_op jit(solution)/shard_map/ppermute | solution.py:25
  84.0 7.0 %collective-permute-start.20 = (bf16[128,1024]{1,0:T(8,128)(2,1)S(1)}, bf16[128,1024]{1,0:T(8,128)(2,1)S(1)}, u32[]{:S(2)}, u32[]{:S(2)}) collective-permute-start(bf16[128,1024]{1,0:T(8,128)(2,1)S(1)} %convolution_convert_fusion.2), channel_id=1, source_target_pairs={{0,2},{1,3},{2,0},{3,1},{4,6},{5,7},{6,4},{7,5},{8,10},{9,11},{10,... | collective-permute-start | bytes 786440 | tf_op jit(solution)/shard_map/ppermute | solution.py:25
  85.8 10.3 %collective-permute-start.21 = (bf16[128,1024]{1,0:T(8,128)(2,1)S(1)}, bf16[128,1024]{1,0:T(8,128)(2,1)S(1)}, u32[]{:S(2)}, u32[]{:S(2)}) collective-permute-start(bf16[128,1024]{1,0:T(8,128)(2,1)S(1)} %convolution_convert_fusion.1), channel_id=1, source_target_pairs={{0,2},{1,3},{2,0},{3,1},{4,6},{5,7},{6,4},{7,5},{8,10},{9,11},{10,... | collective-permute-start | bytes 786440 | tf_op jit(solution)/shard_map/ppermute | solution.py:25
  96.4 8.1 %collective-permute-start.24 = (bf16[128,1024]{1,0:T(8,128)(2,1)S(1)}, bf16[128,1024]{1,0:T(8,128)(2,1)S(1)}, u32[]{:S(2)}, u32[]{:S(2)}) collective-permute-start(bf16[128,1024]{1,0:T(8,128)(2,1)S(1)} %fusion.6), channel_id=1, source_target_pairs={{0,8},{4,12},{8,0},{12,4},{16,24},{20,28},{24,16},{28,20},{1,9},{5... | collective-permute-start | bytes 786440 | tf_op jit(solution)/shard_map/ppermute | solution.py:25
  96.5 7.7 %collective-permute-start.23 = (bf16[128,1024]{1,0:T(8,128)(2,1)S(1)}, bf16[128,1024]{1,0:T(8,128)(2,1)S(1)}, u32[]{:S(2)}, u32[]{:S(2)}) collective-permute-start(bf16[128,1024]{1,0:T(8,128)(2,1)S(1)} %convolution_convert_fusion), channel_id=1, source_target_pairs={{0,2},{1,3},{2,0},{3,1},{4,6},{5,7},{6,4},{7,5},{8,10},{9,11},{10,... | collective-permute-start | bytes 786440 | tf_op jit(solution)/shard_map/ppermute | solution.py:25
  98.2 8.4 %collective-permute-start.27 = (f32[64,1088]{1,0:T(8,128)S(1)}, f32[64,1088]{1,0:T(8,128)S(1)}, u32[]{:S(2)}, u32[]{:S(2)}) collective-permute-start(f32[64,1088]{1,0:T(8,128)S(1)} %pad_maximum_fusion), channel_id=1, source_target_pairs={{0,1},{1,0},{2,3},{3,2},{4,5},{5,4},{6,7},{7,6},{8,9},{9,8},{10,11... | collective-permute-start | bytes 835592 | tf_op jit(solution)/shard_map/ppermute | solution.py:25
  98.5 14.9 %collective-permute-start.22 = (bf16[128,1024]{1,0:T(8,128)(2,1)S(1)}, bf16[128,1024]{1,0:T(8,128)(2,1)S(1)}, u32[]{:S(2)}, u32[]{:S(2)}) collective-permute-start(bf16[128,1024]{1,0:T(8,128)(2,1)S(1)} %convolution_convert_fusion.3), channel_id=1, source_target_pairs={{0,2},{1,3},{2,0},{3,1},{4,6},{5,7},{6,4},{7,5},{8,10},{9,11},{10,... | collective-permute-start | bytes 786440 | tf_op jit(solution)/shard_map/ppermute | solution.py:25
  104.5 8.9 %collective-permute-start.25 = (bf16[128,1024]{1,0:T(8,128)(2,1)S(1)}, bf16[128,1024]{1,0:T(8,128)(2,1)S(1)}, u32[]{:S(2)}, u32[]{:S(2)}) collective-permute-start(bf16[128,1024]{1,0:T(8,128)(2,1)S(1)} %fusion.7), channel_id=1, source_target_pairs={{0,8},{4,12},{8,0},{12,4},{16,24},{20,28},{24,16},{28,20},{1,9},{5... | collective-permute-start | bytes 786440 | tf_op jit(solution)/shard_map/ppermute | solution.py:25
  106.6 5.4 %collective-permute-start.28 = (bf16[64,1088]{1,0:T(8,128)(2,1)S(1)}, bf16[64,1088]{1,0:T(8,128)(2,1)S(1)}, u32[]{:S(2)}, u32[]{:S(2)}) collective-permute-start(bf16[64,1088]{1,0:T(8,128)(2,1)S(1)} %convert_element_type.112), channel_id=1, source_target_pairs={{0,2},{1,3},{2,0},{3,1},{4,6},{5,7},{6,4},{7,5},{8,10},{9,11},{10,... | collective-permute-start | bytes 417800 | tf_op jit(solution)/shard_map/ppermute | solution.py:25
  109.3 10.0 %collective-permute-start.26 = (bf16[128,1024]{1,0:T(8,128)(2,1)S(1)}, bf16[128,1024]{1,0:T(8,128)(2,1)S(1)}, u32[]{:S(2)}, u32[]{:S(2)}) collective-permute-start(bf16[128,1024]{1,0:T(8,128)(2,1)S(1)} %fusion.5), channel_id=1, source_target_pairs={{0,16},{4,20},{8,24},{12,28},{16,0},{20,4},{24,8},{28,12},{1,17},{... | collective-permute-start | bytes 786440 | tf_op jit(solution)/shard_map/ppermute | solution.py:25
  (3 other events, 89.2 us)

commit v10 on v9

--- a/solution.py
+++ b/solution.py
@@ -134,7 +134,7 @@
     def start_of(j, other):
         return (lax.axis_index("vocab") ^ (2 * j + other)) * width
 
-    cuts = [0, 1, n_z]
+    cuts = [0, n_z]
     chunks = [range(a, b) for a, b in zip(cuts, cuts[1:]) if a < b]
     sends = copy_blocks(
         [(rows, len(chunk) * width) for chunk in chunks],
@@ -152,42 +152,37 @@
         moves = lambda: [(0, (start_of(j, 0), width), 0, 0, j * width) for j in range(n_z)]
         return copy_blocks([(array.shape[0], depth)], moves, array)[0]
 
-    kept = half(head, beside[0])
-    kept_core = swap_core(kept)
-
-    later, _ = lax.optimization_barrier((hidden, sends[0]))
-    shards, cross = {0: hidden}, {0: swap_x(later)}
+    after, _ = lax.optimization_barrier((hidden, sends[0]))
+    shards, cross = {0: hidden}, {0: swap_x(hidden)}
     for bit in reversed(bits):
-        near = swap_z(hidden if bit == bits[-1] else later, bit)
+        near = swap_z(hidden if bit == 1 else hidden, bit)
         for j in [j for j in shards if j]:
-            shards[j], *_ = lax.optimization_barrier((shards[j], near, beside[0]))
+            shards[j], *_ = lax.optimization_barrier((shards[j], near))
             shards[j ^ bit] = swap_z(shards[j], bit)
         shards[bit] = near
     for j in range(1, n_z):
         sent = shards[j]
-        if j == 1:
-            sent, *_ = lax.optimization_barrier((sent, shards[n_z // 2]))
-        if j > 1:
-            sent, *_ = lax.optimization_barrier((sent, cross[j - 2]))
+        waits = [] if j == 1 else [cross[j - 2]] if j < n_z - 1 else [cross[j - 2], beside[0]]
+        if waits:
+            sent, *_ = lax.optimization_barrier((sent, *waits))
         cross[j] = swap_x(sent)
-    basis_half = half(factor_basis, shards[n_z // 2])
+    kept = half(head, cross[1])
+    kept_core = swap_core(kept)
+    basis_half = half(factor_basis, cross[0])
 
     beside_core = []
     for n, came in enumerate(beside):
-        came, *_ = lax.optimization_barrier((came, cross[1], cross[n_z - 2], shards[n_z - 1]))
+        came, *_ = lax.optimization_barrier((came, cross[n_z - 2], shards[n_z - 1]))
         beside_core.append(swap_core(came))
 
     in_order = lambda parts: [parts[j] for j in range(n_z)]
-    basis_ready, *_ = lax.optimization_barrier((basis_half, cross[n_z - 2], shards[n_z - 1]))
+    basis_ready, *_ = lax.optimization_barrier((basis_half, cross[1]))
     upper = [[kept], [kept_core], [basis_ready]]
     upper_own = logits_of(upper, in_order(shards))
     beside_core[-1], *_ = lax.optimization_barrier((beside_core[-1], upper_own))
     lower_own = logits_of([beside, beside_core], in_order(shards))
     cross[0], _ = lax.optimization_barrier((cross[0], lower_own))
-    rows_all, _ = lax.optimization_barrier((factor_rows, shards[n_z - 1]))
-    for bit in bits:
-        rows_all = jnp.concatenate([rows_all, swap_z(rows_all, bit)], axis=0)
-    both_cross = logits_of(upper + [beside, beside_core], in_order(cross), rows_all)
+    both_cross = logits_of(upper + [beside, beside_core], in_order(cross), factor_rows)
     n_up = 2 * rows + rank
 
     def add_over_y(up, low, up_came, low_came):
@@ -206,7 +201,7 @@
 
     n_rows = n_up + 2 * rows
     rows_came = cross_came[n_rows:].astype(bf16)
-    rows_all = jnp.concatenate([rows_all, rows_came[:, :rank], rows_came[:, rank:]], axis=0)
+    rows_pair = jnp.concatenate([factor_rows, rows_came[:, :rank], rows_came[:, rank:]], axis=0)
 
     def merge(a, b):
         top = jnp.maximum(a[0], b[0])
@@ -229,12 +224,12 @@
     info = jnp.concatenate([info, came[2:, :toks]], axis=1)
     target_row = info[0].astype(jnp.int32)
     weight_row = loss_scale * info[1]
+    fresh = lax.dot_general(
+        rows_pair, hidden_basis, (((1,), (0,)), ((), ())), preferred_element_type=f32
+    )
+    stats = merge(stats, local(fresh))
     for bit in bits:
         stats = merge(stats, swap_z(stats, bit))
-    fresh = lax.dot_general(
-        rows_all, hidden_basis, (((1,), (0,)), ((), ())), preferred_element_type=f32
-    )
-    stats = merge(stats, local(fresh))
     row_top, sum_exp = stats[0], stats[1]
     scale_row = weight_row / sum_exp
 
@@ -273,17 +268,17 @@
         sums[j] = part(grad_own, j) + from_x[j].astype(f32)
         if first_z is None:
             first_z = sums[j].astype(bf16)
-    fresh, _ = lax.optimization_barrier((fresh, from_x[max(0, n_z - 2)]))
-    fresh_iota = lax.broadcasted_iota(jnp.int32, (n_vocab * new_here, toks), 0)
-    in_block = fresh_iota & (new_here - 1)
-    from_block = fresh_iota - in_block
-    from_block = ((from_block & (n_z * new_here - 1)) << 1) + (from_block & (n_z * new_here)) // n_z
-    fresh_ids = ((from_block + in_block) ^ new_first) + rows * n_tok * n_vocab
+    fresh, _ = lax.optimization_barrier((fresh, first_send))
+    fresh_ids = lax.broadcasted_iota(jnp.int32, (2 * new_here, toks), 0) ^ new_first
+    fresh_ids = fresh_ids + rows * n_tok * n_vocab
     fresh_hit = jnp.where(fresh_ids == targets[None, :], weight_row[None, :toks], 0.0)
     fresh_grad = (
         jnp.exp(fresh[:, :toks] - row_top[None, :toks]) * scale_row[None, :toks] - fresh_hit
     ).astype(bf16)
-    mix_total = dot_first(rows_all, fresh_grad).astype(bf16)
+    mix_total = dot_first(rows_pair, fresh_grad)
+    for bit in bits:
+        mix_total = mix_total + swap_z(mix_total, bit)
+    mix_total = mix_total.astype(bf16)
     rows_part = dot_last(fresh_grad[:new_here], hidden_basis[:, :toks])
     basis_part = jnp.dot(mix_total, hidden, preferred_element_type=f32)
 

time: 121 us -> 103 us (0.85)
  starting transfers between devices: 37.4 us -> 28.1 us
  waiting for transfers between devices: 67.9 us -> 60.4 us
    ppermute x29 -> x27, starting transfers between devices: 37.4 us -> 28.1 us  [swap(): return lax.ppermute(value, axis, [(i, i ^ bit) for i in range(size)])]
    ppermute x29 -> x27, waiting for transfers between devices: 67.9 us -> 60.4 us  [swap(): return lax.ppermute(value, axis, [(i, i ^ bit) for i in range(size)])]
  transfers between devices with their start and end apart: 29 -> 27, of which waited for: 16 -> 17; matrix products, arithmetic and copies ran while one was open for 4% -> 4% of each run, Pallas kernels for 4% -> 5%
where the time goes in v10:
time: 103 us
  waiting for transfers between devices  60.4 us (59%)
  starting transfers between devices  28.1 us (27%)
  Pallas kernels  5 us (5%)
  matrix products  4.27 us (4%)
  local copies, waits for them, and re-layouts  3.04 us (3%)
  between operations  1.03 us (1%)
    ppermute x27, waiting for transfers between devices, swap(): return lax.ppermute(value, axis, [(i, i ^ bit) for i in range(size)])  60.4 us
    ppermute x27, starting transfers between devices, swap(): return lax.ppermute(value, axis, [(i, i ^ bit) for i in range(size)])  28.1 us
    dot_general x10, matrix products, dot_first(): return lax.dot_general(a, b, contract_first, preferred_element_type=f32)  3.82 us
    pallas_call x3, Pallas kernels, logits_of(): pl.pallas_call(kernel, out_shape=jax.ShapeDtypeStruct((total + extra, tok...  3.3 us
  transfers between devices with their start and end apart: 27, of which 17 were waited for; matrix products, arithmetic and copies ran while one was open for 4% of the time, Pallas kernels for 5%

profile of v10, /device:TPU:0, one launch (start us, length us, event | category | flops | bytes accessed | tf_op | source)
XLA Modules:
  0.0 102.8 jit_solution(12039435624595997022)
XLA Ops:
  0.7 1.6 %copy-done = bf16[128,8192]{1,0:T(8,128)(2,1)S(1)} copy-done((bf16[128,8192]{1,0:T(8,128)(2,1)S(1)}, bf16[128,8192]{1,0:T(8,128)(2,1)}, u32[]{:S(2)}) %copy-start) | copy-done | bytes 2097176
  2.6 3.0 %collective-permute-start.6 = (bf16[128,4096]{1,0:T(8,128)(2,1)S(1)}, bf16[128,4096]{1,0:T(8,128)(2,1)S(1)}, u32[]{:S(2)}, u32[]{:S(2)}) collective-permute-start(bf16[128,4096]{1,0:T(8,128)(2,1)S(1)} %shard_map.88), channel_id=1, source_target_pairs={{0,4},{4,0},{8,12},{12,8},{16,20},{20,16},{24,28},{28,24},{1,5},{5... | collective-permute-start | bytes 3145736 | tf_op jit(solution)/shard_map/ppermute | solution.py:25
  5.7 1.6 %collective-permute-start = (bf16[128,1024]{1,0:T(8,128)(2,1)}, bf16[128,1024]{1,0:T(8,128)(2,1)S(1)}, u32[]{:S(2)}, u32[]{:S(2)}) collective-permute-start(bf16[128,1024]{1,0:T(8,128)(2,1)} %refs_2_), channel_id=1, source_target_pairs={{0,8},{4,12},{8,0},{12,4},{16,24},{20,28},{24,16},{28,20},{1,9},{5... | collective-permute-start | bytes 786440 | tf_op jit(solution)/shard_map/ppermute | solution.py:25
  7.2 2.6 %collective-permute-start.4 = (bf16[128,1024]{1,0:T(8,128)(2,1)}, bf16[128,1024]{1,0:T(8,128)(2,1)S(1)}, u32[]{:S(2)}, u32[]{:S(2)}) collective-permute-start(bf16[128,1024]{1,0:T(8,128)(2,1)} %refs_2_), channel_id=1, source_target_pairs={{0,16},{4,20},{8,24},{12,28},{16,0},{20,4},{24,8},{28,12},{1,17},{... | collective-permute-start | bytes 786440 | tf_op jit(solution)/shard_map/ppermute | solution.py:25
  9.8 1.5 %collective-permute-start.3 = (bf16[128,1024]{1,0:T(8,128)(2,1)}, bf16[128,1024]{1,0:T(8,128)(2,1)S(1)}, u32[]{:S(2)}, u32[]{:S(2)}) collective-permute-start(bf16[128,1024]{1,0:T(8,128)(2,1)} %refs_2_), channel_id=1, source_target_pairs={{0,2},{1,3},{2,0},{3,1},{4,6},{5,7},{6,4},{7,5},{8,10},{9,11},{10,... | collective-permute-start | bytes 786440 | tf_op jit(solution)/shard_map/ppermute | solution.py:25
  11.3 7.8 %collective-permute-done.refs_4_.refs_3_ = bf16[128,1024]{1,0:T(8,128)(2,1)S(1)} collective-permute-done((bf16[128,1024]{1,0:T(8,128)(2,1)}, bf16[128,1024]{1,0:T(8,128)(2,1)S(1)}, u32[]{:S(2)}, u32[]{:S(2)}) %collective-permute-start) | collective-permute-done | bytes 262176 | tf_op jit(solution)/shard_map/ppermute | solution.py:25
  19.1 1.5 %collective-permute-start.1 = (bf16[128,1024]{1,0:T(8,128)(2,1)S(1)}, bf16[128,1024]{1,0:T(8,128)(2,1)S(1)}, u32[]{:S(2)}, u32[]{:S(2)}) collective-permute-start(bf16[128,1024]{1,0:T(8,128)(2,1)S(1)} %collective-permute-done.refs_4_.refs_3_), channel_id=1, source_target_pairs={{0,2},{1,3},{2,0},{3,1},{4,6},{5,7},{6,4},{7,5},{8,10},{9,11},{10,... | collective-permute-start | bytes 786440 | tf_op jit(solution)/shard_map/ppermute | solution.py:25
  22.0 1.5 %collective-permute-start.7 = (bf16[128,1024]{1,0:T(8,128)(2,1)S(1)}, bf16[128,1024]{1,0:T(8,128)(2,1)S(1)}, u32[]{:S(2)}, u32[]{:S(2)}) collective-permute-start(bf16[128,1024]{1,0:T(8,128)(2,1)S(1)} %collective-permute-done.4.refs_5_.refs_4_), channel_id=1, source_target_pairs={{0,2},{1,3},{2,0},{3,1},{4,6},{5,7},{6,4},{7,5},{8,10},{9,11},{10,... | collective-permute-start | bytes 786440 | tf_op jit(solution)/shard_map/ppermute | solution.py:25
  23.5 4.9 %collective-permute-done.1.refs_6_ = bf16[128,1024]{1,0:T(8,128)(2,1)S(1)} collective-permute-done((bf16[128,1024]{1,0:T(8,128)(2,1)S(1)}, bf16[128,1024]{1,0:T(8,128)(2,1)S(1)}, u32[]{:S(2)}, u32[]{:S(2)}) %collective-permute-start.1) | collective-permute-done | bytes 262176 | tf_op jit(solution)/shard_map/ppermute | solution.py:25
  28.8 2.8 %collective-permute-done.7.refs_7_ = bf16[128,1024]{1,0:T(8,128)(2,1)S(1)} collective-permute-done((bf16[128,1024]{1,0:T(8,128)(2,1)S(1)}, bf16[128,1024]{1,0:T(8,128)(2,1)S(1)}, u32[]{:S(2)}, u32[]{:S(2)}) %collective-permute-start.7) | collective-permute-done | bytes 262176 | tf_op jit(solution)/shard_map/ppermute | solution.py:25
  31.6 1.6 %collective-permute-start.11 = (bf16[128,1024]{1,0:T(8,128)(2,1)S(1)}, bf16[128,1024]{1,0:T(8,128)(2,1)S(1)}, u32[]{:S(2)}, u32[]{:S(2)}) collective-permute-start(bf16[128,1024]{1,0:T(8,128)(2,1)S(1)} %collective-permute-done.5.refs_6_.refs_5_), channel_id=1, source_target_pairs={{0,2},{1,3},{2,0},{3,1},{4,6},{5,7},{6,4},{7,5},{8,10},{9,11},{10,... | collective-permute-start | bytes 786440 | tf_op jit(solution)/shard_map/ppermute | solution.py:25
  36.0 1.6 %collective-permute-start.9 = (f32[256,128]{1,0:T(8,128)S(1)}, f32[256,128]{1,0:T(8,128)S(1)}, u32[]{:S(2)}, u32[]{:S(2)}) collective-permute-start(f32[256,128]{1,0:T(8,128)S(1)} %shard_map.89), channel_id=1, source_target_pairs={{0,4},{4,0},{8,12},{12,8},{16,20},{20,16},{24,28},{28,24},{1,5},{5... | collective-permute-start | bytes 393224 | tf_op jit(solution)/shard_map/ppermute | solution.py:25
  37.5 2.9 %collective-permute-done.11.refs_8_ = bf16[128,1024]{1,0:T(8,128)(2,1)S(1)} collective-permute-done((bf16[128,1024]{1,0:T(8,128)(2,1)S(1)}, bf16[128,1024]{1,0:T(8,128)(2,1)S(1)}, u32[]{:S(2)}, u32[]{:S(2)}) %collective-permute-start.11) | collective-permute-done | bytes 262176 | tf_op jit(solution)/shard_map/ppermute | solution.py:25
  40.4 1.6 %shard_map.90 = f32[608,128]{1,0:T(8,128)S(1)} custom-call(bf16[128,4096]{1,0:T(8,128)(2,1)S(1)} %shard_map.85.refs_0_, bf16[128,4096]{1,0:T(8,128)(2,1)S(1)} %collective-permute-done.2.refs_1_, bf16[64,4096]{1,0:T(8,128)(2,1)S(1)} %shard_map.86.refs_2_, bf16[128,4096]{1,0:T(8,128)(2,1)S(1)} %collective-permute-done.6.refs_0_.refs_3_.refs_2_, ...), custom_call_target="tpu_custom_call" | custom-call | flops 603979776 | bytes 6062080 | tf_op jit(solution)/shard_map/pallas_call | solution.py:100
  44.0 7.0 %collective-permute-done.12 = f32[608,128]{1,0:T(8,128)S(1)} collective-permute-done((f32[608,128]{1,0:T(8,128)S(1)}, f32[608,128]{1,0:T(8,128)S(1)}, u32[]{:S(2)}, u32[]{:S(2)}) %collective-permute-start.12) | collective-permute-done | bytes 311328 | tf_op jit(solution)/shard_map/ppermute | solution.py:25
  51.3 1.6 %collective-permute-start.13 = (f32[4,256]{1,0:T(4,128)S(1)}, f32[4,256]{1,0:T(4,128)S(1)}, u32[]{:S(2)}, u32[]{:S(2)}) collective-permute-start(f32[4,256]{1,0:T(4,128)S(1)} %maximum_maximum_fusion), channel_id=1, source_target_pairs={{0,2},{1,3},{2,0},{3,1},{4,6},{5,7},{6,4},{7,5},{8,10},{9,11},{10,... | collective-permute-start | bytes 12296 | tf_op jit(solution)/shard_map/ppermute | solution.py:25
  53.1 1.9 %collective-permute-done.13 = f32[4,256]{1,0:T(4,128)S(1)} collective-permute-done((f32[4,256]{1,0:T(4,128)S(1)}, f32[4,256]{1,0:T(4,128)S(1)}, u32[]{:S(2)}, u32[]{:S(2)}) %collective-permute-start.13) | collective-permute-done | bytes 4128 | tf_op jit(solution)/shard_map/ppermute | solution.py:25
  55.1 3.5 %collective-permute-done.14 = f32[2,256]{1,0:T(2,128)S(1)} collective-permute-done((f32[2,256]{1,0:T(2,128)S(1)}, f32[2,256]{1,0:T(2,128)S(1)}, u32[]{:S(2)}, u32[]{:S(2)}) %collective-permute-start.14) | collective-permute-done | bytes 2080 | tf_op jit(solution)/shard_map/ppermute | solution.py:25
  58.7 1.3 %collective-permute-start.15 = (f32[2,256]{1,0:T(2,128)S(1)}, f32[2,256]{1,0:T(2,128)S(1)}, u32[]{:S(2)}, u32[]{:S(2)}) collective-permute-start(f32[2,256]{1,0:T(2,128)S(1)} %pad_maximum_fusion.7), channel_id=1, source_target_pairs={{0,16},{4,20},{8,24},{12,28},{16,0},{20,4},{24,8},{28,12},{1,17},{... | collective-permute-start | bytes 6152 | tf_op jit(solution)/shard_map/ppermute | solution.py:25
  60.0 3.2 %collective-permute-done.15 = f32[2,256]{1,0:T(2,128)S(1)} collective-permute-done((f32[2,256]{1,0:T(2,128)S(1)}, f32[2,256]{1,0:T(2,128)S(1)}, u32[]{:S(2)}, u32[]{:S(2)}) %collective-permute-start.15) | collective-permute-done | bytes 2080 | tf_op jit(solution)/shard_map/ppermute | solution.py:25
  64.1 1.7 %collective-permute-start.17 = (bf16[128,1024]{1,0:T(8,128)(2,1)S(1)}, bf16[128,1024]{1,0:T(8,128)(2,1)S(1)}, u32[]{:S(2)}, u32[]{:S(2)}) collective-permute-start(bf16[128,1024]{1,0:T(8,128)(2,1)S(1)} %convolution_convert_fusion.1), channel_id=1, source_target_pairs={{0,2},{1,3},{2,0},{3,1},{4,6},{5,7},{6,4},{7,5},{8,10},{9,11},{10,... | collective-permute-start | bytes 786440 | tf_op jit(solution)/shard_map/ppermute | solution.py:25
  67.0 3.3 %collective-permute-done.23 = f32[64,128]{1,0:T(8,128)S(1)} collective-permute-done((f32[64,128]{1,0:T(8,128)S(1)}, f32[64,128]{1,0:T(8,128)S(1)}, u32[]{:S(2)}, u32[]{:S(2)}) %collective-permute-start.23) | collective-permute-done | bytes 32800 | tf_op jit(solution)/shard_map/ppermute | solution.py:25
  70.3 1.3 %collective-permute-start.24 = (f32[64,128]{1,0:T(8,128)S(1)}, f32[64,128]{1,0:T(8,128)S(1)}, u32[]{:S(2)}, u32[]{:S(2)}) collective-permute-start(f32[64,128]{1,0:T(8,128)S(1)} %add.166), channel_id=1, source_target_pairs={{0,16},{4,20},{8,24},{12,28},{16,0},{20,4},{24,8},{28,12},{1,17},{... | collective-permute-start | bytes 98312 | tf_op jit(solution)/shard_map/ppermute | solution.py:25
  72.2 3.1 %collective-permute-done.24 = f32[64,128]{1,0:T(8,128)S(1)} collective-permute-done((f32[64,128]{1,0:T(8,128)S(1)}, f32[64,128]{1,0:T(8,128)S(1)}, u32[]{:S(2)}, u32[]{:S(2)}) %collective-permute-start.24) | collective-permute-done | bytes 32800 | tf_op jit(solution)/shard_map/ppermute | solution.py:25
  76.9 1.2 %collective-permute-done.16 = bf16[128,1024]{1,0:T(8,128)(2,1)S(1)} collective-permute-done((bf16[128,1024]{1,0:T(8,128)(2,1)S(1)}, bf16[128,1024]{1,0:T(8,128)(2,1)S(1)}, u32[]{:S(2)}, u32[]{:S(2)}) %collective-permute-start.16) | collective-permute-done | bytes 262176 | tf_op jit(solution)/shard_map/ppermute | solution.py:25
  78.6 7.0 %collective-permute-done.19 = bf16[128,1024]{1,0:T(8,128)(2,1)S(1)} collective-permute-done((bf16[128,1024]{1,0:T(8,128)(2,1)S(1)}, bf16[128,1024]{1,0:T(8,128)(2,1)S(1)}, u32[]{:S(2)}, u32[]{:S(2)}) %collective-permute-start.19) | collective-permute-done | bytes 262176 | tf_op jit(solution)/shard_map/ppermute | solution.py:25
  86.5 1.9 %collective-permute-start.21 = (bf16[128,1024]{1,0:T(8,128)(2,1)S(1)}, bf16[128,1024]{1,0:T(8,128)(2,1)S(1)}, u32[]{:S(2)}, u32[]{:S(2)}) collective-permute-start(bf16[128,1024]{1,0:T(8,128)(2,1)S(1)} %fusion.7), channel_id=1, source_target_pairs={{0,8},{4,12},{8,0},{12,4},{16,24},{20,28},{24,16},{28,20},{1,9},{5... | collective-permute-start | bytes 786440 | tf_op jit(solution)/shard_map/ppermute | solution.py:25
  88.7 1.2 %collective-permute-start.22 = (bf16[128,1024]{1,0:T(8,128)(2,1)S(1)}, bf16[128,1024]{1,0:T(8,128)(2,1)S(1)}, u32[]{:S(2)}, u32[]{:S(2)}) collective-permute-start(bf16[128,1024]{1,0:T(8,128)(2,1)S(1)} %fusion.5), channel_id=1, source_target_pairs={{0,16},{4,20},{8,24},{12,28},{16,0},{20,4},{24,8},{28,12},{1,17},{... | collective-permute-start | bytes 786440 | tf_op jit(solution)/shard_map/ppermute | solution.py:25
  89.9 3.9 %collective-permute-done.26 = bf16[64,1088]{1,0:T(8,128)(2,1)S(1)} collective-permute-done((bf16[64,1088]{1,0:T(8,128)(2,1)S(1)}, bf16[64,1088]{1,0:T(8,128)(2,1)S(1)}, u32[]{:S(2)}, u32[]{:S(2)}) %collective-permute-start.26) | collective-permute-done | bytes 139296 | tf_op jit(solution)/shard_map/ppermute | solution.py:25
  95.2 3.5 %collective-permute-done.21 = bf16[128,1024]{1,0:T(8,128)(2,1)S(1)} collective-permute-done((bf16[128,1024]{1,0:T(8,128)(2,1)S(1)}, bf16[128,1024]{1,0:T(8,128)(2,1)S(1)}, u32[]{:S(2)}, u32[]{:S(2)}) %collective-permute-start.21) | collective-permute-done | bytes 262176 | tf_op jit(solution)/shard_map/ppermute | solution.py:25
  98.7 3.0 %collective-permute-done.22 = bf16[128,1024]{1,0:T(8,128)(2,1)S(1)} collective-permute-done((bf16[128,1024]{1,0:T(8,128)(2,1)S(1)}, bf16[128,1024]{1,0:T(8,128)(2,1)S(1)}, u32[]{:S(2)}, u32[]{:S(2)}) %collective-permute-start.22) | collective-permute-done | bytes 262176 | tf_op jit(solution)/shard_map/ppermute | solution.py:25
  101.7 1.1 %fusion.4 = bf16[128,1024]{1,0:T(8,128)(2,1)} fusion(f32[128,1024]{1,0:T(8,128)S(1)} %fusion.16, bf16[512,4096]{1,0:T(8,128)(2,1)S(1)} %shard_map.91, bf16[128,1024]{1,0:T(8,128)(2,1)S(1)} %collective-permute-done.22, bf16[128,1024]{1,0:T(8,128)(2,1)S(1)} %collective-permute-done.21, bf16[128,1024]{1,0:T(8,128)(2,1)S(1)} %collective-permute-done.18, ...), kind=kOutput, calls=%fused_computation.8 | convolution fusion | flops 135528448 | bytes 2752512 | tf_op jit(solution)/shard_map/dot_general | solution.py:20
  (96 shorter events, 14.7 us)
Async XLA Ops:
  0.6 31.0 %copy-start.4 = (s32[128]{0:T(128)S(1)}, s32[128]{0:T(128)}, u32[]{:S(2)}) copy-start(s32[128]{0:T(128)} %param.10) | copy-start | bytes 1540
  0.6 31.0 %copy-start.5 = (s32[128]{0:T(128)S(1)}, s32[128]{0:T(128)}, u32[]{:S(2)}) copy-start(s32[128]{0:T(128)} %param.11) | copy-start | bytes 1540
  2.3 30.9 %copy-start.2 = (bf16[64,8192]{1,0:T(8,128)(2,1)S(1)}, bf16[64,8192]{1,0:T(8,128)(2,1)}, u32[]{:S(2)}) copy-start(bf16[64,8192]{1,0:T(8,128)(2,1)} %refs_0_.1) | copy-start | bytes 3145732
  2.3 31.4 %copy-start.1 = (bf16[128,1024]{1,0:T(8,128)(2,1)S(1)}, bf16[128,1024]{1,0:T(8,128)(2,1)}, u32[]{:S(2)}) copy-start(bf16[128,1024]{1,0:T(8,128)(2,1)} %refs_2_) | copy-start | bytes 786436
  2.6 29.0 %collective-permute-start.6 = (bf16[128,4096]{1,0:T(8,128)(2,1)S(1)}, bf16[128,4096]{1,0:T(8,128)(2,1)S(1)}, u32[]{:S(2)}, u32[]{:S(2)}) collective-permute-start(bf16[128,4096]{1,0:T(8,128)(2,1)S(1)} %shard_map.88), channel_id=1, source_target_pairs={{0,4},{4,0},{8,12},{12,8},{16,20},{20,16},{24,28},{28,24},{1,5},{5... | collective-permute-start | bytes 3145736 | tf_op jit(solution)/shard_map/ppermute | solution.py:25
  5.7 13.5 %collective-permute-start = (bf16[128,1024]{1,0:T(8,128)(2,1)}, bf16[128,1024]{1,0:T(8,128)(2,1)S(1)}, u32[]{:S(2)}, u32[]{:S(2)}) collective-permute-start(bf16[128,1024]{1,0:T(8,128)(2,1)} %refs_2_), channel_id=1, source_target_pairs={{0,8},{4,12},{8,0},{12,4},{16,24},{20,28},{24,16},{28,20},{1,9},{5... | collective-permute-start | bytes 786440 | tf_op jit(solution)/shard_map/ppermute | solution.py:25
  7.2 14.3 %collective-permute-start.4 = (bf16[128,1024]{1,0:T(8,128)(2,1)}, bf16[128,1024]{1,0:T(8,128)(2,1)S(1)}, u32[]{:S(2)}, u32[]{:S(2)}) collective-permute-start(bf16[128,1024]{1,0:T(8,128)(2,1)} %refs_2_), channel_id=1, source_target_pairs={{0,16},{4,20},{8,24},{12,28},{16,0},{20,4},{24,8},{28,12},{1,17},{... | collective-permute-start | bytes 786440 | tf_op jit(solution)/shard_map/ppermute | solution.py:25
  9.8 12.1 %collective-permute-start.3 = (bf16[128,1024]{1,0:T(8,128)(2,1)}, bf16[128,1024]{1,0:T(8,128)(2,1)S(1)}, u32[]{:S(2)}, u32[]{:S(2)}) collective-permute-start(bf16[128,1024]{1,0:T(8,128)(2,1)} %refs_2_), channel_id=1, source_target_pairs={{0,2},{1,3},{2,0},{3,1},{4,6},{5,7},{6,4},{7,5},{8,10},{9,11},{10,... | collective-permute-start | bytes 786440 | tf_op jit(solution)/shard_map/ppermute | solution.py:25
  19.1 9.2 %collective-permute-start.1 = (bf16[128,1024]{1,0:T(8,128)(2,1)S(1)}, bf16[128,1024]{1,0:T(8,128)(2,1)S(1)}, u32[]{:S(2)}, u32[]{:S(2)}) collective-permute-start(bf16[128,1024]{1,0:T(8,128)(2,1)S(1)} %collective-permute-done.refs_4_.refs_3_), channel_id=1, source_target_pairs={{0,2},{1,3},{2,0},{3,1},{4,6},{5,7},{6,4},{7,5},{8,10},{9,11},{10,... | collective-permute-start | bytes 786440 | tf_op jit(solution)/shard_map/ppermute | solution.py:25
  21.5 7.3 %collective-permute-start.5 = (bf16[128,1024]{1,0:T(8,128)(2,1)S(1)}, bf16[128,1024]{1,0:T(8,128)(2,1)S(1)}, u32[]{:S(2)}, u32[]{:S(2)}) collective-permute-start(bf16[128,1024]{1,0:T(8,128)(2,1)S(1)} %collective-permute-done.4.refs_5_.refs_4_), channel_id=1, source_target_pairs={{0,8},{4,12},{8,0},{12,4},{16,24},{20,28},{24,16},{28,20},{1,9},{5... | collective-permute-start | bytes 786440 | tf_op jit(solution)/shard_map/ppermute | solution.py:25
  22.0 9.6 %collective-permute-start.7 = (bf16[128,1024]{1,0:T(8,128)(2,1)S(1)}, bf16[128,1024]{1,0:T(8,128)(2,1)S(1)}, u32[]{:S(2)}, u32[]{:S(2)}) collective-permute-start(bf16[128,1024]{1,0:T(8,128)(2,1)S(1)} %collective-permute-done.4.refs_5_.refs_4_), channel_id=1, source_target_pairs={{0,2},{1,3},{2,0},{3,1},{4,6},{5,7},{6,4},{7,5},{8,10},{9,11},{10,... | collective-permute-start | bytes 786440 | tf_op jit(solution)/shard_map/ppermute | solution.py:25
  28.7 4.9 %collective-permute-start.2 = (bf16[128,4096]{1,0:T(8,128)(2,1)S(1)}, bf16[128,4096]{1,0:T(8,128)(2,1)S(1)}, u32[]{:S(2)}, u32[]{:S(2)}) collective-permute-start(bf16[128,4096]{1,0:T(8,128)(2,1)S(1)} %shard_map.85.refs_0_), channel_id=1, source_target_pairs={{0,1},{1,0},{2,3},{3,2},{4,5},{5,4},{6,7},{7,6},{8,9},{9,8},{10,11... | collective-permute-start | bytes 3145736 | tf_op jit(solution)/shard_map/ppermute | solution.py:25
  31.6 3.6 %collective-permute-start.8 = (bf16[128,4096]{1,0:T(8,128)(2,1)S(1)}, bf16[128,4096]{1,0:T(8,128)(2,1)S(1)}, u32[]{:S(2)}, u32[]{:S(2)}) collective-permute-start(bf16[128,4096]{1,0:T(8,128)(2,1)S(1)} %collective-permute-done.6.refs_0_.refs_3_.refs_2_), channel_id=1, source_target_pairs={{0,1},{1,0},{2,3},{3,2},{4,5},{5,4},{6,7},{7,6},{8,9},{9,8},{10,11... | collective-permute-start | bytes 3145736 | tf_op jit(solution)/shard_map/ppermute | solution.py:25
  31.6 8.8 %collective-permute-start.11 = (bf16[128,1024]{1,0:T(8,128)(2,1)S(1)}, bf16[128,1024]{1,0:T(8,128)(2,1)S(1)}, u32[]{:S(2)}, u32[]{:S(2)}) collective-permute-start(bf16[128,1024]{1,0:T(8,128)(2,1)S(1)} %collective-permute-done.5.refs_6_.refs_5_), channel_id=1, source_target_pairs={{0,2},{1,3},{2,0},{3,1},{4,6},{5,7},{6,4},{7,5},{8,10},{9,11},{10,... | collective-permute-start | bytes 786440 | tf_op jit(solution)/shard_map/ppermute | solution.py:25
  33.2 7.2 %copy-start.3 = (bf16[64,64]{1,0:T(8,128)(2,1)S(1)}, bf16[64,64]{1,0:T(8,128)(2,1)}, u32[]{:S(2)}) copy-start(bf16[64,64]{1,0:T(8,128)(2,1)} %refs_9_.1) | copy-start | bytes 24580
  34.7 8.1 %collective-permute-start.10 = (f32[320,128]{1,0:T(8,128)S(1)}, f32[320,128]{1,0:T(8,128)S(1)}, u32[]{:S(2)}, u32[]{:S(2)}) collective-permute-start(f32[320,128]{1,0:T(8,128)S(1)} %shard_map.87), channel_id=1, source_target_pairs={{0,4},{4,0},{8,12},{12,8},{16,20},{20,16},{24,28},{28,24},{1,5},{5... | collective-permute-start | bytes 491528 | tf_op jit(solution)/shard_map/ppermute | solution.py:25
  36.0 7.9 %collective-permute-start.9 = (f32[256,128]{1,0:T(8,128)S(1)}, f32[256,128]{1,0:T(8,128)S(1)}, u32[]{:S(2)}, u32[]{:S(2)}) collective-permute-start(f32[256,128]{1,0:T(8,128)S(1)} %shard_map.89), channel_id=1, source_target_pairs={{0,4},{4,0},{8,12},{12,8},{16,20},{20,16},{24,28},{28,24},{1,5},{5... | collective-permute-start | bytes 393224 | tf_op jit(solution)/shard_map/ppermute | solution.py:25
  42.0 9.0 %collective-permute-start.12 = (f32[608,128]{1,0:T(8,128)S(1)}, f32[608,128]{1,0:T(8,128)S(1)}, u32[]{:S(2)}, u32[]{:S(2)}) collective-permute-start(f32[608,128]{1,0:T(8,128)S(1)} %shard_map.90), channel_id=1, source_target_pairs={{0,4},{4,0},{8,12},{12,8},{16,20},{20,16},{24,28},{28,24},{1,5},{5... | collective-permute-start | bytes 933896 | tf_op jit(solution)/shard_map/ppermute | solution.py:25
  51.3 3.7 %collective-permute-start.13 = (f32[4,256]{1,0:T(4,128)S(1)}, f32[4,256]{1,0:T(4,128)S(1)}, u32[]{:S(2)}, u32[]{:S(2)}) collective-permute-start(f32[4,256]{1,0:T(4,128)S(1)} %maximum_maximum_fusion), channel_id=1, source_target_pairs={{0,2},{1,3},{2,0},{3,1},{4,6},{5,7},{6,4},{7,5},{8,10},{9,11},{10,... | collective-permute-start | bytes 12296 | tf_op jit(solution)/shard_map/ppermute | solution.py:25
  55.0 3.7 %collective-permute-start.14 = (f32[2,256]{1,0:T(2,128)S(1)}, f32[2,256]{1,0:T(2,128)S(1)}, u32[]{:S(2)}, u32[]{:S(2)}) collective-permute-start(f32[2,256]{1,0:T(2,128)S(1)} %pad_maximum_fusion.6), channel_id=1, source_target_pairs={{0,8},{4,12},{8,0},{12,4},{16,24},{20,28},{24,16},{28,20},{1,9},{5... | collective-permute-start | bytes 6152 | tf_op jit(solution)/shard_map/ppermute | solution.py:25
  58.7 4.5 %collective-permute-start.15 = (f32[2,256]{1,0:T(2,128)S(1)}, f32[2,256]{1,0:T(2,128)S(1)}, u32[]{:S(2)}, u32[]{:S(2)}) collective-permute-start(f32[2,256]{1,0:T(2,128)S(1)} %pad_maximum_fusion.7), channel_id=1, source_target_pairs={{0,16},{4,20},{8,24},{12,28},{16,0},{20,4},{24,8},{28,12},{1,17},{... | collective-permute-start | bytes 6152 | tf_op jit(solution)/shard_map/ppermute | solution.py:25
  64.1 11.7 %collective-permute-start.17 = (bf16[128,1024]{1,0:T(8,128)(2,1)S(1)}, bf16[128,1024]{1,0:T(8,128)(2,1)S(1)}, u32[]{:S(2)}, u32[]{:S(2)}) collective-permute-start(bf16[128,1024]{1,0:T(8,128)(2,1)S(1)} %convolution_convert_fusion.1), channel_id=1, source_target_pairs={{0,2},{1,3},{2,0},{3,1},{4,6},{5,7},{6,4},{7,5},{8,10},{9,11},{10,... | collective-permute-start | bytes 786440 | tf_op jit(solution)/shard_map/ppermute | solution.py:25
  66.4 3.9 %collective-permute-start.23 = (f32[64,128]{1,0:T(8,128)S(1)}, f32[64,128]{1,0:T(8,128)S(1)}, u32[]{:S(2)}, u32[]{:S(2)}) collective-permute-start(f32[64,128]{1,0:T(8,128)S(1)} %fusion.26), channel_id=1, source_target_pairs={{0,8},{4,12},{8,0},{12,4},{16,24},{20,28},{24,16},{28,20},{1,9},{5... | collective-permute-start | bytes 98312 | tf_op jit(solution)/shard_map/ppermute | solution.py:25
  70.3 5.0 %collective-permute-start.24 = (f32[64,128]{1,0:T(8,128)S(1)}, f32[64,128]{1,0:T(8,128)S(1)}, u32[]{:S(2)}, u32[]{:S(2)}) collective-permute-start(f32[64,128]{1,0:T(8,128)S(1)} %add.166), channel_id=1, source_target_pairs={{0,16},{4,20},{8,24},{12,28},{16,0},{20,4},{24,8},{28,12},{1,17},{... | collective-permute-start | bytes 98312 | tf_op jit(solution)/shard_map/ppermute | solution.py:25
  71.7 6.4 %collective-permute-start.16 = (bf16[128,1024]{1,0:T(8,128)(2,1)S(1)}, bf16[128,1024]{1,0:T(8,128)(2,1)S(1)}, u32[]{:S(2)}, u32[]{:S(2)}) collective-permute-start(bf16[128,1024]{1,0:T(8,128)(2,1)S(1)} %convolution_convert_fusion.2), channel_id=1, source_target_pairs={{0,2},{1,3},{2,0},{3,1},{4,6},{5,7},{6,4},{7,5},{8,10},{9,11},{10,... | collective-permute-start | bytes 786440 | tf_op jit(solution)/shard_map/ppermute | solution.py:25
  75.5 3.0 %collective-permute-start.25 = (f32[64,1088]{1,0:T(8,128)S(1)}, f32[64,1088]{1,0:T(8,128)S(1)}, u32[]{:S(2)}, u32[]{:S(2)}) collective-permute-start(f32[64,1088]{1,0:T(8,128)S(1)} %pad_maximum_fusion), channel_id=1, source_target_pairs={{0,1},{1,0},{2,3},{3,2},{4,5},{5,4},{6,7},{7,6},{8,9},{9,8},{10,11... | collective-permute-start | bytes 835592 | tf_op jit(solution)/shard_map/ppermute | solution.py:25
  76.2 10.3 %collective-permute-start.20 = (bf16[128,1024]{1,0:T(8,128)(2,1)S(1)}, bf16[128,1024]{1,0:T(8,128)(2,1)S(1)}, u32[]{:S(2)}, u32[]{:S(2)}) collective-permute-start(bf16[128,1024]{1,0:T(8,128)(2,1)S(1)} %fusion.6), channel_id=1, source_target_pairs={{0,8},{4,12},{8,0},{12,4},{16,24},{20,28},{24,16},{28,20},{1,9},{5... | collective-permute-start | bytes 786440 | tf_op jit(solution)/shard_map/ppermute | solution.py:25
  76.5 9.1 %collective-permute-start.19 = (bf16[128,1024]{1,0:T(8,128)(2,1)S(1)}, bf16[128,1024]{1,0:T(8,128)(2,1)S(1)}, u32[]{:S(2)}, u32[]{:S(2)}) collective-permute-start(bf16[128,1024]{1,0:T(8,128)(2,1)S(1)} %convolution_convert_fusion), channel_id=1, source_target_pairs={{0,2},{1,3},{2,0},{3,1},{4,6},{5,7},{6,4},{7,5},{8,10},{9,11},{10,... | collective-permute-start | bytes 786440 | tf_op jit(solution)/shard_map/ppermute | solution.py:25
  78.1 17.1 %collective-permute-start.18 = (bf16[128,1024]{1,0:T(8,128)(2,1)S(1)}, bf16[128,1024]{1,0:T(8,128)(2,1)S(1)}, u32[]{:S(2)}, u32[]{:S(2)}) collective-permute-start(bf16[128,1024]{1,0:T(8,128)(2,1)S(1)} %convolution_convert_fusion.3), channel_id=1, source_target_pairs={{0,2},{1,3},{2,0},{3,1},{4,6},{5,7},{6,4},{7,5},{8,10},{9,11},{10,... | collective-permute-start | bytes 786440 | tf_op jit(solution)/shard_map/ppermute | solution.py:25
  85.6 8.2 %collective-permute-start.26 = (bf16[64,1088]{1,0:T(8,128)(2,1)S(1)}, bf16[64,1088]{1,0:T(8,128)(2,1)S(1)}, u32[]{:S(2)}, u32[]{:S(2)}) collective-permute-start(bf16[64,1088]{1,0:T(8,128)(2,1)S(1)} %convert_element_type.112), channel_id=1, source_target_pairs={{0,2},{1,3},{2,0},{3,1},{4,6},{5,7},{6,4},{7,5},{8,10},{9,11},{10,... | collective-permute-start | bytes 417800 | tf_op jit(solution)/shard_map/ppermute | solution.py:25
  86.5 12.2 %collective-permute-start.21 = (bf16[128,1024]{1,0:T(8,128)(2,1)S(1)}, bf16[128,1024]{1,0:T(8,128)(2,1)S(1)}, u32[]{:S(2)}, u32[]{:S(2)}) collective-permute-start(bf16[128,1024]{1,0:T(8,128)(2,1)S(1)} %fusion.7), channel_id=1, source_target_pairs={{0,8},{4,12},{8,0},{12,4},{16,24},{20,28},{24,16},{28,20},{1,9},{5... | collective-permute-start | bytes 786440 | tf_op jit(solution)/shard_map/ppermute | solution.py:25
  88.7 13.0 %collective-permute-start.22 = (bf16[128,1024]{1,0:T(8,128)(2,1)S(1)}, bf16[128,1024]{1,0:T(8,128)(2,1)S(1)}, u32[]{:S(2)}, u32[]{:S(2)}) collective-permute-start(bf16[128,1024]{1,0:T(8,128)(2,1)S(1)} %fusion.5), channel_id=1, source_target_pairs={{0,16},{4,20},{8,24},{12,28},{16,0},{20,4},{24,8},{28,12},{1,17},{... | collective-permute-start | bytes 786440 | tf_op jit(solution)/shard_map/ppermute | solution.py:25
  (1 other events, 1.6 us)

commit v11 on v10

--- a/solution.py
+++ b/solution.py
@@ -109,6 +109,22 @@
             transcendentals=0,
         ),
     )(*flat, *tokens, *riders)
+
+
+def finish(total, came):
+    def kernel(total_ref, came_ref, out):
+        out[...] = (total_ref[...] + came_ref[...].astype(f32)).astype(bf16)
+
+    return pl.pallas_call(
+        kernel,
+        out_shape=jax.ShapeDtypeStruct(total.shape, bf16),
+        in_specs=[in_vmem] * 2,
+        out_specs=in_vmem,
+        compiler_params=pltpu.CompilerParams(vmem_limit_bytes=4 << 20),
+        cost_estimate=pl.CostEstimate(
+            flops=8 * total.size, bytes_accessed=8 * total.size, transcendentals=0
+        ),
+    )(total, came)
 
 
 def on_few(hidden, head, factor_rows, factor_basis, targets, loss_mask):
@@ -262,13 +278,17 @@
     for j in reversed(range(n_z)):
         send = part(grad_cross, j).astype(bf16)
         if j + 2 in from_x:
-            send, _, _ = lax.optimization_barrier((send, from_x[j + 2], first_z))
+            waits = (from_x[j + 2], first_came) if j == 0 else (first_z, first_z)
+            send, *_ = lax.optimization_barrier((send, *waits))
+        if j == n_z - 2:
+            send, _ = lax.optimization_barrier((send, first_send))
         first_send = send if j == n_z - 1 else first_send
         from_x[j] = swap_x(send)
         sums[j] = part(grad_own, j) + from_x[j].astype(f32)
         if first_z is None:
             first_z = sums[j].astype(bf16)
-    fresh, _ = lax.optimization_barrier((fresh, first_send))
+            first_came = swap_z(first_z, bits[0]) if bits else first_z
+    fresh, _ = lax.optimization_barrier((fresh, first_z))
     fresh_ids = lax.broadcasted_iota(jnp.int32, (2 * new_here, toks), 0) ^ new_first
     fresh_ids = fresh_ids + rows * n_tok * n_vocab
     fresh_hit = jnp.where(fresh_ids == targets[None, :], weight_row[None, :toks], 0.0)
@@ -277,6 +297,8 @@
     ).astype(bf16)
     mix_total = dot_first(rows_pair, fresh_grad)
     for bit in bits:
+        if bit > 1:
+            mix_total, *_ = lax.optimization_barrier((mix_total, first_came))
         mix_total = mix_total + swap_z(mix_total, bit)
     mix_total = mix_total.astype(bf16)
     rows_part = dot_last(fresh_grad[:new_here], hidden_basis[:, :toks])
@@ -289,10 +311,11 @@
             send = first_z if j == n_z - 1 else total.astype(bf16)
             if bit == bits[0] and came_z is not None:
                 send, _ = lax.optimization_barrier((send, came_z))
-            came = swap_z(send, bit)
+            came = first_came if j == n_z - 1 else swap_z(send, bit)
             came_z = came if came_z is None else came_z
-            sums[j ^ bit] = sums[j ^ bit] + came.astype(f32)
-    hidden_grad = (sums[0] + dot_first(mix_total, basis_half[:, :width])).astype(bf16)
+            total = sums[j ^ bit]
+            sums[j ^ bit] = total + came.astype(f32)
+    hidden_grad = finish(total + dot_first(mix_total, basis_half[:, :width]), came)
 
     factor_part = jnp.concatenate([basis_part, rows_part], axis=1)
     factor_two = lax.reduce_precision(factor_part + swap_core(factor_part), 8, 7)

time: 103 us -> 99.6 us (0.967)
  waiting for transfers between devices: 60.4 us -> 53.3 us
  starting transfers between devices: 28.1 us -> 31.8 us
    ppermute x27, waiting for transfers between devices: 60.4 us -> 53.3 us  [swap(): return lax.ppermute(value, axis, [(i, i ^ bit) for i in range(size)])]
    ppermute x27, starting transfers between devices: 28.1 us -> 31.8 us  [swap(): return lax.ppermute(value, axis, [(i, i ^ bit) for i in range(size)])]
  transfers between devices with their start and end apart: 27 -> 27, of which waited for: 17 -> 16; matrix products, arithmetic and copies ran while one was open for 4% -> 3% of each run, Pallas kernels for 5% -> 5%
where the time goes in v11:
time: 99.6 us; the launch traced here: 99.4 us
  waiting for transfers between devices  53.3 us (54%)
  starting transfers between devices  31.8 us (32%)
  Pallas kernels  5.75 us (6%)
  matrix products  3.52 us (4%)
  local copies, waits for them, and re-layouts  3.04 us (3%)
  between operations  1.05 us (1%)
    ppermute x27, waiting for transfers between devices, swap(): return lax.ppermute(value, axis, [(i, i ^ bit) for i in range(size)])  53.3 us
    ppermute x27, starting transfers between devices, swap(): return lax.ppermute(value, axis, [(i, i ^ bit) for i in range(size)])  31.8 us
    pallas_call x3, Pallas kernels, logits_of(): pl.pallas_call(kernel, out_shape=jax.ShapeDtypeStruct((total + extra, tok...  3.3 us
    dot_general x10, matrix products, dot_first(): return lax.dot_general(a, b, contract_first, preferred_element_type=f32)  3.07 us
  transfers between devices with their start and end apart: 27, of which 16 were waited for; matrix products, arithmetic and copies ran while one was open for 3% of the time, Pallas kernels for 5%

profile of v11, /device:TPU:0, one launch (start us, length us, event | category | flops | bytes accessed | tf_op | source)
XLA Modules:
  0.0 99.4 jit_solution(1387814789027406413)
XLA Ops:
  0.7 1.6 %copy-done = bf16[128,8192]{1,0:T(8,128)(2,1)S(1)} copy-done((bf16[128,8192]{1,0:T(8,128)(2,1)S(1)}, bf16[128,8192]{1,0:T(8,128)(2,1)}, u32[]{:S(2)}) %copy-start) | copy-done | bytes 2097176
  2.6 3.0 %collective-permute-start.6 = (bf16[128,4096]{1,0:T(8,128)(2,1)S(1)}, bf16[128,4096]{1,0:T(8,128)(2,1)S(1)}, u32[]{:S(2)}, u32[]{:S(2)}) collective-permute-start(bf16[128,4096]{1,0:T(8,128)(2,1)S(1)} %shard_map.88), channel_id=1, source_target_pairs={{0,4},{4,0},{8,12},{12,8},{16,20},{20,16},{24,28},{28,24},{1,5},{5... | collective-permute-start | bytes 3145736 | tf_op jit(solution)/shard_map/ppermute | solution.py:25
  5.7 1.6 %collective-permute-start = (bf16[128,1024]{1,0:T(8,128)(2,1)}, bf16[128,1024]{1,0:T(8,128)(2,1)S(1)}, u32[]{:S(2)}, u32[]{:S(2)}) collective-permute-start(bf16[128,1024]{1,0:T(8,128)(2,1)} %refs_2_), channel_id=1, source_target_pairs={{0,8},{4,12},{8,0},{12,4},{16,24},{20,28},{24,16},{28,20},{1,9},{5... | collective-permute-start | bytes 786440 | tf_op jit(solution)/shard_map/ppermute | solution.py:25
  7.2 2.6 %collective-permute-start.4 = (bf16[128,1024]{1,0:T(8,128)(2,1)}, bf16[128,1024]{1,0:T(8,128)(2,1)S(1)}, u32[]{:S(2)}, u32[]{:S(2)}) collective-permute-start(bf16[128,1024]{1,0:T(8,128)(2,1)} %refs_2_), channel_id=1, source_target_pairs={{0,16},{4,20},{8,24},{12,28},{16,0},{20,4},{24,8},{28,12},{1,17},{... | collective-permute-start | bytes 786440 | tf_op jit(solution)/shard_map/ppermute | solution.py:25
  9.8 1.5 %collective-permute-start.3 = (bf16[128,1024]{1,0:T(8,128)(2,1)}, bf16[128,1024]{1,0:T(8,128)(2,1)S(1)}, u32[]{:S(2)}, u32[]{:S(2)}) collective-permute-start(bf16[128,1024]{1,0:T(8,128)(2,1)} %refs_2_), channel_id=1, source_target_pairs={{0,2},{1,3},{2,0},{3,1},{4,6},{5,7},{6,4},{7,5},{8,10},{9,11},{10,... | collective-permute-start | bytes 786440 | tf_op jit(solution)/shard_map/ppermute | solution.py:25
  11.3 7.8 %collective-permute-done.refs_4_.refs_3_ = bf16[128,1024]{1,0:T(8,128)(2,1)S(1)} collective-permute-done((bf16[128,1024]{1,0:T(8,128)(2,1)}, bf16[128,1024]{1,0:T(8,128)(2,1)S(1)}, u32[]{:S(2)}, u32[]{:S(2)}) %collective-permute-start) | collective-permute-done | bytes 262176 | tf_op jit(solution)/shard_map/ppermute | solution.py:25
  19.1 1.5 %collective-permute-start.1 = (bf16[128,1024]{1,0:T(8,128)(2,1)S(1)}, bf16[128,1024]{1,0:T(8,128)(2,1)S(1)}, u32[]{:S(2)}, u32[]{:S(2)}) collective-permute-start(bf16[128,1024]{1,0:T(8,128)(2,1)S(1)} %collective-permute-done.refs_4_.refs_3_), channel_id=1, source_target_pairs={{0,2},{1,3},{2,0},{3,1},{4,6},{5,7},{6,4},{7,5},{8,10},{9,11},{10,... | collective-permute-start | bytes 786440 | tf_op jit(solution)/shard_map/ppermute | solution.py:25
  20.6 0.9 collective-permute-done.4.refs_5_.refs_4_
  22.0 1.5 %collective-permute-start.7 = (bf16[128,1024]{1,0:T(8,128)(2,1)S(1)}, bf16[128,1024]{1,0:T(8,128)(2,1)S(1)}, u32[]{:S(2)}, u32[]{:S(2)}) collective-permute-start(bf16[128,1024]{1,0:T(8,128)(2,1)S(1)} %collective-permute-done.4.refs_5_.refs_4_), channel_id=1, source_target_pairs={{0,2},{1,3},{2,0},{3,1},{4,6},{5,7},{6,4},{7,5},{8,10},{9,11},{10,... | collective-permute-start | bytes 786440 | tf_op jit(solution)/shard_map/ppermute | solution.py:25
  23.5 4.9 %collective-permute-done.1.refs_6_ = bf16[128,1024]{1,0:T(8,128)(2,1)S(1)} collective-permute-done((bf16[128,1024]{1,0:T(8,128)(2,1)S(1)}, bf16[128,1024]{1,0:T(8,128)(2,1)S(1)}, u32[]{:S(2)}, u32[]{:S(2)}) %collective-permute-start.1) | collective-permute-done | bytes 262176 | tf_op jit(solution)/shard_map/ppermute | solution.py:25
  28.8 2.8 %collective-permute-done.7.refs_7_ = bf16[128,1024]{1,0:T(8,128)(2,1)S(1)} collective-permute-done((bf16[128,1024]{1,0:T(8,128)(2,1)S(1)}, bf16[128,1024]{1,0:T(8,128)(2,1)S(1)}, u32[]{:S(2)}, u32[]{:S(2)}) %collective-permute-start.7) | collective-permute-done | bytes 262176 | tf_op jit(solution)/shard_map/ppermute | solution.py:25
  31.6 1.6 %collective-permute-start.11 = (bf16[128,1024]{1,0:T(8,128)(2,1)S(1)}, bf16[128,1024]{1,0:T(8,128)(2,1)S(1)}, u32[]{:S(2)}, u32[]{:S(2)}) collective-permute-start(bf16[128,1024]{1,0:T(8,128)(2,1)S(1)} %collective-permute-done.5.refs_6_.refs_5_), channel_id=1, source_target_pairs={{0,2},{1,3},{2,0},{3,1},{4,6},{5,7},{6,4},{7,5},{8,10},{9,11},{10,... | collective-permute-start | bytes 786440 | tf_op jit(solution)/shard_map/ppermute | solution.py:25
  33.6 1.0 %shard_map.87 = f32[320,128]{1,0:T(8,128)S(1)} custom-call(bf16[128,4096]{1,0:T(8,128)(2,1)S(1)} %shard_map.85.refs_0_, bf16[128,4096]{1,0:T(8,128)(2,1)S(1)} %collective-permute-done.2.refs_1_, bf16[64,4096]{1,0:T(8,128)(2,1)S(1)} %shard_map.86.refs_2_, bf16[128,1024]{1,0:T(8,128)(2,1)S(1)} %copy-done.1, ...), custom_call_target="tpu_custom_call" | custom-call | flops 335544320 | bytes 3833856 | tf_op jit(solution)/shard_map/pallas_call | solution.py:100
  36.0 1.6 %collective-permute-start.9 = (f32[256,128]{1,0:T(8,128)S(1)}, f32[256,128]{1,0:T(8,128)S(1)}, u32[]{:S(2)}, u32[]{:S(2)}) collective-permute-start(f32[256,128]{1,0:T(8,128)S(1)} %shard_map.89), channel_id=1, source_target_pairs={{0,4},{4,0},{8,12},{12,8},{16,20},{20,16},{24,28},{28,24},{1,5},{5... | collective-permute-start | bytes 393224 | tf_op jit(solution)/shard_map/ppermute | solution.py:25
  37.5 2.9 %collective-permute-done.11.refs_8_ = bf16[128,1024]{1,0:T(8,128)(2,1)S(1)} collective-permute-done((bf16[128,1024]{1,0:T(8,128)(2,1)S(1)}, bf16[128,1024]{1,0:T(8,128)(2,1)S(1)}, u32[]{:S(2)}, u32[]{:S(2)}) %collective-permute-start.11) | collective-permute-done | bytes 262176 | tf_op jit(solution)/shard_map/ppermute | solution.py:25
  40.4 1.6 %shard_map.90 = f32[608,128]{1,0:T(8,128)S(1)} custom-call(bf16[128,4096]{1,0:T(8,128)(2,1)S(1)} %shard_map.85.refs_0_, bf16[128,4096]{1,0:T(8,128)(2,1)S(1)} %collective-permute-done.2.refs_1_, bf16[64,4096]{1,0:T(8,128)(2,1)S(1)} %shard_map.86.refs_2_, bf16[128,4096]{1,0:T(8,128)(2,1)S(1)} %collective-permute-done.6.refs_0_.refs_3_.refs_2_, ...), custom_call_target="tpu_custom_call" | custom-call | flops 603979776 | bytes 6062080 | tf_op jit(solution)/shard_map/pallas_call | solution.py:100
  44.0 7.0 %collective-permute-done.12 = f32[608,128]{1,0:T(8,128)S(1)} collective-permute-done((f32[608,128]{1,0:T(8,128)S(1)}, f32[608,128]{1,0:T(8,128)S(1)}, u32[]{:S(2)}, u32[]{:S(2)}) %collective-permute-start.12) | collective-permute-done | bytes 311328 | tf_op jit(solution)/shard_map/ppermute | solution.py:25
  51.3 1.6 %collective-permute-start.13 = (f32[4,256]{1,0:T(4,128)S(1)}, f32[4,256]{1,0:T(4,128)S(1)}, u32[]{:S(2)}, u32[]{:S(2)}) collective-permute-start(f32[4,256]{1,0:T(4,128)S(1)} %maximum_maximum_fusion), channel_id=1, source_target_pairs={{0,2},{1,3},{2,0},{3,1},{4,6},{5,7},{6,4},{7,5},{8,10},{9,11},{10,... | collective-permute-start | bytes 12296 | tf_op jit(solution)/shard_map/ppermute | solution.py:25
  53.1 1.9 %collective-permute-done.13 = f32[4,256]{1,0:T(4,128)S(1)} collective-permute-done((f32[4,256]{1,0:T(4,128)S(1)}, f32[4,256]{1,0:T(4,128)S(1)}, u32[]{:S(2)}, u32[]{:S(2)}) %collective-permute-start.13) | collective-permute-done | bytes 4128 | tf_op jit(solution)/shard_map/ppermute | solution.py:25
  55.1 3.5 %collective-permute-done.14 = f32[2,256]{1,0:T(2,128)S(1)} collective-permute-done((f32[2,256]{1,0:T(2,128)S(1)}, f32[2,256]{1,0:T(2,128)S(1)}, u32[]{:S(2)}, u32[]{:S(2)}) %collective-permute-start.14) | collective-permute-done | bytes 2080 | tf_op jit(solution)/shard_map/ppermute | solution.py:25
  58.7 1.3 %collective-permute-start.15 = (f32[2,256]{1,0:T(2,128)S(1)}, f32[2,256]{1,0:T(2,128)S(1)}, u32[]{:S(2)}, u32[]{:S(2)}) collective-permute-start(f32[2,256]{1,0:T(2,128)S(1)} %pad_maximum_fusion.7), channel_id=1, source_target_pairs={{0,16},{4,20},{8,24},{12,28},{16,0},{20,4},{24,8},{28,12},{1,17},{... | collective-permute-start | bytes 6152 | tf_op jit(solution)/shard_map/ppermute | solution.py:25
  60.0 3.2 %collective-permute-done.15 = f32[2,256]{1,0:T(2,128)S(1)} collective-permute-done((f32[2,256]{1,0:T(2,128)S(1)}, f32[2,256]{1,0:T(2,128)S(1)}, u32[]{:S(2)}, u32[]{:S(2)}) %collective-permute-start.15) | collective-permute-done | bytes 2080 | tf_op jit(solution)/shard_map/ppermute | solution.py:25
  64.1 1.6 %collective-permute-start.17 = (bf16[128,1024]{1,0:T(8,128)(2,1)S(1)}, bf16[128,1024]{1,0:T(8,128)(2,1)S(1)}, u32[]{:S(2)}, u32[]{:S(2)}) collective-permute-start(bf16[128,1024]{1,0:T(8,128)(2,1)S(1)} %convolution_convert_fusion.1), channel_id=1, source_target_pairs={{0,2},{1,3},{2,0},{3,1},{4,6},{5,7},{6,4},{7,5},{8,10},{9,11},{10,... | collective-permute-start | bytes 786440 | tf_op jit(solution)/shard_map/ppermute | solution.py:25
  67.0 4.5 %collective-permute-done.17 = bf16[128,1024]{1,0:T(8,128)(2,1)S(1)} collective-permute-done((bf16[128,1024]{1,0:T(8,128)(2,1)S(1)}, bf16[128,1024]{1,0:T(8,128)(2,1)S(1)}, u32[]{:S(2)}, u32[]{:S(2)}) %collective-permute-start.17) | collective-permute-done | bytes 262176 | tf_op jit(solution)/shard_map/ppermute | solution.py:25
  72.8 1.4 %collective-permute-start.22 = (f32[64,128]{1,0:T(8,128)S(1)}, f32[64,128]{1,0:T(8,128)S(1)}, u32[]{:S(2)}, u32[]{:S(2)}) collective-permute-start(f32[64,128]{1,0:T(8,128)S(1)} %fusion.24), channel_id=1, source_target_pairs={{0,8},{4,12},{8,0},{12,4},{16,24},{20,28},{24,16},{28,20},{1,9},{5... | collective-permute-start | bytes 98312 | tf_op jit(solution)/shard_map/ppermute | solution.py:25
  74.3 1.5 %collective-permute-start.20 = (bf16[128,1024]{1,0:T(8,128)(2,1)S(1)}, bf16[128,1024]{1,0:T(8,128)(2,1)S(1)}, u32[]{:S(2)}, u32[]{:S(2)}) collective-permute-start(bf16[128,1024]{1,0:T(8,128)(2,1)S(1)} %convolution_convert_fusion), channel_id=1, source_target_pairs={{0,2},{1,3},{2,0},{3,1},{4,6},{5,7},{6,4},{7,5},{8,10},{9,11},{10,... | collective-permute-start | bytes 786440 | tf_op jit(solution)/shard_map/ppermute | solution.py:25
  75.8 5.6 %collective-permute-done.22 = f32[64,128]{1,0:T(8,128)S(1)} collective-permute-done((f32[64,128]{1,0:T(8,128)S(1)}, f32[64,128]{1,0:T(8,128)S(1)}, u32[]{:S(2)}, u32[]{:S(2)}) %collective-permute-start.22) | collective-permute-done | bytes 32800 | tf_op jit(solution)/shard_map/ppermute | solution.py:25
  82.6 2.2 %collective-permute-start.24 = (bf16[128,1024]{1,0:T(8,128)(2,1)S(1)}, bf16[128,1024]{1,0:T(8,128)(2,1)S(1)}, u32[]{:S(2)}, u32[]{:S(2)}) collective-permute-start(bf16[128,1024]{1,0:T(8,128)(2,1)S(1)} %fusion.3), channel_id=1, source_target_pairs={{0,16},{4,20},{8,24},{12,28},{16,0},{20,4},{24,8},{28,12},{1,17},{... | collective-permute-start | bytes 786440 | tf_op jit(solution)/shard_map/ppermute | solution.py:25
  84.8 1.5 %collective-permute-start.19 = (bf16[128,1024]{1,0:T(8,128)(2,1)S(1)}, bf16[128,1024]{1,0:T(8,128)(2,1)S(1)}, u32[]{:S(2)}, u32[]{:S(2)}) collective-permute-start(bf16[128,1024]{1,0:T(8,128)(2,1)S(1)} %convolution_convert_fusion.3), channel_id=1, source_target_pairs={{0,2},{1,3},{2,0},{3,1},{4,6},{5,7},{6,4},{7,5},{8,10},{9,11},{10,... | collective-permute-start | bytes 786440 | tf_op jit(solution)/shard_map/ppermute | solution.py:25
  88.4 1.6 %collective-permute-start.26 = (bf16[64,1088]{1,0:T(8,128)(2,1)S(1)}, bf16[64,1088]{1,0:T(8,128)(2,1)S(1)}, u32[]{:S(2)}, u32[]{:S(2)}) collective-permute-start(bf16[64,1088]{1,0:T(8,128)(2,1)S(1)} %convert_element_type.104), channel_id=1, source_target_pairs={{0,2},{1,3},{2,0},{3,1},{4,6},{5,7},{6,4},{7,5},{8,10},{9,11},{10,... | collective-permute-start | bytes 417800 | tf_op jit(solution)/shard_map/ppermute | solution.py:25
  89.9 1.3 %collective-permute-done.19 = bf16[128,1024]{1,0:T(8,128)(2,1)S(1)} collective-permute-done((bf16[128,1024]{1,0:T(8,128)(2,1)S(1)}, bf16[128,1024]{1,0:T(8,128)(2,1)S(1)}, u32[]{:S(2)}, u32[]{:S(2)}) %collective-permute-start.19) | collective-permute-done | bytes 262176 | tf_op jit(solution)/shard_map/ppermute | solution.py:25
  91.2 5.8 %collective-permute-done.21 = bf16[128,1024]{1,0:T(8,128)(2,1)S(1)} collective-permute-done((bf16[128,1024]{1,0:T(8,128)(2,1)S(1)}, bf16[128,1024]{1,0:T(8,128)(2,1)S(1)}, u32[]{:S(2)}, u32[]{:S(2)}) %collective-permute-start.21) | collective-permute-done | bytes 262176 | tf_op jit(solution)/shard_map/ppermute | solution.py:25
  (97 shorter events, 14.8 us)
Async XLA Ops:
  0.6 31.0 %copy-start.4 = (s32[128]{0:T(128)S(1)}, s32[128]{0:T(128)}, u32[]{:S(2)}) copy-start(s32[128]{0:T(128)} %param.10) | copy-start | bytes 1540
  0.6 31.0 %copy-start.5 = (s32[128]{0:T(128)S(1)}, s32[128]{0:T(128)}, u32[]{:S(2)}) copy-start(s32[128]{0:T(128)} %param.11) | copy-start | bytes 1540
  2.3 30.9 %copy-start.2 = (bf16[64,8192]{1,0:T(8,128)(2,1)S(1)}, bf16[64,8192]{1,0:T(8,128)(2,1)}, u32[]{:S(2)}) copy-start(bf16[64,8192]{1,0:T(8,128)(2,1)} %refs_0_.1) | copy-start | bytes 3145732
  2.3 31.4 %copy-start.1 = (bf16[128,1024]{1,0:T(8,128)(2,1)S(1)}, bf16[128,1024]{1,0:T(8,128)(2,1)}, u32[]{:S(2)}) copy-start(bf16[128,1024]{1,0:T(8,128)(2,1)} %refs_2_) | copy-start | bytes 786436
  2.6 29.0 %collective-permute-start.6 = (bf16[128,4096]{1,0:T(8,128)(2,1)S(1)}, bf16[128,4096]{1,0:T(8,128)(2,1)S(1)}, u32[]{:S(2)}, u32[]{:S(2)}) collective-permute-start(bf16[128,4096]{1,0:T(8,128)(2,1)S(1)} %shard_map.88), channel_id=1, source_target_pairs={{0,4},{4,0},{8,12},{12,8},{16,20},{20,16},{24,28},{28,24},{1,5},{5... | collective-permute-start | bytes 3145736 | tf_op jit(solution)/shard_map/ppermute | solution.py:25
  5.7 13.5 %collective-permute-start = (bf16[128,1024]{1,0:T(8,128)(2,1)}, bf16[128,1024]{1,0:T(8,128)(2,1)S(1)}, u32[]{:S(2)}, u32[]{:S(2)}) collective-permute-start(bf16[128,1024]{1,0:T(8,128)(2,1)} %refs_2_), channel_id=1, source_target_pairs={{0,8},{4,12},{8,0},{12,4},{16,24},{20,28},{24,16},{28,20},{1,9},{5... | collective-permute-start | bytes 786440 | tf_op jit(solution)/shard_map/ppermute | solution.py:25
  7.2 14.3 %collective-permute-start.4 = (bf16[128,1024]{1,0:T(8,128)(2,1)}, bf16[128,1024]{1,0:T(8,128)(2,1)S(1)}, u32[]{:S(2)}, u32[]{:S(2)}) collective-permute-start(bf16[128,1024]{1,0:T(8,128)(2,1)} %refs_2_), channel_id=1, source_target_pairs={{0,16},{4,20},{8,24},{12,28},{16,0},{20,4},{24,8},{28,12},{1,17},{... | collective-permute-start | bytes 786440 | tf_op jit(solution)/shard_map/ppermute | solution.py:25
  9.8 12.1 %collective-permute-start.3 = (bf16[128,1024]{1,0:T(8,128)(2,1)}, bf16[128,1024]{1,0:T(8,128)(2,1)S(1)}, u32[]{:S(2)}, u32[]{:S(2)}) collective-permute-start(bf16[128,1024]{1,0:T(8,128)(2,1)} %refs_2_), channel_id=1, source_target_pairs={{0,2},{1,3},{2,0},{3,1},{4,6},{5,7},{6,4},{7,5},{8,10},{9,11},{10,... | collective-permute-start | bytes 786440 | tf_op jit(solution)/shard_map/ppermute | solution.py:25
  19.1 9.2 %collective-permute-start.1 = (bf16[128,1024]{1,0:T(8,128)(2,1)S(1)}, bf16[128,1024]{1,0:T(8,128)(2,1)S(1)}, u32[]{:S(2)}, u32[]{:S(2)}) collective-permute-start(bf16[128,1024]{1,0:T(8,128)(2,1)S(1)} %collective-permute-done.refs_4_.refs_3_), channel_id=1, source_target_pairs={{0,2},{1,3},{2,0},{3,1},{4,6},{5,7},{6,4},{7,5},{8,10},{9,11},{10,... | collective-permute-start | bytes 786440 | tf_op jit(solution)/shard_map/ppermute | solution.py:25
  21.5 7.3 %collective-permute-start.5 = (bf16[128,1024]{1,0:T(8,128)(2,1)S(1)}, bf16[128,1024]{1,0:T(8,128)(2,1)S(1)}, u32[]{:S(2)}, u32[]{:S(2)}) collective-permute-start(bf16[128,1024]{1,0:T(8,128)(2,1)S(1)} %collective-permute-done.4.refs_5_.refs_4_), channel_id=1, source_target_pairs={{0,8},{4,12},{8,0},{12,4},{16,24},{20,28},{24,16},{28,20},{1,9},{5... | collective-permute-start | bytes 786440 | tf_op jit(solution)/shard_map/ppermute | solution.py:25
  22.0 9.6 %collective-permute-start.7 = (bf16[128,1024]{1,0:T(8,128)(2,1)S(1)}, bf16[128,1024]{1,0:T(8,128)(2,1)S(1)}, u32[]{:S(2)}, u32[]{:S(2)}) collective-permute-start(bf16[128,1024]{1,0:T(8,128)(2,1)S(1)} %collective-permute-done.4.refs_5_.refs_4_), channel_id=1, source_target_pairs={{0,2},{1,3},{2,0},{3,1},{4,6},{5,7},{6,4},{7,5},{8,10},{9,11},{10,... | collective-permute-start | bytes 786440 | tf_op jit(solution)/shard_map/ppermute | solution.py:25
  28.7 4.9 %collective-permute-start.2 = (bf16[128,4096]{1,0:T(8,128)(2,1)S(1)}, bf16[128,4096]{1,0:T(8,128)(2,1)S(1)}, u32[]{:S(2)}, u32[]{:S(2)}) collective-permute-start(bf16[128,4096]{1,0:T(8,128)(2,1)S(1)} %shard_map.85.refs_0_), channel_id=1, source_target_pairs={{0,1},{1,0},{2,3},{3,2},{4,5},{5,4},{6,7},{7,6},{8,9},{9,8},{10,11... | collective-permute-start | bytes 3145736 | tf_op jit(solution)/shard_map/ppermute | solution.py:25
  31.6 3.6 %collective-permute-start.8 = (bf16[128,4096]{1,0:T(8,128)(2,1)S(1)}, bf16[128,4096]{1,0:T(8,128)(2,1)S(1)}, u32[]{:S(2)}, u32[]{:S(2)}) collective-permute-start(bf16[128,4096]{1,0:T(8,128)(2,1)S(1)} %collective-permute-done.6.refs_0_.refs_3_.refs_2_), channel_id=1, source_target_pairs={{0,1},{1,0},{2,3},{3,2},{4,5},{5,4},{6,7},{7,6},{8,9},{9,8},{10,11... | collective-permute-start | bytes 3145736 | tf_op jit(solution)/shard_map/ppermute | solution.py:25
  31.6 8.8 %collective-permute-start.11 = (bf16[128,1024]{1,0:T(8,128)(2,1)S(1)}, bf16[128,1024]{1,0:T(8,128)(2,1)S(1)}, u32[]{:S(2)}, u32[]{:S(2)}) collective-permute-start(bf16[128,1024]{1,0:T(8,128)(2,1)S(1)} %collective-permute-done.5.refs_6_.refs_5_), channel_id=1, source_target_pairs={{0,2},{1,3},{2,0},{3,1},{4,6},{5,7},{6,4},{7,5},{8,10},{9,11},{10,... | collective-permute-start | bytes 786440 | tf_op jit(solution)/shard_map/ppermute | solution.py:25
  33.2 7.2 %copy-start.3 = (bf16[64,64]{1,0:T(8,128)(2,1)S(1)}, bf16[64,64]{1,0:T(8,128)(2,1)}, u32[]{:S(2)}) copy-start(bf16[64,64]{1,0:T(8,128)(2,1)} %refs_9_.1) | copy-start | bytes 24580
  34.7 8.1 %collective-permute-start.10 = (f32[320,128]{1,0:T(8,128)S(1)}, f32[320,128]{1,0:T(8,128)S(1)}, u32[]{:S(2)}, u32[]{:S(2)}) collective-permute-start(f32[320,128]{1,0:T(8,128)S(1)} %shard_map.87), channel_id=1, source_target_pairs={{0,4},{4,0},{8,12},{12,8},{16,20},{20,16},{24,28},{28,24},{1,5},{5... | collective-permute-start | bytes 491528 | tf_op jit(solution)/shard_map/ppermute | solution.py:25
  36.0 7.9 %collective-permute-start.9 = (f32[256,128]{1,0:T(8,128)S(1)}, f32[256,128]{1,0:T(8,128)S(1)}, u32[]{:S(2)}, u32[]{:S(2)}) collective-permute-start(f32[256,128]{1,0:T(8,128)S(1)} %shard_map.89), channel_id=1, source_target_pairs={{0,4},{4,0},{8,12},{12,8},{16,20},{20,16},{24,28},{28,24},{1,5},{5... | collective-permute-start | bytes 393224 | tf_op jit(solution)/shard_map/ppermute | solution.py:25
  42.0 9.0 %collective-permute-start.12 = (f32[608,128]{1,0:T(8,128)S(1)}, f32[608,128]{1,0:T(8,128)S(1)}, u32[]{:S(2)}, u32[]{:S(2)}) collective-permute-start(f32[608,128]{1,0:T(8,128)S(1)} %shard_map.90), channel_id=1, source_target_pairs={{0,4},{4,0},{8,12},{12,8},{16,20},{20,16},{24,28},{28,24},{1,5},{5... | collective-permute-start | bytes 933896 | tf_op jit(solution)/shard_map/ppermute | solution.py:25
  51.3 3.7 %collective-permute-start.13 = (f32[4,256]{1,0:T(4,128)S(1)}, f32[4,256]{1,0:T(4,128)S(1)}, u32[]{:S(2)}, u32[]{:S(2)}) collective-permute-start(f32[4,256]{1,0:T(4,128)S(1)} %maximum_maximum_fusion), channel_id=1, source_target_pairs={{0,2},{1,3},{2,0},{3,1},{4,6},{5,7},{6,4},{7,5},{8,10},{9,11},{10,... | collective-permute-start | bytes 12296 | tf_op jit(solution)/shard_map/ppermute | solution.py:25
  55.0 3.7 %collective-permute-start.14 = (f32[2,256]{1,0:T(2,128)S(1)}, f32[2,256]{1,0:T(2,128)S(1)}, u32[]{:S(2)}, u32[]{:S(2)}) collective-permute-start(f32[2,256]{1,0:T(2,128)S(1)} %pad_maximum_fusion.6), channel_id=1, source_target_pairs={{0,8},{4,12},{8,0},{12,4},{16,24},{20,28},{24,16},{28,20},{1,9},{5... | collective-permute-start | bytes 6152 | tf_op jit(solution)/shard_map/ppermute | solution.py:25
  58.7 4.5 %collective-permute-start.15 = (f32[2,256]{1,0:T(2,128)S(1)}, f32[2,256]{1,0:T(2,128)S(1)}, u32[]{:S(2)}, u32[]{:S(2)}) collective-permute-start(f32[2,256]{1,0:T(2,128)S(1)} %pad_maximum_fusion.7), channel_id=1, source_target_pairs={{0,16},{4,20},{8,24},{12,28},{16,0},{20,4},{24,8},{28,12},{1,17},{... | collective-permute-start | bytes 6152 | tf_op jit(solution)/shard_map/ppermute | solution.py:25
  64.1 7.3 %collective-permute-start.17 = (bf16[128,1024]{1,0:T(8,128)(2,1)S(1)}, bf16[128,1024]{1,0:T(8,128)(2,1)S(1)}, u32[]{:S(2)}, u32[]{:S(2)}) collective-permute-start(bf16[128,1024]{1,0:T(8,128)(2,1)S(1)} %convolution_convert_fusion.1), channel_id=1, source_target_pairs={{0,2},{1,3},{2,0},{3,1},{4,6},{5,7},{6,4},{7,5},{8,10},{9,11},{10,... | collective-permute-start | bytes 786440 | tf_op jit(solution)/shard_map/ppermute | solution.py:25
  66.0 16.2 %collective-permute-start.16 = (bf16[128,1024]{1,0:T(8,128)(2,1)S(1)}, bf16[128,1024]{1,0:T(8,128)(2,1)S(1)}, u32[]{:S(2)}, u32[]{:S(2)}) collective-permute-start(bf16[128,1024]{1,0:T(8,128)(2,1)S(1)} %convolution_convert_fusion.2), channel_id=1, source_target_pairs={{0,2},{1,3},{2,0},{3,1},{4,6},{5,7},{6,4},{7,5},{8,10},{9,11},{10,... | collective-permute-start | bytes 786440 | tf_op jit(solution)/shard_map/ppermute | solution.py:25
  71.8 9.6 %collective-permute-start.18 = (bf16[128,1024]{1,0:T(8,128)(2,1)S(1)}, bf16[128,1024]{1,0:T(8,128)(2,1)S(1)}, u32[]{:S(2)}, u32[]{:S(2)}) collective-permute-start(bf16[128,1024]{1,0:T(8,128)(2,1)S(1)} %fusion.4), channel_id=1, source_target_pairs={{0,8},{4,12},{8,0},{12,4},{16,24},{20,28},{24,16},{28,20},{1,9},{5... | collective-permute-start | bytes 786440 | tf_op jit(solution)/shard_map/ppermute | solution.py:25
  72.8 8.6 %collective-permute-start.22 = (f32[64,128]{1,0:T(8,128)S(1)}, f32[64,128]{1,0:T(8,128)S(1)}, u32[]{:S(2)}, u32[]{:S(2)}) collective-permute-start(f32[64,128]{1,0:T(8,128)S(1)} %fusion.24), channel_id=1, source_target_pairs={{0,8},{4,12},{8,0},{12,4},{16,24},{20,28},{24,16},{28,20},{1,9},{5... | collective-permute-start | bytes 98312 | tf_op jit(solution)/shard_map/ppermute | solution.py:25
  74.3 12.4 %collective-permute-start.20 = (bf16[128,1024]{1,0:T(8,128)(2,1)S(1)}, bf16[128,1024]{1,0:T(8,128)(2,1)S(1)}, u32[]{:S(2)}, u32[]{:S(2)}) collective-permute-start(bf16[128,1024]{1,0:T(8,128)(2,1)S(1)} %convolution_convert_fusion), channel_id=1, source_target_pairs={{0,2},{1,3},{2,0},{3,1},{4,6},{5,7},{6,4},{7,5},{8,10},{9,11},{10,... | collective-permute-start | bytes 786440 | tf_op jit(solution)/shard_map/ppermute | solution.py:25
  81.4 5.0 %collective-permute-start.23 = (f32[64,128]{1,0:T(8,128)S(1)}, f32[64,128]{1,0:T(8,128)S(1)}, u32[]{:S(2)}, u32[]{:S(2)}) collective-permute-start(f32[64,128]{1,0:T(8,128)S(1)} %add.160), channel_id=1, source_target_pairs={{0,16},{4,20},{8,24},{12,28},{16,0},{20,4},{24,8},{28,12},{1,17},{... | collective-permute-start | bytes 98312 | tf_op jit(solution)/shard_map/ppermute | solution.py:25
  82.6 14.7 %collective-permute-start.24 = (bf16[128,1024]{1,0:T(8,128)(2,1)S(1)}, bf16[128,1024]{1,0:T(8,128)(2,1)S(1)}, u32[]{:S(2)}, u32[]{:S(2)}) collective-permute-start(bf16[128,1024]{1,0:T(8,128)(2,1)S(1)} %fusion.3), channel_id=1, source_target_pairs={{0,16},{4,20},{8,24},{12,28},{16,0},{20,4},{24,8},{28,12},{1,17},{... | collective-permute-start | bytes 786440 | tf_op jit(solution)/shard_map/ppermute | solution.py:25
  84.8 6.4 %collective-permute-start.19 = (bf16[128,1024]{1,0:T(8,128)(2,1)S(1)}, bf16[128,1024]{1,0:T(8,128)(2,1)S(1)}, u32[]{:S(2)}, u32[]{:S(2)}) collective-permute-start(bf16[128,1024]{1,0:T(8,128)(2,1)S(1)} %convolution_convert_fusion.3), channel_id=1, source_target_pairs={{0,2},{1,3},{2,0},{3,1},{4,6},{5,7},{6,4},{7,5},{8,10},{9,11},{10,... | collective-permute-start | bytes 786440 | tf_op jit(solution)/shard_map/ppermute | solution.py:25
  86.6 1.6 %collective-permute-start.25 = (f32[64,1088]{1,0:T(8,128)S(1)}, f32[64,1088]{1,0:T(8,128)S(1)}, u32[]{:S(2)}, u32[]{:S(2)}) collective-permute-start(f32[64,1088]{1,0:T(8,128)S(1)} %pad_maximum_fusion), channel_id=1, source_target_pairs={{0,1},{1,0},{2,3},{3,2},{4,5},{5,4},{6,7},{7,6},{8,9},{9,8},{10,11... | collective-permute-start | bytes 835592 | tf_op jit(solution)/shard_map/ppermute | solution.py:25
  87.1 9.9 %collective-permute-start.21 = (bf16[128,1024]{1,0:T(8,128)(2,1)S(1)}, bf16[128,1024]{1,0:T(8,128)(2,1)S(1)}, u32[]{:S(2)}, u32[]{:S(2)}) collective-permute-start(bf16[128,1024]{1,0:T(8,128)(2,1)S(1)} %fusion.5), channel_id=1, source_target_pairs={{0,8},{4,12},{8,0},{12,4},{16,24},{20,28},{24,16},{28,20},{1,9},{5... | collective-permute-start | bytes 786440 | tf_op jit(solution)/shard_map/ppermute | solution.py:25
  88.4 9.7 %collective-permute-start.26 = (bf16[64,1088]{1,0:T(8,128)(2,1)S(1)}, bf16[64,1088]{1,0:T(8,128)(2,1)S(1)}, u32[]{:S(2)}, u32[]{:S(2)}) collective-permute-start(bf16[64,1088]{1,0:T(8,128)(2,1)S(1)} %convert_element_type.104), channel_id=1, source_target_pairs={{0,2},{1,3},{2,0},{3,1},{4,6},{5,7},{6,4},{7,5},{8,10},{9,11},{10,... | collective-permute-start | bytes 417800 | tf_op jit(solution)/shard_map/ppermute | solution.py:25
  (1 other events, 1.6 us)

commit v12 on v11

--- a/solution.py
+++ b/solution.py
@@ -296,8 +296,8 @@
         jnp.exp(fresh[:, :toks] - row_top[None, :toks]) * scale_row[None, :toks] - fresh_hit
     ).astype(bf16)
     mix_total = dot_first(rows_pair, fresh_grad)
-    for bit in bits:
-        if bit > 1:
+    for bit in reversed(bits):
+        if bit == 1:
             mix_total, *_ = lax.optimization_barrier((mix_total, first_came))
         mix_total = mix_total + swap_z(mix_total, bit)
     mix_total = mix_total.astype(bf16)
@@ -315,13 +315,14 @@
             came_z = came if came_z is None else came_z
             total = sums[j ^ bit]
             sums[j ^ bit] = total + came.astype(f32)
-    hidden_grad = finish(total + dot_first(mix_total, basis_half[:, :width]), came)
-
     factor_part = jnp.concatenate([basis_part, rows_part], axis=1)
     factor_two = lax.reduce_precision(factor_part + swap_core(factor_part), 8, 7)
     factor_two, _ = lax.optimization_barrier((factor_two, from_x[min(1, n_z - 1)]))
     factor_grad = factor_two + swap_x(factor_two.astype(bf16)).astype(f32)
     basis_grad, rows_grad = factor_grad[:, :width], factor_grad[:, width:]
+    came, basis_grad, rows_grad = lax.optimization_barrier((came, basis_grad, rows_grad))
+    hidden_grad = finish(total + dot_first(mix_total, basis_half[:, :width]), came)
+
     return hidden_grad, rows_grad, basis_grad
 
 

time: 99.6 us -> 101 us (1.014)
  starting transfers between devices: 31.8 us -> 37 us
  waiting for transfers between devices: 53.3 us -> 49.1 us
    ppermute x27, starting transfers between devices: 31.8 us -> 37 us  [swap(): return lax.ppermute(value, axis, [(i, i ^ bit) for i in range(size)])]
    ppermute x27, waiting for transfers between devices: 53.3 us -> 49.1 us  [swap(): return lax.ppermute(value, axis, [(i, i ^ bit) for i in range(size)])]
  transfers between devices with their start and end apart: 27 -> 27, of which waited for: 16 -> 14; matrix products, arithmetic and copies ran while one was open for 3% -> 5% of each run, Pallas kernels for 5% -> 5%
where the time goes in v12:
time: 101 us; the launch traced here: 100 us
  waiting for transfers between devices  49.1 us (49%)
  starting transfers between devices  37 us (37%)
  Pallas kernels  5.75 us (6%)
  matrix products  3.53 us (3%)
  local copies, waits for them, and re-layouts  3.04 us (3%)
  between operations  1.05 us (1%)
    ppermute x27, waiting for transfers between devices, swap(): return lax.ppermute(value, axis, [(i, i ^ bit) for i in range(size)])  49.1 us
    ppermute x27, starting transfers between devices, swap(): return lax.ppermute(value, axis, [(i, i ^ bit) for i in range(size)])  37 us
    pallas_call x3, Pallas kernels, logits_of(): pl.pallas_call(kernel, out_shape=jax.ShapeDtypeStruct((total + extra, tok...  3.3 us
    dot_general x10, matrix products, dot_first(): return lax.dot_general(a, b, contract_first, preferred_element_type=f32)  3.08 us
  transfers between devices with their start and end apart: 27, of which 14 were waited for; matrix products, arithmetic and copies ran while one was open for 5% of the time, Pallas kernels for 5%

profile of v12, /device:TPU:0, one launch (start us, length us, event | category | flops | bytes accessed | tf_op | source)
XLA Modules:
  0.0 100.4 jit_solution(15397242510512715967)
XLA Ops:
  0.7 1.6 %copy-done = bf16[128,8192]{1,0:T(8,128)(2,1)S(1)} copy-done((bf16[128,8192]{1,0:T(8,128)(2,1)S(1)}, bf16[128,8192]{1,0:T(8,128)(2,1)}, u32[]{:S(2)}) %copy-start) | copy-done | bytes 2097176
  2.6 3.0 %collective-permute-start.6 = (bf16[128,4096]{1,0:T(8,128)(2,1)S(1)}, bf16[128,4096]{1,0:T(8,128)(2,1)S(1)}, u32[]{:S(2)}, u32[]{:S(2)}) collective-permute-start(bf16[128,4096]{1,0:T(8,128)(2,1)S(1)} %shard_map.88), channel_id=1, source_target_pairs={{0,4},{4,0},{8,12},{12,8},{16,20},{20,16},{24,28},{28,24},{1,5},{5... | collective-permute-start | bytes 3145736 | tf_op jit(solution)/shard_map/ppermute | solution.py:25
  5.7 1.6 %collective-permute-start = (bf16[128,1024]{1,0:T(8,128)(2,1)}, bf16[128,1024]{1,0:T(8,128)(2,1)S(1)}, u32[]{:S(2)}, u32[]{:S(2)}) collective-permute-start(bf16[128,1024]{1,0:T(8,128)(2,1)} %refs_2_), channel_id=1, source_target_pairs={{0,8},{4,12},{8,0},{12,4},{16,24},{20,28},{24,16},{28,20},{1,9},{5... | collective-permute-start | bytes 786440 | tf_op jit(solution)/shard_map/ppermute | solution.py:25
  7.2 2.6 %collective-permute-start.4 = (bf16[128,1024]{1,0:T(8,128)(2,1)}, bf16[128,1024]{1,0:T(8,128)(2,1)S(1)}, u32[]{:S(2)}, u32[]{:S(2)}) collective-permute-start(bf16[128,1024]{1,0:T(8,128)(2,1)} %refs_2_), channel_id=1, source_target_pairs={{0,16},{4,20},{8,24},{12,28},{16,0},{20,4},{24,8},{28,12},{1,17},{... | collective-permute-start | bytes 786440 | tf_op jit(solution)/shard_map/ppermute | solution.py:25
  9.8 1.5 %collective-permute-start.3 = (bf16[128,1024]{1,0:T(8,128)(2,1)}, bf16[128,1024]{1,0:T(8,128)(2,1)S(1)}, u32[]{:S(2)}, u32[]{:S(2)}) collective-permute-start(bf16[128,1024]{1,0:T(8,128)(2,1)} %refs_2_), channel_id=1, source_target_pairs={{0,2},{1,3},{2,0},{3,1},{4,6},{5,7},{6,4},{7,5},{8,10},{9,11},{10,... | collective-permute-start | bytes 786440 | tf_op jit(solution)/shard_map/ppermute | solution.py:25
  11.3 7.8 %collective-permute-done.refs_4_.refs_3_ = bf16[128,1024]{1,0:T(8,128)(2,1)S(1)} collective-permute-done((bf16[128,1024]{1,0:T(8,128)(2,1)}, bf16[128,1024]{1,0:T(8,128)(2,1)S(1)}, u32[]{:S(2)}, u32[]{:S(2)}) %collective-permute-start) | collective-permute-done | bytes 262176 | tf_op jit(solution)/shard_map/ppermute | solution.py:25
  19.1 1.5 %collective-permute-start.1 = (bf16[128,1024]{1,0:T(8,128)(2,1)S(1)}, bf16[128,1024]{1,0:T(8,128)(2,1)S(1)}, u32[]{:S(2)}, u32[]{:S(2)}) collective-permute-start(bf16[128,1024]{1,0:T(8,128)(2,1)S(1)} %collective-permute-done.refs_4_.refs_3_), channel_id=1, source_target_pairs={{0,2},{1,3},{2,0},{3,1},{4,6},{5,7},{6,4},{7,5},{8,10},{9,11},{10,... | collective-permute-start | bytes 786440 | tf_op jit(solution)/shard_map/ppermute | solution.py:25
  22.0 1.5 %collective-permute-start.7 = (bf16[128,1024]{1,0:T(8,128)(2,1)S(1)}, bf16[128,1024]{1,0:T(8,128)(2,1)S(1)}, u32[]{:S(2)}, u32[]{:S(2)}) collective-permute-start(bf16[128,1024]{1,0:T(8,128)(2,1)S(1)} %collective-permute-done.4.refs_5_.refs_4_), channel_id=1, source_target_pairs={{0,2},{1,3},{2,0},{3,1},{4,6},{5,7},{6,4},{7,5},{8,10},{9,11},{10,... | collective-permute-start | bytes 786440 | tf_op jit(solution)/shard_map/ppermute | solution.py:25
  23.5 4.9 %collective-permute-done.1.refs_6_ = bf16[128,1024]{1,0:T(8,128)(2,1)S(1)} collective-permute-done((bf16[128,1024]{1,0:T(8,128)(2,1)S(1)}, bf16[128,1024]{1,0:T(8,128)(2,1)S(1)}, u32[]{:S(2)}, u32[]{:S(2)}) %collective-permute-start.1) | collective-permute-done | bytes 262176 | tf_op jit(solution)/shard_map/ppermute | solution.py:25
  28.8 2.8 %collective-permute-done.7.refs_7_ = bf16[128,1024]{1,0:T(8,128)(2,1)S(1)} collective-permute-done((bf16[128,1024]{1,0:T(8,128)(2,1)S(1)}, bf16[128,1024]{1,0:T(8,128)(2,1)S(1)}, u32[]{:S(2)}, u32[]{:S(2)}) %collective-permute-start.7) | collective-permute-done | bytes 262176 | tf_op jit(solution)/shard_map/ppermute | solution.py:25
  31.6 1.6 %collective-permute-start.11 = (bf16[128,1024]{1,0:T(8,128)(2,1)S(1)}, bf16[128,1024]{1,0:T(8,128)(2,1)S(1)}, u32[]{:S(2)}, u32[]{:S(2)}) collective-permute-start(bf16[128,1024]{1,0:T(8,128)(2,1)S(1)} %collective-permute-done.5.refs_6_.refs_5_), channel_id=1, source_target_pairs={{0,2},{1,3},{2,0},{3,1},{4,6},{5,7},{6,4},{7,5},{8,10},{9,11},{10,... | collective-permute-start | bytes 786440 | tf_op jit(solution)/shard_map/ppermute | solution.py:25
  33.6 1.0 %shard_map.87 = f32[320,128]{1,0:T(8,128)S(1)} custom-call(bf16[128,4096]{1,0:T(8,128)(2,1)S(1)} %shard_map.85.refs_0_, bf16[128,4096]{1,0:T(8,128)(2,1)S(1)} %collective-permute-done.2.refs_1_, bf16[64,4096]{1,0:T(8,128)(2,1)S(1)} %shard_map.86.refs_2_, bf16[128,1024]{1,0:T(8,128)(2,1)S(1)} %copy-done.1, ...), custom_call_target="tpu_custom_call" | custom-call | flops 335544320 | bytes 3833856 | tf_op jit(solution)/shard_map/pallas_call | solution.py:100
  36.0 1.6 %collective-permute-start.9 = (f32[256,128]{1,0:T(8,128)S(1)}, f32[256,128]{1,0:T(8,128)S(1)}, u32[]{:S(2)}, u32[]{:S(2)}) collective-permute-start(f32[256,128]{1,0:T(8,128)S(1)} %shard_map.89), channel_id=1, source_target_pairs={{0,4},{4,0},{8,12},{12,8},{16,20},{20,16},{24,28},{28,24},{1,5},{5... | collective-permute-start | bytes 393224 | tf_op jit(solution)/shard_map/ppermute | solution.py:25
  37.5 2.9 %collective-permute-done.11.refs_8_ = bf16[128,1024]{1,0:T(8,128)(2,1)S(1)} collective-permute-done((bf16[128,1024]{1,0:T(8,128)(2,1)S(1)}, bf16[128,1024]{1,0:T(8,128)(2,1)S(1)}, u32[]{:S(2)}, u32[]{:S(2)}) %collective-permute-start.11) | collective-permute-done | bytes 262176 | tf_op jit(solution)/shard_map/ppermute | solution.py:25
  40.4 1.6 %shard_map.90 = f32[608,128]{1,0:T(8,128)S(1)} custom-call(bf16[128,4096]{1,0:T(8,128)(2,1)S(1)} %shard_map.85.refs_0_, bf16[128,4096]{1,0:T(8,128)(2,1)S(1)} %collective-permute-done.2.refs_1_, bf16[64,4096]{1,0:T(8,128)(2,1)S(1)} %shard_map.86.refs_2_, bf16[128,4096]{1,0:T(8,128)(2,1)S(1)} %collective-permute-done.6.refs_0_.refs_3_.refs_2_, ...), custom_call_target="tpu_custom_call" | custom-call | flops 603979776 | bytes 6062080 | tf_op jit(solution)/shard_map/pallas_call | solution.py:100
  44.0 7.0 %collective-permute-done.12 = f32[608,128]{1,0:T(8,128)S(1)} collective-permute-done((f32[608,128]{1,0:T(8,128)S(1)}, f32[608,128]{1,0:T(8,128)S(1)}, u32[]{:S(2)}, u32[]{:S(2)}) %collective-permute-start.12) | collective-permute-done | bytes 311328 | tf_op jit(solution)/shard_map/ppermute | solution.py:25
  51.3 1.6 %collective-permute-start.13 = (f32[4,256]{1,0:T(4,128)S(1)}, f32[4,256]{1,0:T(4,128)S(1)}, u32[]{:S(2)}, u32[]{:S(2)}) collective-permute-start(f32[4,256]{1,0:T(4,128)S(1)} %maximum_maximum_fusion), channel_id=1, source_target_pairs={{0,2},{1,3},{2,0},{3,1},{4,6},{5,7},{6,4},{7,5},{8,10},{9,11},{10,... | collective-permute-start | bytes 12296 | tf_op jit(solution)/shard_map/ppermute | solution.py:25
  53.1 1.9 %collective-permute-done.13 = f32[4,256]{1,0:T(4,128)S(1)} collective-permute-done((f32[4,256]{1,0:T(4,128)S(1)}, f32[4,256]{1,0:T(4,128)S(1)}, u32[]{:S(2)}, u32[]{:S(2)}) %collective-permute-start.13) | collective-permute-done | bytes 4128 | tf_op jit(solution)/shard_map/ppermute | solution.py:25
  55.1 3.5 %collective-permute-done.14 = f32[2,256]{1,0:T(2,128)S(1)} collective-permute-done((f32[2,256]{1,0:T(2,128)S(1)}, f32[2,256]{1,0:T(2,128)S(1)}, u32[]{:S(2)}, u32[]{:S(2)}) %collective-permute-start.14) | collective-permute-done | bytes 2080 | tf_op jit(solution)/shard_map/ppermute | solution.py:25
  58.7 1.3 %collective-permute-start.15 = (f32[2,256]{1,0:T(2,128)S(1)}, f32[2,256]{1,0:T(2,128)S(1)}, u32[]{:S(2)}, u32[]{:S(2)}) collective-permute-start(f32[2,256]{1,0:T(2,128)S(1)} %pad_maximum_fusion.7), channel_id=1, source_target_pairs={{0,16},{4,20},{8,24},{12,28},{16,0},{20,4},{24,8},{28,12},{1,17},{... | collective-permute-start | bytes 6152 | tf_op jit(solution)/shard_map/ppermute | solution.py:25
  60.0 3.2 %collective-permute-done.15 = f32[2,256]{1,0:T(2,128)S(1)} collective-permute-done((f32[2,256]{1,0:T(2,128)S(1)}, f32[2,256]{1,0:T(2,128)S(1)}, u32[]{:S(2)}, u32[]{:S(2)}) %collective-permute-start.15) | collective-permute-done | bytes 2080 | tf_op jit(solution)/shard_map/ppermute | solution.py:25
  64.2 1.6 %collective-permute-start.17 = (bf16[128,1024]{1,0:T(8,128)(2,1)S(1)}, bf16[128,1024]{1,0:T(8,128)(2,1)S(1)}, u32[]{:S(2)}, u32[]{:S(2)}) collective-permute-start(bf16[128,1024]{1,0:T(8,128)(2,1)S(1)} %convolution_convert_fusion.1), channel_id=1, source_target_pairs={{0,2},{1,3},{2,0},{3,1},{4,6},{5,7},{6,4},{7,5},{8,10},{9,11},{10,... | collective-permute-start | bytes 786440 | tf_op jit(solution)/shard_map/ppermute | solution.py:25
  67.0 3.6 %collective-permute-done.17 = bf16[128,1024]{1,0:T(8,128)(2,1)S(1)} collective-permute-done((bf16[128,1024]{1,0:T(8,128)(2,1)S(1)}, bf16[128,1024]{1,0:T(8,128)(2,1)S(1)}, u32[]{:S(2)}, u32[]{:S(2)}) %collective-permute-start.17) | collective-permute-done | bytes 262176 | tf_op jit(solution)/shard_map/ppermute | solution.py:25
  71.9 3.9 %collective-permute-start.22 = (f32[64,128]{1,0:T(8,128)S(1)}, f32[64,128]{1,0:T(8,128)S(1)}, u32[]{:S(2)}, u32[]{:S(2)}) collective-permute-start(f32[64,128]{1,0:T(8,128)S(1)} %fusion.24), channel_id=1, source_target_pairs={{0,16},{4,20},{8,24},{12,28},{16,0},{20,4},{24,8},{28,12},{1,17},{... | collective-permute-start | bytes 98312 | tf_op jit(solution)/shard_map/ppermute | solution.py:25
  75.9 1.5 %collective-permute-start.20 = (bf16[128,1024]{1,0:T(8,128)(2,1)S(1)}, bf16[128,1024]{1,0:T(8,128)(2,1)S(1)}, u32[]{:S(2)}, u32[]{:S(2)}) collective-permute-start(bf16[128,1024]{1,0:T(8,128)(2,1)S(1)} %convolution_convert_fusion), channel_id=1, source_target_pairs={{0,2},{1,3},{2,0},{3,1},{4,6},{5,7},{6,4},{7,5},{8,10},{9,11},{10,... | collective-permute-start | bytes 786440 | tf_op jit(solution)/shard_map/ppermute | solution.py:25
  77.5 1.4 %collective-permute-done.22 = f32[64,128]{1,0:T(8,128)S(1)} collective-permute-done((f32[64,128]{1,0:T(8,128)S(1)}, f32[64,128]{1,0:T(8,128)S(1)}, u32[]{:S(2)}, u32[]{:S(2)}) %collective-permute-start.22) | collective-permute-done | bytes 32800 | tf_op jit(solution)/shard_map/ppermute | solution.py:25
  78.8 4.0 %collective-permute-start.23 = (f32[64,128]{1,0:T(8,128)S(1)}, f32[64,128]{1,0:T(8,128)S(1)}, u32[]{:S(2)}, u32[]{:S(2)}) collective-permute-start(f32[64,128]{1,0:T(8,128)S(1)} %add.160), channel_id=1, source_target_pairs={{0,8},{4,12},{8,0},{12,4},{16,24},{20,28},{24,16},{28,20},{1,9},{5... | collective-permute-start | bytes 98312 | tf_op jit(solution)/shard_map/ppermute | solution.py:25
  83.1 1.2 %collective-permute-start.24 = (bf16[128,1024]{1,0:T(8,128)(2,1)S(1)}, bf16[128,1024]{1,0:T(8,128)(2,1)S(1)}, u32[]{:S(2)}, u32[]{:S(2)}) collective-permute-start(bf16[128,1024]{1,0:T(8,128)(2,1)S(1)} %fusion.3), channel_id=1, source_target_pairs={{0,16},{4,20},{8,24},{12,28},{16,0},{20,4},{24,8},{28,12},{1,17},{... | collective-permute-start | bytes 786440 | tf_op jit(solution)/shard_map/ppermute | solution.py:25
  84.3 1.5 %collective-permute-start.19 = (bf16[128,1024]{1,0:T(8,128)(2,1)S(1)}, bf16[128,1024]{1,0:T(8,128)(2,1)S(1)}, u32[]{:S(2)}, u32[]{:S(2)}) collective-permute-start(bf16[128,1024]{1,0:T(8,128)(2,1)S(1)} %convolution_convert_fusion.3), channel_id=1, source_target_pairs={{0,2},{1,3},{2,0},{3,1},{4,6},{5,7},{6,4},{7,5},{8,10},{9,11},{10,... | collective-permute-start | bytes 786440 | tf_op jit(solution)/shard_map/ppermute | solution.py:25
  87.8 1.5 %collective-permute-start.26 = (bf16[64,1088]{1,0:T(8,128)(2,1)S(1)}, bf16[64,1088]{1,0:T(8,128)(2,1)S(1)}, u32[]{:S(2)}, u32[]{:S(2)}) collective-permute-start(bf16[64,1088]{1,0:T(8,128)(2,1)S(1)} %convert_element_type.104), channel_id=1, source_target_pairs={{0,2},{1,3},{2,0},{3,1},{4,6},{5,7},{6,4},{7,5},{8,10},{9,11},{10,... | collective-permute-start | bytes 417800 | tf_op jit(solution)/shard_map/ppermute | solution.py:25
  89.3 1.5 %collective-permute-done.19 = bf16[128,1024]{1,0:T(8,128)(2,1)S(1)} collective-permute-done((bf16[128,1024]{1,0:T(8,128)(2,1)S(1)}, bf16[128,1024]{1,0:T(8,128)(2,1)S(1)}, u32[]{:S(2)}, u32[]{:S(2)}) %collective-permute-start.19) | collective-permute-done | bytes 262176 | tf_op jit(solution)/shard_map/ppermute | solution.py:25
  90.7 7.2 %collective-permute-done.21 = bf16[128,1024]{1,0:T(8,128)(2,1)S(1)} collective-permute-done((bf16[128,1024]{1,0:T(8,128)(2,1)S(1)}, bf16[128,1024]{1,0:T(8,128)(2,1)S(1)}, u32[]{:S(2)}, u32[]{:S(2)}) %collective-permute-start.21) | collective-permute-done | bytes 262176 | tf_op jit(solution)/shard_map/ppermute | solution.py:25
  (97 shorter events, 14.7 us)
Async XLA Ops:
  0.6 31.0 %copy-start.4 = (s32[128]{0:T(128)S(1)}, s32[128]{0:T(128)}, u32[]{:S(2)}) copy-start(s32[128]{0:T(128)} %param.10) | copy-start | bytes 1540
  0.6 31.0 %copy-start.5 = (s32[128]{0:T(128)S(1)}, s32[128]{0:T(128)}, u32[]{:S(2)}) copy-start(s32[128]{0:T(128)} %param.11) | copy-start | bytes 1540
  2.3 30.9 %copy-start.2 = (bf16[64,8192]{1,0:T(8,128)(2,1)S(1)}, bf16[64,8192]{1,0:T(8,128)(2,1)}, u32[]{:S(2)}) copy-start(bf16[64,8192]{1,0:T(8,128)(2,1)} %refs_0_.1) | copy-start | bytes 3145732
  2.3 31.4 %copy-start.1 = (bf16[128,1024]{1,0:T(8,128)(2,1)S(1)}, bf16[128,1024]{1,0:T(8,128)(2,1)}, u32[]{:S(2)}) copy-start(bf16[128,1024]{1,0:T(8,128)(2,1)} %refs_2_) | copy-start | bytes 786436
  2.6 29.0 %collective-permute-start.6 = (bf16[128,4096]{1,0:T(8,128)(2,1)S(1)}, bf16[128,4096]{1,0:T(8,128)(2,1)S(1)}, u32[]{:S(2)}, u32[]{:S(2)}) collective-permute-start(bf16[128,4096]{1,0:T(8,128)(2,1)S(1)} %shard_map.88), channel_id=1, source_target_pairs={{0,4},{4,0},{8,12},{12,8},{16,20},{20,16},{24,28},{28,24},{1,5},{5... | collective-permute-start | bytes 3145736 | tf_op jit(solution)/shard_map/ppermute | solution.py:25
  5.7 13.5 %collective-permute-start = (bf16[128,1024]{1,0:T(8,128)(2,1)}, bf16[128,1024]{1,0:T(8,128)(2,1)S(1)}, u32[]{:S(2)}, u32[]{:S(2)}) collective-permute-start(bf16[128,1024]{1,0:T(8,128)(2,1)} %refs_2_), channel_id=1, source_target_pairs={{0,8},{4,12},{8,0},{12,4},{16,24},{20,28},{24,16},{28,20},{1,9},{5... | collective-permute-start | bytes 786440 | tf_op jit(solution)/shard_map/ppermute | solution.py:25
  7.2 14.3 %collective-permute-start.4 = (bf16[128,1024]{1,0:T(8,128)(2,1)}, bf16[128,1024]{1,0:T(8,128)(2,1)S(1)}, u32[]{:S(2)}, u32[]{:S(2)}) collective-permute-start(bf16[128,1024]{1,0:T(8,128)(2,1)} %refs_2_), channel_id=1, source_target_pairs={{0,16},{4,20},{8,24},{12,28},{16,0},{20,4},{24,8},{28,12},{1,17},{... | collective-permute-start | bytes 786440 | tf_op jit(solution)/shard_map/ppermute | solution.py:25
  9.8 12.1 %collective-permute-start.3 = (bf16[128,1024]{1,0:T(8,128)(2,1)}, bf16[128,1024]{1,0:T(8,128)(2,1)S(1)}, u32[]{:S(2)}, u32[]{:S(2)}) collective-permute-start(bf16[128,1024]{1,0:T(8,128)(2,1)} %refs_2_), channel_id=1, source_target_pairs={{0,2},{1,3},{2,0},{3,1},{4,6},{5,7},{6,4},{7,5},{8,10},{9,11},{10,... | collective-permute-start | bytes 786440 | tf_op jit(solution)/shard_map/ppermute | solution.py:25
  19.1 9.2 %collective-permute-start.1 = (bf16[128,1024]{1,0:T(8,128)(2,1)S(1)}, bf16[128,1024]{1,0:T(8,128)(2,1)S(1)}, u32[]{:S(2)}, u32[]{:S(2)}) collective-permute-start(bf16[128,1024]{1,0:T(8,128)(2,1)S(1)} %collective-permute-done.refs_4_.refs_3_), channel_id=1, source_target_pairs={{0,2},{1,3},{2,0},{3,1},{4,6},{5,7},{6,4},{7,5},{8,10},{9,11},{10,... | collective-permute-start | bytes 786440 | tf_op jit(solution)/shard_map/ppermute | solution.py:25
  21.5 7.3 %collective-permute-start.5 = (bf16[128,1024]{1,0:T(8,128)(2,1)S(1)}, bf16[128,1024]{1,0:T(8,128)(2,1)S(1)}, u32[]{:S(2)}, u32[]{:S(2)}) collective-permute-start(bf16[128,1024]{1,0:T(8,128)(2,1)S(1)} %collective-permute-done.4.refs_5_.refs_4_), channel_id=1, source_target_pairs={{0,8},{4,12},{8,0},{12,4},{16,24},{20,28},{24,16},{28,20},{1,9},{5... | collective-permute-start | bytes 786440 | tf_op jit(solution)/shard_map/ppermute | solution.py:25
  22.0 9.6 %collective-permute-start.7 = (bf16[128,1024]{1,0:T(8,128)(2,1)S(1)}, bf16[128,1024]{1,0:T(8,128)(2,1)S(1)}, u32[]{:S(2)}, u32[]{:S(2)}) collective-permute-start(bf16[128,1024]{1,0:T(8,128)(2,1)S(1)} %collective-permute-done.4.refs_5_.refs_4_), channel_id=1, source_target_pairs={{0,2},{1,3},{2,0},{3,1},{4,6},{5,7},{6,4},{7,5},{8,10},{9,11},{10,... | collective-permute-start | bytes 786440 | tf_op jit(solution)/shard_map/ppermute | solution.py:25
  28.7 4.9 %collective-permute-start.2 = (bf16[128,4096]{1,0:T(8,128)(2,1)S(1)}, bf16[128,4096]{1,0:T(8,128)(2,1)S(1)}, u32[]{:S(2)}, u32[]{:S(2)}) collective-permute-start(bf16[128,4096]{1,0:T(8,128)(2,1)S(1)} %shard_map.85.refs_0_), channel_id=1, source_target_pairs={{0,1},{1,0},{2,3},{3,2},{4,5},{5,4},{6,7},{7,6},{8,9},{9,8},{10,11... | collective-permute-start | bytes 3145736 | tf_op jit(solution)/shard_map/ppermute | solution.py:25
  31.6 3.6 %collective-permute-start.8 = (bf16[128,4096]{1,0:T(8,128)(2,1)S(1)}, bf16[128,4096]{1,0:T(8,128)(2,1)S(1)}, u32[]{:S(2)}, u32[]{:S(2)}) collective-permute-start(bf16[128,4096]{1,0:T(8,128)(2,1)S(1)} %collective-permute-done.6.refs_0_.refs_3_.refs_2_), channel_id=1, source_target_pairs={{0,1},{1,0},{2,3},{3,2},{4,5},{5,4},{6,7},{7,6},{8,9},{9,8},{10,11... | collective-permute-start | bytes 3145736 | tf_op jit(solution)/shard_map/ppermute | solution.py:25
  31.6 8.8 %collective-permute-start.11 = (bf16[128,1024]{1,0:T(8,128)(2,1)S(1)}, bf16[128,1024]{1,0:T(8,128)(2,1)S(1)}, u32[]{:S(2)}, u32[]{:S(2)}) collective-permute-start(bf16[128,1024]{1,0:T(8,128)(2,1)S(1)} %collective-permute-done.5.refs_6_.refs_5_), channel_id=1, source_target_pairs={{0,2},{1,3},{2,0},{3,1},{4,6},{5,7},{6,4},{7,5},{8,10},{9,11},{10,... | collective-permute-start | bytes 786440 | tf_op jit(solution)/shard_map/ppermute | solution.py:25
  33.2 7.2 %copy-start.3 = (bf16[64,64]{1,0:T(8,128)(2,1)S(1)}, bf16[64,64]{1,0:T(8,128)(2,1)}, u32[]{:S(2)}) copy-start(bf16[64,64]{1,0:T(8,128)(2,1)} %refs_9_.1) | copy-start | bytes 24580
  34.7 8.1 %collective-permute-start.10 = (f32[320,128]{1,0:T(8,128)S(1)}, f32[320,128]{1,0:T(8,128)S(1)}, u32[]{:S(2)}, u32[]{:S(2)}) collective-permute-start(f32[320,128]{1,0:T(8,128)S(1)} %shard_map.87), channel_id=1, source_target_pairs={{0,4},{4,0},{8,12},{12,8},{16,20},{20,16},{24,28},{28,24},{1,5},{5... | collective-permute-start | bytes 491528 | tf_op jit(solution)/shard_map/ppermute | solution.py:25
  36.0 7.9 %collective-permute-start.9 = (f32[256,128]{1,0:T(8,128)S(1)}, f32[256,128]{1,0:T(8,128)S(1)}, u32[]{:S(2)}, u32[]{:S(2)}) collective-permute-start(f32[256,128]{1,0:T(8,128)S(1)} %shard_map.89), channel_id=1, source_target_pairs={{0,4},{4,0},{8,12},{12,8},{16,20},{20,16},{24,28},{28,24},{1,5},{5... | collective-permute-start | bytes 393224 | tf_op jit(solution)/shard_map/ppermute | solution.py:25
  42.0 9.0 %collective-permute-start.12 = (f32[608,128]{1,0:T(8,128)S(1)}, f32[608,128]{1,0:T(8,128)S(1)}, u32[]{:S(2)}, u32[]{:S(2)}) collective-permute-start(f32[608,128]{1,0:T(8,128)S(1)} %shard_map.90), channel_id=1, source_target_pairs={{0,4},{4,0},{8,12},{12,8},{16,20},{20,16},{24,28},{28,24},{1,5},{5... | collective-permute-start | bytes 933896 | tf_op jit(solution)/shard_map/ppermute | solution.py:25
  51.3 3.7 %collective-permute-start.13 = (f32[4,256]{1,0:T(4,128)S(1)}, f32[4,256]{1,0:T(4,128)S(1)}, u32[]{:S(2)}, u32[]{:S(2)}) collective-permute-start(f32[4,256]{1,0:T(4,128)S(1)} %maximum_maximum_fusion), channel_id=1, source_target_pairs={{0,2},{1,3},{2,0},{3,1},{4,6},{5,7},{6,4},{7,5},{8,10},{9,11},{10,... | collective-permute-start | bytes 12296 | tf_op jit(solution)/shard_map/ppermute | solution.py:25
  55.0 3.7 %collective-permute-start.14 = (f32[2,256]{1,0:T(2,128)S(1)}, f32[2,256]{1,0:T(2,128)S(1)}, u32[]{:S(2)}, u32[]{:S(2)}) collective-permute-start(f32[2,256]{1,0:T(2,128)S(1)} %pad_maximum_fusion.6), channel_id=1, source_target_pairs={{0,8},{4,12},{8,0},{12,4},{16,24},{20,28},{24,16},{28,20},{1,9},{5... | collective-permute-start | bytes 6152 | tf_op jit(solution)/shard_map/ppermute | solution.py:25
  58.7 4.5 %collective-permute-start.15 = (f32[2,256]{1,0:T(2,128)S(1)}, f32[2,256]{1,0:T(2,128)S(1)}, u32[]{:S(2)}, u32[]{:S(2)}) collective-permute-start(f32[2,256]{1,0:T(2,128)S(1)} %pad_maximum_fusion.7), channel_id=1, source_target_pairs={{0,16},{4,20},{8,24},{12,28},{16,0},{20,4},{24,8},{28,12},{1,17},{... | collective-permute-start | bytes 6152 | tf_op jit(solution)/shard_map/ppermute | solution.py:25
  64.2 6.5 %collective-permute-start.17 = (bf16[128,1024]{1,0:T(8,128)(2,1)S(1)}, bf16[128,1024]{1,0:T(8,128)(2,1)S(1)}, u32[]{:S(2)}, u32[]{:S(2)}) collective-permute-start(bf16[128,1024]{1,0:T(8,128)(2,1)S(1)} %convolution_convert_fusion.1), channel_id=1, source_target_pairs={{0,2},{1,3},{2,0},{3,1},{4,6},{5,7},{6,4},{7,5},{8,10},{9,11},{10,... | collective-permute-start | bytes 786440 | tf_op jit(solution)/shard_map/ppermute | solution.py:25
  66.0 16.7 %collective-permute-start.16 = (bf16[128,1024]{1,0:T(8,128)(2,1)S(1)}, bf16[128,1024]{1,0:T(8,128)(2,1)S(1)}, u32[]{:S(2)}, u32[]{:S(2)}) collective-permute-start(bf16[128,1024]{1,0:T(8,128)(2,1)S(1)} %convolution_convert_fusion.2), channel_id=1, source_target_pairs={{0,2},{1,3},{2,0},{3,1},{4,6},{5,7},{6,4},{7,5},{8,10},{9,11},{10,... | collective-permute-start | bytes 786440 | tf_op jit(solution)/shard_map/ppermute | solution.py:25
  70.9 7.9 %collective-permute-start.18 = (bf16[128,1024]{1,0:T(8,128)(2,1)S(1)}, bf16[128,1024]{1,0:T(8,128)(2,1)S(1)}, u32[]{:S(2)}, u32[]{:S(2)}) collective-permute-start(bf16[128,1024]{1,0:T(8,128)(2,1)S(1)} %fusion.4), channel_id=1, source_target_pairs={{0,8},{4,12},{8,0},{12,4},{16,24},{20,28},{24,16},{28,20},{1,9},{5... | collective-permute-start | bytes 786440 | tf_op jit(solution)/shard_map/ppermute | solution.py:25
  71.9 6.9 %collective-permute-start.22 = (f32[64,128]{1,0:T(8,128)S(1)}, f32[64,128]{1,0:T(8,128)S(1)}, u32[]{:S(2)}, u32[]{:S(2)}) collective-permute-start(f32[64,128]{1,0:T(8,128)S(1)} %fusion.24), channel_id=1, source_target_pairs={{0,16},{4,20},{8,24},{12,28},{16,0},{20,4},{24,8},{28,12},{1,17},{... | collective-permute-start | bytes 98312 | tf_op jit(solution)/shard_map/ppermute | solution.py:25
  75.9 10.2 %collective-permute-start.20 = (bf16[128,1024]{1,0:T(8,128)(2,1)S(1)}, bf16[128,1024]{1,0:T(8,128)(2,1)S(1)}, u32[]{:S(2)}, u32[]{:S(2)}) collective-permute-start(bf16[128,1024]{1,0:T(8,128)(2,1)S(1)} %convolution_convert_fusion), channel_id=1, source_target_pairs={{0,2},{1,3},{2,0},{3,1},{4,6},{5,7},{6,4},{7,5},{8,10},{9,11},{10,... | collective-permute-start | bytes 786440 | tf_op jit(solution)/shard_map/ppermute | solution.py:25
  78.8 7.0 %collective-permute-start.23 = (f32[64,128]{1,0:T(8,128)S(1)}, f32[64,128]{1,0:T(8,128)S(1)}, u32[]{:S(2)}, u32[]{:S(2)}) collective-permute-start(f32[64,128]{1,0:T(8,128)S(1)} %add.160), channel_id=1, source_target_pairs={{0,8},{4,12},{8,0},{12,4},{16,24},{20,28},{24,16},{28,20},{1,9},{5... | collective-permute-start | bytes 98312 | tf_op jit(solution)/shard_map/ppermute | solution.py:25
  83.1 16.6 %collective-permute-start.24 = (bf16[128,1024]{1,0:T(8,128)(2,1)S(1)}, bf16[128,1024]{1,0:T(8,128)(2,1)S(1)}, u32[]{:S(2)}, u32[]{:S(2)}) collective-permute-start(bf16[128,1024]{1,0:T(8,128)(2,1)S(1)} %fusion.3), channel_id=1, source_target_pairs={{0,16},{4,20},{8,24},{12,28},{16,0},{20,4},{24,8},{28,12},{1,17},{... | collective-permute-start | bytes 786440 | tf_op jit(solution)/shard_map/ppermute | solution.py:25
  84.3 6.4 %collective-permute-start.19 = (bf16[128,1024]{1,0:T(8,128)(2,1)S(1)}, bf16[128,1024]{1,0:T(8,128)(2,1)S(1)}, u32[]{:S(2)}, u32[]{:S(2)}) collective-permute-start(bf16[128,1024]{1,0:T(8,128)(2,1)S(1)} %convolution_convert_fusion.3), channel_id=1, source_target_pairs={{0,2},{1,3},{2,0},{3,1},{4,6},{5,7},{6,4},{7,5},{8,10},{9,11},{10,... | collective-permute-start | bytes 786440 | tf_op jit(solution)/shard_map/ppermute | solution.py:25
  86.1 1.6 %collective-permute-start.25 = (f32[64,1088]{1,0:T(8,128)S(1)}, f32[64,1088]{1,0:T(8,128)S(1)}, u32[]{:S(2)}, u32[]{:S(2)}) collective-permute-start(f32[64,1088]{1,0:T(8,128)S(1)} %pad_maximum_fusion), channel_id=1, source_target_pairs={{0,1},{1,0},{2,3},{3,2},{4,5},{5,4},{6,7},{7,6},{8,9},{9,8},{10,11... | collective-permute-start | bytes 835592 | tf_op jit(solution)/shard_map/ppermute | solution.py:25
  86.5 11.5 %collective-permute-start.21 = (bf16[128,1024]{1,0:T(8,128)(2,1)S(1)}, bf16[128,1024]{1,0:T(8,128)(2,1)S(1)}, u32[]{:S(2)}, u32[]{:S(2)}) collective-permute-start(bf16[128,1024]{1,0:T(8,128)(2,1)S(1)} %fusion.5), channel_id=1, source_target_pairs={{0,8},{4,12},{8,0},{12,4},{16,24},{20,28},{24,16},{28,20},{1,9},{5... | collective-permute-start | bytes 786440 | tf_op jit(solution)/shard_map/ppermute | solution.py:25
  87.8 10.5 %collective-permute-start.26 = (bf16[64,1088]{1,0:T(8,128)(2,1)S(1)}, bf16[64,1088]{1,0:T(8,128)(2,1)S(1)}, u32[]{:S(2)}, u32[]{:S(2)}) collective-permute-start(bf16[64,1088]{1,0:T(8,128)(2,1)S(1)} %convert_element_type.104), channel_id=1, source_target_pairs={{0,2},{1,3},{2,0},{3,1},{4,6},{5,7},{6,4},{7,5},{8,10},{9,11},{10,... | collective-permute-start | bytes 417800 | tf_op jit(solution)/shard_map/ppermute | solution.py:25
  (1 other events, 1.6 us)

commit v13 on v11

--- a/solution.py
+++ b/solution.py
@@ -71,12 +71,13 @@
     )(*arrays)
 
 
-def logits_of(groups, tokens, rider=None):
+def logits_of(groups, tokens, rider=None, first=0, before=None):
     toks, width = tokens[0].shape
     heights = [group[0].shape[0] for group in groups]
     total, depth = sum(heights), width * len(tokens)
+    blocks = range(first, first + len(tokens))
     flat = [a for group in groups for a in group]
-    riders = [] if rider is None else [rider]
+    riders = [a for a in (before, rider) if a is not None]
     extra = 0 if rider is None else rider.shape[0] // 2
     n_flat, n_all = len(flat), len(flat) + len(tokens) + len(riders)
 
@@ -85,9 +86,14 @@
         at, row = 0, 0
         for group, height in zip(groups, heights):
             result, column = None, 0
+            if before is not None:
+                result = refs[n_flat + len(tokens)][row : row + height, :]
             for part in group:
                 for c in range(0, part.shape[1], width):
-                    token = refs[n_flat + (column + c) // width]
+                    block = (column + c) // width
+                    if block not in blocks:
+                        continue
+                    token = refs[n_flat + block - first]
                     term = dot_last(refs[at][:, c : c + width], token[...])
                     result = term if result is None else result + term
                 at, column = at + 1, column + part.shape[1]
@@ -111,20 +117,34 @@
     )(*flat, *tokens, *riders)
 
 
-def finish(total, came):
-    def kernel(total_ref, came_ref, out):
-        out[...] = (total_ref[...] + came_ref[...].astype(f32)).astype(bf16)
-
+def finish(total, pieces, factor, factor_came):
+    width = total.shape[1]
+
+    def kernel(total_ref, *refs):
+        result = total_ref[...]
+        for piece in refs[: len(pieces)]:
+            result = result + piece[...].astype(f32)
+        factor_ref, came_ref, hidden_out, basis_out, rows_out = refs[len(pieces) :]
+        hidden_out[...] = result.astype(bf16)
+        both = factor_ref[...] + came_ref[...].astype(f32)
+        basis_out[...] = both[:, :width]
+        rows_out[...] = both[:, width:]
+
+    rank, wide = factor.shape
     return pl.pallas_call(
         kernel,
-        out_shape=jax.ShapeDtypeStruct(total.shape, bf16),
-        in_specs=[in_vmem] * 2,
-        out_specs=in_vmem,
+        out_shape=[
+            jax.ShapeDtypeStruct(total.shape, bf16),
+            jax.ShapeDtypeStruct((rank, width), f32),
+            jax.ShapeDtypeStruct((rank, wide - width), f32),
+        ],
+        in_specs=[in_vmem] * (3 + len(pieces)),
+        out_specs=[in_vmem] * 3,
         compiler_params=pltpu.CompilerParams(vmem_limit_bytes=4 << 20),
         cost_estimate=pl.CostEstimate(
-            flops=8 * total.size, bytes_accessed=8 * total.size, transcendentals=0
+            flops=3 * total.size, bytes_accessed=12 * total.size, transcendentals=0
         ),
-    )(total, came)
+    )(total, *pieces, factor, factor_came)
 
 
 def on_few(hidden, head, factor_rows, factor_basis, targets, loss_mask):
@@ -198,7 +218,9 @@
     beside_core[-1], *_ = lax.optimization_barrier((beside_core[-1], upper_own))
     lower_own = logits_of([beside, beside_core], in_order(shards))
     cross[0], _ = lax.optimization_barrier((cross[0], lower_own))
-    both_cross = logits_of(upper + [beside, beside_core], in_order(cross), factor_rows)
+    every = upper + [beside, beside_core]
+    early_cross = logits_of(every, in_order(cross)[:-1]) if n_z > 1 else None
+    both_cross = logits_of(every, in_order(cross)[-1:], factor_rows, n_z - 1, early_cross)
     n_up = 2 * rows + rank
 
     def add_over_y(up, low, up_came, low_came):
@@ -304,7 +326,7 @@
     rows_part = dot_last(fresh_grad[:new_here], hidden_basis[:, :toks])
     basis_part = jnp.dot(mix_total, hidden, preferred_element_type=f32)
 
-    came_z = None
+    came_z, pieces = None, []
     for bit in bits:
         for j in [j for j in sorted(sums, reverse=True) if j & bit]:
             total = sums.pop(j)
@@ -313,15 +335,17 @@
                 send, _ = lax.optimization_barrier((send, came_z))
             came = first_came if j == n_z - 1 else swap_z(send, bit)
             came_z = came if came_z is None else came_z
-            total = sums[j ^ bit]
-            sums[j ^ bit] = total + came.astype(f32)
-    hidden_grad = finish(total + dot_first(mix_total, basis_half[:, :width]), came)
+            if j ^ bit:
+                sums[j ^ bit] = sums[j ^ bit] + came.astype(f32)
+            else:
+                pieces.append(came)
+    total = sums[0] + dot_first(mix_total, basis_half[:, :width])
 
     factor_part = jnp.concatenate([basis_part, rows_part], axis=1)
     factor_two = lax.reduce_precision(factor_part + swap_core(factor_part), 8, 7)
     factor_two, _ = lax.optimization_barrier((factor_two, from_x[min(1, n_z - 1)]))
-    factor_grad = factor_two + swap_x(factor_two.astype(bf16)).astype(f32)
-    basis_grad, rows_grad = factor_grad[:, :width], factor_grad[:, width:]
+    factor_came = swap_x(factor_two.astype(bf16))
+    hidden_grad, basis_grad, rows_grad = finish(total, pieces, factor_two, factor_came)
     return hidden_grad, rows_grad, basis_grad
 
 

time: 99.6 us -> 100 us (level)
  waiting for transfers between devices: 53.3 us -> 57.6 us
  starting transfers between devices: 31.8 us -> 29.2 us
  local copies, waits for them, and re-layouts: 3.04 us -> 1.7 us
    ppermute x27, waiting for transfers between devices: 53.3 us -> 57.6 us  [swap(): return lax.ppermute(value, axis, [(i, i ^ bit) for i in range(size)])]
    ppermute x27, starting transfers between devices: 31.8 us -> 29.2 us  [swap(): return lax.ppermute(value, axis, [(i, i ^ bit) for i in range(size)])]
    slice x2 -> x0, local copies, waits for them, and re-layouts: 1.34 us -> none  [on_few(): basis_grad, rows_grad = (factor_grad[:, :width], factor_grad[:, width:])]
    pallas_call x3 -> x4, Pallas kernels: 3.3 us -> 3.47 us  [logits_of(): pl.pallas_call(kernel, out_shape=jax.ShapeDtypeStruct((total + extra, tok...]
  transfers between devices with their start and end apart: 27 -> 27, of which waited for: 16 -> 17; matrix products, arithmetic and copies ran while one was open for 3% -> 3% of each run, Pallas kernels for 5% -> 5%
where the time goes in v13:
time: 100 us; the launch traced here: 99.9 us
  waiting for transfers between devices  57.6 us (58%)
  starting transfers between devices  29.2 us (29%)
  Pallas kernels  6.02 us (6%)
  matrix products  3.51 us (4%)
  local copies, waits for them, and re-layouts  1.7 us (2%)
  between operations  1.05 us (1%)
    ppermute x27, waiting for transfers between devices, swap(): return lax.ppermute(value, axis, [(i, i ^ bit) for i in range(size)])  57.6 us
    ppermute x27, starting transfers between devices, swap(): return lax.ppermute(value, axis, [(i, i ^ bit) for i in range(size)])  29.2 us
    pallas_call x4, Pallas kernels, logits_of(): pl.pallas_call(kernel, out_shape=jax.ShapeDtypeStruct((total + extra, tok...  3.47 us
    dot_general x10, matrix products, dot_first(): return lax.dot_general(a, b, contract_first, preferred_element_type=f32)  3.05 us
  transfers between devices with their start and end apart: 27, of which 17 were waited for; matrix products, arithmetic and copies ran while one was open for 3% of the time, Pallas kernels for 5%

profile of v13, /device:TPU:0, one launch (start us, length us, event | category | flops | bytes accessed | tf_op | source)
XLA Modules:
  0.0 99.9 jit_solution(16935721444954857013)
XLA Ops:
  0.7 1.6 %copy-done = bf16[128,8192]{1,0:T(8,128)(2,1)S(1)} copy-done((bf16[128,8192]{1,0:T(8,128)(2,1)S(1)}, bf16[128,8192]{1,0:T(8,128)(2,1)}, u32[]{:S(2)}) %copy-start) | copy-done | bytes 2097176
  2.6 3.0 %collective-permute-start.6 = (bf16[128,4096]{1,0:T(8,128)(2,1)S(1)}, bf16[128,4096]{1,0:T(8,128)(2,1)S(1)}, u32[]{:S(2)}, u32[]{:S(2)}) collective-permute-start(bf16[128,4096]{1,0:T(8,128)(2,1)S(1)} %shard_map.88), channel_id=1, source_target_pairs={{0,4},{4,0},{8,12},{12,8},{16,20},{20,16},{24,28},{28,24},{1,5},{5... | collective-permute-start | bytes 3145736 | tf_op jit(solution)/shard_map/ppermute | solution.py:25
  5.7 1.6 %collective-permute-start = (bf16[128,1024]{1,0:T(8,128)(2,1)}, bf16[128,1024]{1,0:T(8,128)(2,1)S(1)}, u32[]{:S(2)}, u32[]{:S(2)}) collective-permute-start(bf16[128,1024]{1,0:T(8,128)(2,1)} %refs_2_), channel_id=1, source_target_pairs={{0,8},{4,12},{8,0},{12,4},{16,24},{20,28},{24,16},{28,20},{1,9},{5... | collective-permute-start | bytes 786440 | tf_op jit(solution)/shard_map/ppermute | solution.py:25
  7.2 2.6 %collective-permute-start.4 = (bf16[128,1024]{1,0:T(8,128)(2,1)}, bf16[128,1024]{1,0:T(8,128)(2,1)S(1)}, u32[]{:S(2)}, u32[]{:S(2)}) collective-permute-start(bf16[128,1024]{1,0:T(8,128)(2,1)} %refs_2_), channel_id=1, source_target_pairs={{0,16},{4,20},{8,24},{12,28},{16,0},{20,4},{24,8},{28,12},{1,17},{... | collective-permute-start | bytes 786440 | tf_op jit(solution)/shard_map/ppermute | solution.py:25
  9.8 1.5 %collective-permute-start.3 = (bf16[128,1024]{1,0:T(8,128)(2,1)}, bf16[128,1024]{1,0:T(8,128)(2,1)S(1)}, u32[]{:S(2)}, u32[]{:S(2)}) collective-permute-start(bf16[128,1024]{1,0:T(8,128)(2,1)} %refs_2_), channel_id=1, source_target_pairs={{0,2},{1,3},{2,0},{3,1},{4,6},{5,7},{6,4},{7,5},{8,10},{9,11},{10,... | collective-permute-start | bytes 786440 | tf_op jit(solution)/shard_map/ppermute | solution.py:25
  11.3 7.8 %collective-permute-done.refs_4_.refs_3_ = bf16[128,1024]{1,0:T(8,128)(2,1)S(1)} collective-permute-done((bf16[128,1024]{1,0:T(8,128)(2,1)}, bf16[128,1024]{1,0:T(8,128)(2,1)S(1)}, u32[]{:S(2)}, u32[]{:S(2)}) %collective-permute-start) | collective-permute-done | bytes 262176 | tf_op jit(solution)/shard_map/ppermute | solution.py:25
  19.1 1.5 %collective-permute-start.1 = (bf16[128,1024]{1,0:T(8,128)(2,1)S(1)}, bf16[128,1024]{1,0:T(8,128)(2,1)S(1)}, u32[]{:S(2)}, u32[]{:S(2)}) collective-permute-start(bf16[128,1024]{1,0:T(8,128)(2,1)S(1)} %collective-permute-done.refs_4_.refs_3_), channel_id=1, source_target_pairs={{0,2},{1,3},{2,0},{3,1},{4,6},{5,7},{6,4},{7,5},{8,10},{9,11},{10,... | collective-permute-start | bytes 786440 | tf_op jit(solution)/shard_map/ppermute | solution.py:25
  22.0 1.5 %collective-permute-start.7 = (bf16[128,1024]{1,0:T(8,128)(2,1)S(1)}, bf16[128,1024]{1,0:T(8,128)(2,1)S(1)}, u32[]{:S(2)}, u32[]{:S(2)}) collective-permute-start(bf16[128,1024]{1,0:T(8,128)(2,1)S(1)} %collective-permute-done.4.refs_5_.refs_4_), channel_id=1, source_target_pairs={{0,2},{1,3},{2,0},{3,1},{4,6},{5,7},{6,4},{7,5},{8,10},{9,11},{10,... | collective-permute-start | bytes 786440 | tf_op jit(solution)/shard_map/ppermute | solution.py:25
  23.5 4.9 %collective-permute-done.1.refs_6_ = bf16[128,1024]{1,0:T(8,128)(2,1)S(1)} collective-permute-done((bf16[128,1024]{1,0:T(8,128)(2,1)S(1)}, bf16[128,1024]{1,0:T(8,128)(2,1)S(1)}, u32[]{:S(2)}, u32[]{:S(2)}) %collective-permute-start.1) | collective-permute-done | bytes 262176 | tf_op jit(solution)/shard_map/ppermute | solution.py:25
  28.8 2.8 %collective-permute-done.7.refs_7_ = bf16[128,1024]{1,0:T(8,128)(2,1)S(1)} collective-permute-done((bf16[128,1024]{1,0:T(8,128)(2,1)S(1)}, bf16[128,1024]{1,0:T(8,128)(2,1)S(1)}, u32[]{:S(2)}, u32[]{:S(2)}) %collective-permute-start.7) | collective-permute-done | bytes 262176 | tf_op jit(solution)/shard_map/ppermute | solution.py:25
  31.6 1.6 %collective-permute-start.11 = (bf16[128,1024]{1,0:T(8,128)(2,1)S(1)}, bf16[128,1024]{1,0:T(8,128)(2,1)S(1)}, u32[]{:S(2)}, u32[]{:S(2)}) collective-permute-start(bf16[128,1024]{1,0:T(8,128)(2,1)S(1)} %collective-permute-done.5.refs_6_.refs_5_), channel_id=1, source_target_pairs={{0,2},{1,3},{2,0},{3,1},{4,6},{5,7},{6,4},{7,5},{8,10},{9,11},{10,... | collective-permute-start | bytes 786440 | tf_op jit(solution)/shard_map/ppermute | solution.py:25
  33.6 1.0 %shard_map.87 = f32[320,128]{1,0:T(8,128)S(1)} custom-call(bf16[128,4096]{1,0:T(8,128)(2,1)S(1)} %shard_map.85.refs_0_, bf16[128,4096]{1,0:T(8,128)(2,1)S(1)} %collective-permute-done.2.refs_1_, bf16[64,4096]{1,0:T(8,128)(2,1)S(1)} %shard_map.86.refs_2_, bf16[128,1024]{1,0:T(8,128)(2,1)S(1)} %copy-done.1, ...), custom_call_target="tpu_custom_call" | custom-call | flops 335544320 | bytes 3833856 | tf_op jit(solution)/shard_map/pallas_call | solution.py:106
  35.9 1.6 %collective-permute-start.9 = (f32[256,128]{1,0:T(8,128)S(1)}, f32[256,128]{1,0:T(8,128)S(1)}, u32[]{:S(2)}, u32[]{:S(2)}) collective-permute-start(f32[256,128]{1,0:T(8,128)S(1)} %shard_map.89), channel_id=1, source_target_pairs={{0,4},{4,0},{8,12},{12,8},{16,20},{20,16},{24,28},{28,24},{1,5},{5... | collective-permute-start | bytes 393224 | tf_op jit(solution)/shard_map/ppermute | solution.py:25
  37.5 1.2 %shard_map.90.refs_6_ = f32[576,128]{1,0:T(8,128)S(1)} custom-call(bf16[128,4096]{1,0:T(8,128)(2,1)S(1)} %shard_map.85.refs_0_, bf16[128,4096]{1,0:T(8,128)(2,1)S(1)} %collective-permute-done.2.refs_1_, bf16[64,4096]{1,0:T(8,128)(2,1)S(1)} %shard_map.86.refs_2_, bf16[128,4096]{1,0:T(8,128)(2,1)S(1)} %collective-permute-done.6.refs_0_.refs_3_.refs_2_, ...), custom_call_target="tpu_custom_call" | custom-call | flops 452984832 | bytes 4620288 | tf_op jit(solution)/shard_map/pallas_call | solution.py:106
  38.7 1.7 %collective-permute-done.11.refs_5_ = bf16[128,1024]{1,0:T(8,128)(2,1)S(1)} collective-permute-done((bf16[128,1024]{1,0:T(8,128)(2,1)S(1)}, bf16[128,1024]{1,0:T(8,128)(2,1)S(1)}, u32[]{:S(2)}, u32[]{:S(2)}) %collective-permute-start.11) | collective-permute-done | bytes 262176 | tf_op jit(solution)/shard_map/ppermute | solution.py:25
  42.4 1.9 %collective-permute-done.9 = f32[256,128]{1,0:T(8,128)S(1)} collective-permute-done((f32[256,128]{1,0:T(8,128)S(1)}, f32[256,128]{1,0:T(8,128)S(1)}, u32[]{:S(2)}, u32[]{:S(2)}) %collective-permute-start.9) | collective-permute-done | bytes 131104 | tf_op jit(solution)/shard_map/ppermute | solution.py:25
  44.4 6.1 %collective-permute-done.12 = f32[608,128]{1,0:T(8,128)S(1)} collective-permute-done((f32[608,128]{1,0:T(8,128)S(1)}, f32[608,128]{1,0:T(8,128)S(1)}, u32[]{:S(2)}, u32[]{:S(2)}) %collective-permute-start.12) | collective-permute-done | bytes 311328 | tf_op jit(solution)/shard_map/ppermute | solution.py:25
  50.8 1.1 %collective-permute-start.13 = (f32[4,256]{1,0:T(4,128)S(1)}, f32[4,256]{1,0:T(4,128)S(1)}, u32[]{:S(2)}, u32[]{:S(2)}) collective-permute-start(f32[4,256]{1,0:T(4,128)S(1)} %maximum_maximum_fusion), channel_id=1, source_target_pairs={{0,2},{1,3},{2,0},{3,1},{4,6},{5,7},{6,4},{7,5},{8,10},{9,11},{10,... | collective-permute-start | bytes 12296 | tf_op jit(solution)/shard_map/ppermute | solution.py:25
  52.1 2.4 %collective-permute-done.13 = f32[4,256]{1,0:T(4,128)S(1)} collective-permute-done((f32[4,256]{1,0:T(4,128)S(1)}, f32[4,256]{1,0:T(4,128)S(1)}, u32[]{:S(2)}, u32[]{:S(2)}) %collective-permute-start.13) | collective-permute-done | bytes 4128 | tf_op jit(solution)/shard_map/ppermute | solution.py:25
  54.6 3.5 %collective-permute-done.14 = f32[2,256]{1,0:T(2,128)S(1)} collective-permute-done((f32[2,256]{1,0:T(2,128)S(1)}, f32[2,256]{1,0:T(2,128)S(1)}, u32[]{:S(2)}, u32[]{:S(2)}) %collective-permute-start.14) | collective-permute-done | bytes 2080 | tf_op jit(solution)/shard_map/ppermute | solution.py:25
  58.2 1.4 %collective-permute-start.15 = (f32[2,256]{1,0:T(2,128)S(1)}, f32[2,256]{1,0:T(2,128)S(1)}, u32[]{:S(2)}, u32[]{:S(2)}) collective-permute-start(f32[2,256]{1,0:T(2,128)S(1)} %pad_maximum_fusion.7), channel_id=1, source_target_pairs={{0,16},{4,20},{8,24},{12,28},{16,0},{20,4},{24,8},{28,12},{1,17},{... | collective-permute-start | bytes 6152 | tf_op jit(solution)/shard_map/ppermute | solution.py:25
  59.5 3.2 %collective-permute-done.15 = f32[2,256]{1,0:T(2,128)S(1)} collective-permute-done((f32[2,256]{1,0:T(2,128)S(1)}, f32[2,256]{1,0:T(2,128)S(1)}, u32[]{:S(2)}, u32[]{:S(2)}) %collective-permute-start.15) | collective-permute-done | bytes 2080 | tf_op jit(solution)/shard_map/ppermute | solution.py:25
  63.6 1.1 %collective-permute-start.17 = (bf16[128,1024]{1,0:T(8,128)(2,1)S(1)}, bf16[128,1024]{1,0:T(8,128)(2,1)S(1)}, u32[]{:S(2)}, u32[]{:S(2)}) collective-permute-start(bf16[128,1024]{1,0:T(8,128)(2,1)S(1)} %convolution_convert_fusion.1), channel_id=1, source_target_pairs={{0,2},{1,3},{2,0},{3,1},{4,6},{5,7},{6,4},{7,5},{8,10},{9,11},{10,... | collective-permute-start | bytes 786440 | tf_op jit(solution)/shard_map/ppermute | solution.py:25
  65.0 1.1 %collective-permute-start.16 = (bf16[128,1024]{1,0:T(8,128)(2,1)S(1)}, bf16[128,1024]{1,0:T(8,128)(2,1)S(1)}, u32[]{:S(2)}, u32[]{:S(2)}) collective-permute-start(bf16[128,1024]{1,0:T(8,128)(2,1)S(1)} %convolution_convert_fusion.2), channel_id=1, source_target_pairs={{0,2},{1,3},{2,0},{3,1},{4,6},{5,7},{6,4},{7,5},{8,10},{9,11},{10,... | collective-permute-start | bytes 786440 | tf_op jit(solution)/shard_map/ppermute | solution.py:25
  66.4 5.0 %collective-permute-done.17 = bf16[128,1024]{1,0:T(8,128)(2,1)S(1)} collective-permute-done((bf16[128,1024]{1,0:T(8,128)(2,1)S(1)}, bf16[128,1024]{1,0:T(8,128)(2,1)S(1)}, u32[]{:S(2)}, u32[]{:S(2)}) %collective-permute-start.17) | collective-permute-done | bytes 262176 | tf_op jit(solution)/shard_map/ppermute | solution.py:25
  72.8 1.3 %collective-permute-start.20 = (f32[64,128]{1,0:T(8,128)S(1)}, f32[64,128]{1,0:T(8,128)S(1)}, u32[]{:S(2)}, u32[]{:S(2)}) collective-permute-start(f32[64,128]{1,0:T(8,128)S(1)} %fusion.23), channel_id=1, source_target_pairs={{0,8},{4,12},{8,0},{12,4},{16,24},{20,28},{24,16},{28,20},{1,9},{5... | collective-permute-start | bytes 98312 | tf_op jit(solution)/shard_map/ppermute | solution.py:25
  74.8 6.6 %collective-permute-done.20 = f32[64,128]{1,0:T(8,128)S(1)} collective-permute-done((f32[64,128]{1,0:T(8,128)S(1)}, f32[64,128]{1,0:T(8,128)S(1)}, u32[]{:S(2)}, u32[]{:S(2)}) %collective-permute-start.20) | collective-permute-done | bytes 32800 | tf_op jit(solution)/shard_map/ppermute | solution.py:25
  82.6 2.2 %collective-permute-start.24 = (bf16[128,1024]{1,0:T(8,128)(2,1)S(1)}, bf16[128,1024]{1,0:T(8,128)(2,1)S(1)}, u32[]{:S(2)}, u32[]{:S(2)}) collective-permute-start(bf16[128,1024]{1,0:T(8,128)(2,1)S(1)} %fusion.2), channel_id=1, source_target_pairs={{0,16},{4,20},{8,24},{12,28},{16,0},{20,4},{24,8},{28,12},{1,17},{... | collective-permute-start | bytes 786440 | tf_op jit(solution)/shard_map/ppermute | solution.py:25
  84.8 1.7 %collective-permute-done.21 = f32[64,128]{1,0:T(8,128)S(1)} collective-permute-done((f32[64,128]{1,0:T(8,128)S(1)}, f32[64,128]{1,0:T(8,128)S(1)}, u32[]{:S(2)}, u32[]{:S(2)}) %collective-permute-start.21) | collective-permute-done | bytes 32800 | tf_op jit(solution)/shard_map/ppermute | solution.py:25
  88.4 1.4 %collective-permute-start.26 = (bf16[64,1088]{1,0:T(8,128)(2,1)S(1)}, bf16[64,1088]{1,0:T(8,128)(2,1)S(1)}, u32[]{:S(2)}, u32[]{:S(2)}) collective-permute-start(bf16[64,1088]{1,0:T(8,128)(2,1)S(1)} %convert_element_type.97), channel_id=1, source_target_pairs={{0,2},{1,3},{2,0},{3,1},{4,6},{5,7},{6,4},{7,5},{8,10},{9,11},{10,... | collective-permute-start | bytes 417800 | tf_op jit(solution)/shard_map/ppermute | solution.py:25
  89.8 6.7 %collective-permute-done.19 = bf16[128,1024]{1,0:T(8,128)(2,1)S(1)} collective-permute-done((bf16[128,1024]{1,0:T(8,128)(2,1)S(1)}, bf16[128,1024]{1,0:T(8,128)(2,1)S(1)}, u32[]{:S(2)}, u32[]{:S(2)}) %collective-permute-start.19) | collective-permute-done | bytes 262176 | tf_op jit(solution)/shard_map/ppermute | solution.py:25
  96.9 2.1 %collective-permute-done.26.refs_3_ = bf16[64,1088]{1,0:T(8,128)(2,1)S(1)} collective-permute-done((bf16[64,1088]{1,0:T(8,128)(2,1)S(1)}, bf16[64,1088]{1,0:T(8,128)(2,1)S(1)}, u32[]{:S(2)}, u32[]{:S(2)}) %collective-permute-start.26) | collective-permute-done | bytes 139296 | tf_op jit(solution)/shard_map/ppermute | solution.py:25
  (95 shorter events, 14.4 us)
Async XLA Ops:
  0.6 31.0 %copy-start.4 = (s32[128]{0:T(128)S(1)}, s32[128]{0:T(128)}, u32[]{:S(2)}) copy-start(s32[128]{0:T(128)} %param.10) | copy-start | bytes 1540
  0.6 31.0 %copy-start.5 = (s32[128]{0:T(128)S(1)}, s32[128]{0:T(128)}, u32[]{:S(2)}) copy-start(s32[128]{0:T(128)} %param.11) | copy-start | bytes 1540
  2.3 30.9 %copy-start.2 = (bf16[64,8192]{1,0:T(8,128)(2,1)S(1)}, bf16[64,8192]{1,0:T(8,128)(2,1)}, u32[]{:S(2)}) copy-start(bf16[64,8192]{1,0:T(8,128)(2,1)} %refs_0_.1) | copy-start | bytes 3145732
  2.3 31.3 %copy-start.1 = (bf16[128,1024]{1,0:T(8,128)(2,1)S(1)}, bf16[128,1024]{1,0:T(8,128)(2,1)}, u32[]{:S(2)}) copy-start(bf16[128,1024]{1,0:T(8,128)(2,1)} %refs_2_) | copy-start | bytes 786436
  2.6 29.0 %collective-permute-start.6 = (bf16[128,4096]{1,0:T(8,128)(2,1)S(1)}, bf16[128,4096]{1,0:T(8,128)(2,1)S(1)}, u32[]{:S(2)}, u32[]{:S(2)}) collective-permute-start(bf16[128,4096]{1,0:T(8,128)(2,1)S(1)} %shard_map.88), channel_id=1, source_target_pairs={{0,4},{4,0},{8,12},{12,8},{16,20},{20,16},{24,28},{28,24},{1,5},{5... | collective-permute-start | bytes 3145736 | tf_op jit(solution)/shard_map/ppermute | solution.py:25
  5.7 13.5 %collective-permute-start = (bf16[128,1024]{1,0:T(8,128)(2,1)}, bf16[128,1024]{1,0:T(8,128)(2,1)S(1)}, u32[]{:S(2)}, u32[]{:S(2)}) collective-permute-start(bf16[128,1024]{1,0:T(8,128)(2,1)} %refs_2_), channel_id=1, source_target_pairs={{0,8},{4,12},{8,0},{12,4},{16,24},{20,28},{24,16},{28,20},{1,9},{5... | collective-permute-start | bytes 786440 | tf_op jit(solution)/shard_map/ppermute | solution.py:25
  7.2 14.3 %collective-permute-start.4 = (bf16[128,1024]{1,0:T(8,128)(2,1)}, bf16[128,1024]{1,0:T(8,128)(2,1)S(1)}, u32[]{:S(2)}, u32[]{:S(2)}) collective-permute-start(bf16[128,1024]{1,0:T(8,128)(2,1)} %refs_2_), channel_id=1, source_target_pairs={{0,16},{4,20},{8,24},{12,28},{16,0},{20,4},{24,8},{28,12},{1,17},{... | collective-permute-start | bytes 786440 | tf_op jit(solution)/shard_map/ppermute | solution.py:25
  9.8 12.1 %collective-permute-start.3 = (bf16[128,1024]{1,0:T(8,128)(2,1)}, bf16[128,1024]{1,0:T(8,128)(2,1)S(1)}, u32[]{:S(2)}, u32[]{:S(2)}) collective-permute-start(bf16[128,1024]{1,0:T(8,128)(2,1)} %refs_2_), channel_id=1, source_target_pairs={{0,2},{1,3},{2,0},{3,1},{4,6},{5,7},{6,4},{7,5},{8,10},{9,11},{10,... | collective-permute-start | bytes 786440 | tf_op jit(solution)/shard_map/ppermute | solution.py:25
  19.1 9.2 %collective-permute-start.1 = (bf16[128,1024]{1,0:T(8,128)(2,1)S(1)}, bf16[128,1024]{1,0:T(8,128)(2,1)S(1)}, u32[]{:S(2)}, u32[]{:S(2)}) collective-permute-start(bf16[128,1024]{1,0:T(8,128)(2,1)S(1)} %collective-permute-done.refs_4_.refs_3_), channel_id=1, source_target_pairs={{0,2},{1,3},{2,0},{3,1},{4,6},{5,7},{6,4},{7,5},{8,10},{9,11},{10,... | collective-permute-start | bytes 786440 | tf_op jit(solution)/shard_map/ppermute | solution.py:25
  21.5 7.3 %collective-permute-start.5 = (bf16[128,1024]{1,0:T(8,128)(2,1)S(1)}, bf16[128,1024]{1,0:T(8,128)(2,1)S(1)}, u32[]{:S(2)}, u32[]{:S(2)}) collective-permute-start(bf16[128,1024]{1,0:T(8,128)(2,1)S(1)} %collective-permute-done.4.refs_5_.refs_4_), channel_id=1, source_target_pairs={{0,8},{4,12},{8,0},{12,4},{16,24},{20,28},{24,16},{28,20},{1,9},{5... | collective-permute-start | bytes 786440 | tf_op jit(solution)/shard_map/ppermute | solution.py:25
  22.0 9.6 %collective-permute-start.7 = (bf16[128,1024]{1,0:T(8,128)(2,1)S(1)}, bf16[128,1024]{1,0:T(8,128)(2,1)S(1)}, u32[]{:S(2)}, u32[]{:S(2)}) collective-permute-start(bf16[128,1024]{1,0:T(8,128)(2,1)S(1)} %collective-permute-done.4.refs_5_.refs_4_), channel_id=1, source_target_pairs={{0,2},{1,3},{2,0},{3,1},{4,6},{5,7},{6,4},{7,5},{8,10},{9,11},{10,... | collective-permute-start | bytes 786440 | tf_op jit(solution)/shard_map/ppermute | solution.py:25
  28.7 4.8 %collective-permute-start.2 = (bf16[128,4096]{1,0:T(8,128)(2,1)S(1)}, bf16[128,4096]{1,0:T(8,128)(2,1)S(1)}, u32[]{:S(2)}, u32[]{:S(2)}) collective-permute-start(bf16[128,4096]{1,0:T(8,128)(2,1)S(1)} %shard_map.85.refs_0_), channel_id=1, source_target_pairs={{0,1},{1,0},{2,3},{3,2},{4,5},{5,4},{6,7},{7,6},{8,9},{9,8},{10,11... | collective-permute-start | bytes 3145736 | tf_op jit(solution)/shard_map/ppermute | solution.py:25
  31.6 3.6 %collective-permute-start.8 = (bf16[128,4096]{1,0:T(8,128)(2,1)S(1)}, bf16[128,4096]{1,0:T(8,128)(2,1)S(1)}, u32[]{:S(2)}, u32[]{:S(2)}) collective-permute-start(bf16[128,4096]{1,0:T(8,128)(2,1)S(1)} %collective-permute-done.6.refs_0_.refs_3_.refs_2_), channel_id=1, source_target_pairs={{0,1},{1,0},{2,3},{3,2},{4,5},{5,4},{6,7},{7,6},{8,9},{9,8},{10,11... | collective-permute-start | bytes 3145736 | tf_op jit(solution)/shard_map/ppermute | solution.py:25
  31.6 8.8 %collective-permute-start.11 = (bf16[128,1024]{1,0:T(8,128)(2,1)S(1)}, bf16[128,1024]{1,0:T(8,128)(2,1)S(1)}, u32[]{:S(2)}, u32[]{:S(2)}) collective-permute-start(bf16[128,1024]{1,0:T(8,128)(2,1)S(1)} %collective-permute-done.5.refs_6_.refs_5_), channel_id=1, source_target_pairs={{0,2},{1,3},{2,0},{3,1},{4,6},{5,7},{6,4},{7,5},{8,10},{9,11},{10,... | collective-permute-start | bytes 786440 | tf_op jit(solution)/shard_map/ppermute | solution.py:25
  34.6 7.1 %collective-permute-start.10 = (f32[320,128]{1,0:T(8,128)S(1)}, f32[320,128]{1,0:T(8,128)S(1)}, u32[]{:S(2)}, u32[]{:S(2)}) collective-permute-start(f32[320,128]{1,0:T(8,128)S(1)} %shard_map.87), channel_id=1, source_target_pairs={{0,4},{4,0},{8,12},{12,8},{16,20},{20,16},{24,28},{28,24},{1,5},{5... | collective-permute-start | bytes 491528 | tf_op jit(solution)/shard_map/ppermute | solution.py:25
  35.2 5.2 %copy-start.3 = (bf16[64,64]{1,0:T(8,128)(2,1)S(1)}, bf16[64,64]{1,0:T(8,128)(2,1)}, u32[]{:S(2)}) copy-start(bf16[64,64]{1,0:T(8,128)(2,1)} %refs_7_.1) | copy-start | bytes 24580
  35.9 8.3 %collective-permute-start.9 = (f32[256,128]{1,0:T(8,128)S(1)}, f32[256,128]{1,0:T(8,128)S(1)}, u32[]{:S(2)}, u32[]{:S(2)}) collective-permute-start(f32[256,128]{1,0:T(8,128)S(1)} %shard_map.89), channel_id=1, source_target_pairs={{0,4},{4,0},{8,12},{12,8},{16,20},{20,16},{24,28},{28,24},{1,5},{5... | collective-permute-start | bytes 393224 | tf_op jit(solution)/shard_map/ppermute | solution.py:25
  41.0 9.5 %collective-permute-start.12 = (f32[608,128]{1,0:T(8,128)S(1)}, f32[608,128]{1,0:T(8,128)S(1)}, u32[]{:S(2)}, u32[]{:S(2)}) collective-permute-start(f32[608,128]{1,0:T(8,128)S(1)} %shard_map.91), channel_id=1, source_target_pairs={{0,4},{4,0},{8,12},{12,8},{16,20},{20,16},{24,28},{28,24},{1,5},{5... | collective-permute-start | bytes 933896 | tf_op jit(solution)/shard_map/ppermute | solution.py:25
  50.8 3.7 %collective-permute-start.13 = (f32[4,256]{1,0:T(4,128)S(1)}, f32[4,256]{1,0:T(4,128)S(1)}, u32[]{:S(2)}, u32[]{:S(2)}) collective-permute-start(f32[4,256]{1,0:T(4,128)S(1)} %maximum_maximum_fusion), channel_id=1, source_target_pairs={{0,2},{1,3},{2,0},{3,1},{4,6},{5,7},{6,4},{7,5},{8,10},{9,11},{10,... | collective-permute-start | bytes 12296 | tf_op jit(solution)/shard_map/ppermute | solution.py:25
  54.5 3.7 %collective-permute-start.14 = (f32[2,256]{1,0:T(2,128)S(1)}, f32[2,256]{1,0:T(2,128)S(1)}, u32[]{:S(2)}, u32[]{:S(2)}) collective-permute-start(f32[2,256]{1,0:T(2,128)S(1)} %pad_maximum_fusion.6), channel_id=1, source_target_pairs={{0,8},{4,12},{8,0},{12,4},{16,24},{20,28},{24,16},{28,20},{1,9},{5... | collective-permute-start | bytes 6152 | tf_op jit(solution)/shard_map/ppermute | solution.py:25
  58.2 4.5 %collective-permute-start.15 = (f32[2,256]{1,0:T(2,128)S(1)}, f32[2,256]{1,0:T(2,128)S(1)}, u32[]{:S(2)}, u32[]{:S(2)}) collective-permute-start(f32[2,256]{1,0:T(2,128)S(1)} %pad_maximum_fusion.7), channel_id=1, source_target_pairs={{0,16},{4,20},{8,24},{12,28},{16,0},{20,4},{24,8},{28,12},{1,17},{... | collective-permute-start | bytes 6152 | tf_op jit(solution)/shard_map/ppermute | solution.py:25
  63.6 7.8 %collective-permute-start.17 = (bf16[128,1024]{1,0:T(8,128)(2,1)S(1)}, bf16[128,1024]{1,0:T(8,128)(2,1)S(1)}, u32[]{:S(2)}, u32[]{:S(2)}) collective-permute-start(bf16[128,1024]{1,0:T(8,128)(2,1)S(1)} %convolution_convert_fusion.1), channel_id=1, source_target_pairs={{0,2},{1,3},{2,0},{3,1},{4,6},{5,7},{6,4},{7,5},{8,10},{9,11},{10,... | collective-permute-start | bytes 786440 | tf_op jit(solution)/shard_map/ppermute | solution.py:25
  65.0 17.2 %collective-permute-start.16 = (bf16[128,1024]{1,0:T(8,128)(2,1)S(1)}, bf16[128,1024]{1,0:T(8,128)(2,1)S(1)}, u32[]{:S(2)}, u32[]{:S(2)}) collective-permute-start(bf16[128,1024]{1,0:T(8,128)(2,1)S(1)} %convolution_convert_fusion.2), channel_id=1, source_target_pairs={{0,2},{1,3},{2,0},{3,1},{4,6},{5,7},{6,4},{7,5},{8,10},{9,11},{10,... | collective-permute-start | bytes 786440 | tf_op jit(solution)/shard_map/ppermute | solution.py:25
  71.8 9.6 %collective-permute-start.18 = (bf16[128,1024]{1,0:T(8,128)(2,1)S(1)}, bf16[128,1024]{1,0:T(8,128)(2,1)S(1)}, u32[]{:S(2)}, u32[]{:S(2)}) collective-permute-start(bf16[128,1024]{1,0:T(8,128)(2,1)S(1)} %fusion.3), channel_id=1, source_target_pairs={{0,8},{4,12},{8,0},{12,4},{16,24},{20,28},{24,16},{28,20},{1,9},{5... | collective-permute-start | bytes 786440 | tf_op jit(solution)/shard_map/ppermute | solution.py:25
  72.8 8.6 %collective-permute-start.20 = (f32[64,128]{1,0:T(8,128)S(1)}, f32[64,128]{1,0:T(8,128)S(1)}, u32[]{:S(2)}, u32[]{:S(2)}) collective-permute-start(f32[64,128]{1,0:T(8,128)S(1)} %fusion.23), channel_id=1, source_target_pairs={{0,8},{4,12},{8,0},{12,4},{16,24},{20,28},{24,16},{28,20},{1,9},{5... | collective-permute-start | bytes 98312 | tf_op jit(solution)/shard_map/ppermute | solution.py:25
  74.2 12.5 %collective-permute-start.22 = (bf16[128,1024]{1,0:T(8,128)(2,1)S(1)}, bf16[128,1024]{1,0:T(8,128)(2,1)S(1)}, u32[]{:S(2)}, u32[]{:S(2)}) collective-permute-start(bf16[128,1024]{1,0:T(8,128)(2,1)S(1)} %convolution_convert_fusion), channel_id=1, source_target_pairs={{0,2},{1,3},{2,0},{3,1},{4,6},{5,7},{6,4},{7,5},{8,10},{9,11},{10,... | collective-permute-start | bytes 786440 | tf_op jit(solution)/shard_map/ppermute | solution.py:25
  81.4 5.1 %collective-permute-start.21 = (f32[64,128]{1,0:T(8,128)S(1)}, f32[64,128]{1,0:T(8,128)S(1)}, u32[]{:S(2)}, u32[]{:S(2)}) collective-permute-start(f32[64,128]{1,0:T(8,128)S(1)} %add.152), channel_id=1, source_target_pairs={{0,16},{4,20},{8,24},{12,28},{16,0},{20,4},{24,8},{28,12},{1,17},{... | collective-permute-start | bytes 98312 | tf_op jit(solution)/shard_map/ppermute | solution.py:25
  82.6 14.3 %collective-permute-start.24 = (bf16[128,1024]{1,0:T(8,128)(2,1)S(1)}, bf16[128,1024]{1,0:T(8,128)(2,1)S(1)}, u32[]{:S(2)}, u32[]{:S(2)}) collective-permute-start(bf16[128,1024]{1,0:T(8,128)(2,1)S(1)} %fusion.2), channel_id=1, source_target_pairs={{0,16},{4,20},{8,24},{12,28},{16,0},{20,4},{24,8},{28,12},{1,17},{... | collective-permute-start | bytes 786440 | tf_op jit(solution)/shard_map/ppermute | solution.py:25
  86.7 1.6 %collective-permute-start.25 = (f32[64,1088]{1,0:T(8,128)S(1)}, f32[64,1088]{1,0:T(8,128)S(1)}, u32[]{:S(2)}, u32[]{:S(2)}) collective-permute-start(f32[64,1088]{1,0:T(8,128)S(1)} %pad_maximum_fusion), channel_id=1, source_target_pairs={{0,1},{1,0},{2,3},{3,2},{4,5},{5,4},{6,7},{7,6},{8,9},{9,8},{10,11... | collective-permute-start | bytes 835592 | tf_op jit(solution)/shard_map/ppermute | solution.py:25
  87.1 9.9 %collective-permute-start.23 = (bf16[128,1024]{1,0:T(8,128)(2,1)S(1)}, bf16[128,1024]{1,0:T(8,128)(2,1)S(1)}, u32[]{:S(2)}, u32[]{:S(2)}) collective-permute-start(bf16[128,1024]{1,0:T(8,128)(2,1)S(1)} %fusion.4), channel_id=1, source_target_pairs={{0,8},{4,12},{8,0},{12,4},{16,24},{20,28},{24,16},{28,20},{1,9},{5... | collective-permute-start | bytes 786440 | tf_op jit(solution)/shard_map/ppermute | solution.py:25
  87.4 9.1 %collective-permute-start.19 = (bf16[128,1024]{1,0:T(8,128)(2,1)S(1)}, bf16[128,1024]{1,0:T(8,128)(2,1)S(1)}, u32[]{:S(2)}, u32[]{:S(2)}) collective-permute-start(bf16[128,1024]{1,0:T(8,128)(2,1)S(1)} %convolution_convert_fusion.3), channel_id=1, source_target_pairs={{0,2},{1,3},{2,0},{3,1},{4,6},{5,7},{6,4},{7,5},{8,10},{9,11},{10,... | collective-permute-start | bytes 786440 | tf_op jit(solution)/shard_map/ppermute | solution.py:25
  88.4 10.7 %collective-permute-start.26 = (bf16[64,1088]{1,0:T(8,128)(2,1)S(1)}, bf16[64,1088]{1,0:T(8,128)(2,1)S(1)}, u32[]{:S(2)}, u32[]{:S(2)}) collective-permute-start(bf16[64,1088]{1,0:T(8,128)(2,1)S(1)} %convert_element_type.97), channel_id=1, source_target_pairs={{0,2},{1,3},{2,0},{3,1},{4,6},{5,7},{6,4},{7,5},{8,10},{9,11},{10,... | collective-permute-start | bytes 417800 | tf_op jit(solution)/shard_map/ppermute | solution.py:25
  (1 other events, 1.6 us)

commit v14 on v13

--- a/solution.py
+++ b/solution.py
@@ -335,7 +335,7 @@
                 send, _ = lax.optimization_barrier((send, came_z))
             came = first_came if j == n_z - 1 else swap_z(send, bit)
             came_z = came if came_z is None else came_z
-            if j ^ bit:
+            if j ^ bit or bit != bits[-1]:
                 sums[j ^ bit] = sums[j ^ bit] + came.astype(f32)
             else:
                 pieces.append(came)

time: 100 us -> 98.4 us (0.984)
  transfers between devices with their start and end apart: 27 -> 27, of which waited for: 17 -> 16; matrix products, arithmetic and copies ran while one was open for 3% -> 3% of each run, Pallas kernels for 5% -> 5%
where the time goes in v14:
time: 98.4 us; the launch traced here: 98.2 us
  waiting for transfers between devices  56.7 us (58%)
  starting transfers between devices  28.4 us (29%)
  Pallas kernels  6.01 us (6%)
  matrix products  3.53 us (4%)
  local copies, waits for them, and re-layouts  1.7 us (2%)
  between operations  1.06 us (1%)
    ppermute x27, waiting for transfers between devices, swap(): return lax.ppermute(value, axis, [(i, i ^ bit) for i in range(size)])  56.7 us
    ppermute x27, starting transfers between devices, swap(): return lax.ppermute(value, axis, [(i, i ^ bit) for i in range(size)])  28.4 us
    pallas_call x4, Pallas kernels, logits_of(): pl.pallas_call(kernel, out_shape=jax.ShapeDtypeStruct((total + extra, tok...  3.47 us
    dot_general x10, matrix products, dot_first(): return lax.dot_general(a, b, contract_first, preferred_element_type=f32)  3.07 us
  transfers between devices with their start and end apart: 27, of which 16 were waited for; matrix products, arithmetic and copies ran while one was open for 3% of the time, Pallas kernels for 5%

profile of v14, /device:TPU:0, one launch (start us, length us, event | category | flops | bytes accessed | tf_op | source)
XLA Modules:
  0.0 98.2 jit_solution(14947841402598022476)
XLA Ops:
  0.7 1.6 %copy-done = bf16[128,8192]{1,0:T(8,128)(2,1)S(1)} copy-done((bf16[128,8192]{1,0:T(8,128)(2,1)S(1)}, bf16[128,8192]{1,0:T(8,128)(2,1)}, u32[]{:S(2)}) %copy-start) | copy-done | bytes 2097176
  2.6 3.0 %collective-permute-start.6 = (bf16[128,4096]{1,0:T(8,128)(2,1)S(1)}, bf16[128,4096]{1,0:T(8,128)(2,1)S(1)}, u32[]{:S(2)}, u32[]{:S(2)}) collective-permute-start(bf16[128,4096]{1,0:T(8,128)(2,1)S(1)} %shard_map.88), channel_id=1, source_target_pairs={{0,4},{4,0},{8,12},{12,8},{16,20},{20,16},{24,28},{28,24},{1,5},{5... | collective-permute-start | bytes 3145736 | tf_op jit(solution)/shard_map/ppermute | solution.py:25
  5.7 1.6 %collective-permute-start = (bf16[128,1024]{1,0:T(8,128)(2,1)}, bf16[128,1024]{1,0:T(8,128)(2,1)S(1)}, u32[]{:S(2)}, u32[]{:S(2)}) collective-permute-start(bf16[128,1024]{1,0:T(8,128)(2,1)} %refs_2_), channel_id=1, source_target_pairs={{0,8},{4,12},{8,0},{12,4},{16,24},{20,28},{24,16},{28,20},{1,9},{5... | collective-permute-start | bytes 786440 | tf_op jit(solution)/shard_map/ppermute | solution.py:25
  7.2 2.6 %collective-permute-start.4 = (bf16[128,1024]{1,0:T(8,128)(2,1)}, bf16[128,1024]{1,0:T(8,128)(2,1)S(1)}, u32[]{:S(2)}, u32[]{:S(2)}) collective-permute-start(bf16[128,1024]{1,0:T(8,128)(2,1)} %refs_2_), channel_id=1, source_target_pairs={{0,16},{4,20},{8,24},{12,28},{16,0},{20,4},{24,8},{28,12},{1,17},{... | collective-permute-start | bytes 786440 | tf_op jit(solution)/shard_map/ppermute | solution.py:25
  9.8 1.5 %collective-permute-start.3 = (bf16[128,1024]{1,0:T(8,128)(2,1)}, bf16[128,1024]{1,0:T(8,128)(2,1)S(1)}, u32[]{:S(2)}, u32[]{:S(2)}) collective-permute-start(bf16[128,1024]{1,0:T(8,128)(2,1)} %refs_2_), channel_id=1, source_target_pairs={{0,2},{1,3},{2,0},{3,1},{4,6},{5,7},{6,4},{7,5},{8,10},{9,11},{10,... | collective-permute-start | bytes 786440 | tf_op jit(solution)/shard_map/ppermute | solution.py:25
  11.3 7.8 %collective-permute-done.refs_4_.refs_3_ = bf16[128,1024]{1,0:T(8,128)(2,1)S(1)} collective-permute-done((bf16[128,1024]{1,0:T(8,128)(2,1)}, bf16[128,1024]{1,0:T(8,128)(2,1)S(1)}, u32[]{:S(2)}, u32[]{:S(2)}) %collective-permute-start) | collective-permute-done | bytes 262176 | tf_op jit(solution)/shard_map/ppermute | solution.py:25
  19.1 1.5 %collective-permute-start.1 = (bf16[128,1024]{1,0:T(8,128)(2,1)S(1)}, bf16[128,1024]{1,0:T(8,128)(2,1)S(1)}, u32[]{:S(2)}, u32[]{:S(2)}) collective-permute-start(bf16[128,1024]{1,0:T(8,128)(2,1)S(1)} %collective-permute-done.refs_4_.refs_3_), channel_id=1, source_target_pairs={{0,2},{1,3},{2,0},{3,1},{4,6},{5,7},{6,4},{7,5},{8,10},{9,11},{10,... | collective-permute-start | bytes 786440 | tf_op jit(solution)/shard_map/ppermute | solution.py:25
  20.6 0.9 collective-permute-done.4.refs_5_.refs_4_
  22.0 1.5 %collective-permute-start.7 = (bf16[128,1024]{1,0:T(8,128)(2,1)S(1)}, bf16[128,1024]{1,0:T(8,128)(2,1)S(1)}, u32[]{:S(2)}, u32[]{:S(2)}) collective-permute-start(bf16[128,1024]{1,0:T(8,128)(2,1)S(1)} %collective-permute-done.4.refs_5_.refs_4_), channel_id=1, source_target_pairs={{0,2},{1,3},{2,0},{3,1},{4,6},{5,7},{6,4},{7,5},{8,10},{9,11},{10,... | collective-permute-start | bytes 786440 | tf_op jit(solution)/shard_map/ppermute | solution.py:25
  23.5 4.9 %collective-permute-done.1.refs_6_ = bf16[128,1024]{1,0:T(8,128)(2,1)S(1)} collective-permute-done((bf16[128,1024]{1,0:T(8,128)(2,1)S(1)}, bf16[128,1024]{1,0:T(8,128)(2,1)S(1)}, u32[]{:S(2)}, u32[]{:S(2)}) %collective-permute-start.1) | collective-permute-done | bytes 262176 | tf_op jit(solution)/shard_map/ppermute | solution.py:25
  28.8 2.8 %collective-permute-done.7.refs_7_ = bf16[128,1024]{1,0:T(8,128)(2,1)S(1)} collective-permute-done((bf16[128,1024]{1,0:T(8,128)(2,1)S(1)}, bf16[128,1024]{1,0:T(8,128)(2,1)S(1)}, u32[]{:S(2)}, u32[]{:S(2)}) %collective-permute-start.7) | collective-permute-done | bytes 262176 | tf_op jit(solution)/shard_map/ppermute | solution.py:25
  31.6 1.6 %collective-permute-start.11 = (bf16[128,1024]{1,0:T(8,128)(2,1)S(1)}, bf16[128,1024]{1,0:T(8,128)(2,1)S(1)}, u32[]{:S(2)}, u32[]{:S(2)}) collective-permute-start(bf16[128,1024]{1,0:T(8,128)(2,1)S(1)} %collective-permute-done.5.refs_6_.refs_5_), channel_id=1, source_target_pairs={{0,2},{1,3},{2,0},{3,1},{4,6},{5,7},{6,4},{7,5},{8,10},{9,11},{10,... | collective-permute-start | bytes 786440 | tf_op jit(solution)/shard_map/ppermute | solution.py:25
  33.6 1.0 %shard_map.87 = f32[320,128]{1,0:T(8,128)S(1)} custom-call(bf16[128,4096]{1,0:T(8,128)(2,1)S(1)} %shard_map.85.refs_0_, bf16[128,4096]{1,0:T(8,128)(2,1)S(1)} %collective-permute-done.2.refs_1_, bf16[64,4096]{1,0:T(8,128)(2,1)S(1)} %shard_map.86.refs_2_, bf16[128,1024]{1,0:T(8,128)(2,1)S(1)} %copy-done.1, ...), custom_call_target="tpu_custom_call" | custom-call | flops 335544320 | bytes 3833856 | tf_op jit(solution)/shard_map/pallas_call | solution.py:106
  35.9 1.6 %collective-permute-start.9 = (f32[256,128]{1,0:T(8,128)S(1)}, f32[256,128]{1,0:T(8,128)S(1)}, u32[]{:S(2)}, u32[]{:S(2)}) collective-permute-start(f32[256,128]{1,0:T(8,128)S(1)} %shard_map.89), channel_id=1, source_target_pairs={{0,4},{4,0},{8,12},{12,8},{16,20},{20,16},{24,28},{28,24},{1,5},{5... | collective-permute-start | bytes 393224 | tf_op jit(solution)/shard_map/ppermute | solution.py:25
  37.5 1.2 %shard_map.90.refs_6_ = f32[576,128]{1,0:T(8,128)S(1)} custom-call(bf16[128,4096]{1,0:T(8,128)(2,1)S(1)} %shard_map.85.refs_0_, bf16[128,4096]{1,0:T(8,128)(2,1)S(1)} %collective-permute-done.2.refs_1_, bf16[64,4096]{1,0:T(8,128)(2,1)S(1)} %shard_map.86.refs_2_, bf16[128,4096]{1,0:T(8,128)(2,1)S(1)} %collective-permute-done.6.refs_0_.refs_3_.refs_2_, ...), custom_call_target="tpu_custom_call" | custom-call | flops 452984832 | bytes 4620288 | tf_op jit(solution)/shard_map/pallas_call | solution.py:106
  38.7 1.7 %collective-permute-done.11.refs_5_ = bf16[128,1024]{1,0:T(8,128)(2,1)S(1)} collective-permute-done((bf16[128,1024]{1,0:T(8,128)(2,1)S(1)}, bf16[128,1024]{1,0:T(8,128)(2,1)S(1)}, u32[]{:S(2)}, u32[]{:S(2)}) %collective-permute-start.11) | collective-permute-done | bytes 262176 | tf_op jit(solution)/shard_map/ppermute | solution.py:25
  42.4 1.9 %collective-permute-done.9 = f32[256,128]{1,0:T(8,128)S(1)} collective-permute-done((f32[256,128]{1,0:T(8,128)S(1)}, f32[256,128]{1,0:T(8,128)S(1)}, u32[]{:S(2)}, u32[]{:S(2)}) %collective-permute-start.9) | collective-permute-done | bytes 131104 | tf_op jit(solution)/shard_map/ppermute | solution.py:25
  44.4 6.1 %collective-permute-done.12 = f32[608,128]{1,0:T(8,128)S(1)} collective-permute-done((f32[608,128]{1,0:T(8,128)S(1)}, f32[608,128]{1,0:T(8,128)S(1)}, u32[]{:S(2)}, u32[]{:S(2)}) %collective-permute-start.12) | collective-permute-done | bytes 311328 | tf_op jit(solution)/shard_map/ppermute | solution.py:25
  50.8 1.1 %collective-permute-start.13 = (f32[4,256]{1,0:T(4,128)S(1)}, f32[4,256]{1,0:T(4,128)S(1)}, u32[]{:S(2)}, u32[]{:S(2)}) collective-permute-start(f32[4,256]{1,0:T(4,128)S(1)} %maximum_maximum_fusion), channel_id=1, source_target_pairs={{0,2},{1,3},{2,0},{3,1},{4,6},{5,7},{6,4},{7,5},{8,10},{9,11},{10,... | collective-permute-start | bytes 12296 | tf_op jit(solution)/shard_map/ppermute | solution.py:25
  52.1 2.4 %collective-permute-done.13 = f32[4,256]{1,0:T(4,128)S(1)} collective-permute-done((f32[4,256]{1,0:T(4,128)S(1)}, f32[4,256]{1,0:T(4,128)S(1)}, u32[]{:S(2)}, u32[]{:S(2)}) %collective-permute-start.13) | collective-permute-done | bytes 4128 | tf_op jit(solution)/shard_map/ppermute | solution.py:25
  54.6 3.5 %collective-permute-done.14 = f32[2,256]{1,0:T(2,128)S(1)} collective-permute-done((f32[2,256]{1,0:T(2,128)S(1)}, f32[2,256]{1,0:T(2,128)S(1)}, u32[]{:S(2)}, u32[]{:S(2)}) %collective-permute-start.14) | collective-permute-done | bytes 2080 | tf_op jit(solution)/shard_map/ppermute | solution.py:25
  58.2 1.4 %collective-permute-start.15 = (f32[2,256]{1,0:T(2,128)S(1)}, f32[2,256]{1,0:T(2,128)S(1)}, u32[]{:S(2)}, u32[]{:S(2)}) collective-permute-start(f32[2,256]{1,0:T(2,128)S(1)} %pad_maximum_fusion.7), channel_id=1, source_target_pairs={{0,16},{4,20},{8,24},{12,28},{16,0},{20,4},{24,8},{28,12},{1,17},{... | collective-permute-start | bytes 6152 | tf_op jit(solution)/shard_map/ppermute | solution.py:25
  59.5 3.2 %collective-permute-done.15 = f32[2,256]{1,0:T(2,128)S(1)} collective-permute-done((f32[2,256]{1,0:T(2,128)S(1)}, f32[2,256]{1,0:T(2,128)S(1)}, u32[]{:S(2)}, u32[]{:S(2)}) %collective-permute-start.15) | collective-permute-done | bytes 2080 | tf_op jit(solution)/shard_map/ppermute | solution.py:25
  63.6 1.1 %collective-permute-start.17 = (bf16[128,1024]{1,0:T(8,128)(2,1)S(1)}, bf16[128,1024]{1,0:T(8,128)(2,1)S(1)}, u32[]{:S(2)}, u32[]{:S(2)}) collective-permute-start(bf16[128,1024]{1,0:T(8,128)(2,1)S(1)} %convolution_convert_fusion.1), channel_id=1, source_target_pairs={{0,2},{1,3},{2,0},{3,1},{4,6},{5,7},{6,4},{7,5},{8,10},{9,11},{10,... | collective-permute-start | bytes 786440 | tf_op jit(solution)/shard_map/ppermute | solution.py:25
  65.0 1.1 %collective-permute-start.16 = (bf16[128,1024]{1,0:T(8,128)(2,1)S(1)}, bf16[128,1024]{1,0:T(8,128)(2,1)S(1)}, u32[]{:S(2)}, u32[]{:S(2)}) collective-permute-start(bf16[128,1024]{1,0:T(8,128)(2,1)S(1)} %convolution_convert_fusion.2), channel_id=1, source_target_pairs={{0,2},{1,3},{2,0},{3,1},{4,6},{5,7},{6,4},{7,5},{8,10},{9,11},{10,... | collective-permute-start | bytes 786440 | tf_op jit(solution)/shard_map/ppermute | solution.py:25
  66.4 5.0 %collective-permute-done.17 = bf16[128,1024]{1,0:T(8,128)(2,1)S(1)} collective-permute-done((bf16[128,1024]{1,0:T(8,128)(2,1)S(1)}, bf16[128,1024]{1,0:T(8,128)(2,1)S(1)}, u32[]{:S(2)}, u32[]{:S(2)}) %collective-permute-start.17) | collective-permute-done | bytes 262176 | tf_op jit(solution)/shard_map/ppermute | solution.py:25
  72.8 1.3 %collective-permute-start.22 = (f32[64,128]{1,0:T(8,128)S(1)}, f32[64,128]{1,0:T(8,128)S(1)}, u32[]{:S(2)}, u32[]{:S(2)}) collective-permute-start(f32[64,128]{1,0:T(8,128)S(1)} %fusion.24), channel_id=1, source_target_pairs={{0,8},{4,12},{8,0},{12,4},{16,24},{20,28},{24,16},{28,20},{1,9},{5... | collective-permute-start | bytes 98312 | tf_op jit(solution)/shard_map/ppermute | solution.py:25
  74.8 6.6 %collective-permute-done.22 = f32[64,128]{1,0:T(8,128)S(1)} collective-permute-done((f32[64,128]{1,0:T(8,128)S(1)}, f32[64,128]{1,0:T(8,128)S(1)}, u32[]{:S(2)}, u32[]{:S(2)}) %collective-permute-start.22) | collective-permute-done | bytes 32800 | tf_op jit(solution)/shard_map/ppermute | solution.py:25
  82.6 2.2 %collective-permute-start.24 = (bf16[128,1024]{1,0:T(8,128)(2,1)S(1)}, bf16[128,1024]{1,0:T(8,128)(2,1)S(1)}, u32[]{:S(2)}, u32[]{:S(2)}) collective-permute-start(bf16[128,1024]{1,0:T(8,128)(2,1)S(1)} %fusion.3), channel_id=1, source_target_pairs={{0,16},{4,20},{8,24},{12,28},{16,0},{20,4},{24,8},{28,12},{1,17},{... | collective-permute-start | bytes 786440 | tf_op jit(solution)/shard_map/ppermute | solution.py:25
  85.3 1.1 %collective-permute-done.23 = f32[64,128]{1,0:T(8,128)S(1)} collective-permute-done((f32[64,128]{1,0:T(8,128)S(1)}, f32[64,128]{1,0:T(8,128)S(1)}, u32[]{:S(2)}, u32[]{:S(2)}) %collective-permute-start.23) | collective-permute-done | bytes 32800 | tf_op jit(solution)/shard_map/ppermute | solution.py:25
  88.9 2.3 %collective-permute-done.19 = bf16[128,1024]{1,0:T(8,128)(2,1)S(1)} collective-permute-done((bf16[128,1024]{1,0:T(8,128)(2,1)S(1)}, bf16[128,1024]{1,0:T(8,128)(2,1)S(1)}, u32[]{:S(2)}, u32[]{:S(2)}) %collective-permute-start.19) | collective-permute-done | bytes 262176 | tf_op jit(solution)/shard_map/ppermute | solution.py:25
  91.1 5.8 %collective-permute-done.21 = bf16[128,1024]{1,0:T(8,128)(2,1)S(1)} collective-permute-done((bf16[128,1024]{1,0:T(8,128)(2,1)S(1)}, bf16[128,1024]{1,0:T(8,128)(2,1)S(1)}, u32[]{:S(2)}, u32[]{:S(2)}) %collective-permute-start.21) | collective-permute-done | bytes 262176 | tf_op jit(solution)/shard_map/ppermute | solution.py:25
  (95 shorter events, 14.5 us)
Async XLA Ops:
  0.6 31.0 %copy-start.4 = (s32[128]{0:T(128)S(1)}, s32[128]{0:T(128)}, u32[]{:S(2)}) copy-start(s32[128]{0:T(128)} %param.10) | copy-start | bytes 1540
  0.6 31.0 %copy-start.5 = (s32[128]{0:T(128)S(1)}, s32[128]{0:T(128)}, u32[]{:S(2)}) copy-start(s32[128]{0:T(128)} %param.11) | copy-start | bytes 1540
  2.3 30.9 %copy-start.2 = (bf16[64,8192]{1,0:T(8,128)(2,1)S(1)}, bf16[64,8192]{1,0:T(8,128)(2,1)}, u32[]{:S(2)}) copy-start(bf16[64,8192]{1,0:T(8,128)(2,1)} %refs_0_.1) | copy-start | bytes 3145732
  2.3 31.3 %copy-start.1 = (bf16[128,1024]{1,0:T(8,128)(2,1)S(1)}, bf16[128,1024]{1,0:T(8,128)(2,1)}, u32[]{:S(2)}) copy-start(bf16[128,1024]{1,0:T(8,128)(2,1)} %refs_2_) | copy-start | bytes 786436
  2.6 29.0 %collective-permute-start.6 = (bf16[128,4096]{1,0:T(8,128)(2,1)S(1)}, bf16[128,4096]{1,0:T(8,128)(2,1)S(1)}, u32[]{:S(2)}, u32[]{:S(2)}) collective-permute-start(bf16[128,4096]{1,0:T(8,128)(2,1)S(1)} %shard_map.88), channel_id=1, source_target_pairs={{0,4},{4,0},{8,12},{12,8},{16,20},{20,16},{24,28},{28,24},{1,5},{5... | collective-permute-start | bytes 3145736 | tf_op jit(solution)/shard_map/ppermute | solution.py:25
  5.7 13.5 %collective-permute-start = (bf16[128,1024]{1,0:T(8,128)(2,1)}, bf16[128,1024]{1,0:T(8,128)(2,1)S(1)}, u32[]{:S(2)}, u32[]{:S(2)}) collective-permute-start(bf16[128,1024]{1,0:T(8,128)(2,1)} %refs_2_), channel_id=1, source_target_pairs={{0,8},{4,12},{8,0},{12,4},{16,24},{20,28},{24,16},{28,20},{1,9},{5... | collective-permute-start | bytes 786440 | tf_op jit(solution)/shard_map/ppermute | solution.py:25
  7.2 14.3 %collective-permute-start.4 = (bf16[128,1024]{1,0:T(8,128)(2,1)}, bf16[128,1024]{1,0:T(8,128)(2,1)S(1)}, u32[]{:S(2)}, u32[]{:S(2)}) collective-permute-start(bf16[128,1024]{1,0:T(8,128)(2,1)} %refs_2_), channel_id=1, source_target_pairs={{0,16},{4,20},{8,24},{12,28},{16,0},{20,4},{24,8},{28,12},{1,17},{... | collective-permute-start | bytes 786440 | tf_op jit(solution)/shard_map/ppermute | solution.py:25
  9.8 12.1 %collective-permute-start.3 = (bf16[128,1024]{1,0:T(8,128)(2,1)}, bf16[128,1024]{1,0:T(8,128)(2,1)S(1)}, u32[]{:S(2)}, u32[]{:S(2)}) collective-permute-start(bf16[128,1024]{1,0:T(8,128)(2,1)} %refs_2_), channel_id=1, source_target_pairs={{0,2},{1,3},{2,0},{3,1},{4,6},{5,7},{6,4},{7,5},{8,10},{9,11},{10,... | collective-permute-start | bytes 786440 | tf_op jit(solution)/shard_map/ppermute | solution.py:25
  19.1 9.2 %collective-permute-start.1 = (bf16[128,1024]{1,0:T(8,128)(2,1)S(1)}, bf16[128,1024]{1,0:T(8,128)(2,1)S(1)}, u32[]{:S(2)}, u32[]{:S(2)}) collective-permute-start(bf16[128,1024]{1,0:T(8,128)(2,1)S(1)} %collective-permute-done.refs_4_.refs_3_), channel_id=1, source_target_pairs={{0,2},{1,3},{2,0},{3,1},{4,6},{5,7},{6,4},{7,5},{8,10},{9,11},{10,... | collective-permute-start | bytes 786440 | tf_op jit(solution)/shard_map/ppermute | solution.py:25
  21.5 7.3 %collective-permute-start.5 = (bf16[128,1024]{1,0:T(8,128)(2,1)S(1)}, bf16[128,1024]{1,0:T(8,128)(2,1)S(1)}, u32[]{:S(2)}, u32[]{:S(2)}) collective-permute-start(bf16[128,1024]{1,0:T(8,128)(2,1)S(1)} %collective-permute-done.4.refs_5_.refs_4_), channel_id=1, source_target_pairs={{0,8},{4,12},{8,0},{12,4},{16,24},{20,28},{24,16},{28,20},{1,9},{5... | collective-permute-start | bytes 786440 | tf_op jit(solution)/shard_map/ppermute | solution.py:25
  22.0 9.6 %collective-permute-start.7 = (bf16[128,1024]{1,0:T(8,128)(2,1)S(1)}, bf16[128,1024]{1,0:T(8,128)(2,1)S(1)}, u32[]{:S(2)}, u32[]{:S(2)}) collective-permute-start(bf16[128,1024]{1,0:T(8,128)(2,1)S(1)} %collective-permute-done.4.refs_5_.refs_4_), channel_id=1, source_target_pairs={{0,2},{1,3},{2,0},{3,1},{4,6},{5,7},{6,4},{7,5},{8,10},{9,11},{10,... | collective-permute-start | bytes 786440 | tf_op jit(solution)/shard_map/ppermute | solution.py:25
  28.7 4.8 %collective-permute-start.2 = (bf16[128,4096]{1,0:T(8,128)(2,1)S(1)}, bf16[128,4096]{1,0:T(8,128)(2,1)S(1)}, u32[]{:S(2)}, u32[]{:S(2)}) collective-permute-start(bf16[128,4096]{1,0:T(8,128)(2,1)S(1)} %shard_map.85.refs_0_), channel_id=1, source_target_pairs={{0,1},{1,0},{2,3},{3,2},{4,5},{5,4},{6,7},{7,6},{8,9},{9,8},{10,11... | collective-permute-start | bytes 3145736 | tf_op jit(solution)/shard_map/ppermute | solution.py:25
  31.6 3.6 %collective-permute-start.8 = (bf16[128,4096]{1,0:T(8,128)(2,1)S(1)}, bf16[128,4096]{1,0:T(8,128)(2,1)S(1)}, u32[]{:S(2)}, u32[]{:S(2)}) collective-permute-start(bf16[128,4096]{1,0:T(8,128)(2,1)S(1)} %collective-permute-done.6.refs_0_.refs_3_.refs_2_), channel_id=1, source_target_pairs={{0,1},{1,0},{2,3},{3,2},{4,5},{5,4},{6,7},{7,6},{8,9},{9,8},{10,11... | collective-permute-start | bytes 3145736 | tf_op jit(solution)/shard_map/ppermute | solution.py:25
  31.6 8.8 %collective-permute-start.11 = (bf16[128,1024]{1,0:T(8,128)(2,1)S(1)}, bf16[128,1024]{1,0:T(8,128)(2,1)S(1)}, u32[]{:S(2)}, u32[]{:S(2)}) collective-permute-start(bf16[128,1024]{1,0:T(8,128)(2,1)S(1)} %collective-permute-done.5.refs_6_.refs_5_), channel_id=1, source_target_pairs={{0,2},{1,3},{2,0},{3,1},{4,6},{5,7},{6,4},{7,5},{8,10},{9,11},{10,... | collective-permute-start | bytes 786440 | tf_op jit(solution)/shard_map/ppermute | solution.py:25
  34.6 7.1 %collective-permute-start.10 = (f32[320,128]{1,0:T(8,128)S(1)}, f32[320,128]{1,0:T(8,128)S(1)}, u32[]{:S(2)}, u32[]{:S(2)}) collective-permute-start(f32[320,128]{1,0:T(8,128)S(1)} %shard_map.87), channel_id=1, source_target_pairs={{0,4},{4,0},{8,12},{12,8},{16,20},{20,16},{24,28},{28,24},{1,5},{5... | collective-permute-start | bytes 491528 | tf_op jit(solution)/shard_map/ppermute | solution.py:25
  35.2 5.2 %copy-start.3 = (bf16[64,64]{1,0:T(8,128)(2,1)S(1)}, bf16[64,64]{1,0:T(8,128)(2,1)}, u32[]{:S(2)}) copy-start(bf16[64,64]{1,0:T(8,128)(2,1)} %refs_7_.1) | copy-start | bytes 24580
  35.9 8.3 %collective-permute-start.9 = (f32[256,128]{1,0:T(8,128)S(1)}, f32[256,128]{1,0:T(8,128)S(1)}, u32[]{:S(2)}, u32[]{:S(2)}) collective-permute-start(f32[256,128]{1,0:T(8,128)S(1)} %shard_map.89), channel_id=1, source_target_pairs={{0,4},{4,0},{8,12},{12,8},{16,20},{20,16},{24,28},{28,24},{1,5},{5... | collective-permute-start | bytes 393224 | tf_op jit(solution)/shard_map/ppermute | solution.py:25
  41.0 9.5 %collective-permute-start.12 = (f32[608,128]{1,0:T(8,128)S(1)}, f32[608,128]{1,0:T(8,128)S(1)}, u32[]{:S(2)}, u32[]{:S(2)}) collective-permute-start(f32[608,128]{1,0:T(8,128)S(1)} %shard_map.91), channel_id=1, source_target_pairs={{0,4},{4,0},{8,12},{12,8},{16,20},{20,16},{24,28},{28,24},{1,5},{5... | collective-permute-start | bytes 933896 | tf_op jit(solution)/shard_map/ppermute | solution.py:25
  50.8 3.7 %collective-permute-start.13 = (f32[4,256]{1,0:T(4,128)S(1)}, f32[4,256]{1,0:T(4,128)S(1)}, u32[]{:S(2)}, u32[]{:S(2)}) collective-permute-start(f32[4,256]{1,0:T(4,128)S(1)} %maximum_maximum_fusion), channel_id=1, source_target_pairs={{0,2},{1,3},{2,0},{3,1},{4,6},{5,7},{6,4},{7,5},{8,10},{9,11},{10,... | collective-permute-start | bytes 12296 | tf_op jit(solution)/shard_map/ppermute | solution.py:25
  54.5 3.7 %collective-permute-start.14 = (f32[2,256]{1,0:T(2,128)S(1)}, f32[2,256]{1,0:T(2,128)S(1)}, u32[]{:S(2)}, u32[]{:S(2)}) collective-permute-start(f32[2,256]{1,0:T(2,128)S(1)} %pad_maximum_fusion.6), channel_id=1, source_target_pairs={{0,8},{4,12},{8,0},{12,4},{16,24},{20,28},{24,16},{28,20},{1,9},{5... | collective-permute-start | bytes 6152 | tf_op jit(solution)/shard_map/ppermute | solution.py:25
  58.2 4.5 %collective-permute-start.15 = (f32[2,256]{1,0:T(2,128)S(1)}, f32[2,256]{1,0:T(2,128)S(1)}, u32[]{:S(2)}, u32[]{:S(2)}) collective-permute-start(f32[2,256]{1,0:T(2,128)S(1)} %pad_maximum_fusion.7), channel_id=1, source_target_pairs={{0,16},{4,20},{8,24},{12,28},{16,0},{20,4},{24,8},{28,12},{1,17},{... | collective-permute-start | bytes 6152 | tf_op jit(solution)/shard_map/ppermute | solution.py:25
  63.6 7.8 %collective-permute-start.17 = (bf16[128,1024]{1,0:T(8,128)(2,1)S(1)}, bf16[128,1024]{1,0:T(8,128)(2,1)S(1)}, u32[]{:S(2)}, u32[]{:S(2)}) collective-permute-start(bf16[128,1024]{1,0:T(8,128)(2,1)S(1)} %convolution_convert_fusion.1), channel_id=1, source_target_pairs={{0,2},{1,3},{2,0},{3,1},{4,6},{5,7},{6,4},{7,5},{8,10},{9,11},{10,... | collective-permute-start | bytes 786440 | tf_op jit(solution)/shard_map/ppermute | solution.py:25
  65.0 17.2 %collective-permute-start.16 = (bf16[128,1024]{1,0:T(8,128)(2,1)S(1)}, bf16[128,1024]{1,0:T(8,128)(2,1)S(1)}, u32[]{:S(2)}, u32[]{:S(2)}) collective-permute-start(bf16[128,1024]{1,0:T(8,128)(2,1)S(1)} %convolution_convert_fusion.2), channel_id=1, source_target_pairs={{0,2},{1,3},{2,0},{3,1},{4,6},{5,7},{6,4},{7,5},{8,10},{9,11},{10,... | collective-permute-start | bytes 786440 | tf_op jit(solution)/shard_map/ppermute | solution.py:25
  71.8 9.6 %collective-permute-start.18 = (bf16[128,1024]{1,0:T(8,128)(2,1)S(1)}, bf16[128,1024]{1,0:T(8,128)(2,1)S(1)}, u32[]{:S(2)}, u32[]{:S(2)}) collective-permute-start(bf16[128,1024]{1,0:T(8,128)(2,1)S(1)} %fusion.4), channel_id=1, source_target_pairs={{0,8},{4,12},{8,0},{12,4},{16,24},{20,28},{24,16},{28,20},{1,9},{5... | collective-permute-start | bytes 786440 | tf_op jit(solution)/shard_map/ppermute | solution.py:25
  72.8 8.6 %collective-permute-start.22 = (f32[64,128]{1,0:T(8,128)S(1)}, f32[64,128]{1,0:T(8,128)S(1)}, u32[]{:S(2)}, u32[]{:S(2)}) collective-permute-start(f32[64,128]{1,0:T(8,128)S(1)} %fusion.24), channel_id=1, source_target_pairs={{0,8},{4,12},{8,0},{12,4},{16,24},{20,28},{24,16},{28,20},{1,9},{5... | collective-permute-start | bytes 98312 | tf_op jit(solution)/shard_map/ppermute | solution.py:25
  74.2 12.5 %collective-permute-start.20 = (bf16[128,1024]{1,0:T(8,128)(2,1)S(1)}, bf16[128,1024]{1,0:T(8,128)(2,1)S(1)}, u32[]{:S(2)}, u32[]{:S(2)}) collective-permute-start(bf16[128,1024]{1,0:T(8,128)(2,1)S(1)} %convolution_convert_fusion), channel_id=1, source_target_pairs={{0,2},{1,3},{2,0},{3,1},{4,6},{5,7},{6,4},{7,5},{8,10},{9,11},{10,... | collective-permute-start | bytes 786440 | tf_op jit(solution)/shard_map/ppermute | solution.py:25
  81.4 5.1 %collective-permute-start.23 = (f32[64,128]{1,0:T(8,128)S(1)}, f32[64,128]{1,0:T(8,128)S(1)}, u32[]{:S(2)}, u32[]{:S(2)}) collective-permute-start(f32[64,128]{1,0:T(8,128)S(1)} %add.157), channel_id=1, source_target_pairs={{0,16},{4,20},{8,24},{12,28},{16,0},{20,4},{24,8},{28,12},{1,17},{... | collective-permute-start | bytes 98312 | tf_op jit(solution)/shard_map/ppermute | solution.py:25
  82.6 14.7 %collective-permute-start.24 = (bf16[128,1024]{1,0:T(8,128)(2,1)S(1)}, bf16[128,1024]{1,0:T(8,128)(2,1)S(1)}, u32[]{:S(2)}, u32[]{:S(2)}) collective-permute-start(bf16[128,1024]{1,0:T(8,128)(2,1)S(1)} %fusion.3), channel_id=1, source_target_pairs={{0,16},{4,20},{8,24},{12,28},{16,0},{20,4},{24,8},{28,12},{1,17},{... | collective-permute-start | bytes 786440 | tf_op jit(solution)/shard_map/ppermute | solution.py:25
  84.8 6.4 %collective-permute-start.19 = (bf16[128,1024]{1,0:T(8,128)(2,1)S(1)}, bf16[128,1024]{1,0:T(8,128)(2,1)S(1)}, u32[]{:S(2)}, u32[]{:S(2)}) collective-permute-start(bf16[128,1024]{1,0:T(8,128)(2,1)S(1)} %convolution_convert_fusion.3), channel_id=1, source_target_pairs={{0,2},{1,3},{2,0},{3,1},{4,6},{5,7},{6,4},{7,5},{8,10},{9,11},{10,... | collective-permute-start | bytes 786440 | tf_op jit(solution)/shard_map/ppermute | solution.py:25
  86.6 1.6 %collective-permute-start.25 = (f32[64,1088]{1,0:T(8,128)S(1)}, f32[64,1088]{1,0:T(8,128)S(1)}, u32[]{:S(2)}, u32[]{:S(2)}) collective-permute-start(f32[64,1088]{1,0:T(8,128)S(1)} %pad_maximum_fusion), channel_id=1, source_target_pairs={{0,1},{1,0},{2,3},{3,2},{4,5},{5,4},{6,7},{7,6},{8,9},{9,8},{10,11... | collective-permute-start | bytes 835592 | tf_op jit(solution)/shard_map/ppermute | solution.py:25
  87.1 9.9 %collective-permute-start.21 = (bf16[128,1024]{1,0:T(8,128)(2,1)S(1)}, bf16[128,1024]{1,0:T(8,128)(2,1)S(1)}, u32[]{:S(2)}, u32[]{:S(2)}) collective-permute-start(bf16[128,1024]{1,0:T(8,128)(2,1)S(1)} %fusion.5), channel_id=1, source_target_pairs={{0,8},{4,12},{8,0},{12,4},{16,24},{20,28},{24,16},{28,20},{1,9},{5... | collective-permute-start | bytes 786440 | tf_op jit(solution)/shard_map/ppermute | solution.py:25
  88.4 9.0 %collective-permute-start.26 = (bf16[64,1088]{1,0:T(8,128)(2,1)S(1)}, bf16[64,1088]{1,0:T(8,128)(2,1)S(1)}, u32[]{:S(2)}, u32[]{:S(2)}) collective-permute-start(bf16[64,1088]{1,0:T(8,128)(2,1)S(1)} %convert_element_type.101), channel_id=1, source_target_pairs={{0,2},{1,3},{2,0},{3,1},{4,6},{5,7},{6,4},{7,5},{8,10},{9,11},{10,... | collective-permute-start | bytes 417800 | tf_op jit(solution)/shard_map/ppermute | solution.py:25
  (1 other events, 1.6 us)

commit v15 on v14

--- a/solution.py
+++ b/solution.py
@@ -189,7 +189,7 @@
         return copy_blocks([(array.shape[0], depth)], moves, array)[0]
 
     after, _ = lax.optimization_barrier((hidden, sends[0]))
-    shards, cross = {0: hidden}, {0: swap_x(hidden)}
+    shards, cross = {0: hidden}, {0: swap_x(after)}
     for bit in reversed(bits):
         near = swap_z(hidden if bit == 1 else hidden, bit)
         for j in [j for j in shards if j]:
@@ -198,7 +198,7 @@
         shards[bit] = near
     for j in range(1, n_z):
         sent = shards[j]
-        waits = [] if j == 1 else [cross[j - 2]] if j < n_z - 1 else [cross[j - 2], beside[0]]
+        waits = [] if j == 1 else [cross[j - 2]] if j < n_z - 1 else [cross[j - 2]]
         if waits:
             sent, *_ = lax.optimization_barrier((sent, *waits))
         cross[j] = swap_x(sent)
@@ -208,11 +208,11 @@
 
     beside_core = []
     for n, came in enumerate(beside):
-        came, *_ = lax.optimization_barrier((came, cross[n_z - 2], shards[n_z - 1]))
+        came, *_ = lax.optimization_barrier((came, cross[1], cross[n_z - 2], shards[n_z - 1]))
         beside_core.append(swap_core(came))
 
     in_order = lambda parts: [parts[j] for j in range(n_z)]
-    basis_ready, *_ = lax.optimization_barrier((basis_half, cross[1]))
+    basis_ready, *_ = lax.optimization_barrier((basis_half, cross[n_z - 2], shards[n_z - 1]))
     upper = [[kept], [kept_core], [basis_ready]]
     upper_own = logits_of(upper, in_order(shards))
     beside_core[-1], *_ = lax.optimization_barrier((beside_core[-1], upper_own))

time: 98.4 us -> 98.3 us (level)
  no operation moved by 1% of the time
where the time goes in v15:
time: 98.3 us; the launch traced here: 98.2 us
  waiting for transfers between devices  56.6 us (58%)
  starting transfers between devices  28.4 us (29%)
  Pallas kernels  6.03 us (6%)
  matrix products  3.54 us (4%)
  local copies, waits for them, and re-layouts  1.7 us (2%)
  between operations  1.05 us (1%)
    ppermute x27, waiting for transfers between devices, swap(): return lax.ppermute(value, axis, [(i, i ^ bit) for i in range(size)])  56.6 us
    ppermute x27, starting transfers between devices, swap(): return lax.ppermute(value, axis, [(i, i ^ bit) for i in range(size)])  28.4 us
    pallas_call x4, Pallas kernels, logits_of(): pl.pallas_call(kernel, out_shape=jax.ShapeDtypeStruct((total + extra, tok...  3.49 us
    dot_general x10, matrix products, dot_first(): return lax.dot_general(a, b, contract_first, preferred_element_type=f32)  3.08 us
  transfers between devices with their start and end apart: 27, of which 16 were waited for; matrix products, arithmetic and copies ran while one was open for 3% of the time, Pallas kernels for 5%

profile of v15, /device:TPU:0, one launch (start us, length us, event | category | flops | bytes accessed | tf_op | source)
XLA Modules:
  0.0 98.2 jit_solution(4996839041199132063)
XLA Ops:
  0.7 1.6 %copy-done = bf16[128,8192]{1,0:T(8,128)(2,1)S(1)} copy-done((bf16[128,8192]{1,0:T(8,128)(2,1)S(1)}, bf16[128,8192]{1,0:T(8,128)(2,1)}, u32[]{:S(2)}) %copy-start) | copy-done | bytes 2097176
  2.6 3.0 %collective-permute-start.7 = (bf16[128,4096]{1,0:T(8,128)(2,1)S(1)}, bf16[128,4096]{1,0:T(8,128)(2,1)S(1)}, u32[]{:S(2)}, u32[]{:S(2)}) collective-permute-start(bf16[128,4096]{1,0:T(8,128)(2,1)S(1)} %shard_map.86), channel_id=1, source_target_pairs={{0,4},{4,0},{8,12},{12,8},{16,20},{20,16},{24,28},{28,24},{1,5},{5... | collective-permute-start | bytes 3145736 | tf_op jit(solution)/shard_map/ppermute | solution.py:25
  5.7 1.6 %collective-permute-start = (bf16[128,1024]{1,0:T(8,128)(2,1)}, bf16[128,1024]{1,0:T(8,128)(2,1)S(1)}, u32[]{:S(2)}, u32[]{:S(2)}) collective-permute-start(bf16[128,1024]{1,0:T(8,128)(2,1)} %refs_2_), channel_id=1, source_target_pairs={{0,8},{4,12},{8,0},{12,4},{16,24},{20,28},{24,16},{28,20},{1,9},{5... | collective-permute-start | bytes 786440 | tf_op jit(solution)/shard_map/ppermute | solution.py:25
  7.2 2.6 %collective-permute-start.4 = (bf16[128,1024]{1,0:T(8,128)(2,1)}, bf16[128,1024]{1,0:T(8,128)(2,1)S(1)}, u32[]{:S(2)}, u32[]{:S(2)}) collective-permute-start(bf16[128,1024]{1,0:T(8,128)(2,1)} %refs_2_), channel_id=1, source_target_pairs={{0,16},{4,20},{8,24},{12,28},{16,0},{20,4},{24,8},{28,12},{1,17},{... | collective-permute-start | bytes 786440 | tf_op jit(solution)/shard_map/ppermute | solution.py:25
  9.8 1.5 %collective-permute-start.3 = (bf16[128,1024]{1,0:T(8,128)(2,1)}, bf16[128,1024]{1,0:T(8,128)(2,1)S(1)}, u32[]{:S(2)}, u32[]{:S(2)}) collective-permute-start(bf16[128,1024]{1,0:T(8,128)(2,1)} %refs_2_), channel_id=1, source_target_pairs={{0,2},{1,3},{2,0},{3,1},{4,6},{5,7},{6,4},{7,5},{8,10},{9,11},{10,... | collective-permute-start | bytes 786440 | tf_op jit(solution)/shard_map/ppermute | solution.py:25
  11.3 7.8 %collective-permute-done.refs_4_.refs_3_ = bf16[128,1024]{1,0:T(8,128)(2,1)S(1)} collective-permute-done((bf16[128,1024]{1,0:T(8,128)(2,1)}, bf16[128,1024]{1,0:T(8,128)(2,1)S(1)}, u32[]{:S(2)}, u32[]{:S(2)}) %collective-permute-start) | collective-permute-done | bytes 262176 | tf_op jit(solution)/shard_map/ppermute | solution.py:25
  19.1 1.5 %collective-permute-start.1 = (bf16[128,1024]{1,0:T(8,128)(2,1)S(1)}, bf16[128,1024]{1,0:T(8,128)(2,1)S(1)}, u32[]{:S(2)}, u32[]{:S(2)}) collective-permute-start(bf16[128,1024]{1,0:T(8,128)(2,1)S(1)} %collective-permute-done.refs_4_.refs_3_), channel_id=1, source_target_pairs={{0,2},{1,3},{2,0},{3,1},{4,6},{5,7},{6,4},{7,5},{8,10},{9,11},{10,... | collective-permute-start | bytes 786440 | tf_op jit(solution)/shard_map/ppermute | solution.py:25
  20.6 0.9 collective-permute-done.4.refs_5_.refs_4_
  21.5 1.5 %collective-permute-start.5 = (bf16[128,1024]{1,0:T(8,128)(2,1)S(1)}, bf16[128,1024]{1,0:T(8,128)(2,1)S(1)}, u32[]{:S(2)}, u32[]{:S(2)}) collective-permute-start(bf16[128,1024]{1,0:T(8,128)(2,1)S(1)} %collective-permute-done.4.refs_5_.refs_4_), channel_id=1, source_target_pairs={{0,2},{1,3},{2,0},{3,1},{4,6},{5,7},{6,4},{7,5},{8,10},{9,11},{10,... | collective-permute-start | bytes 786440 | tf_op jit(solution)/shard_map/ppermute | solution.py:25
  23.5 4.9 %collective-permute-done.1.refs_6_ = bf16[128,1024]{1,0:T(8,128)(2,1)S(1)} collective-permute-done((bf16[128,1024]{1,0:T(8,128)(2,1)S(1)}, bf16[128,1024]{1,0:T(8,128)(2,1)S(1)}, u32[]{:S(2)}, u32[]{:S(2)}) %collective-permute-start.1) | collective-permute-done | bytes 262176 | tf_op jit(solution)/shard_map/ppermute | solution.py:25
  28.8 2.8 %collective-permute-done.5.refs_7_ = bf16[128,1024]{1,0:T(8,128)(2,1)S(1)} collective-permute-done((bf16[128,1024]{1,0:T(8,128)(2,1)S(1)}, bf16[128,1024]{1,0:T(8,128)(2,1)S(1)}, u32[]{:S(2)}, u32[]{:S(2)}) %collective-permute-start.5) | collective-permute-done | bytes 262176 | tf_op jit(solution)/shard_map/ppermute | solution.py:25
  31.7 1.6 %collective-permute-start.11 = (bf16[128,1024]{1,0:T(8,128)(2,1)S(1)}, bf16[128,1024]{1,0:T(8,128)(2,1)S(1)}, u32[]{:S(2)}, u32[]{:S(2)}) collective-permute-start(bf16[128,1024]{1,0:T(8,128)(2,1)S(1)} %collective-permute-done.6.refs_6_.refs_5_), channel_id=1, source_target_pairs={{0,2},{1,3},{2,0},{3,1},{4,6},{5,7},{6,4},{7,5},{8,10},{9,11},{10,... | collective-permute-start | bytes 786440 | tf_op jit(solution)/shard_map/ppermute | solution.py:25
  33.6 1.0 %shard_map.88 = f32[320,128]{1,0:T(8,128)S(1)} custom-call(bf16[128,4096]{1,0:T(8,128)(2,1)S(1)} %shard_map.85.refs_0_, bf16[128,4096]{1,0:T(8,128)(2,1)S(1)} %collective-permute-done.2.refs_1_, bf16[64,4096]{1,0:T(8,128)(2,1)S(1)} %shard_map.87.refs_2_, bf16[128,1024]{1,0:T(8,128)(2,1)S(1)} %copy-done.1, ...), custom_call_target="tpu_custom_call" | custom-call | flops 335544320 | bytes 3833856 | tf_op jit(solution)/shard_map/pallas_call | solution.py:106
  36.0 1.6 %collective-permute-start.9 = (f32[256,128]{1,0:T(8,128)S(1)}, f32[256,128]{1,0:T(8,128)S(1)}, u32[]{:S(2)}, u32[]{:S(2)}) collective-permute-start(f32[256,128]{1,0:T(8,128)S(1)} %shard_map.89), channel_id=1, source_target_pairs={{0,4},{4,0},{8,12},{12,8},{16,20},{20,16},{24,28},{28,24},{1,5},{5... | collective-permute-start | bytes 393224 | tf_op jit(solution)/shard_map/ppermute | solution.py:25
  37.5 1.2 %shard_map.90.refs_6_ = f32[576,128]{1,0:T(8,128)S(1)} custom-call(bf16[128,4096]{1,0:T(8,128)(2,1)S(1)} %shard_map.85.refs_0_, bf16[128,4096]{1,0:T(8,128)(2,1)S(1)} %collective-permute-done.2.refs_1_, bf16[64,4096]{1,0:T(8,128)(2,1)S(1)} %shard_map.87.refs_2_, bf16[128,4096]{1,0:T(8,128)(2,1)S(1)} %collective-permute-done.7.refs_0_.refs_3_.refs_2_, ...), custom_call_target="tpu_custom_call" | custom-call | flops 452984832 | bytes 4620288 | tf_op jit(solution)/shard_map/pallas_call | solution.py:106
  38.8 1.7 %collective-permute-done.11.refs_5_ = bf16[128,1024]{1,0:T(8,128)(2,1)S(1)} collective-permute-done((bf16[128,1024]{1,0:T(8,128)(2,1)S(1)}, bf16[128,1024]{1,0:T(8,128)(2,1)S(1)}, u32[]{:S(2)}, u32[]{:S(2)}) %collective-permute-start.11) | collective-permute-done | bytes 262176 | tf_op jit(solution)/shard_map/ppermute | solution.py:25
  42.4 1.8 %collective-permute-done.9 = f32[256,128]{1,0:T(8,128)S(1)} collective-permute-done((f32[256,128]{1,0:T(8,128)S(1)}, f32[256,128]{1,0:T(8,128)S(1)}, u32[]{:S(2)}, u32[]{:S(2)}) %collective-permute-start.9) | collective-permute-done | bytes 131104 | tf_op jit(solution)/shard_map/ppermute | solution.py:25
  44.4 6.1 %collective-permute-done.12 = f32[608,128]{1,0:T(8,128)S(1)} collective-permute-done((f32[608,128]{1,0:T(8,128)S(1)}, f32[608,128]{1,0:T(8,128)S(1)}, u32[]{:S(2)}, u32[]{:S(2)}) %collective-permute-start.12) | collective-permute-done | bytes 311328 | tf_op jit(solution)/shard_map/ppermute | solution.py:25
  50.8 1.1 %collective-permute-start.13 = (f32[4,256]{1,0:T(4,128)S(1)}, f32[4,256]{1,0:T(4,128)S(1)}, u32[]{:S(2)}, u32[]{:S(2)}) collective-permute-start(f32[4,256]{1,0:T(4,128)S(1)} %maximum_maximum_fusion), channel_id=1, source_target_pairs={{0,2},{1,3},{2,0},{3,1},{4,6},{5,7},{6,4},{7,5},{8,10},{9,11},{10,... | collective-permute-start | bytes 12296 | tf_op jit(solution)/shard_map/ppermute | solution.py:25
  52.1 2.4 %collective-permute-done.13 = f32[4,256]{1,0:T(4,128)S(1)} collective-permute-done((f32[4,256]{1,0:T(4,128)S(1)}, f32[4,256]{1,0:T(4,128)S(1)}, u32[]{:S(2)}, u32[]{:S(2)}) %collective-permute-start.13) | collective-permute-done | bytes 4128 | tf_op jit(solution)/shard_map/ppermute | solution.py:25
  54.6 3.5 %collective-permute-done.14 = f32[2,256]{1,0:T(2,128)S(1)} collective-permute-done((f32[2,256]{1,0:T(2,128)S(1)}, f32[2,256]{1,0:T(2,128)S(1)}, u32[]{:S(2)}, u32[]{:S(2)}) %collective-permute-start.14) | collective-permute-done | bytes 2080 | tf_op jit(solution)/shard_map/ppermute | solution.py:25
  58.1 1.4 %collective-permute-start.15 = (f32[2,256]{1,0:T(2,128)S(1)}, f32[2,256]{1,0:T(2,128)S(1)}, u32[]{:S(2)}, u32[]{:S(2)}) collective-permute-start(f32[2,256]{1,0:T(2,128)S(1)} %pad_maximum_fusion.7), channel_id=1, source_target_pairs={{0,16},{4,20},{8,24},{12,28},{16,0},{20,4},{24,8},{28,12},{1,17},{... | collective-permute-start | bytes 6152 | tf_op jit(solution)/shard_map/ppermute | solution.py:25
  59.5 3.2 %collective-permute-done.15 = f32[2,256]{1,0:T(2,128)S(1)} collective-permute-done((f32[2,256]{1,0:T(2,128)S(1)}, f32[2,256]{1,0:T(2,128)S(1)}, u32[]{:S(2)}, u32[]{:S(2)}) %collective-permute-start.15) | collective-permute-done | bytes 2080 | tf_op jit(solution)/shard_map/ppermute | solution.py:25
  63.6 1.1 %collective-permute-start.17 = (bf16[128,1024]{1,0:T(8,128)(2,1)S(1)}, bf16[128,1024]{1,0:T(8,128)(2,1)S(1)}, u32[]{:S(2)}, u32[]{:S(2)}) collective-permute-start(bf16[128,1024]{1,0:T(8,128)(2,1)S(1)} %convolution_convert_fusion.1), channel_id=1, source_target_pairs={{0,2},{1,3},{2,0},{3,1},{4,6},{5,7},{6,4},{7,5},{8,10},{9,11},{10,... | collective-permute-start | bytes 786440 | tf_op jit(solution)/shard_map/ppermute | solution.py:25
  65.0 1.1 %collective-permute-start.16 = (bf16[128,1024]{1,0:T(8,128)(2,1)S(1)}, bf16[128,1024]{1,0:T(8,128)(2,1)S(1)}, u32[]{:S(2)}, u32[]{:S(2)}) collective-permute-start(bf16[128,1024]{1,0:T(8,128)(2,1)S(1)} %convolution_convert_fusion.2), channel_id=1, source_target_pairs={{0,2},{1,3},{2,0},{3,1},{4,6},{5,7},{6,4},{7,5},{8,10},{9,11},{10,... | collective-permute-start | bytes 786440 | tf_op jit(solution)/shard_map/ppermute | solution.py:25
  66.4 5.0 %collective-permute-done.17 = bf16[128,1024]{1,0:T(8,128)(2,1)S(1)} collective-permute-done((bf16[128,1024]{1,0:T(8,128)(2,1)S(1)}, bf16[128,1024]{1,0:T(8,128)(2,1)S(1)}, u32[]{:S(2)}, u32[]{:S(2)}) %collective-permute-start.17) | collective-permute-done | bytes 262176 | tf_op jit(solution)/shard_map/ppermute | solution.py:25
  72.8 1.3 %collective-permute-start.22 = (f32[64,128]{1,0:T(8,128)S(1)}, f32[64,128]{1,0:T(8,128)S(1)}, u32[]{:S(2)}, u32[]{:S(2)}) collective-permute-start(f32[64,128]{1,0:T(8,128)S(1)} %fusion.24), channel_id=1, source_target_pairs={{0,8},{4,12},{8,0},{12,4},{16,24},{20,28},{24,16},{28,20},{1,9},{5... | collective-permute-start | bytes 98312 | tf_op jit(solution)/shard_map/ppermute | solution.py:25
  74.7 6.6 %collective-permute-done.22 = f32[64,128]{1,0:T(8,128)S(1)} collective-permute-done((f32[64,128]{1,0:T(8,128)S(1)}, f32[64,128]{1,0:T(8,128)S(1)}, u32[]{:S(2)}, u32[]{:S(2)}) %collective-permute-start.22) | collective-permute-done | bytes 32800 | tf_op jit(solution)/shard_map/ppermute | solution.py:25
  82.6 2.2 %collective-permute-start.24 = (bf16[128,1024]{1,0:T(8,128)(2,1)S(1)}, bf16[128,1024]{1,0:T(8,128)(2,1)S(1)}, u32[]{:S(2)}, u32[]{:S(2)}) collective-permute-start(bf16[128,1024]{1,0:T(8,128)(2,1)S(1)} %fusion.3), channel_id=1, source_target_pairs={{0,16},{4,20},{8,24},{12,28},{16,0},{20,4},{24,8},{28,12},{1,17},{... | collective-permute-start | bytes 786440 | tf_op jit(solution)/shard_map/ppermute | solution.py:25
  85.3 1.2 %collective-permute-done.23 = f32[64,128]{1,0:T(8,128)S(1)} collective-permute-done((f32[64,128]{1,0:T(8,128)S(1)}, f32[64,128]{1,0:T(8,128)S(1)}, u32[]{:S(2)}, u32[]{:S(2)}) %collective-permute-start.23) | collective-permute-done | bytes 32800 | tf_op jit(solution)/shard_map/ppermute | solution.py:25
  88.9 2.2 %collective-permute-done.19 = bf16[128,1024]{1,0:T(8,128)(2,1)S(1)} collective-permute-done((bf16[128,1024]{1,0:T(8,128)(2,1)S(1)}, bf16[128,1024]{1,0:T(8,128)(2,1)S(1)}, u32[]{:S(2)}, u32[]{:S(2)}) %collective-permute-start.19) | collective-permute-done | bytes 262176 | tf_op jit(solution)/shard_map/ppermute | solution.py:25
  91.1 5.8 %collective-permute-done.21 = bf16[128,1024]{1,0:T(8,128)(2,1)S(1)} collective-permute-done((bf16[128,1024]{1,0:T(8,128)(2,1)S(1)}, bf16[128,1024]{1,0:T(8,128)(2,1)S(1)}, u32[]{:S(2)}, u32[]{:S(2)}) %collective-permute-start.21) | collective-permute-done | bytes 262176 | tf_op jit(solution)/shard_map/ppermute | solution.py:25
  (95 shorter events, 14.5 us)
Async XLA Ops:
  0.6 31.0 %copy-start.4 = (s32[128]{0:T(128)S(1)}, s32[128]{0:T(128)}, u32[]{:S(2)}) copy-start(s32[128]{0:T(128)} %param.10) | copy-start | bytes 1540
  0.6 31.0 %copy-start.5 = (s32[128]{0:T(128)S(1)}, s32[128]{0:T(128)}, u32[]{:S(2)}) copy-start(s32[128]{0:T(128)} %param.11) | copy-start | bytes 1540
  2.3 31.0 %copy-start.2 = (bf16[64,8192]{1,0:T(8,128)(2,1)S(1)}, bf16[64,8192]{1,0:T(8,128)(2,1)}, u32[]{:S(2)}) copy-start(bf16[64,8192]{1,0:T(8,128)(2,1)} %refs_0_.2) | copy-start | bytes 3145732
  2.3 31.4 %copy-start.1 = (bf16[128,1024]{1,0:T(8,128)(2,1)S(1)}, bf16[128,1024]{1,0:T(8,128)(2,1)}, u32[]{:S(2)}) copy-start(bf16[128,1024]{1,0:T(8,128)(2,1)} %refs_2_) | copy-start | bytes 786436
  2.6 29.0 %collective-permute-start.7 = (bf16[128,4096]{1,0:T(8,128)(2,1)S(1)}, bf16[128,4096]{1,0:T(8,128)(2,1)S(1)}, u32[]{:S(2)}, u32[]{:S(2)}) collective-permute-start(bf16[128,4096]{1,0:T(8,128)(2,1)S(1)} %shard_map.86), channel_id=1, source_target_pairs={{0,4},{4,0},{8,12},{12,8},{16,20},{20,16},{24,28},{28,24},{1,5},{5... | collective-permute-start | bytes 3145736 | tf_op jit(solution)/shard_map/ppermute | solution.py:25
  5.7 13.5 %collective-permute-start = (bf16[128,1024]{1,0:T(8,128)(2,1)}, bf16[128,1024]{1,0:T(8,128)(2,1)S(1)}, u32[]{:S(2)}, u32[]{:S(2)}) collective-permute-start(bf16[128,1024]{1,0:T(8,128)(2,1)} %refs_2_), channel_id=1, source_target_pairs={{0,8},{4,12},{8,0},{12,4},{16,24},{20,28},{24,16},{28,20},{1,9},{5... | collective-permute-start | bytes 786440 | tf_op jit(solution)/shard_map/ppermute | solution.py:25
  7.2 14.3 %collective-permute-start.4 = (bf16[128,1024]{1,0:T(8,128)(2,1)}, bf16[128,1024]{1,0:T(8,128)(2,1)S(1)}, u32[]{:S(2)}, u32[]{:S(2)}) collective-permute-start(bf16[128,1024]{1,0:T(8,128)(2,1)} %refs_2_), channel_id=1, source_target_pairs={{0,16},{4,20},{8,24},{12,28},{16,0},{20,4},{24,8},{28,12},{1,17},{... | collective-permute-start | bytes 786440 | tf_op jit(solution)/shard_map/ppermute | solution.py:25
  9.8 11.7 %collective-permute-start.3 = (bf16[128,1024]{1,0:T(8,128)(2,1)}, bf16[128,1024]{1,0:T(8,128)(2,1)S(1)}, u32[]{:S(2)}, u32[]{:S(2)}) collective-permute-start(bf16[128,1024]{1,0:T(8,128)(2,1)} %refs_2_), channel_id=1, source_target_pairs={{0,2},{1,3},{2,0},{3,1},{4,6},{5,7},{6,4},{7,5},{8,10},{9,11},{10,... | collective-permute-start | bytes 786440 | tf_op jit(solution)/shard_map/ppermute | solution.py:25
  19.1 9.2 %collective-permute-start.1 = (bf16[128,1024]{1,0:T(8,128)(2,1)S(1)}, bf16[128,1024]{1,0:T(8,128)(2,1)S(1)}, u32[]{:S(2)}, u32[]{:S(2)}) collective-permute-start(bf16[128,1024]{1,0:T(8,128)(2,1)S(1)} %collective-permute-done.refs_4_.refs_3_), channel_id=1, source_target_pairs={{0,2},{1,3},{2,0},{3,1},{4,6},{5,7},{6,4},{7,5},{8,10},{9,11},{10,... | collective-permute-start | bytes 786440 | tf_op jit(solution)/shard_map/ppermute | solution.py:25
  21.5 10.1 %collective-permute-start.5 = (bf16[128,1024]{1,0:T(8,128)(2,1)S(1)}, bf16[128,1024]{1,0:T(8,128)(2,1)S(1)}, u32[]{:S(2)}, u32[]{:S(2)}) collective-permute-start(bf16[128,1024]{1,0:T(8,128)(2,1)S(1)} %collective-permute-done.4.refs_5_.refs_4_), channel_id=1, source_target_pairs={{0,2},{1,3},{2,0},{3,1},{4,6},{5,7},{6,4},{7,5},{8,10},{9,11},{10,... | collective-permute-start | bytes 786440 | tf_op jit(solution)/shard_map/ppermute | solution.py:25
  23.0 8.6 %collective-permute-start.6 = (bf16[128,1024]{1,0:T(8,128)(2,1)S(1)}, bf16[128,1024]{1,0:T(8,128)(2,1)S(1)}, u32[]{:S(2)}, u32[]{:S(2)}) collective-permute-start(bf16[128,1024]{1,0:T(8,128)(2,1)S(1)} %collective-permute-done.4.refs_5_.refs_4_), channel_id=1, source_target_pairs={{0,8},{4,12},{8,0},{12,4},{16,24},{20,28},{24,16},{28,20},{1,9},{5... | collective-permute-start | bytes 786440 | tf_op jit(solution)/shard_map/ppermute | solution.py:25
  28.7 4.9 %collective-permute-start.2 = (bf16[128,4096]{1,0:T(8,128)(2,1)S(1)}, bf16[128,4096]{1,0:T(8,128)(2,1)S(1)}, u32[]{:S(2)}, u32[]{:S(2)}) collective-permute-start(bf16[128,4096]{1,0:T(8,128)(2,1)S(1)} %shard_map.85.refs_0_), channel_id=1, source_target_pairs={{0,1},{1,0},{2,3},{3,2},{4,5},{5,4},{6,7},{7,6},{8,9},{9,8},{10,11... | collective-permute-start | bytes 3145736 | tf_op jit(solution)/shard_map/ppermute | solution.py:25
  31.6 3.6 %collective-permute-start.8 = (bf16[128,4096]{1,0:T(8,128)(2,1)S(1)}, bf16[128,4096]{1,0:T(8,128)(2,1)S(1)}, u32[]{:S(2)}, u32[]{:S(2)}) collective-permute-start(bf16[128,4096]{1,0:T(8,128)(2,1)S(1)} %collective-permute-done.7.refs_0_.refs_3_.refs_2_), channel_id=1, source_target_pairs={{0,1},{1,0},{2,3},{3,2},{4,5},{5,4},{6,7},{7,6},{8,9},{9,8},{10,11... | collective-permute-start | bytes 3145736 | tf_op jit(solution)/shard_map/ppermute | solution.py:25
  31.7 8.8 %collective-permute-start.11 = (bf16[128,1024]{1,0:T(8,128)(2,1)S(1)}, bf16[128,1024]{1,0:T(8,128)(2,1)S(1)}, u32[]{:S(2)}, u32[]{:S(2)}) collective-permute-start(bf16[128,1024]{1,0:T(8,128)(2,1)S(1)} %collective-permute-done.6.refs_6_.refs_5_), channel_id=1, source_target_pairs={{0,2},{1,3},{2,0},{3,1},{4,6},{5,7},{6,4},{7,5},{8,10},{9,11},{10,... | collective-permute-start | bytes 786440 | tf_op jit(solution)/shard_map/ppermute | solution.py:25
  34.7 7.1 %collective-permute-start.10 = (f32[320,128]{1,0:T(8,128)S(1)}, f32[320,128]{1,0:T(8,128)S(1)}, u32[]{:S(2)}, u32[]{:S(2)}) collective-permute-start(f32[320,128]{1,0:T(8,128)S(1)} %shard_map.88), channel_id=1, source_target_pairs={{0,4},{4,0},{8,12},{12,8},{16,20},{20,16},{24,28},{28,24},{1,5},{5... | collective-permute-start | bytes 491528 | tf_op jit(solution)/shard_map/ppermute | solution.py:25
  35.2 5.2 %copy-start.3 = (bf16[64,64]{1,0:T(8,128)(2,1)S(1)}, bf16[64,64]{1,0:T(8,128)(2,1)}, u32[]{:S(2)}) copy-start(bf16[64,64]{1,0:T(8,128)(2,1)} %refs_7_.1) | copy-start | bytes 24580
  36.0 8.3 %collective-permute-start.9 = (f32[256,128]{1,0:T(8,128)S(1)}, f32[256,128]{1,0:T(8,128)S(1)}, u32[]{:S(2)}, u32[]{:S(2)}) collective-permute-start(f32[256,128]{1,0:T(8,128)S(1)} %shard_map.89), channel_id=1, source_target_pairs={{0,4},{4,0},{8,12},{12,8},{16,20},{20,16},{24,28},{28,24},{1,5},{5... | collective-permute-start | bytes 393224 | tf_op jit(solution)/shard_map/ppermute | solution.py:25
  41.0 9.5 %collective-permute-start.12 = (f32[608,128]{1,0:T(8,128)S(1)}, f32[608,128]{1,0:T(8,128)S(1)}, u32[]{:S(2)}, u32[]{:S(2)}) collective-permute-start(f32[608,128]{1,0:T(8,128)S(1)} %shard_map.91), channel_id=1, source_target_pairs={{0,4},{4,0},{8,12},{12,8},{16,20},{20,16},{24,28},{28,24},{1,5},{5... | collective-permute-start | bytes 933896 | tf_op jit(solution)/shard_map/ppermute | solution.py:25
  50.8 3.7 %collective-permute-start.13 = (f32[4,256]{1,0:T(4,128)S(1)}, f32[4,256]{1,0:T(4,128)S(1)}, u32[]{:S(2)}, u32[]{:S(2)}) collective-permute-start(f32[4,256]{1,0:T(4,128)S(1)} %maximum_maximum_fusion), channel_id=1, source_target_pairs={{0,2},{1,3},{2,0},{3,1},{4,6},{5,7},{6,4},{7,5},{8,10},{9,11},{10,... | collective-permute-start | bytes 12296 | tf_op jit(solution)/shard_map/ppermute | solution.py:25
  54.5 3.7 %collective-permute-start.14 = (f32[2,256]{1,0:T(2,128)S(1)}, f32[2,256]{1,0:T(2,128)S(1)}, u32[]{:S(2)}, u32[]{:S(2)}) collective-permute-start(f32[2,256]{1,0:T(2,128)S(1)} %pad_maximum_fusion.6), channel_id=1, source_target_pairs={{0,8},{4,12},{8,0},{12,4},{16,24},{20,28},{24,16},{28,20},{1,9},{5... | collective-permute-start | bytes 6152 | tf_op jit(solution)/shard_map/ppermute | solution.py:25
  58.1 4.5 %collective-permute-start.15 = (f32[2,256]{1,0:T(2,128)S(1)}, f32[2,256]{1,0:T(2,128)S(1)}, u32[]{:S(2)}, u32[]{:S(2)}) collective-permute-start(f32[2,256]{1,0:T(2,128)S(1)} %pad_maximum_fusion.7), channel_id=1, source_target_pairs={{0,16},{4,20},{8,24},{12,28},{16,0},{20,4},{24,8},{28,12},{1,17},{... | collective-permute-start | bytes 6152 | tf_op jit(solution)/shard_map/ppermute | solution.py:25
  63.6 7.8 %collective-permute-start.17 = (bf16[128,1024]{1,0:T(8,128)(2,1)S(1)}, bf16[128,1024]{1,0:T(8,128)(2,1)S(1)}, u32[]{:S(2)}, u32[]{:S(2)}) collective-permute-start(bf16[128,1024]{1,0:T(8,128)(2,1)S(1)} %convolution_convert_fusion.1), channel_id=1, source_target_pairs={{0,2},{1,3},{2,0},{3,1},{4,6},{5,7},{6,4},{7,5},{8,10},{9,11},{10,... | collective-permute-start | bytes 786440 | tf_op jit(solution)/shard_map/ppermute | solution.py:25
  65.0 17.2 %collective-permute-start.16 = (bf16[128,1024]{1,0:T(8,128)(2,1)S(1)}, bf16[128,1024]{1,0:T(8,128)(2,1)S(1)}, u32[]{:S(2)}, u32[]{:S(2)}) collective-permute-start(bf16[128,1024]{1,0:T(8,128)(2,1)S(1)} %convolution_convert_fusion.2), channel_id=1, source_target_pairs={{0,2},{1,3},{2,0},{3,1},{4,6},{5,7},{6,4},{7,5},{8,10},{9,11},{10,... | collective-permute-start | bytes 786440 | tf_op jit(solution)/shard_map/ppermute | solution.py:25
  71.7 9.6 %collective-permute-start.18 = (bf16[128,1024]{1,0:T(8,128)(2,1)S(1)}, bf16[128,1024]{1,0:T(8,128)(2,1)S(1)}, u32[]{:S(2)}, u32[]{:S(2)}) collective-permute-start(bf16[128,1024]{1,0:T(8,128)(2,1)S(1)} %fusion.4), channel_id=1, source_target_pairs={{0,8},{4,12},{8,0},{12,4},{16,24},{20,28},{24,16},{28,20},{1,9},{5... | collective-permute-start | bytes 786440 | tf_op jit(solution)/shard_map/ppermute | solution.py:25
  72.8 8.6 %collective-permute-start.22 = (f32[64,128]{1,0:T(8,128)S(1)}, f32[64,128]{1,0:T(8,128)S(1)}, u32[]{:S(2)}, u32[]{:S(2)}) collective-permute-start(f32[64,128]{1,0:T(8,128)S(1)} %fusion.24), channel_id=1, source_target_pairs={{0,8},{4,12},{8,0},{12,4},{16,24},{20,28},{24,16},{28,20},{1,9},{5... | collective-permute-start | bytes 98312 | tf_op jit(solution)/shard_map/ppermute | solution.py:25
  74.2 12.5 %collective-permute-start.20 = (bf16[128,1024]{1,0:T(8,128)(2,1)S(1)}, bf16[128,1024]{1,0:T(8,128)(2,1)S(1)}, u32[]{:S(2)}, u32[]{:S(2)}) collective-permute-start(bf16[128,1024]{1,0:T(8,128)(2,1)S(1)} %convolution_convert_fusion), channel_id=1, source_target_pairs={{0,2},{1,3},{2,0},{3,1},{4,6},{5,7},{6,4},{7,5},{8,10},{9,11},{10,... | collective-permute-start | bytes 786440 | tf_op jit(solution)/shard_map/ppermute | solution.py:25
  81.3 5.1 %collective-permute-start.23 = (f32[64,128]{1,0:T(8,128)S(1)}, f32[64,128]{1,0:T(8,128)S(1)}, u32[]{:S(2)}, u32[]{:S(2)}) collective-permute-start(f32[64,128]{1,0:T(8,128)S(1)} %add.157), channel_id=1, source_target_pairs={{0,16},{4,20},{8,24},{12,28},{16,0},{20,4},{24,8},{28,12},{1,17},{... | collective-permute-start | bytes 98312 | tf_op jit(solution)/shard_map/ppermute | solution.py:25
  82.6 14.7 %collective-permute-start.24 = (bf16[128,1024]{1,0:T(8,128)(2,1)S(1)}, bf16[128,1024]{1,0:T(8,128)(2,1)S(1)}, u32[]{:S(2)}, u32[]{:S(2)}) collective-permute-start(bf16[128,1024]{1,0:T(8,128)(2,1)S(1)} %fusion.3), channel_id=1, source_target_pairs={{0,16},{4,20},{8,24},{12,28},{16,0},{20,4},{24,8},{28,12},{1,17},{... | collective-permute-start | bytes 786440 | tf_op jit(solution)/shard_map/ppermute | solution.py:25
  84.8 6.4 %collective-permute-start.19 = (bf16[128,1024]{1,0:T(8,128)(2,1)S(1)}, bf16[128,1024]{1,0:T(8,128)(2,1)S(1)}, u32[]{:S(2)}, u32[]{:S(2)}) collective-permute-start(bf16[128,1024]{1,0:T(8,128)(2,1)S(1)} %convolution_convert_fusion.3), channel_id=1, source_target_pairs={{0,2},{1,3},{2,0},{3,1},{4,6},{5,7},{6,4},{7,5},{8,10},{9,11},{10,... | collective-permute-start | bytes 786440 | tf_op jit(solution)/shard_map/ppermute | solution.py:25
  86.7 1.6 %collective-permute-start.25 = (f32[64,1088]{1,0:T(8,128)S(1)}, f32[64,1088]{1,0:T(8,128)S(1)}, u32[]{:S(2)}, u32[]{:S(2)}) collective-permute-start(f32[64,1088]{1,0:T(8,128)S(1)} %pad_maximum_fusion), channel_id=1, source_target_pairs={{0,1},{1,0},{2,3},{3,2},{4,5},{5,4},{6,7},{7,6},{8,9},{9,8},{10,11... | collective-permute-start | bytes 835592 | tf_op jit(solution)/shard_map/ppermute | solution.py:25
  87.1 9.9 %collective-permute-start.21 = (bf16[128,1024]{1,0:T(8,128)(2,1)S(1)}, bf16[128,1024]{1,0:T(8,128)(2,1)S(1)}, u32[]{:S(2)}, u32[]{:S(2)}) collective-permute-start(bf16[128,1024]{1,0:T(8,128)(2,1)S(1)} %fusion.5), channel_id=1, source_target_pairs={{0,8},{4,12},{8,0},{12,4},{16,24},{20,28},{24,16},{28,20},{1,9},{5... | collective-permute-start | bytes 786440 | tf_op jit(solution)/shard_map/ppermute | solution.py:25
  88.4 8.9 %collective-permute-start.26 = (bf16[64,1088]{1,0:T(8,128)(2,1)S(1)}, bf16[64,1088]{1,0:T(8,128)(2,1)S(1)}, u32[]{:S(2)}, u32[]{:S(2)}) collective-permute-start(bf16[64,1088]{1,0:T(8,128)(2,1)S(1)} %convert_element_type.101), channel_id=1, source_target_pairs={{0,2},{1,3},{2,0},{3,1},{4,6},{5,7},{6,4},{7,5},{8,10},{9,11},{10,... | collective-permute-start | bytes 417800 | tf_op jit(solution)/shard_map/ppermute | solution.py:25
  (1 other events, 1.6 us)

commit v16 on v14

--- a/solution.py
+++ b/solution.py
@@ -302,8 +302,6 @@
         if j + 2 in from_x:
             waits = (from_x[j + 2], first_came) if j == 0 else (first_z, first_z)
             send, *_ = lax.optimization_barrier((send, *waits))
-        if j == n_z - 2:
-            send, _ = lax.optimization_barrier((send, first_send))
         first_send = send if j == n_z - 1 else first_send
         from_x[j] = swap_x(send)
         sums[j] = part(grad_own, j) + from_x[j].astype(f32)

time: 98.4 us -> 98.3 us (level)
  no operation moved by 1% of the time
where the time goes in v16:
time: 98.3 us; the launch traced here: 98.2 us
  waiting for transfers between devices  56.6 us (58%)
  starting transfers between devices  28.4 us (29%)
  Pallas kernels  6.01 us (6%)
  matrix products  3.53 us (4%)
  local copies, waits for them, and re-layouts  1.7 us (2%)
  between operations  1.06 us (1%)
    ppermute x27, waiting for transfers between devices, swap(): return lax.ppermute(value, axis, [(i, i ^ bit) for i in range(size)])  56.6 us
    ppermute x27, starting transfers between devices, swap(): return lax.ppermute(value, axis, [(i, i ^ bit) for i in range(size)])  28.4 us
    pallas_call x4, Pallas kernels, logits_of(): pl.pallas_call(kernel, out_shape=jax.ShapeDtypeStruct((total + extra, tok...  3.47 us
    dot_general x10, matrix products, dot_first(): return lax.dot_general(a, b, contract_first, preferred_element_type=f32)  3.07 us
  transfers between devices with their start and end apart: 27, of which 16 were waited for; matrix products, arithmetic and copies ran while one was open for 3% of the time, Pallas kernels for 5%

profile of v16, /device:TPU:0, one launch (start us, length us, event | category | flops | bytes accessed | tf_op | source)
XLA Modules:
  0.0 98.2 jit_solution(8510199854697840505)
XLA Ops:
  0.7 1.6 %copy-done = bf16[128,8192]{1,0:T(8,128)(2,1)S(1)} copy-done((bf16[128,8192]{1,0:T(8,128)(2,1)S(1)}, bf16[128,8192]{1,0:T(8,128)(2,1)}, u32[]{:S(2)}) %copy-start) | copy-done | bytes 2097176
  2.6 3.0 %collective-permute-start.6 = (bf16[128,4096]{1,0:T(8,128)(2,1)S(1)}, bf16[128,4096]{1,0:T(8,128)(2,1)S(1)}, u32[]{:S(2)}, u32[]{:S(2)}) collective-permute-start(bf16[128,4096]{1,0:T(8,128)(2,1)S(1)} %shard_map.88), channel_id=1, source_target_pairs={{0,4},{4,0},{8,12},{12,8},{16,20},{20,16},{24,28},{28,24},{1,5},{5... | collective-permute-start | bytes 3145736 | tf_op jit(solution)/shard_map/ppermute | solution.py:25
  5.7 1.6 %collective-permute-start = (bf16[128,1024]{1,0:T(8,128)(2,1)}, bf16[128,1024]{1,0:T(8,128)(2,1)S(1)}, u32[]{:S(2)}, u32[]{:S(2)}) collective-permute-start(bf16[128,1024]{1,0:T(8,128)(2,1)} %refs_2_), channel_id=1, source_target_pairs={{0,8},{4,12},{8,0},{12,4},{16,24},{20,28},{24,16},{28,20},{1,9},{5... | collective-permute-start | bytes 786440 | tf_op jit(solution)/shard_map/ppermute | solution.py:25
  7.2 2.6 %collective-permute-start.4 = (bf16[128,1024]{1,0:T(8,128)(2,1)}, bf16[128,1024]{1,0:T(8,128)(2,1)S(1)}, u32[]{:S(2)}, u32[]{:S(2)}) collective-permute-start(bf16[128,1024]{1,0:T(8,128)(2,1)} %refs_2_), channel_id=1, source_target_pairs={{0,16},{4,20},{8,24},{12,28},{16,0},{20,4},{24,8},{28,12},{1,17},{... | collective-permute-start | bytes 786440 | tf_op jit(solution)/shard_map/ppermute | solution.py:25
  9.8 1.5 %collective-permute-start.3 = (bf16[128,1024]{1,0:T(8,128)(2,1)}, bf16[128,1024]{1,0:T(8,128)(2,1)S(1)}, u32[]{:S(2)}, u32[]{:S(2)}) collective-permute-start(bf16[128,1024]{1,0:T(8,128)(2,1)} %refs_2_), channel_id=1, source_target_pairs={{0,2},{1,3},{2,0},{3,1},{4,6},{5,7},{6,4},{7,5},{8,10},{9,11},{10,... | collective-permute-start | bytes 786440 | tf_op jit(solution)/shard_map/ppermute | solution.py:25
  11.3 7.8 %collective-permute-done.refs_4_.refs_3_ = bf16[128,1024]{1,0:T(8,128)(2,1)S(1)} collective-permute-done((bf16[128,1024]{1,0:T(8,128)(2,1)}, bf16[128,1024]{1,0:T(8,128)(2,1)S(1)}, u32[]{:S(2)}, u32[]{:S(2)}) %collective-permute-start) | collective-permute-done | bytes 262176 | tf_op jit(solution)/shard_map/ppermute | solution.py:25
  19.1 1.5 %collective-permute-start.1 = (bf16[128,1024]{1,0:T(8,128)(2,1)S(1)}, bf16[128,1024]{1,0:T(8,128)(2,1)S(1)}, u32[]{:S(2)}, u32[]{:S(2)}) collective-permute-start(bf16[128,1024]{1,0:T(8,128)(2,1)S(1)} %collective-permute-done.refs_4_.refs_3_), channel_id=1, source_target_pairs={{0,2},{1,3},{2,0},{3,1},{4,6},{5,7},{6,4},{7,5},{8,10},{9,11},{10,... | collective-permute-start | bytes 786440 | tf_op jit(solution)/shard_map/ppermute | solution.py:25
  20.6 0.9 collective-permute-done.4.refs_5_.refs_4_
  22.0 1.5 %collective-permute-start.7 = (bf16[128,1024]{1,0:T(8,128)(2,1)S(1)}, bf16[128,1024]{1,0:T(8,128)(2,1)S(1)}, u32[]{:S(2)}, u32[]{:S(2)}) collective-permute-start(bf16[128,1024]{1,0:T(8,128)(2,1)S(1)} %collective-permute-done.4.refs_5_.refs_4_), channel_id=1, source_target_pairs={{0,2},{1,3},{2,0},{3,1},{4,6},{5,7},{6,4},{7,5},{8,10},{9,11},{10,... | collective-permute-start | bytes 786440 | tf_op jit(solution)/shard_map/ppermute | solution.py:25
  23.5 4.9 %collective-permute-done.1.refs_6_ = bf16[128,1024]{1,0:T(8,128)(2,1)S(1)} collective-permute-done((bf16[128,1024]{1,0:T(8,128)(2,1)S(1)}, bf16[128,1024]{1,0:T(8,128)(2,1)S(1)}, u32[]{:S(2)}, u32[]{:S(2)}) %collective-permute-start.1) | collective-permute-done | bytes 262176 | tf_op jit(solution)/shard_map/ppermute | solution.py:25
  28.8 2.8 %collective-permute-done.7.refs_7_ = bf16[128,1024]{1,0:T(8,128)(2,1)S(1)} collective-permute-done((bf16[128,1024]{1,0:T(8,128)(2,1)S(1)}, bf16[128,1024]{1,0:T(8,128)(2,1)S(1)}, u32[]{:S(2)}, u32[]{:S(2)}) %collective-permute-start.7) | collective-permute-done | bytes 262176 | tf_op jit(solution)/shard_map/ppermute | solution.py:25
  31.6 1.6 %collective-permute-start.11 = (bf16[128,1024]{1,0:T(8,128)(2,1)S(1)}, bf16[128,1024]{1,0:T(8,128)(2,1)S(1)}, u32[]{:S(2)}, u32[]{:S(2)}) collective-permute-start(bf16[128,1024]{1,0:T(8,128)(2,1)S(1)} %collective-permute-done.5.refs_6_.refs_5_), channel_id=1, source_target_pairs={{0,2},{1,3},{2,0},{3,1},{4,6},{5,7},{6,4},{7,5},{8,10},{9,11},{10,... | collective-permute-start | bytes 786440 | tf_op jit(solution)/shard_map/ppermute | solution.py:25
  33.6 1.0 %shard_map.87 = f32[320,128]{1,0:T(8,128)S(1)} custom-call(bf16[128,4096]{1,0:T(8,128)(2,1)S(1)} %shard_map.85.refs_0_, bf16[128,4096]{1,0:T(8,128)(2,1)S(1)} %collective-permute-done.2.refs_1_, bf16[64,4096]{1,0:T(8,128)(2,1)S(1)} %shard_map.86.refs_2_, bf16[128,1024]{1,0:T(8,128)(2,1)S(1)} %copy-done.1, ...), custom_call_target="tpu_custom_call" | custom-call | flops 335544320 | bytes 3833856 | tf_op jit(solution)/shard_map/pallas_call | solution.py:106
  35.9 1.6 %collective-permute-start.9 = (f32[256,128]{1,0:T(8,128)S(1)}, f32[256,128]{1,0:T(8,128)S(1)}, u32[]{:S(2)}, u32[]{:S(2)}) collective-permute-start(f32[256,128]{1,0:T(8,128)S(1)} %shard_map.89), channel_id=1, source_target_pairs={{0,4},{4,0},{8,12},{12,8},{16,20},{20,16},{24,28},{28,24},{1,5},{5... | collective-permute-start | bytes 393224 | tf_op jit(solution)/shard_map/ppermute | solution.py:25
  37.5 1.2 %shard_map.90.refs_6_ = f32[576,128]{1,0:T(8,128)S(1)} custom-call(bf16[128,4096]{1,0:T(8,128)(2,1)S(1)} %shard_map.85.refs_0_, bf16[128,4096]{1,0:T(8,128)(2,1)S(1)} %collective-permute-done.2.refs_1_, bf16[64,4096]{1,0:T(8,128)(2,1)S(1)} %shard_map.86.refs_2_, bf16[128,4096]{1,0:T(8,128)(2,1)S(1)} %collective-permute-done.6.refs_0_.refs_3_.refs_2_, ...), custom_call_target="tpu_custom_call" | custom-call | flops 452984832 | bytes 4620288 | tf_op jit(solution)/shard_map/pallas_call | solution.py:106
  38.7 1.7 %collective-permute-done.11.refs_5_ = bf16[128,1024]{1,0:T(8,128)(2,1)S(1)} collective-permute-done((bf16[128,1024]{1,0:T(8,128)(2,1)S(1)}, bf16[128,1024]{1,0:T(8,128)(2,1)S(1)}, u32[]{:S(2)}, u32[]{:S(2)}) %collective-permute-start.11) | collective-permute-done | bytes 262176 | tf_op jit(solution)/shard_map/ppermute | solution.py:25
  42.4 1.9 %collective-permute-done.9 = f32[256,128]{1,0:T(8,128)S(1)} collective-permute-done((f32[256,128]{1,0:T(8,128)S(1)}, f32[256,128]{1,0:T(8,128)S(1)}, u32[]{:S(2)}, u32[]{:S(2)}) %collective-permute-start.9) | collective-permute-done | bytes 131104 | tf_op jit(solution)/shard_map/ppermute | solution.py:25
  44.4 6.1 %collective-permute-done.12 = f32[608,128]{1,0:T(8,128)S(1)} collective-permute-done((f32[608,128]{1,0:T(8,128)S(1)}, f32[608,128]{1,0:T(8,128)S(1)}, u32[]{:S(2)}, u32[]{:S(2)}) %collective-permute-start.12) | collective-permute-done | bytes 311328 | tf_op jit(solution)/shard_map/ppermute | solution.py:25
  50.8 1.1 %collective-permute-start.13 = (f32[4,256]{1,0:T(4,128)S(1)}, f32[4,256]{1,0:T(4,128)S(1)}, u32[]{:S(2)}, u32[]{:S(2)}) collective-permute-start(f32[4,256]{1,0:T(4,128)S(1)} %maximum_maximum_fusion), channel_id=1, source_target_pairs={{0,2},{1,3},{2,0},{3,1},{4,6},{5,7},{6,4},{7,5},{8,10},{9,11},{10,... | collective-permute-start | bytes 12296 | tf_op jit(solution)/shard_map/ppermute | solution.py:25
  52.1 2.4 %collective-permute-done.13 = f32[4,256]{1,0:T(4,128)S(1)} collective-permute-done((f32[4,256]{1,0:T(4,128)S(1)}, f32[4,256]{1,0:T(4,128)S(1)}, u32[]{:S(2)}, u32[]{:S(2)}) %collective-permute-start.13) | collective-permute-done | bytes 4128 | tf_op jit(solution)/shard_map/ppermute | solution.py:25
  54.6 3.5 %collective-permute-done.14 = f32[2,256]{1,0:T(2,128)S(1)} collective-permute-done((f32[2,256]{1,0:T(2,128)S(1)}, f32[2,256]{1,0:T(2,128)S(1)}, u32[]{:S(2)}, u32[]{:S(2)}) %collective-permute-start.14) | collective-permute-done | bytes 2080 | tf_op jit(solution)/shard_map/ppermute | solution.py:25
  58.2 1.4 %collective-permute-start.15 = (f32[2,256]{1,0:T(2,128)S(1)}, f32[2,256]{1,0:T(2,128)S(1)}, u32[]{:S(2)}, u32[]{:S(2)}) collective-permute-start(f32[2,256]{1,0:T(2,128)S(1)} %pad_maximum_fusion.7), channel_id=1, source_target_pairs={{0,16},{4,20},{8,24},{12,28},{16,0},{20,4},{24,8},{28,12},{1,17},{... | collective-permute-start | bytes 6152 | tf_op jit(solution)/shard_map/ppermute | solution.py:25
  59.5 3.2 %collective-permute-done.15 = f32[2,256]{1,0:T(2,128)S(1)} collective-permute-done((f32[2,256]{1,0:T(2,128)S(1)}, f32[2,256]{1,0:T(2,128)S(1)}, u32[]{:S(2)}, u32[]{:S(2)}) %collective-permute-start.15) | collective-permute-done | bytes 2080 | tf_op jit(solution)/shard_map/ppermute | solution.py:25
  63.6 1.1 %collective-permute-start.17 = (bf16[128,1024]{1,0:T(8,128)(2,1)S(1)}, bf16[128,1024]{1,0:T(8,128)(2,1)S(1)}, u32[]{:S(2)}, u32[]{:S(2)}) collective-permute-start(bf16[128,1024]{1,0:T(8,128)(2,1)S(1)} %convolution_convert_fusion.1), channel_id=1, source_target_pairs={{0,2},{1,3},{2,0},{3,1},{4,6},{5,7},{6,4},{7,5},{8,10},{9,11},{10,... | collective-permute-start | bytes 786440 | tf_op jit(solution)/shard_map/ppermute | solution.py:25
  65.0 1.1 %collective-permute-start.16 = (bf16[128,1024]{1,0:T(8,128)(2,1)S(1)}, bf16[128,1024]{1,0:T(8,128)(2,1)S(1)}, u32[]{:S(2)}, u32[]{:S(2)}) collective-permute-start(bf16[128,1024]{1,0:T(8,128)(2,1)S(1)} %convolution_convert_fusion.2), channel_id=1, source_target_pairs={{0,2},{1,3},{2,0},{3,1},{4,6},{5,7},{6,4},{7,5},{8,10},{9,11},{10,... | collective-permute-start | bytes 786440 | tf_op jit(solution)/shard_map/ppermute | solution.py:25
  66.4 5.0 %collective-permute-done.17 = bf16[128,1024]{1,0:T(8,128)(2,1)S(1)} collective-permute-done((bf16[128,1024]{1,0:T(8,128)(2,1)S(1)}, bf16[128,1024]{1,0:T(8,128)(2,1)S(1)}, u32[]{:S(2)}, u32[]{:S(2)}) %collective-permute-start.17) | collective-permute-done | bytes 262176 | tf_op jit(solution)/shard_map/ppermute | solution.py:25
  72.8 1.3 %collective-permute-start.22 = (f32[64,128]{1,0:T(8,128)S(1)}, f32[64,128]{1,0:T(8,128)S(1)}, u32[]{:S(2)}, u32[]{:S(2)}) collective-permute-start(f32[64,128]{1,0:T(8,128)S(1)} %fusion.24), channel_id=1, source_target_pairs={{0,8},{4,12},{8,0},{12,4},{16,24},{20,28},{24,16},{28,20},{1,9},{5... | collective-permute-start | bytes 98312 | tf_op jit(solution)/shard_map/ppermute | solution.py:25
  74.8 6.6 %collective-permute-done.22 = f32[64,128]{1,0:T(8,128)S(1)} collective-permute-done((f32[64,128]{1,0:T(8,128)S(1)}, f32[64,128]{1,0:T(8,128)S(1)}, u32[]{:S(2)}, u32[]{:S(2)}) %collective-permute-start.22) | collective-permute-done | bytes 32800 | tf_op jit(solution)/shard_map/ppermute | solution.py:25
  82.6 2.2 %collective-permute-start.24 = (bf16[128,1024]{1,0:T(8,128)(2,1)S(1)}, bf16[128,1024]{1,0:T(8,128)(2,1)S(1)}, u32[]{:S(2)}, u32[]{:S(2)}) collective-permute-start(bf16[128,1024]{1,0:T(8,128)(2,1)S(1)} %fusion.3), channel_id=1, source_target_pairs={{0,16},{4,20},{8,24},{12,28},{16,0},{20,4},{24,8},{28,12},{1,17},{... | collective-permute-start | bytes 786440 | tf_op jit(solution)/shard_map/ppermute | solution.py:25
  85.3 1.1 %collective-permute-done.23 = f32[64,128]{1,0:T(8,128)S(1)} collective-permute-done((f32[64,128]{1,0:T(8,128)S(1)}, f32[64,128]{1,0:T(8,128)S(1)}, u32[]{:S(2)}, u32[]{:S(2)}) %collective-permute-start.23) | collective-permute-done | bytes 32800 | tf_op jit(solution)/shard_map/ppermute | solution.py:25
  88.9 2.3 %collective-permute-done.19 = bf16[128,1024]{1,0:T(8,128)(2,1)S(1)} collective-permute-done((bf16[128,1024]{1,0:T(8,128)(2,1)S(1)}, bf16[128,1024]{1,0:T(8,128)(2,1)S(1)}, u32[]{:S(2)}, u32[]{:S(2)}) %collective-permute-start.19) | collective-permute-done | bytes 262176 | tf_op jit(solution)/shard_map/ppermute | solution.py:25
  91.1 5.8 %collective-permute-done.21 = bf16[128,1024]{1,0:T(8,128)(2,1)S(1)} collective-permute-done((bf16[128,1024]{1,0:T(8,128)(2,1)S(1)}, bf16[128,1024]{1,0:T(8,128)(2,1)S(1)}, u32[]{:S(2)}, u32[]{:S(2)}) %collective-permute-start.21) | collective-permute-done | bytes 262176 | tf_op jit(solution)/shard_map/ppermute | solution.py:25
  (95 shorter events, 14.5 us)
Async XLA Ops:
  0.6 31.0 %copy-start.4 = (s32[128]{0:T(128)S(1)}, s32[128]{0:T(128)}, u32[]{:S(2)}) copy-start(s32[128]{0:T(128)} %param.10) | copy-start | bytes 1540
  0.6 31.0 %copy-start.5 = (s32[128]{0:T(128)S(1)}, s32[128]{0:T(128)}, u32[]{:S(2)}) copy-start(s32[128]{0:T(128)} %param.11) | copy-start | bytes 1540
  2.3 30.9 %copy-start.2 = (bf16[64,8192]{1,0:T(8,128)(2,1)S(1)}, bf16[64,8192]{1,0:T(8,128)(2,1)}, u32[]{:S(2)}) copy-start(bf16[64,8192]{1,0:T(8,128)(2,1)} %refs_0_.1) | copy-start | bytes 3145732
  2.3 31.3 %copy-start.1 = (bf16[128,1024]{1,0:T(8,128)(2,1)S(1)}, bf16[128,1024]{1,0:T(8,128)(2,1)}, u32[]{:S(2)}) copy-start(bf16[128,1024]{1,0:T(8,128)(2,1)} %refs_2_) | copy-start | bytes 786436
  2.6 29.0 %collective-permute-start.6 = (bf16[128,4096]{1,0:T(8,128)(2,1)S(1)}, bf16[128,4096]{1,0:T(8,128)(2,1)S(1)}, u32[]{:S(2)}, u32[]{:S(2)}) collective-permute-start(bf16[128,4096]{1,0:T(8,128)(2,1)S(1)} %shard_map.88), channel_id=1, source_target_pairs={{0,4},{4,0},{8,12},{12,8},{16,20},{20,16},{24,28},{28,24},{1,5},{5... | collective-permute-start | bytes 3145736 | tf_op jit(solution)/shard_map/ppermute | solution.py:25
  5.7 13.5 %collective-permute-start = (bf16[128,1024]{1,0:T(8,128)(2,1)}, bf16[128,1024]{1,0:T(8,128)(2,1)S(1)}, u32[]{:S(2)}, u32[]{:S(2)}) collective-permute-start(bf16[128,1024]{1,0:T(8,128)(2,1)} %refs_2_), channel_id=1, source_target_pairs={{0,8},{4,12},{8,0},{12,4},{16,24},{20,28},{24,16},{28,20},{1,9},{5... | collective-permute-start | bytes 786440 | tf_op jit(solution)/shard_map/ppermute | solution.py:25
  7.2 14.3 %collective-permute-start.4 = (bf16[128,1024]{1,0:T(8,128)(2,1)}, bf16[128,1024]{1,0:T(8,128)(2,1)S(1)}, u32[]{:S(2)}, u32[]{:S(2)}) collective-permute-start(bf16[128,1024]{1,0:T(8,128)(2,1)} %refs_2_), channel_id=1, source_target_pairs={{0,16},{4,20},{8,24},{12,28},{16,0},{20,4},{24,8},{28,12},{1,17},{... | collective-permute-start | bytes 786440 | tf_op jit(solution)/shard_map/ppermute | solution.py:25
  9.8 12.1 %collective-permute-start.3 = (bf16[128,1024]{1,0:T(8,128)(2,1)}, bf16[128,1024]{1,0:T(8,128)(2,1)S(1)}, u32[]{:S(2)}, u32[]{:S(2)}) collective-permute-start(bf16[128,1024]{1,0:T(8,128)(2,1)} %refs_2_), channel_id=1, source_target_pairs={{0,2},{1,3},{2,0},{3,1},{4,6},{5,7},{6,4},{7,5},{8,10},{9,11},{10,... | collective-permute-start | bytes 786440 | tf_op jit(solution)/shard_map/ppermute | solution.py:25
  19.1 9.2 %collective-permute-start.1 = (bf16[128,1024]{1,0:T(8,128)(2,1)S(1)}, bf16[128,1024]{1,0:T(8,128)(2,1)S(1)}, u32[]{:S(2)}, u32[]{:S(2)}) collective-permute-start(bf16[128,1024]{1,0:T(8,128)(2,1)S(1)} %collective-permute-done.refs_4_.refs_3_), channel_id=1, source_target_pairs={{0,2},{1,3},{2,0},{3,1},{4,6},{5,7},{6,4},{7,5},{8,10},{9,11},{10,... | collective-permute-start | bytes 786440 | tf_op jit(solution)/shard_map/ppermute | solution.py:25
  21.5 7.3 %collective-permute-start.5 = (bf16[128,1024]{1,0:T(8,128)(2,1)S(1)}, bf16[128,1024]{1,0:T(8,128)(2,1)S(1)}, u32[]{:S(2)}, u32[]{:S(2)}) collective-permute-start(bf16[128,1024]{1,0:T(8,128)(2,1)S(1)} %collective-permute-done.4.refs_5_.refs_4_), channel_id=1, source_target_pairs={{0,8},{4,12},{8,0},{12,4},{16,24},{20,28},{24,16},{28,20},{1,9},{5... | collective-permute-start | bytes 786440 | tf_op jit(solution)/shard_map/ppermute | solution.py:25
  22.0 9.6 %collective-permute-start.7 = (bf16[128,1024]{1,0:T(8,128)(2,1)S(1)}, bf16[128,1024]{1,0:T(8,128)(2,1)S(1)}, u32[]{:S(2)}, u32[]{:S(2)}) collective-permute-start(bf16[128,1024]{1,0:T(8,128)(2,1)S(1)} %collective-permute-done.4.refs_5_.refs_4_), channel_id=1, source_target_pairs={{0,2},{1,3},{2,0},{3,1},{4,6},{5,7},{6,4},{7,5},{8,10},{9,11},{10,... | collective-permute-start | bytes 786440 | tf_op jit(solution)/shard_map/ppermute | solution.py:25
  28.7 4.8 %collective-permute-start.2 = (bf16[128,4096]{1,0:T(8,128)(2,1)S(1)}, bf16[128,4096]{1,0:T(8,128)(2,1)S(1)}, u32[]{:S(2)}, u32[]{:S(2)}) collective-permute-start(bf16[128,4096]{1,0:T(8,128)(2,1)S(1)} %shard_map.85.refs_0_), channel_id=1, source_target_pairs={{0,1},{1,0},{2,3},{3,2},{4,5},{5,4},{6,7},{7,6},{8,9},{9,8},{10,11... | collective-permute-start | bytes 3145736 | tf_op jit(solution)/shard_map/ppermute | solution.py:25
  31.6 3.6 %collective-permute-start.8 = (bf16[128,4096]{1,0:T(8,128)(2,1)S(1)}, bf16[128,4096]{1,0:T(8,128)(2,1)S(1)}, u32[]{:S(2)}, u32[]{:S(2)}) collective-permute-start(bf16[128,4096]{1,0:T(8,128)(2,1)S(1)} %collective-permute-done.6.refs_0_.refs_3_.refs_2_), channel_id=1, source_target_pairs={{0,1},{1,0},{2,3},{3,2},{4,5},{5,4},{6,7},{7,6},{8,9},{9,8},{10,11... | collective-permute-start | bytes 3145736 | tf_op jit(solution)/shard_map/ppermute | solution.py:25
  31.6 8.8 %collective-permute-start.11 = (bf16[128,1024]{1,0:T(8,128)(2,1)S(1)}, bf16[128,1024]{1,0:T(8,128)(2,1)S(1)}, u32[]{:S(2)}, u32[]{:S(2)}) collective-permute-start(bf16[128,1024]{1,0:T(8,128)(2,1)S(1)} %collective-permute-done.5.refs_6_.refs_5_), channel_id=1, source_target_pairs={{0,2},{1,3},{2,0},{3,1},{4,6},{5,7},{6,4},{7,5},{8,10},{9,11},{10,... | collective-permute-start | bytes 786440 | tf_op jit(solution)/shard_map/ppermute | solution.py:25
  34.6 7.1 %collective-permute-start.10 = (f32[320,128]{1,0:T(8,128)S(1)}, f32[320,128]{1,0:T(8,128)S(1)}, u32[]{:S(2)}, u32[]{:S(2)}) collective-permute-start(f32[320,128]{1,0:T(8,128)S(1)} %shard_map.87), channel_id=1, source_target_pairs={{0,4},{4,0},{8,12},{12,8},{16,20},{20,16},{24,28},{28,24},{1,5},{5... | collective-permute-start | bytes 491528 | tf_op jit(solution)/shard_map/ppermute | solution.py:25
  35.2 5.2 %copy-start.3 = (bf16[64,64]{1,0:T(8,128)(2,1)S(1)}, bf16[64,64]{1,0:T(8,128)(2,1)}, u32[]{:S(2)}) copy-start(bf16[64,64]{1,0:T(8,128)(2,1)} %refs_7_.1) | copy-start | bytes 24580
  35.9 8.3 %collective-permute-start.9 = (f32[256,128]{1,0:T(8,128)S(1)}, f32[256,128]{1,0:T(8,128)S(1)}, u32[]{:S(2)}, u32[]{:S(2)}) collective-permute-start(f32[256,128]{1,0:T(8,128)S(1)} %shard_map.89), channel_id=1, source_target_pairs={{0,4},{4,0},{8,12},{12,8},{16,20},{20,16},{24,28},{28,24},{1,5},{5... | collective-permute-start | bytes 393224 | tf_op jit(solution)/shard_map/ppermute | solution.py:25
  41.0 9.5 %collective-permute-start.12 = (f32[608,128]{1,0:T(8,128)S(1)}, f32[608,128]{1,0:T(8,128)S(1)}, u32[]{:S(2)}, u32[]{:S(2)}) collective-permute-start(f32[608,128]{1,0:T(8,128)S(1)} %shard_map.91), channel_id=1, source_target_pairs={{0,4},{4,0},{8,12},{12,8},{16,20},{20,16},{24,28},{28,24},{1,5},{5... | collective-permute-start | bytes 933896 | tf_op jit(solution)/shard_map/ppermute | solution.py:25
  50.8 3.7 %collective-permute-start.13 = (f32[4,256]{1,0:T(4,128)S(1)}, f32[4,256]{1,0:T(4,128)S(1)}, u32[]{:S(2)}, u32[]{:S(2)}) collective-permute-start(f32[4,256]{1,0:T(4,128)S(1)} %maximum_maximum_fusion), channel_id=1, source_target_pairs={{0,2},{1,3},{2,0},{3,1},{4,6},{5,7},{6,4},{7,5},{8,10},{9,11},{10,... | collective-permute-start | bytes 12296 | tf_op jit(solution)/shard_map/ppermute | solution.py:25
  54.5 3.7 %collective-permute-start.14 = (f32[2,256]{1,0:T(2,128)S(1)}, f32[2,256]{1,0:T(2,128)S(1)}, u32[]{:S(2)}, u32[]{:S(2)}) collective-permute-start(f32[2,256]{1,0:T(2,128)S(1)} %pad_maximum_fusion.6), channel_id=1, source_target_pairs={{0,8},{4,12},{8,0},{12,4},{16,24},{20,28},{24,16},{28,20},{1,9},{5... | collective-permute-start | bytes 6152 | tf_op jit(solution)/shard_map/ppermute | solution.py:25
  58.2 4.5 %collective-permute-start.15 = (f32[2,256]{1,0:T(2,128)S(1)}, f32[2,256]{1,0:T(2,128)S(1)}, u32[]{:S(2)}, u32[]{:S(2)}) collective-permute-start(f32[2,256]{1,0:T(2,128)S(1)} %pad_maximum_fusion.7), channel_id=1, source_target_pairs={{0,16},{4,20},{8,24},{12,28},{16,0},{20,4},{24,8},{28,12},{1,17},{... | collective-permute-start | bytes 6152 | tf_op jit(solution)/shard_map/ppermute | solution.py:25
  63.6 7.8 %collective-permute-start.17 = (bf16[128,1024]{1,0:T(8,128)(2,1)S(1)}, bf16[128,1024]{1,0:T(8,128)(2,1)S(1)}, u32[]{:S(2)}, u32[]{:S(2)}) collective-permute-start(bf16[128,1024]{1,0:T(8,128)(2,1)S(1)} %convolution_convert_fusion.1), channel_id=1, source_target_pairs={{0,2},{1,3},{2,0},{3,1},{4,6},{5,7},{6,4},{7,5},{8,10},{9,11},{10,... | collective-permute-start | bytes 786440 | tf_op jit(solution)/shard_map/ppermute | solution.py:25
  65.0 17.2 %collective-permute-start.16 = (bf16[128,1024]{1,0:T(8,128)(2,1)S(1)}, bf16[128,1024]{1,0:T(8,128)(2,1)S(1)}, u32[]{:S(2)}, u32[]{:S(2)}) collective-permute-start(bf16[128,1024]{1,0:T(8,128)(2,1)S(1)} %convolution_convert_fusion.2), channel_id=1, source_target_pairs={{0,2},{1,3},{2,0},{3,1},{4,6},{5,7},{6,4},{7,5},{8,10},{9,11},{10,... | collective-permute-start | bytes 786440 | tf_op jit(solution)/shard_map/ppermute | solution.py:25
  71.8 9.6 %collective-permute-start.18 = (bf16[128,1024]{1,0:T(8,128)(2,1)S(1)}, bf16[128,1024]{1,0:T(8,128)(2,1)S(1)}, u32[]{:S(2)}, u32[]{:S(2)}) collective-permute-start(bf16[128,1024]{1,0:T(8,128)(2,1)S(1)} %fusion.4), channel_id=1, source_target_pairs={{0,8},{4,12},{8,0},{12,4},{16,24},{20,28},{24,16},{28,20},{1,9},{5... | collective-permute-start | bytes 786440 | tf_op jit(solution)/shard_map/ppermute | solution.py:25
  72.8 8.6 %collective-permute-start.22 = (f32[64,128]{1,0:T(8,128)S(1)}, f32[64,128]{1,0:T(8,128)S(1)}, u32[]{:S(2)}, u32[]{:S(2)}) collective-permute-start(f32[64,128]{1,0:T(8,128)S(1)} %fusion.24), channel_id=1, source_target_pairs={{0,8},{4,12},{8,0},{12,4},{16,24},{20,28},{24,16},{28,20},{1,9},{5... | collective-permute-start | bytes 98312 | tf_op jit(solution)/shard_map/ppermute | solution.py:25
  74.2 12.5 %collective-permute-start.20 = (bf16[128,1024]{1,0:T(8,128)(2,1)S(1)}, bf16[128,1024]{1,0:T(8,128)(2,1)S(1)}, u32[]{:S(2)}, u32[]{:S(2)}) collective-permute-start(bf16[128,1024]{1,0:T(8,128)(2,1)S(1)} %convolution_convert_fusion), channel_id=1, source_target_pairs={{0,2},{1,3},{2,0},{3,1},{4,6},{5,7},{6,4},{7,5},{8,10},{9,11},{10,... | collective-permute-start | bytes 786440 | tf_op jit(solution)/shard_map/ppermute | solution.py:25
  81.4 5.1 %collective-permute-start.23 = (f32[64,128]{1,0:T(8,128)S(1)}, f32[64,128]{1,0:T(8,128)S(1)}, u32[]{:S(2)}, u32[]{:S(2)}) collective-permute-start(f32[64,128]{1,0:T(8,128)S(1)} %add.157), channel_id=1, source_target_pairs={{0,16},{4,20},{8,24},{12,28},{16,0},{20,4},{24,8},{28,12},{1,17},{... | collective-permute-start | bytes 98312 | tf_op jit(solution)/shard_map/ppermute | solution.py:25
  82.6 14.7 %collective-permute-start.24 = (bf16[128,1024]{1,0:T(8,128)(2,1)S(1)}, bf16[128,1024]{1,0:T(8,128)(2,1)S(1)}, u32[]{:S(2)}, u32[]{:S(2)}) collective-permute-start(bf16[128,1024]{1,0:T(8,128)(2,1)S(1)} %fusion.3), channel_id=1, source_target_pairs={{0,16},{4,20},{8,24},{12,28},{16,0},{20,4},{24,8},{28,12},{1,17},{... | collective-permute-start | bytes 786440 | tf_op jit(solution)/shard_map/ppermute | solution.py:25
  84.8 6.4 %collective-permute-start.19 = (bf16[128,1024]{1,0:T(8,128)(2,1)S(1)}, bf16[128,1024]{1,0:T(8,128)(2,1)S(1)}, u32[]{:S(2)}, u32[]{:S(2)}) collective-permute-start(bf16[128,1024]{1,0:T(8,128)(2,1)S(1)} %convolution_convert_fusion.3), channel_id=1, source_target_pairs={{0,2},{1,3},{2,0},{3,1},{4,6},{5,7},{6,4},{7,5},{8,10},{9,11},{10,... | collective-permute-start | bytes 786440 | tf_op jit(solution)/shard_map/ppermute | solution.py:25
  86.7 1.6 %collective-permute-start.25 = (f32[64,1088]{1,0:T(8,128)S(1)}, f32[64,1088]{1,0:T(8,128)S(1)}, u32[]{:S(2)}, u32[]{:S(2)}) collective-permute-start(f32[64,1088]{1,0:T(8,128)S(1)} %pad_maximum_fusion), channel_id=1, source_target_pairs={{0,1},{1,0},{2,3},{3,2},{4,5},{5,4},{6,7},{7,6},{8,9},{9,8},{10,11... | collective-permute-start | bytes 835592 | tf_op jit(solution)/shard_map/ppermute | solution.py:25
  87.1 9.9 %collective-permute-start.21 = (bf16[128,1024]{1,0:T(8,128)(2,1)S(1)}, bf16[128,1024]{1,0:T(8,128)(2,1)S(1)}, u32[]{:S(2)}, u32[]{:S(2)}) collective-permute-start(bf16[128,1024]{1,0:T(8,128)(2,1)S(1)} %fusion.5), channel_id=1, source_target_pairs={{0,8},{4,12},{8,0},{12,4},{16,24},{20,28},{24,16},{28,20},{1,9},{5... | collective-permute-start | bytes 786440 | tf_op jit(solution)/shard_map/ppermute | solution.py:25
  88.4 8.9 %collective-permute-start.26 = (bf16[64,1088]{1,0:T(8,128)(2,1)S(1)}, bf16[64,1088]{1,0:T(8,128)(2,1)S(1)}, u32[]{:S(2)}, u32[]{:S(2)}) collective-permute-start(bf16[64,1088]{1,0:T(8,128)(2,1)S(1)} %convert_element_type.101), channel_id=1, source_target_pairs={{0,2},{1,3},{2,0},{3,1},{4,6},{5,7},{6,4},{7,5},{8,10},{9,11},{10,... | collective-permute-start | bytes 417800 | tf_op jit(solution)/shard_map/ppermute | solution.py:25
  (1 other events, 1.6 us)
